TPU v7x, 32 devices: a whole 2x2x4 slice. The times are simulated.
32 devices in a mesh: segment: 2 (over y), rows: 16 (over z, x, core).
Axes of the slice: x: 2, y: 2, z: 4, core: 2. Of those that a mesh axis runs over, the one named last changes fastest.
Arguments:
- incoming: bfloat16 [2, 64, 128, 128], P('segment', 'rows'), may hold values from -6 to 6
- cotangent: bfloat16 [2, 64, 128, 128], P('segment', 'rows'), may hold values from -6 to 6
- main_weight: bfloat16 [2, 3, 3, 128, 128], P('segment'), may hold values from -0.1875 to 0.1875
- second_weight: bfloat16 [2, 3, 3, 128, 128], P('segment'), may hold values from -0.1875 to 0.1875
Outputs:
- output: bfloat16 [2, 64, 128, 128], P('segment', 'rows')
- input_grad: bfloat16 [2, 64, 128, 128], P('segment', 'rows')
- main_grad: float32 [2, 3, 3, 128, 128], P('segment')
- second_grad: float32 [2, 3, 3, 128, 128], P('segment')
All inputs are finite; a program needn't handle non-finite values.
Results may differ from a plain program's by a relative error of at most 0.011.
Values may be sent and summed in bfloat16 or wider, within the bound.
No kernel may reach another device: no remote copies, remote signals or barrier semaphores. Data moves between devices by JAX's collectives and lax.ppermute only.
A program may use at most 64 MiB of HBM per device.

v0:
```python
import math

import jax
import jax.numpy as jnp
from jax import lax
from jax.sharding import PartitionSpec as P


def padded_2(block, sides, width):
    for axis, dim in sides:
        count = lax.axis_size(axis)
        forward = [(i, i + 1) for i in range(count - 1)]
        backward = [(target, source) for source, target in forward]
        low = lax.ppermute(
            lax.slice_in_dim(block, block.shape[dim] - width, None, axis=dim), axis, forward
        )
        high = lax.ppermute(lax.slice_in_dim(block, 0, width, axis=dim), axis, backward)
        block = jnp.concatenate([low, block, high], axis=dim)
    return block


def partner(array, axis, apart):
    return lax.ppermute(array, axis, [(i, i ^ 1 << apart) for i in range(lax.axis_size(axis))])


def silu(values):
    return values * jax.nn.sigmoid(values)


def slope(values):
    gate_value = jax.nn.sigmoid(values)
    return gate_value * (1.0 + values * (1.0 - gate_value))


def widen(padded):
    breadth = padded.shape[1]
    widened = jnp.pad(padded, ((0, 0), (1, 1), (0, 0)))
    return jnp.concatenate(
        [widened[:, 0:breadth], widened[:, 1 : breadth + 1], widened[:, 2 : breadth + 2]], axis=-1
    )


def convolve(padded, weight):
    stacked = widen(padded)
    height = padded.shape[0] - 2
    breadth = padded.shape[1]
    inner_dim = stacked.shape[-1]
    summed = jnp.zeros((height * breadth, weight.shape[-1]), jnp.float32)
    for offset in range(3):
        summed = summed + jnp.dot(
            stacked[offset : offset + height].reshape(-1, inner_dim),
            weight[offset].reshape(inner_dim, -1),
            preferred_element_type=jnp.float32,
        )
    return summed.reshape(height, breadth, -1)


def transpose_conv(padded, weight):
    return convolve(padded, jnp.flip(weight, (0, 1)).transpose(0, 1, 3, 2))


def weight_grad(padded, gradient):
    stacked = widen(padded)
    height = gradient.shape[0]
    inner_dim = stacked.shape[-1]
    outer_dim = gradient.shape[-1]
    pieces = []
    for offset in range(3):
        product = lax.dot_general(
            stacked[offset : offset + height].reshape(-1, inner_dim),
            gradient.reshape(-1, outer_dim),
            (((0,), (0,)), ((), ())),
            preferred_element_type=jnp.float32,
        )
        pieces.append(product.reshape(3, -1, outer_dim))
    return jnp.stack(pieces)


def margin(field):
    return padded_2(field, (("rows", 0),), 1)


def mirror(field, top_bit):
    return partner(field, "segment", top_bit)


def body(incoming, cotangent, main_weight, second_weight):
    source = incoming[0]
    upstream = cotangent[0]
    first_kernel = main_weight[0]
    second_kernel = second_weight[0]
    strip_rows, columns, channels = source.shape
    segments = lax.axis_size("segment")
    top_bit = segments.bit_length() - 2
    encoder = lax.axis_index("segment") < segments // 2
    nothing = jnp.zeros((strip_rows, columns, channels), jnp.float32)
    source_rim = margin(source)
    first_pre = convolve(source_rim, first_kernel)
    hidden = silu(first_pre).astype(jnp.bfloat16)
    hidden_rim = margin(hidden)
    encoder_pre = lax.cond(encoder, lambda: convolve(hidden_rim, second_kernel), lambda: nothing)
    skip_rim = margin(mirror(silu(encoder_pre).astype(jnp.bfloat16), top_bit))
    skip_pre = lax.cond(encoder, lambda: nothing, lambda: convolve(skip_rim, second_kernel))
    final_pre = jnp.where(encoder, encoder_pre, first_pre + skip_pre)
    output = silu(final_pre).astype(jnp.bfloat16)
    decoder_grad = (upstream.astype(jnp.float32) * slope(final_pre)).astype(jnp.bfloat16)
    decoder_rim = margin(decoder_grad)
    skip_grad, decoder_input = lax.cond(
        encoder,
        lambda: (nothing, nothing),
        lambda: (
            transpose_conv(decoder_rim, second_kernel),
            transpose_conv(decoder_rim, first_kernel),
        ),
    )
    returned = mirror(skip_grad.astype(jnp.bfloat16), top_bit)
    encoder_grad = (
        (upstream.astype(jnp.float32) + returned.astype(jnp.float32)) * slope(encoder_pre)
    ).astype(jnp.bfloat16)
    encoder_rim = margin(encoder_grad)
    hidden_back = lax.cond(
        encoder, lambda: transpose_conv(encoder_rim, second_kernel), lambda: nothing
    )
    hidden_grad = (hidden_back * slope(first_pre)).astype(jnp.bfloat16)
    hidden_grad_rim = margin(hidden_grad)
    encoder_input = lax.cond(
        encoder, lambda: transpose_conv(hidden_grad_rim, first_kernel), lambda: nothing
    )
    input_grad = jnp.where(encoder, encoder_input, decoder_input).astype(jnp.bfloat16)
    first_terms = weight_grad(source_rim, jnp.where(encoder, hidden_grad, decoder_grad))
    second_terms = weight_grad(
        jnp.where(encoder, hidden_rim, skip_rim), jnp.where(encoder, encoder_grad, decoder_grad)
    )
    first_sum, second_sum = lax.psum((first_terms, second_terms), "rows")
    factor = 1.0 / math.sqrt(strip_rows * lax.axis_size("rows") * columns)
    return (output[None], input_grad[None], (first_sum * factor)[None], (second_sum * factor)[None])


def solution(mesh):
    return jax.shard_map(
        body,
        mesh=mesh,
        in_specs=(
            P("segment", "rows", None, None),
            P("segment", "rows", None, None),
            P("segment", None, None, None, None),
            P("segment", None, None, None, None),
        ),
        out_specs=(
            P("segment", "rows", None, None),
            P("segment", "rows", None, None),
            P("segment", None, None, None, None),
            P("segment", None, None, None, None),
        ),
        check_vma=False,
    )
```

profile of v0, /device:TPU:0, one launch (start us, length us, event | category | flops | bytes accessed | tf_op | source)
XLA Modules:
  0.0 183.7 jit_solution(12098634100464338934)
XLA Ops:
  8.0 1.3 collective-permute-start.1
  9.3 3.0 %collective-permute-start = (bf16[1,128,128]{2,1,0:T(8,128)(2,1)S(1)}, bf16[1,128,128]{2,1,0:T(8,128)(2,1)S(1)}, u32[]{:S(2)}, u32[]{:S(2)}) collective-permute-start(bf16[1,128,128]{2,1,0:T(8,128)(2,1)S(1)} %get-tuple-element.136), channel_id=1, source_target_pairs={{0,1},{1,2},{2,3},{3,4},{4,5},{5,6},{6,7},{7,8},{8,9},{9,10},{10,1... | collective-permute-start | bytes 98312 | tf_op jit(solution)/shard_map/ppermute | solution.py:14
  12.4 1.0 fusion.25
  14.7 1.3 collective-permute-start.3
  16.0 5.1 %collective-permute-start.2 = (bf16[1,128,128]{2,1,0:T(8,128)(2,1)S(1)}, bf16[1,128,128]{2,1,0:T(8,128)(2,1)S(1)}, u32[]{:S(2)}, u32[]{:S(2)}) collective-permute-start(bf16[1,128,128]{2,1,0:T(8,128)(2,1)S(1)} %get-tuple-element.134), channel_id=1, source_target_pairs={{0,1},{1,2},{2,3},{3,4},{4,5},{5,6},{6,7},{7,8},{8,9},{9,10},{10,1... | collective-permute-start | bytes 98312 | tf_op jit(solution)/shard_map/ppermute | solution.py:14
  22.0 3.1 %conditional.5 = (f32[4,128,128]{2,1,0:T(8,128)}, f32[4,128,128]{2,1,0:T(8,128)S(1)}) conditional(s32[]{:T(128)} %convert_element_type.51, () %tuple.44, (bf16[6,128,128]{2,1,0:T(8,128)(2,1)S(1)}, bf16[3,3,128,128]{2,3,1,0:T(8,128)(2,1)S(1)}) %tuple.116), branch_computations={%region_0.1_spmd, %region_1.2_spmd} | conditional | flops 152961024 | bytes 8618000 | solution.py:101
  23.1 1.0 convolution_add_fusion
  24.1 1.0 negate_exponential_fusion
  25.1 1.0 multiply_convert_fusion.2
  26.2 5.0 %collective-permute-done.4 = bf16[4,128,128]{2,1,0:T(8,128)(2,1)S(1)} collective-permute-done((bf16[4,128,128]{2,1,0:T(8,128)(2,1)S(1)}, bf16[4,128,128]{2,1,0:T(8,128)(2,1)S(1)}, u32[]{:S(2)}, u32[]{:S(2)}) %collective-permute-start.4) | collective-permute-done | bytes 131104 | tf_op jit(solution)/shard_map/ppermute | solution.py:23
  31.2 3.3 %collective-permute-start.5 = (bf16[1,128,128]{2,1,0:T(8,128)(2,1)S(1)}, bf16[1,128,128]{2,1,0:T(8,128)(2,1)S(1)}, u32[]{:S(2)}, u32[]{:S(2)}) collective-permute-start(bf16[1,128,128]{2,1,0:T(8,128)(2,1)S(1)} %get-tuple-element.133), channel_id=1, source_target_pairs={{0,1},{1,2},{2,3},{3,4},{4,5},{5,6},{6,7},{7,8},{8,9},{9,10},{10,1... | collective-permute-start | bytes 98312 | tf_op jit(solution)/shard_map/ppermute | solution.py:14
  34.7 0.9 copy.20
  35.6 1.0 copy.19
  36.6 0.9 copy.18
  37.5 1.3 collective-permute-start.6
  38.9 6.1 %collective-permute-done.6 = bf16[1,128,128]{2,1,0:T(8,128)(2,1)S(1)} collective-permute-done((bf16[1,128,128]{2,1,0:T(8,128)(2,1)S(1)}, bf16[1,128,128]{2,1,0:T(8,128)(2,1)S(1)}, u32[]{:S(2)}, u32[]{:S(2)}) %collective-permute-start.6) | collective-permute-done | bytes 32800 | tf_op jit(solution)/shard_map/ppermute | solution.py:17
  45.9 1.1 fusion.1
  47.0 1.3 collective-permute-start.8
  48.3 5.2 %collective-permute-start.7 = (bf16[1,128,128]{2,1,0:T(8,128)(2,1)S(1)}, bf16[1,128,128]{2,1,0:T(8,128)(2,1)S(1)}, u32[]{:S(2)}, u32[]{:S(2)}) collective-permute-start(bf16[1,128,128]{2,1,0:T(8,128)(2,1)S(1)} %get-tuple-element.130), channel_id=1, source_target_pairs={{0,1},{1,2},{2,3},{3,4},{4,5},{5,6},{6,7},{7,8},{8,9},{9,10},{10,1... | collective-permute-start | bytes 98312 | tf_op jit(solution)/shard_map/ppermute | solution.py:14
  55.7 1.7 collective-permute-start.9
  58.1 3.4 %collective-permute-done.9 = bf16[4,128,128]{2,1,0:T(8,128)(2,1)} collective-permute-done((bf16[4,128,128]{2,1,0:T(8,128)(2,1)}, bf16[4,128,128]{2,1,0:T(8,128)(2,1)}, u32[]{:S(2)}, u32[]{:S(2)}) %collective-permute-start.9) | collective-permute-done | bytes 131104 | tf_op jit(solution)/shard_map/ppermute | solution.py:23
  61.5 1.1 broadcast_select_fusion.1
  62.6 1.3 collective-permute-start.11
  63.9 3.3 %collective-permute-start.10 = (bf16[1,128,128]{2,1,0:T(8,128)(2,1)S(1)}, bf16[1,128,128]{2,1,0:T(8,128)(2,1)S(1)}, u32[]{:S(2)}, u32[]{:S(2)}) collective-permute-start(bf16[1,128,128]{2,1,0:T(8,128)(2,1)S(1)} %get-tuple-element.128), channel_id=1, source_target_pairs={{0,1},{1,2},{2,3},{3,4},{4,5},{5,6},{6,7},{7,8},{8,9},{9,10},{10,1... | collective-permute-start | bytes 98312 | tf_op jit(solution)/shard_map/ppermute | solution.py:14
  68.0 0.9 pad_maximum_fusion.8
  68.9 1.2 conditional.8
  72.4 0.9 pad_maximum_fusion.6
  73.3 1.3 collective-permute-start.13
  74.6 5.6 %collective-permute-start.12 = (bf16[1,128,128]{2,1,0:T(8,128)(2,1)S(1)}, bf16[1,128,128]{2,1,0:T(8,128)(2,1)S(1)}, u32[]{:S(2)}, u32[]{:S(2)}) collective-permute-start(bf16[1,128,128]{2,1,0:T(8,128)(2,1)S(1)} %get-tuple-element.126), channel_id=1, source_target_pairs={{0,1},{1,2},{2,3},{3,4},{4,5},{5,6},{6,7},{7,8},{8,9},{9,10},{10,1... | collective-permute-start | bytes 98312 | tf_op jit(solution)/shard_map/ppermute | solution.py:14
  81.1 1.2 conditional.9
  83.0 91.4 %all-reduce.10.cloned.1.call-done = (f32[3,3,128,128]{3,2,1,0:T(8,128)}, f32[3,3,128,128]{3,2,1,0:T(8,128)}) async-done(((f32[3,3,128,128]{3,2,1,0:T(8,128)}, f32[3,3,128,128]{3,2,1,0:T(8,128)}), (f32[3,3,128,128]{3,2,1,0:T(8,128)}, f32[3,3,128,128]{3,2,1,0:T(8,128)})) %all-reduce.10.cloned.1.call-update) | async-done | bytes 1179664 | tf_op jit(solution)/shard_map/psum | solution.py:134
  174.4 2.4 %multiply_bitcast_fusion = (f32[1,3,3,128,128]{4,3,2,1,0:T(8,128)}, f32[1,3,3,128,128]{4,3,2,1,0:T(8,128)}) fusion(f32[3,3,128,128]{3,2,1,0:T(8,128)} %get-tuple-element.61, f32[3,3,128,128]{3,2,1,0:T(8,128)} %get-tuple-element.60), kind=kLoop, calls=%fused_computation.46 | loop fusion | flops 294912 | bytes 2359296 | tf_op jit(solution)/shard_map/broadcast_in_dim | solution.py:136
  (101 shorter events, 15.8 us)
Async XLA Ops:
  7.2 6.2 %copy-start.4 = (bf16[1,4,128,128]{3,2,1,0:T(8,128)(2,1)S(1)}, bf16[1,4,128,128]{3,2,1,0:T(8,128)(2,1)}, u32[]{:S(2)}) copy-start(bf16[1,4,128,128]{3,2,1,0:T(8,128)(2,1)} %param.14) | copy-start | bytes 393220
  7.2 167.3 %all-reduce.10.cloned.1.call-start = ((), (), s32[]{:S(2)}) async-start(), calls=%async_computation | async-start | bytes 2359296 | tf_op jit(solution)/shard_map/psum | solution.py:134
  8.0 5.3 %collective-permute-start.1 = (bf16[1,128,128]{2,1,0:T(8,128)(2,1)S(1)}, bf16[1,128,128]{2,1,0:T(8,128)(2,1)S(1)}, u32[]{:S(2)}, u32[]{:S(2)}) collective-permute-start(bf16[1,128,128]{2,1,0:T(8,128)(2,1)S(1)} %get-tuple-element.137), channel_id=1, source_target_pairs={{1,0},{2,1},{3,2},{4,3},{5,4},{6,5},{7,6},{8,7},{9,8},{10,9},{11,1... | collective-permute-start | bytes 98312 | tf_op jit(solution)/shard_map/ppermute | solution.py:17
  9.3 4.1 %collective-permute-start = (bf16[1,128,128]{2,1,0:T(8,128)(2,1)S(1)}, bf16[1,128,128]{2,1,0:T(8,128)(2,1)S(1)}, u32[]{:S(2)}, u32[]{:S(2)}) collective-permute-start(bf16[1,128,128]{2,1,0:T(8,128)(2,1)S(1)} %get-tuple-element.136), channel_id=1, source_target_pairs={{0,1},{1,2},{2,3},{3,4},{4,5},{5,6},{6,7},{7,8},{8,9},{9,10},{10,1... | collective-permute-start | bytes 98312 | tf_op jit(solution)/shard_map/ppermute | solution.py:14
  14.3 6.8 %copy-start.9 = (bf16[1,3,3,128,128]{4,3,2,1,0:T(8,128)(2,1)S(1)}, bf16[1,3,3,128,128]{4,3,2,1,0:T(8,128)(2,1)}, u32[]{:S(2)}) copy-start(bf16[1,3,3,128,128]{4,3,2,1,0:T(8,128)(2,1)} %param.17) | copy-start | bytes 884740
  14.7 6.6 %collective-permute-start.3 = (bf16[1,128,128]{2,1,0:T(8,128)(2,1)S(1)}, bf16[1,128,128]{2,1,0:T(8,128)(2,1)S(1)}, u32[]{:S(2)}, u32[]{:S(2)}) collective-permute-start(bf16[1,128,128]{2,1,0:T(8,128)(2,1)S(1)} %get-tuple-element.135), channel_id=1, source_target_pairs={{1,0},{2,1},{3,2},{4,3},{5,4},{6,5},{7,6},{8,7},{9,8},{10,9},{11,1... | collective-permute-start | bytes 98312 | tf_op jit(solution)/shard_map/ppermute | solution.py:17
  16.0 5.9 %collective-permute-start.2 = (bf16[1,128,128]{2,1,0:T(8,128)(2,1)S(1)}, bf16[1,128,128]{2,1,0:T(8,128)(2,1)S(1)}, u32[]{:S(2)}, u32[]{:S(2)}) collective-permute-start(bf16[1,128,128]{2,1,0:T(8,128)(2,1)S(1)} %get-tuple-element.134), channel_id=1, source_target_pairs={{0,1},{1,2},{2,3},{3,4},{4,5},{5,6},{6,7},{7,8},{8,9},{9,10},{10,1... | collective-permute-start | bytes 98312 | tf_op jit(solution)/shard_map/ppermute | solution.py:14
  25.1 9.4 %copy-start.3 = (bf16[1,3,3,128,128]{4,3,2,1,0:T(8,128)(2,1)S(1)}, bf16[1,3,3,128,128]{4,3,2,1,0:T(8,128)(2,1)}, u32[]{:S(2)}) copy-start(bf16[1,3,3,128,128]{4,3,2,1,0:T(8,128)(2,1)} %param.16) | copy-start | bytes 884740
  26.2 5.0 %collective-permute-start.4 = (bf16[4,128,128]{2,1,0:T(8,128)(2,1)S(1)}, bf16[4,128,128]{2,1,0:T(8,128)(2,1)S(1)}, u32[]{:S(2)}, u32[]{:S(2)}) collective-permute-start(bf16[4,128,128]{2,1,0:T(8,128)(2,1)S(1)} %multiply_convert_fusion.2), channel_id=1, source_target_pairs={{0,16},{16,0},{1,17},{17,1},{2,18},{18,2},{3,19},{19,3},{4,20},{20... | collective-permute-start | bytes 393224 | tf_op jit(solution)/shard_map/ppermute | solution.py:23
  31.2 7.6 %collective-permute-start.5 = (bf16[1,128,128]{2,1,0:T(8,128)(2,1)S(1)}, bf16[1,128,128]{2,1,0:T(8,128)(2,1)S(1)}, u32[]{:S(2)}, u32[]{:S(2)}) collective-permute-start(bf16[1,128,128]{2,1,0:T(8,128)(2,1)S(1)} %get-tuple-element.133), channel_id=1, source_target_pairs={{0,1},{1,2},{2,3},{3,4},{4,5},{5,6},{6,7},{7,8},{8,9},{9,10},{10,1... | collective-permute-start | bytes 98312 | tf_op jit(solution)/shard_map/ppermute | solution.py:14
  37.5 7.5 %collective-permute-start.6 = (bf16[1,128,128]{2,1,0:T(8,128)(2,1)S(1)}, bf16[1,128,128]{2,1,0:T(8,128)(2,1)S(1)}, u32[]{:S(2)}, u32[]{:S(2)}) collective-permute-start(bf16[1,128,128]{2,1,0:T(8,128)(2,1)S(1)} %get-tuple-element.132), channel_id=1, source_target_pairs={{1,0},{2,1},{3,2},{4,3},{5,4},{6,5},{7,6},{8,7},{9,8},{10,9},{11,1... | collective-permute-start | bytes 98312 | tf_op jit(solution)/shard_map/ppermute | solution.py:17
  45.0 0.9 copy-start.5
  47.0 6.7 %collective-permute-start.8 = (bf16[1,128,128]{2,1,0:T(8,128)(2,1)S(1)}, bf16[1,128,128]{2,1,0:T(8,128)(2,1)S(1)}, u32[]{:S(2)}, u32[]{:S(2)}) collective-permute-start(bf16[1,128,128]{2,1,0:T(8,128)(2,1)S(1)} %get-tuple-element.131), channel_id=1, source_target_pairs={{1,0},{2,1},{3,2},{4,3},{5,4},{6,5},{7,6},{8,7},{9,8},{10,9},{11,1... | collective-permute-start | bytes 98312 | tf_op jit(solution)/shard_map/ppermute | solution.py:17
  48.3 6.0 %collective-permute-start.7 = (bf16[1,128,128]{2,1,0:T(8,128)(2,1)S(1)}, bf16[1,128,128]{2,1,0:T(8,128)(2,1)S(1)}, u32[]{:S(2)}, u32[]{:S(2)}) collective-permute-start(bf16[1,128,128]{2,1,0:T(8,128)(2,1)S(1)} %get-tuple-element.130), channel_id=1, source_target_pairs={{0,1},{1,2},{2,3},{3,4},{4,5},{5,6},{6,7},{7,8},{8,9},{9,10},{10,1... | collective-permute-start | bytes 98312 | tf_op jit(solution)/shard_map/ppermute | solution.py:14
  55.1 0.6 copy-start.7
  55.7 5.8 %collective-permute-start.9 = (bf16[4,128,128]{2,1,0:T(8,128)(2,1)}, bf16[4,128,128]{2,1,0:T(8,128)(2,1)}, u32[]{:S(2)}, u32[]{:S(2)}) collective-permute-start(bf16[4,128,128]{2,1,0:T(8,128)(2,1)} %get-tuple-element.54), channel_id=1, source_target_pairs={{0,16},{16,0},{1,17},{17,1},{2,18},{18,2},{3,19},{19,3},{4,20},{20... | collective-permute-start | bytes 393224 | tf_op jit(solution)/shard_map/ppermute | solution.py:23
  57.9 3.6 %copy-start.6 = (bf16[1,4,128,128]{3,2,1,0:T(8,128)(2,1)S(1)}, bf16[1,4,128,128]{3,2,1,0:T(8,128)(2,1)}, u32[]{:S(2)}) copy-start(bf16[1,4,128,128]{3,2,1,0:T(8,128)(2,1)} %param.15) | copy-start | bytes 393220
  62.6 6.2 %collective-permute-start.11 = (bf16[1,128,128]{2,1,0:T(8,128)(2,1)S(1)}, bf16[1,128,128]{2,1,0:T(8,128)(2,1)S(1)}, u32[]{:S(2)}, u32[]{:S(2)}) collective-permute-start(bf16[1,128,128]{2,1,0:T(8,128)(2,1)S(1)} %get-tuple-element.129), channel_id=1, source_target_pairs={{1,0},{2,1},{3,2},{4,3},{5,4},{6,5},{7,6},{8,7},{9,8},{10,9},{11,1... | collective-permute-start | bytes 98312 | tf_op jit(solution)/shard_map/ppermute | solution.py:17
  63.9 4.9 %collective-permute-start.10 = (bf16[1,128,128]{2,1,0:T(8,128)(2,1)S(1)}, bf16[1,128,128]{2,1,0:T(8,128)(2,1)S(1)}, u32[]{:S(2)}, u32[]{:S(2)}) collective-permute-start(bf16[1,128,128]{2,1,0:T(8,128)(2,1)S(1)} %get-tuple-element.128), channel_id=1, source_target_pairs={{0,1},{1,2},{2,3},{3,4},{4,5},{5,6},{6,7},{7,8},{8,9},{9,10},{10,1... | collective-permute-start | bytes 98312 | tf_op jit(solution)/shard_map/ppermute | solution.py:14
  70.1 1.0 copy-start
  70.3 1.1 copy-start.1
  71.1 1.0 copy-start.2
  73.3 7.6 %collective-permute-start.13 = (bf16[1,128,128]{2,1,0:T(8,128)(2,1)S(1)}, bf16[1,128,128]{2,1,0:T(8,128)(2,1)S(1)}, u32[]{:S(2)}, u32[]{:S(2)}) collective-permute-start(bf16[1,128,128]{2,1,0:T(8,128)(2,1)S(1)} %get-tuple-element.127), channel_id=1, source_target_pairs={{1,0},{2,1},{3,2},{4,3},{5,4},{6,5},{7,6},{8,7},{9,8},{10,9},{11,1... | collective-permute-start | bytes 98312 | tf_op jit(solution)/shard_map/ppermute | solution.py:17
  74.6 6.4 %collective-permute-start.12 = (bf16[1,128,128]{2,1,0:T(8,128)(2,1)S(1)}, bf16[1,128,128]{2,1,0:T(8,128)(2,1)S(1)}, u32[]{:S(2)}, u32[]{:S(2)}) collective-permute-start(bf16[1,128,128]{2,1,0:T(8,128)(2,1)S(1)} %get-tuple-element.126), channel_id=1, source_target_pairs={{0,1},{1,2},{2,3},{3,4},{4,5},{5,6},{6,7},{7,8},{8,9},{9,10},{10,1... | collective-permute-start | bytes 98312 | tf_op jit(solution)/shard_map/ppermute | solution.py:14
  81.1 1.2 copy-start.8
Sparse Core Ops, SparseCore 0:
  73.4 100.9 all-reduce.9
where the time goes:
time: 184 us
  waiting for transfers between devices  107 us (58%)
  starting transfers between devices  34.9 us (19%)
  between operations  14.6 us (8%)
  local copies, waits for them, and re-layouts  10.8 us (6%)
  other arithmetic  10.5 us (6%)
  matrix products  5.42 us (3%)
    psum x1, waiting for transfers between devices, body(): first_sum, second_sum = lax.psum((first_terms, second_terms), 'rows')  91.4 us
    ppermute x6, starting transfers between devices, padded_2(): lax.ppermute(lax.slice_in_dim(block, block.shape[dim] - width, None, axis...  25.4 us
    ppermute x2, waiting for transfers between devices, partner(): lax.ppermute(array, axis, [(i, i ^ 1 << apart) for i in range(lax.axis_si...  8.32 us
    ppermute x6, starting transfers between devices, padded_2(): lax.ppermute(lax.slice_in_dim(block, 0, width, axis=dim), axis, backward)  7.73 us
    ppermute x6, waiting for transfers between devices, padded_2(): lax.ppermute(lax.slice_in_dim(block, 0, width, axis=dim), axis, backward)  6.15 us
    dot_general x12, matrix products, convolve(): jnp.dot(stacked[offset:offset + height].reshape(-1, inner_dim), weight[of...  3.88 us
  transfers between devices with their start and end apart: 15, of which 7 were waited for; matrix products, arithmetic and copies ran while one was open for 5% of the time, Pallas kernels for 0%

commit v1 on v0

--- a/solution.py
+++ b/solution.py
@@ -9,12 +9,15 @@
 def padded_2(block, sides, width):
     for axis, dim in sides:
         count = lax.axis_size(axis)
-        forward = [(i, i + 1) for i in range(count - 1)]
+        here = lax.axis_index(axis)
+        forward = [(i, (i + 1) % count) for i in range(count)]
         backward = [(target, source) for source, target in forward]
         low = lax.ppermute(
             lax.slice_in_dim(block, block.shape[dim] - width, None, axis=dim), axis, forward
         )
         high = lax.ppermute(lax.slice_in_dim(block, 0, width, axis=dim), axis, backward)
+        low = jnp.where(here > 0, low, jnp.zeros_like(low))
+        high = jnp.where(here < count - 1, high, jnp.zeros_like(high))
         block = jnp.concatenate([low, block, high], axis=dim)
     return block
 
@@ -84,6 +87,30 @@
     return partner(field, "segment", top_bit)
 
 
+def total(terms, axis):
+    count = lax.axis_size(axis)
+    here = lax.axis_index(axis)
+    bits = count.bit_length() - 1
+    current = terms
+    for bit in range(bits):
+        swap = [(i, i ^ (1 << bit)) for i in range(count)]
+        upper = (here >> bit) & 1
+        half = current.shape[0] // 2
+        kept = lax.dynamic_slice_in_dim(current, upper * half, half, 0)
+        sent = lax.dynamic_slice_in_dim(current, (1 - upper) * half, half, 0)
+        got = lax.ppermute(sent.astype(jnp.bfloat16), axis, swap)
+        current = kept + got.astype(jnp.float32)
+    current = current.astype(jnp.bfloat16)
+    for bit in reversed(range(bits)):
+        swap = [(i, i ^ (1 << bit)) for i in range(count)]
+        upper = ((here >> bit) & 1) == 1
+        got = lax.ppermute(current, axis, swap)
+        current = jnp.concatenate(
+            [jnp.where(upper, got, current), jnp.where(upper, current, got)], axis=0
+        )
+    return current.astype(jnp.float32)
+
+
 def body(incoming, cotangent, main_weight, second_weight):
     source = incoming[0]
     upstream = cotangent[0]
@@ -131,7 +158,14 @@
     second_terms = weight_grad(
         jnp.where(encoder, hidden_rim, skip_rim), jnp.where(encoder, encoder_grad, decoder_grad)
     )
-    first_sum, second_sum = lax.psum((first_terms, second_terms), "rows")
+    shape = first_terms.shape
+    flat = total(
+        jnp.concatenate(
+            [first_terms.reshape(-1, shape[-1]), second_terms.reshape(-1, shape[-1])], axis=0
+        ),
+        "rows",
+    )
+    first_sum, second_sum = flat.reshape((2,) + shape)
     factor = 1.0 / math.sqrt(strip_rows * lax.axis_size("rows") * columns)
     return (output[None], input_grad[None], (first_sum * factor)[None], (second_sum * factor)[None])
 

time: 184 us -> 104 us (0.57)
  waiting for transfers between devices: 107 us -> 63.5 us
  starting transfers between devices: 34.9 us -> 10.6 us
  between operations: 14.6 us -> 1.27 us
  local copies, waits for them, and re-layouts: 10.8 us -> 12.9 us
    psum x1 -> x0, waiting for transfers between devices: 91.4 us -> none  [body(): first_sum, second_sum = lax.psum((first_terms, second_terms), 'rows')]
    ppermute x0 -> x8, waiting for transfers between devices: none -> 29.3 us  [the longest x4 15.9 us: total(): got = lax.ppermute(sent.astype(jnp.bfloat16), axis, swap)]
    ppermute x6, starting transfers between devices: 25.4 us -> 2.29 us  [padded_2(): lax.ppermute(lax.slice_in_dim(block, block.shape[dim] - width, None, axis...]
    ppermute x6, waiting for transfers between devices: 1.3 us -> 23.9 us  [padded_2(): lax.ppermute(lax.slice_in_dim(block, block.shape[dim] - width, None, axis...]
    ppermute x6, waiting for transfers between devices: 6.15 us -> 2.58 us  [padded_2(): lax.ppermute(lax.slice_in_dim(block, 0, width, axis=dim), axis, backward)]
    broadcast_in_dim x1 -> x0, other arithmetic: 2.39 us -> none  [body(): (second_sum * factor)[None]]
    ppermute x6, starting transfers between devices: 7.73 us -> 5.66 us  [padded_2(): lax.ppermute(lax.slice_in_dim(block, 0, width, axis=dim), axis, backward)]
    unnamed x24 -> x20, local copies, waits for them, and re-layouts: 3.31 us -> 3.72 us
  transfers between devices with their start and end apart: 15 -> 22, of which waited for: 7 -> 18; matrix products, arithmetic and copies ran while one was open for 5% -> 9% of each run, Pallas kernels for 0% -> 0%
where the time goes in v1:
time: 104 us
  waiting for transfers between devices  63.5 us (61%)
  local copies, waits for them, and re-layouts  12.9 us (12%)
  starting transfers between devices  10.6 us (10%)
  other arithmetic  9.69 us (9%)
  matrix products  5.39 us (5%)
  between operations  1.27 us (1%)
    ppermute x6, waiting for transfers between devices, padded_2(): lax.ppermute(lax.slice_in_dim(block, block.shape[dim] - width, None, axis...  23.9 us
    ppermute x4, waiting for transfers between devices, total(): got = lax.ppermute(sent.astype(jnp.bfloat16), axis, swap)  15.9 us
    ppermute x4, waiting for transfers between devices, total(): got = lax.ppermute(current, axis, swap)  13.4 us
    ppermute x2, waiting for transfers between devices, partner(): lax.ppermute(array, axis, [(i, i ^ 1 << apart) for i in range(lax.axis_si...  7.74 us
    ppermute x6, starting transfers between devices, padded_2(): lax.ppermute(lax.slice_in_dim(block, 0, width, axis=dim), axis, backward)  5.66 us
    dot_general x12, matrix products, convolve(): jnp.dot(stacked[offset:offset + height].reshape(-1, inner_dim), weight[of...  3.85 us
    unnamed x20, local copies, waits for them, and re-layouts  3.72 us
    reshape x3, local copies, waits for them, and re-layouts, convolve(): stacked[offset:offset + height].reshape(-1, inner_dim)  2.83 us
  transfers between devices with their start and end apart: 22, of which 18 were waited for; matrix products, arithmetic and copies ran while one was open for 9% of the time, Pallas kernels for 0%

profile of v1, /device:TPU:0, one launch (start us, length us, event | category | flops | bytes accessed | tf_op | source)
XLA Modules:
  0.0 103.5 jit_solution(11779315470782820402)
XLA Ops:
  1.5 5.4 %collective-permute-start.1 = (bf16[1,128,128]{2,1,0:T(8,128)(2,1)S(1)}, bf16[1,128,128]{2,1,0:T(8,128)(2,1)S(1)}, u32[]{:S(2)}, u32[]{:S(2)}) collective-permute-start(bf16[1,128,128]{2,1,0:T(8,128)(2,1)S(1)} %get-tuple-element.145), channel_id=1, source_target_pairs={{1,0},{2,1},{3,2},{4,3},{5,4},{6,5},{7,6},{8,7},{9,8},{10,9},{11,1... | collective-permute-start | bytes 98312 | tf_op jit(solution)/shard_map/ppermute | solution.py:18
  6.9 1.0 fusion.29
  8.5 4.4 %collective-permute-done = bf16[1,128,128]{2,1,0:T(8,128)(2,1)S(1)} collective-permute-done((bf16[1,128,128]{2,1,0:T(8,128)(2,1)S(1)}, bf16[1,128,128]{2,1,0:T(8,128)(2,1)S(1)}, u32[]{:S(2)}, u32[]{:S(2)}) %collective-permute-start) | collective-permute-done | bytes 32800 | tf_op jit(solution)/shard_map/ppermute | solution.py:15
  12.9 1.0 fusion.12
  16.8 4.9 %collective-permute-done.2 = bf16[1,128,128]{2,1,0:T(8,128)(2,1)S(1)} collective-permute-done((bf16[1,128,128]{2,1,0:T(8,128)(2,1)S(1)}, bf16[1,128,128]{2,1,0:T(8,128)(2,1)S(1)}, u32[]{:S(2)}, u32[]{:S(2)}) %collective-permute-start.2) | collective-permute-done | bytes 32800 | tf_op jit(solution)/shard_map/ppermute | solution.py:15
  21.8 4.8 %conditional.5 = (f32[4,128,128]{2,1,0:T(8,128)}, f32[4,128,128]{2,1,0:T(8,128)S(1)}) conditional(s32[]{:T(128)} %convert_element_type.81, () %tuple.44, (bf16[6,128,128]{2,1,0:T(8,128)(2,1)S(1)}, bf16[3,3,128,128]{2,3,1,0:T(8,128)(2,1)S(1)}) %tuple.118), branch_computations={%region_0.1_spmd, %region_1.2_spmd} | conditional | flops 152961024 | bytes 8618000 | solution.py:128
  23.1 1.0 fusion.17
  24.6 1.0 convolution_add_fusion
  25.6 1.0 negate_exponential_fusion
  26.6 1.0 multiply_convert_fusion.2
  27.6 5.0 %collective-permute-done.4 = bf16[4,128,128]{2,1,0:T(8,128)(2,1)S(1)} collective-permute-done((bf16[4,128,128]{2,1,0:T(8,128)(2,1)S(1)}, bf16[4,128,128]{2,1,0:T(8,128)(2,1)S(1)}, u32[]{:S(2)}, u32[]{:S(2)}) %collective-permute-start.4) | collective-permute-done | bytes 131104 | tf_op jit(solution)/shard_map/ppermute | solution.py:26
  32.6 1.2 %copy.17 = bf16[1,3,3,128,128]{3,4,2,1,0:T(8,128)(2,1)S(1)} copy(bf16[1,3,3,128,128]{4,3,2,1,0:T(8,128)(2,1)} %param.16) | data formatting | bytes 589824 | tf_op args[2]
  33.8 0.9 copy.20
  34.7 0.9 copy.19
  35.7 0.9 copy.18
  37.1 5.5 %collective-permute-done.5 = bf16[1,128,128]{2,1,0:T(8,128)(2,1)S(1)} collective-permute-done((bf16[1,128,128]{2,1,0:T(8,128)(2,1)S(1)}, bf16[1,128,128]{2,1,0:T(8,128)(2,1)S(1)}, u32[]{:S(2)}, u32[]{:S(2)}) %collective-permute-start.5) | collective-permute-done | bytes 32800 | tf_op jit(solution)/shard_map/ppermute | solution.py:15
  43.6 1.1 %fusion.5 = (bf16[4,128,128]{2,1,0:T(8,128)(2,1)S(1)}, f32[4,128,128]{2,1,0:T(8,128)S(1)}) fusion(bf16[1,4,128,128]{3,2,1,0:T(8,128)(2,1)S(1)} %copy-done.4, f32[4,128,128]{2,1,0:T(8,128)} %get-tuple-element.52, f32[4,128,128]{2,1,0:T(8,128)S(1)} %bitcast.176, f32[4,128,128]{2,1,0:T(8,128)S(1)} %get-tuple-element.156, pred[]{:T(512)S(6)} %lt.35), kind=kLoop, calls=%fused_computation.65 | loop fusion | flops 786432 | bytes 1310721 | tf_op jit(solution)/shard_map/convert_element_type | solution.py:133
  46.4 4.5 %collective-permute-done.7 = bf16[1,128,128]{2,1,0:T(8,128)(2,1)S(1)} collective-permute-done((bf16[1,128,128]{2,1,0:T(8,128)(2,1)S(1)}, bf16[1,128,128]{2,1,0:T(8,128)(2,1)S(1)}, u32[]{:S(2)}, u32[]{:S(2)}) %collective-permute-start.7) | collective-permute-done | bytes 32800 | tf_op jit(solution)/shard_map/ppermute | solution.py:15
  52.3 1.6 %collective-permute-start.9 = (bf16[4,128,128]{2,1,0:T(8,128)(2,1)}, bf16[4,128,128]{2,1,0:T(8,128)(2,1)S(1)}, u32[]{:S(2)}, u32[]{:S(2)}) collective-permute-start(bf16[4,128,128]{2,1,0:T(8,128)(2,1)} %get-tuple-element.54), channel_id=1, source_target_pairs={{0,16},{16,0},{1,17},{17,1},{2,18},{18,2},{3,19},{19,3},{4,20},{20... | collective-permute-start | bytes 393224 | tf_op jit(solution)/shard_map/ppermute | solution.py:26
  54.7 2.8 %collective-permute-done.9 = bf16[4,128,128]{2,1,0:T(8,128)(2,1)S(1)} collective-permute-done((bf16[4,128,128]{2,1,0:T(8,128)(2,1)}, bf16[4,128,128]{2,1,0:T(8,128)(2,1)S(1)}, u32[]{:S(2)}, u32[]{:S(2)}) %collective-permute-start.9) | collective-permute-done | bytes 131104 | tf_op jit(solution)/shard_map/ppermute | solution.py:26
  57.5 1.1 %broadcast_select_fusion.5 = (bf16[4,128,128]{2,1,0:T(8,128)(2,1)S(1)}, bf16[4,128,128]{2,1,0:T(8,128)(2,1)S(1)}) fusion(bf16[4,128,128]{2,1,0:T(8,128)(2,1)S(1)} %get-tuple-element.64, pred[]{:T(512)S(6)} %lt.35, f32[4,128,128]{2,1,0:T(8,128)} %get-tuple-element.52, f32[4,128,128]{2,1,0:T(8,128)S(1)} %get-tuple-element.53, ...), kind=kLoop, calls=%fused_computation.97 | loop fusion | flops 786432 | bytes 1179649 | tf_op jit(solution)/shard_map/jit(_where)/select_n | solution.py:159
  60.2 4.5 %collective-permute-done.10 = bf16[1,128,128]{2,1,0:T(8,128)(2,1)S(1)} collective-permute-done((bf16[1,128,128]{2,1,0:T(8,128)(2,1)S(1)}, bf16[1,128,128]{2,1,0:T(8,128)(2,1)S(1)}, u32[]{:S(2)}, u32[]{:S(2)}) %collective-permute-start.10) | collective-permute-done | bytes 32800 | tf_op jit(solution)/shard_map/ppermute | solution.py:15
  64.8 1.2 %conditional.8 = (f32[4,128,128]{2,1,0:T(8,128)S(1)}) conditional(s32[]{:T(128)} %convert_element_type.81, () %tuple.49, (bf16[6,128,128]{2,1,0:T(8,128)(2,1)S(1)}, bf16[3,3,128,128]{2,3,1,0:T(8,128)(2,1)S(1)}) %tuple.121), branch_computations={%region_6.7_spmd, %region_7.8_spmd} | conditional | flops 152895488 | bytes 8093704 | solution.py:148
  68.1 1.6 %collective-permute-done.14 = bf16[1152,128]{1,0:T(8,128)(2,1)S(1)} collective-permute-done((bf16[1152,128]{1,0:T(8,128)(2,1)S(1)}, bf16[1152,128]{1,0:T(8,128)(2,1)S(1)}, u32[]{:S(2)}, u32[]{:S(2)}) %collective-permute-start.14) | collective-permute-done | bytes 294944 | tf_op jit(solution)/shard_map/ppermute | solution.py:101
  70.1 5.9 %collective-permute-done.15 = bf16[576,128]{1,0:T(8,128)(2,1)S(1)} collective-permute-done((bf16[576,128]{1,0:T(8,128)(2,1)S(1)}, bf16[576,128]{1,0:T(8,128)(2,1)S(1)}, u32[]{:S(2)}, u32[]{:S(2)}) %collective-permute-start.15) | collective-permute-done | bytes 147488 | tf_op jit(solution)/shard_map/ppermute | solution.py:101
  76.1 4.3 %collective-permute-done.16 = bf16[288,128]{1,0:T(8,128)(2,1)S(1)} collective-permute-done((bf16[288,128]{1,0:T(8,128)(2,1)S(1)}, bf16[288,128]{1,0:T(8,128)(2,1)S(1)}, u32[]{:S(2)}, u32[]{:S(2)}) %collective-permute-start.16) | collective-permute-done | bytes 73760 | tf_op jit(solution)/shard_map/ppermute | solution.py:101
  81.3 4.1 %collective-permute-done.17 = bf16[144,128]{1,0:T(8,128)(2,1)S(1)} collective-permute-done((bf16[144,128]{1,0:T(8,128)(2,1)S(1)}, bf16[144,128]{1,0:T(8,128)(2,1)S(1)}, u32[]{:S(2)}, u32[]{:S(2)}) %collective-permute-start.17) | collective-permute-done | bytes 36896 | tf_op jit(solution)/shard_map/ppermute | solution.py:101
  86.1 4.3 %collective-permute-done.18 = bf16[144,128]{1,0:T(8,128)(2,1)S(1)} collective-permute-done((bf16[144,128]{1,0:T(8,128)(2,1)S(1)}, bf16[144,128]{1,0:T(8,128)(2,1)S(1)}, u32[]{:S(2)}, u32[]{:S(2)}) %collective-permute-start.18) | collective-permute-done | bytes 36896 | tf_op jit(solution)/shard_map/ppermute | solution.py:107
  90.5 4.3 %collective-permute-done.19 = bf16[288,128]{1,0:T(8,128)(2,1)S(1)} collective-permute-done((bf16[288,128]{1,0:T(8,128)(2,1)S(1)}, bf16[288,128]{1,0:T(8,128)(2,1)S(1)}, u32[]{:S(2)}, u32[]{:S(2)}) %collective-permute-start.19) | collective-permute-done | bytes 73760 | tf_op jit(solution)/shard_map/ppermute | solution.py:107
  95.2 4.8 %collective-permute-done.20 = bf16[576,128]{1,0:T(8,128)(2,1)S(1)} collective-permute-done((bf16[576,128]{1,0:T(8,128)(2,1)S(1)}, bf16[576,128]{1,0:T(8,128)(2,1)S(1)}, u32[]{:S(2)}, u32[]{:S(2)}) %collective-permute-start.20) | collective-permute-done | bytes 147488 | tf_op jit(solution)/shard_map/ppermute | solution.py:107
  100.3 1.2 %conditional.9 = (bf16[4,128,128]{2,1,0:T(8,128)(2,1)S(1)}) conditional(s32[]{:T(128)} %convert_element_type.81, () %tuple.48, (bf16[6,128,128]{2,1,0:T(8,128)(2,1)S(1)}, bf16[3,3,128,128]{2,3,1,0:T(8,128)(2,1)S(1)}) %tuple.123), branch_computations={%region_8.9_spmd, %region_9.10_spmd} | conditional | flops 152961024 | bytes 7962632 | solution.py:153
  102.4 1.1 %slice_multiply_fusion = (f32[1152,128]{1,0:T(8,128)}, f32[1152,128]{1,0:T(8,128)}) fusion(f32[2304,128]{1,0:T(8,128)S(1)} %maximum_convert_fusion), kind=kLoop, calls=%fused_computation.50 | loop fusion | flops 294912 | bytes 2359296 | tf_op jit(solution)/shard_map/mul | solution.py:170
  (137 shorter events, 21.6 us)
Async XLA Ops:
  0.6 13.4 %copy-start.3 = (bf16[1,4,128,128]{3,2,1,0:T(8,128)(2,1)S(1)}, bf16[1,4,128,128]{3,2,1,0:T(8,128)(2,1)}, u32[]{:S(2)}) copy-start(bf16[1,4,128,128]{3,2,1,0:T(8,128)(2,1)} %param.14) | copy-start | bytes 393220
  1.5 7.0 %collective-permute-start.1 = (bf16[1,128,128]{2,1,0:T(8,128)(2,1)S(1)}, bf16[1,128,128]{2,1,0:T(8,128)(2,1)S(1)}, u32[]{:S(2)}, u32[]{:S(2)}) collective-permute-start(bf16[1,128,128]{2,1,0:T(8,128)(2,1)S(1)} %get-tuple-element.145), channel_id=1, source_target_pairs={{1,0},{2,1},{3,2},{4,3},{5,4},{6,5},{7,6},{8,7},{9,8},{10,9},{11,1... | collective-permute-start | bytes 98312 | tf_op jit(solution)/shard_map/ppermute | solution.py:18
  6.9 6.0 %collective-permute-start = (bf16[1,128,128]{2,1,0:T(8,128)(2,1)S(1)}, bf16[1,128,128]{2,1,0:T(8,128)(2,1)S(1)}, u32[]{:S(2)}, u32[]{:S(2)}) collective-permute-start(bf16[1,128,128]{2,1,0:T(8,128)(2,1)S(1)} %get-tuple-element.144), channel_id=1, source_target_pairs={{0,1},{1,2},{2,3},{3,4},{4,5},{5,6},{6,7},{7,8},{8,9},{9,10},{10,1... | collective-permute-start | bytes 98312 | tf_op jit(solution)/shard_map/ppermute | solution.py:15
  14.5 1.0 copy-start.8
  15.1 1.7 %collective-permute-start.3 = (bf16[1,128,128]{2,1,0:T(8,128)(2,1)S(1)}, bf16[1,128,128]{2,1,0:T(8,128)(2,1)S(1)}, u32[]{:S(2)}, u32[]{:S(2)}) collective-permute-start(bf16[1,128,128]{2,1,0:T(8,128)(2,1)S(1)} %get-tuple-element.143), channel_id=1, source_target_pairs={{1,0},{2,1},{3,2},{4,3},{5,4},{6,5},{7,6},{8,7},{9,8},{10,9},{11,1... | collective-permute-start | bytes 98312 | tf_op jit(solution)/shard_map/ppermute | solution.py:18
  15.7 6.1 %collective-permute-start.2 = (bf16[1,128,128]{2,1,0:T(8,128)(2,1)S(1)}, bf16[1,128,128]{2,1,0:T(8,128)(2,1)S(1)}, u32[]{:S(2)}, u32[]{:S(2)}) collective-permute-start(bf16[1,128,128]{2,1,0:T(8,128)(2,1)S(1)} %get-tuple-element.142), channel_id=1, source_target_pairs={{0,1},{1,2},{2,3},{3,4},{4,5},{5,6},{6,7},{7,8},{8,9},{9,10},{10,1... | collective-permute-start | bytes 98312 | tf_op jit(solution)/shard_map/ppermute | solution.py:15
  27.6 5.0 %collective-permute-start.4 = (bf16[4,128,128]{2,1,0:T(8,128)(2,1)S(1)}, bf16[4,128,128]{2,1,0:T(8,128)(2,1)S(1)}, u32[]{:S(2)}, u32[]{:S(2)}) collective-permute-start(bf16[4,128,128]{2,1,0:T(8,128)(2,1)S(1)} %multiply_convert_fusion.2), channel_id=1, source_target_pairs={{0,16},{16,0},{1,17},{17,1},{2,18},{18,2},{3,19},{19,3},{4,20},{20... | collective-permute-start | bytes 393224 | tf_op jit(solution)/shard_map/ppermute | solution.py:26
  32.6 4.5 %collective-permute-start.6 = (bf16[1,128,128]{2,1,0:T(8,128)(2,1)S(1)}, bf16[1,128,128]{2,1,0:T(8,128)(2,1)S(1)}, u32[]{:S(2)}, u32[]{:S(2)}) collective-permute-start(bf16[1,128,128]{2,1,0:T(8,128)(2,1)S(1)} %get-tuple-element.141), channel_id=1, source_target_pairs={{1,0},{2,1},{3,2},{4,3},{5,4},{6,5},{7,6},{8,7},{9,8},{10,9},{11,1... | collective-permute-start | bytes 98312 | tf_op jit(solution)/shard_map/ppermute | solution.py:18
  36.6 6.0 %collective-permute-start.5 = (bf16[1,128,128]{2,1,0:T(8,128)(2,1)S(1)}, bf16[1,128,128]{2,1,0:T(8,128)(2,1)S(1)}, u32[]{:S(2)}, u32[]{:S(2)}) collective-permute-start(bf16[1,128,128]{2,1,0:T(8,128)(2,1)S(1)} %get-tuple-element.140), channel_id=1, source_target_pairs={{0,1},{1,2},{2,3},{3,4},{4,5},{5,6},{6,7},{7,8},{8,9},{9,10},{10,1... | collective-permute-start | bytes 98312 | tf_op jit(solution)/shard_map/ppermute | solution.py:15
  42.7 0.9 copy-start.4
  44.7 1.7 %collective-permute-start.8 = (bf16[1,128,128]{2,1,0:T(8,128)(2,1)S(1)}, bf16[1,128,128]{2,1,0:T(8,128)(2,1)S(1)}, u32[]{:S(2)}, u32[]{:S(2)}) collective-permute-start(bf16[1,128,128]{2,1,0:T(8,128)(2,1)S(1)} %get-tuple-element.139), channel_id=1, source_target_pairs={{1,0},{2,1},{3,2},{4,3},{5,4},{6,5},{7,6},{8,7},{9,8},{10,9},{11,1... | collective-permute-start | bytes 98312 | tf_op jit(solution)/shard_map/ppermute | solution.py:18
  44.8 6.1 %collective-permute-start.7 = (bf16[1,128,128]{2,1,0:T(8,128)(2,1)S(1)}, bf16[1,128,128]{2,1,0:T(8,128)(2,1)S(1)}, u32[]{:S(2)}, u32[]{:S(2)}) collective-permute-start(bf16[1,128,128]{2,1,0:T(8,128)(2,1)S(1)} %get-tuple-element.138), channel_id=1, source_target_pairs={{0,1},{1,2},{2,3},{3,4},{4,5},{5,6},{6,7},{7,8},{8,9},{9,10},{10,1... | collective-permute-start | bytes 98312 | tf_op jit(solution)/shard_map/ppermute | solution.py:15
  51.6 0.7 copy-start.6
  52.3 5.2 %collective-permute-start.9 = (bf16[4,128,128]{2,1,0:T(8,128)(2,1)}, bf16[4,128,128]{2,1,0:T(8,128)(2,1)S(1)}, u32[]{:S(2)}, u32[]{:S(2)}) collective-permute-start(bf16[4,128,128]{2,1,0:T(8,128)(2,1)} %get-tuple-element.54), channel_id=1, source_target_pairs={{0,16},{16,0},{1,17},{17,1},{2,18},{18,2},{3,19},{19,3},{4,20},{20... | collective-permute-start | bytes 393224 | tf_op jit(solution)/shard_map/ppermute | solution.py:26
  54.1 3.4 %copy-start.5 = (bf16[1,4,128,128]{3,2,1,0:T(8,128)(2,1)S(1)}, bf16[1,4,128,128]{3,2,1,0:T(8,128)(2,1)}, u32[]{:S(2)}) copy-start(bf16[1,4,128,128]{3,2,1,0:T(8,128)(2,1)} %param.15) | copy-start | bytes 393220
  58.6 1.7 %collective-permute-start.11 = (bf16[1,128,128]{2,1,0:T(8,128)(2,1)S(1)}, bf16[1,128,128]{2,1,0:T(8,128)(2,1)S(1)}, u32[]{:S(2)}, u32[]{:S(2)}) collective-permute-start(bf16[1,128,128]{2,1,0:T(8,128)(2,1)S(1)} %get-tuple-element.137), channel_id=1, source_target_pairs={{1,0},{2,1},{3,2},{4,3},{5,4},{6,5},{7,6},{8,7},{9,8},{10,9},{11,1... | collective-permute-start | bytes 98312 | tf_op jit(solution)/shard_map/ppermute | solution.py:18
  58.6 6.1 %collective-permute-start.10 = (bf16[1,128,128]{2,1,0:T(8,128)(2,1)S(1)}, bf16[1,128,128]{2,1,0:T(8,128)(2,1)S(1)}, u32[]{:S(2)}, u32[]{:S(2)}) collective-permute-start(bf16[1,128,128]{2,1,0:T(8,128)(2,1)S(1)} %get-tuple-element.136), channel_id=1, source_target_pairs={{0,1},{1,2},{2,3},{3,4},{4,5},{5,6},{6,7},{7,8},{8,9},{9,10},{10,1... | collective-permute-start | bytes 98312 | tf_op jit(solution)/shard_map/ppermute | solution.py:15
  64.8 1.4 %copy-start = (bf16[512,384]{0,1:T(8,128)(2,1)S(1)}, bf16[512,384]{0,1:T(8,128)(2,1)}, u32[]{:S(2)}) copy-start(bf16[512,384]{0,1:T(8,128)(2,1)} %copy.20) | copy-start | bytes 1179652
  66.0 1.0 copy-start.1
  66.0 1.3 %copy-start.2 = (bf16[512,384]{0,1:T(8,128)(2,1)S(1)}, bf16[512,384]{0,1:T(8,128)(2,1)}, u32[]{:S(2)}) copy-start(bf16[512,384]{0,1:T(8,128)(2,1)} %copy.18) | copy-start | bytes 1179652
  68.0 1.6 %collective-permute-start.14 = (bf16[1152,128]{1,0:T(8,128)(2,1)S(1)}, bf16[1152,128]{1,0:T(8,128)(2,1)S(1)}, u32[]{:S(2)}, u32[]{:S(2)}) collective-permute-start(bf16[1152,128]{1,0:T(8,128)(2,1)S(1)} %fusion.1), channel_id=1, source_target_pairs={{0,1},{1,0},{2,3},{3,2},{4,5},{5,4},{6,7},{7,6},{8,9},{9,8},{10,11... | collective-permute-start | bytes 884744 | tf_op jit(solution)/shard_map/ppermute | solution.py:101
  70.0 6.0 %collective-permute-start.15 = (bf16[576,128]{1,0:T(8,128)(2,1)S(1)}, bf16[576,128]{1,0:T(8,128)(2,1)S(1)}, u32[]{:S(2)}, u32[]{:S(2)}) collective-permute-start(bf16[576,128]{1,0:T(8,128)(2,1)S(1)} %dynamic-slice_convert_fusion), channel_id=1, source_target_pairs={{0,2},{1,3},{2,0},{3,1},{4,6},{5,7},{6,4},{7,5},{8,10},{9,11},{10,... | collective-permute-start | bytes 442376 | tf_op jit(solution)/shard_map/ppermute | solution.py:101
  76.0 4.4 %collective-permute-start.16 = (bf16[288,128]{1,0:T(8,128)(2,1)S(1)}, bf16[288,128]{1,0:T(8,128)(2,1)S(1)}, u32[]{:S(2)}, u32[]{:S(2)}) collective-permute-start(bf16[288,128]{1,0:T(8,128)(2,1)S(1)} %dynamic-slice_convert_fusion.1), channel_id=1, source_target_pairs={{0,4},{1,5},{2,6},{3,7},{4,0},{5,1},{6,2},{7,3},{8,12},{9,13},{10,... | collective-permute-start | bytes 221192 | tf_op jit(solution)/shard_map/ppermute | solution.py:101
  80.5 4.9 %collective-permute-start.17 = (bf16[144,128]{1,0:T(8,128)(2,1)S(1)}, bf16[144,128]{1,0:T(8,128)(2,1)S(1)}, u32[]{:S(2)}, u32[]{:S(2)}) collective-permute-start(bf16[144,128]{1,0:T(8,128)(2,1)S(1)} %dynamic-slice_convert_fusion.2), channel_id=1, source_target_pairs={{0,8},{1,9},{2,10},{3,11},{4,12},{5,13},{6,14},{7,15},{8,0},{9,1},... | collective-permute-start | bytes 110600 | tf_op jit(solution)/shard_map/ppermute | solution.py:101
  85.4 4.9 %collective-permute-start.18 = (bf16[144,128]{1,0:T(8,128)(2,1)S(1)}, bf16[144,128]{1,0:T(8,128)(2,1)S(1)}, u32[]{:S(2)}, u32[]{:S(2)}) collective-permute-start(bf16[144,128]{1,0:T(8,128)(2,1)S(1)} %add_convert_fusion), channel_id=1, source_target_pairs={{0,8},{1,9},{2,10},{3,11},{4,12},{5,13},{6,14},{7,15},{8,0},{9,1},... | collective-permute-start | bytes 110600 | tf_op jit(solution)/shard_map/ppermute | solution.py:107
  85.5 4.9 %collective-permute-start.13 = (bf16[1,128,128]{2,1,0:T(8,128)(2,1)S(1)}, bf16[1,128,128]{2,1,0:T(8,128)(2,1)S(1)}, u32[]{:S(2)}, u32[]{:S(2)}) collective-permute-start(bf16[1,128,128]{2,1,0:T(8,128)(2,1)S(1)} %get-tuple-element.135), channel_id=1, source_target_pairs={{1,0},{2,1},{3,2},{4,3},{5,4},{6,5},{7,6},{8,7},{9,8},{10,9},{11,1... | collective-permute-start | bytes 98312 | tf_op jit(solution)/shard_map/ppermute | solution.py:18
  85.6 9.6 %collective-permute-start.12 = (bf16[1,128,128]{2,1,0:T(8,128)(2,1)S(1)}, bf16[1,128,128]{2,1,0:T(8,128)(2,1)S(1)}, u32[]{:S(2)}, u32[]{:S(2)}) collective-permute-start(bf16[1,128,128]{2,1,0:T(8,128)(2,1)S(1)} %get-tuple-element.134), channel_id=1, source_target_pairs={{0,1},{1,2},{2,3},{3,4},{4,5},{5,6},{6,7},{7,8},{8,9},{9,10},{10,1... | collective-permute-start | bytes 98312 | tf_op jit(solution)/shard_map/ppermute | solution.py:15
  90.4 4.4 %collective-permute-start.19 = (bf16[288,128]{1,0:T(8,128)(2,1)S(1)}, bf16[288,128]{1,0:T(8,128)(2,1)S(1)}, u32[]{:S(2)}, u32[]{:S(2)}) collective-permute-start(bf16[288,128]{1,0:T(8,128)(2,1)S(1)} %pad_maximum_fusion.16), channel_id=1, source_target_pairs={{0,4},{1,5},{2,6},{3,7},{4,0},{5,1},{6,2},{7,3},{8,12},{9,13},{10,... | collective-permute-start | bytes 221192 | tf_op jit(solution)/shard_map/ppermute | solution.py:107
  94.8 5.2 %collective-permute-start.20 = (bf16[576,128]{1,0:T(8,128)(2,1)S(1)}, bf16[576,128]{1,0:T(8,128)(2,1)S(1)}, u32[]{:S(2)}, u32[]{:S(2)}) collective-permute-start(bf16[576,128]{1,0:T(8,128)(2,1)S(1)} %pad_maximum_fusion.15), channel_id=1, source_target_pairs={{0,2},{1,3},{2,0},{3,1},{4,6},{5,7},{6,4},{7,5},{8,10},{9,11},{10,... | collective-permute-start | bytes 442376 | tf_op jit(solution)/shard_map/ppermute | solution.py:107
  100.2 2.0 %collective-permute-start.21 = (bf16[1152,128]{1,0:T(8,128)(2,1)S(1)}, bf16[1152,128]{1,0:T(8,128)(2,1)S(1)}, u32[]{:S(2)}, u32[]{:S(2)}) collective-permute-start(bf16[1152,128]{1,0:T(8,128)(2,1)S(1)} %pad_maximum_fusion.9), channel_id=1, source_target_pairs={{0,1},{1,0},{2,3},{3,2},{4,5},{5,4},{6,7},{7,6},{8,9},{9,8},{10,11... | collective-permute-start | bytes 884744 | tf_op jit(solution)/shard_map/ppermute | solution.py:107
  100.3 1.2 %copy-start.7 = (bf16[4,128,128]{2,1,0:T(8,128)(2,1)S(1)}, bf16[4,128,128]{2,1,0:T(8,128)(2,1)}, u32[]{:S(2)}) copy-start(bf16[4,128,128]{2,1,0:T(8,128)(2,1)} %copy-done.6) | copy-start | bytes 393220

commit v2 on v0

v2 whole, which is shorter than its diff:
```python
import functools
import math

import jax
import jax.numpy as jnp
from jax import lax
from jax.experimental import pallas as pl
from jax.experimental.pallas import tpu as pltpu
from jax.sharding import PartitionSpec as P

BF16 = jnp.bfloat16
F32 = jnp.float32
TAPS = [(ty, tx) for ty in range(3) for tx in range(3)]


def silu(values):
    return values * jax.nn.sigmoid(values)


def slope(values):
    gate_value = jax.nn.sigmoid(values)
    return gate_value * (1.0 + values * (1.0 - gate_value))


def place(wide, row, values):
    columns, channels = values.shape
    column = lax.broadcasted_iota(jnp.int32, (columns, channels), 0)
    left = jnp.where(column == 0, 0.0, pltpu.roll(values, 1, 0))
    right = jnp.where(column == columns - 1, 0.0, pltpu.roll(values, columns - 1, 0))
    wide[row, :, 0:channels] = left.astype(BF16)
    wide[row, :, channels : 2 * channels] = values.astype(BF16)
    wide[row, :, 2 * channels : 3 * channels] = right.astype(BF16)


def stacked(wide, start, rows):
    parts = [wide[start + ty : start + ty + rows] for ty in range(3)]
    return jnp.concatenate([part.reshape(rows * part.shape[1], part.shape[2]) for part in parts], axis=1)


def conv(wide, start, rows, kernel):
    lhs = stacked(wide, start, rows)
    out = jnp.dot(lhs, kernel[...].reshape(-1, kernel.shape[-1]), preferred_element_type=F32)
    return out.reshape(rows, -1, out.shape[-1])


def conv_back(wide, start, rows, kernel):
    lhs = stacked(wide, start, rows)
    rhs = jnp.concatenate([kernel[2 - ty, 2 - tx] for ty, tx in TAPS], axis=1)
    out = lax.dot_general(lhs, rhs, (((1,), (1,)), ((), ())), preferred_element_type=F32)
    return out.reshape(rows, -1, out.shape[-1])


def conv_weight(field, wide, start, store):
    rows, columns, channels = field.shape
    lhs = field.reshape(rows * columns, channels)
    for ty in range(3):
        rhs = wide[start + 2 - ty : start + 2 - ty + rows]
        out = lax.dot_general(
            lhs, rhs.reshape(rows * columns, -1), (((0,), (0,)), ((), ())), preferred_element_type=F32
        )
        for tx in range(3):
            store(ty, tx, out[:, (2 - tx) * channels : (3 - tx) * channels])


def here(segments):
    row = lax.axis_index("rows")
    return lax.axis_index("segment") < segments // 2, row, lax.rem(row, 2) == 0


def inside(row, strips, own, offset):
    if offset < 0:
        return row > 0
    if offset >= own:
        return row < strips - 1
    return None


def masked(values, keep):
    return values if keep is None else jnp.where(keep, values, 0.0)


def front_kernel(segments, strips, x, x_core, x_other, main, second, pre1, pre2, hid, skip, xw, hw):
    encoder, row, even = here(segments)
    own = x.shape[0]
    core_at = jnp.where(even, 2 * own, 0)
    other_at = jnp.where(even, 0, 2 * own)
    core_in = jnp.where(even, row < strips - 1, row > 0)
    other_in = jnp.where(even, row > 0, row < strips - 1)
    for i in range(own):
        place(xw, own + i, x[i].astype(F32))
        place(xw, core_at + i, masked(x_core[i].astype(F32), core_in))
        place(xw, other_at + i, masked(x_other[i].astype(F32), other_in))

    @pl.when(encoder)
    def _():
        first = conv(xw, 0, own + 6, main)
        pre1[...] = first[2 : own + 4]
        for i in range(own + 6):
            value = masked(silu(first[i]), inside(row, strips, own, i - 3))
            place(hw, i, value)
            if 3 <= i < own + 3:
                hid[i - 3] = value.astype(BF16)
        final = conv(hw, 0, own + 4, second)
        pre2[...] = final
        for i in range(own + 4):
            skip[i] = masked(silu(final[i]), inside(row, strips, own, i - 2)).astype(BF16)

    @pl.when(jnp.logical_not(encoder))
    def _():
        pre1[...] = conv(xw, 2, own + 2, main)


def middle_kernel(
    segments, strips, skip_here, skip_there, pre1, g, g_core, g_other, second, out, grad, back, edge_core, edge_other, yw, gw
):
    encoder, row, even = here(segments)
    own = g.shape[0]

    @pl.when(encoder)
    def _():
        out[...] = skip_here[2 : own + 2]

    @pl.when(jnp.logical_not(encoder))
    def _():
        for i in range(own + 4):
            place(yw, i, skip_there[i].astype(F32))
        pre = pre1[...] + conv(yw, 0, own + 4 - 2, second)
        for i in range(own + 2):
            if i == 0:
                upstream = jnp.where(even, g_other[own - 1].astype(F32), g_core[own - 1].astype(F32))
            elif i == own + 1:
                upstream = jnp.where(even, g_core[0].astype(F32), g_other[0].astype(F32))
            else:
                upstream = g[i - 1].astype(F32)
                out[i - 1] = silu(pre[i]).astype(BF16)
            value = masked(upstream * slope(pre[i]), inside(row, strips, own, i - 1))
            place(gw, i, value)
            grad[i] = value.astype(BF16)
        back[...] = conv_back(gw, 0, own, second).astype(BF16)
        edge_core[...] = jnp.where(even, back[own - 2 : own], back[0:2])
        edge_other[...] = jnp.where(even, back[0:2], back[own - 2 : own])


def end_kernel(
    segments, strips, x, g, g_core, g_other, back, back_core, back_other, pre1, pre2, hid, skip_there, grad, main, second,
    input_grad, kept, sent, ew, hw,
):
    encoder, row, even = here(segments)
    own = x.shape[0]

    def store(first):
        keep = jnp.logical_xor(even, not first)

        def put(ty, tx, values):
            @pl.when(keep)
            def _():
                kept[ty, tx] = values

            @pl.when(jnp.logical_not(keep))
            def _():
                sent[ty, tx] = values.astype(BF16)

        return put

    @pl.when(encoder)
    def _():
        for i in range(own + 4):
            if i < 2:
                upstream = jnp.where(even, g_other[own - 2 + i].astype(F32), g_core[own - 2 + i].astype(F32))
                returned = jnp.where(even, back_other[i].astype(F32), back_core[i].astype(F32))
            elif i >= own + 2:
                upstream = jnp.where(even, g_core[i - own - 2].astype(F32), g_other[i - own - 2].astype(F32))
                returned = jnp.where(
                    even, back_core[i - own - 2].astype(F32), back_other[i - own - 2].astype(F32)
                )
            else:
                upstream = g[i - 2].astype(F32)
                returned = back[i - 2].astype(F32)
            value = (upstream + returned) * slope(pre2[i])
            place(ew, i, masked(value, inside(row, strips, own, i - 2)))
        hidden_back = conv_back(ew, 0, own + 2, second)
        for i in range(own + 2):
            value = hidden_back[i] * slope(pre1[i])
            place(hw, i, masked(value, inside(row, strips, own, i - 1)))
        conv_weight(hid[...], ew, 1, store(False))

    @pl.when(jnp.logical_not(encoder))
    def _():
        for i in range(own + 2):
            place(hw, i, grad[i].astype(F32))
        conv_weight(skip_there[2 : own + 2], hw, 0, store(False))

    conv_weight(x[...], hw, 0, store(True))
    input_grad[...] = conv_back(hw, 0, own, main).astype(BF16)


def call(kernel, outs, scratch, args, flops):
    moved = sum(math.prod(a.shape) * a.dtype.itemsize for a in list(args) + outs)
    return pl.pallas_call(
        kernel,
        out_shape=outs,
        in_specs=[pl.BlockSpec(memory_space=pltpu.VMEM)] * len(args),
        out_specs=[pl.BlockSpec(memory_space=pltpu.VMEM)] * len(outs),
        scratch_shapes=scratch,
        cost_estimate=pl.CostEstimate(flops=flops, bytes_accessed=moved, transcendentals=0),
        compiler_params=pltpu.CompilerParams(vmem_limit_bytes=32 * 1024 * 1024),
    )(*args)


def body(incoming, cotangent, main_weight, second_weight):
    x, g, main, second = incoming[0], cotangent[0], main_weight[0], second_weight[0]
    own, columns, channels = x.shape
    segments, strips = lax.axis_size("segment"), lax.axis_size("rows")
    half = segments // 2
    row = lax.axis_index("rows")
    even = row % 2 == 0
    everyone = [(s, r) for s in range(segments) for r in range(strips)]

    def core(r):
        return r ^ 1

    def other(r):
        neighbour = r - 1 if r % 2 == 0 else r + 1
        return neighbour if 0 <= neighbour < strips else r

    def same(r):
        return r

    def swap(array, across, to):
        pairs = [
            (s * strips + r, ((s + half) % segments if across else s) * strips + to(r)) for s, r in everyone
        ]
        return lax.ppermute(array, ("segment", "rows"), pairs)

    def like(rows, dtype):
        return jax.ShapeDtypeStruct((rows, columns, channels), dtype)

    def wide(rows):
        return pltpu.VMEM((rows, columns, 3 * channels), BF16)

    work = 2 * columns * 9 * channels * channels
    x_other = swap(x, False, other)
    x_core = swap(x, False, core)
    g_other = swap(g, False, other)
    g_core = swap(g, False, core)
    pre1, pre2, hid, skip_here = call(
        functools.partial(front_kernel, segments, strips),
        [like(own + 2, F32), like(own + 4, F32), like(own, BF16), like(own + 4, BF16)],
        [wide(3 * own), wide(own + 6)],
        (x, x_core, x_other, main, second),
        work * (2 * own + 10),
    )
    skip_there = swap(skip_here, True, same)
    output, grad, back, edge_core, edge_other = call(
        functools.partial(middle_kernel, segments, strips),
        [like(own, BF16), like(own + 2, BF16), like(own, BF16), like(2, BF16), like(2, BF16)],
        [wide(own + 4), wide(own + 2)],
        (skip_here, skip_there, pre1, g, g_core, g_other, second),
        work * (2 * own + 2),
    )
    back_own = swap(back, True, same)
    back_other = swap(edge_other, True, other)
    back_core = swap(edge_core, True, core)
    taps = (3, 3, channels, channels)
    input_grad, kept, sent = call(
        functools.partial(end_kernel, segments, strips),
        [like(own, BF16), jax.ShapeDtypeStruct(taps, F32), jax.ShapeDtypeStruct(taps, BF16)],
        [wide(own + 4), wide(own + 2)],
        (x, g, g_core, g_other, back_own, back_core, back_other, pre1, pre2, hid, skip_there, grad, main, second),
        work * (4 * own + 2),
    )
    chips = strips // 2
    groups = [list(range(0, strips, 2)), list(range(1, strips, 2))]
    mine = (kept + swap(sent, False, core).astype(F32)).astype(BF16)
    mine = mine.reshape(chips, -1, channels)
    mine = lax.all_to_all(mine, "rows", 0, 0, axis_index_groups=groups)
    mine = jnp.sum(mine.astype(F32), axis=0).astype(BF16)
    mine = jnp.broadcast_to(mine[None], (chips,) + mine.shape)
    mine = lax.all_to_all(mine, "rows", 0, 0, axis_index_groups=groups).reshape(taps)
    theirs = swap(mine, False, core)
    factor = 1.0 / math.sqrt(own * strips * columns)
    first_sum = jnp.where(even, mine, theirs).astype(F32) * factor
    second_sum = jnp.where(even, theirs, mine).astype(F32) * factor
    return (output[None], input_grad[None], first_sum[None], second_sum[None])


def solution(mesh):
    field = P("segment", "rows", None, None)
    weight = P("segment", None, None, None, None)
    return jax.shard_map(
        body,
        mesh=mesh,
        in_specs=(field, field, weight, weight),
        out_specs=(field, field, weight, weight),
        check_vma=False,
    )
```

time: 184 us -> 70.9 us (0.39)
  waiting for transfers between devices: 107 us -> 6.14 us
  blocking collectives: 0 us -> 31.3 us
  between operations: 14.6 us -> 0.7 us
  starting transfers between devices: 34.9 us -> 21.1 us
  other arithmetic: 10.5 us -> 1.27 us
  local copies, waits for them, and re-layouts: 10.8 us -> 2.88 us
  Pallas kernels: 0 us -> 7.23 us
  matrix products: 5.42 us -> 0 us
    psum x1 -> x0, waiting for transfers between devices: 91.4 us -> none  [body(): first_sum, second_sum = lax.psum((first_terms, second_terms), 'rows')]
    all_to_all x0 -> x2, blocking collectives: none -> 31.3 us  [the longest x1 18.4 us: body(): mine = lax.all_to_all(mine, 'rows', 0, 0, axis_index_groups=groups)]
    ppermute x14 -> x10, starting transfers between devices: 34.9 us -> 21.1 us  [swap(): return lax.ppermute(array, ('segment', 'rows'), pairs)]
    ppermute x14 -> x10, waiting for transfers between devices: 15.8 us -> 6.14 us  [swap(): return lax.ppermute(array, ('segment', 'rows'), pairs)]
    pallas_call x0 -> x3, Pallas kernels: none -> 7.23 us  [call(): pl.pallas_call(kernel, out_shape=outs, in_specs=[pl.BlockSpec(memory_spac...]
    dot_general x18 -> x0, matrix products: 5.42 us -> none  [the longest x12 3.88 us: convolve(): jnp.dot(stacked[offset:offset + height].reshape(-1, inner_dim), weight[of...]
    reshape x6 -> x0, local copies, waits for them, and re-layouts: 3.41 us -> none  [the longest x3 2.84 us: convolve(): stacked[offset:offset + height].reshape(-1, inner_dim)]
    slice x20 -> x0, local copies, waits for them, and re-layouts: 3.08 us -> none  [the longest x4 1.08 us: convolve(): weight[offset].reshape(inner_dim, -1)]
  transfers between devices with their start and end apart: 15 -> 10, of which waited for: 7 -> 5; matrix products, arithmetic and copies ran while one was open for 5% -> 0% of each run, Pallas kernels for 0% -> 0%
where the time goes in v2:
time: 70.9 us; the launch traced here: 70.6 us
  blocking collectives  31.3 us (44%)
  starting transfers between devices  21.1 us (30%)
  Pallas kernels  7.23 us (10%)
  waiting for transfers between devices  6.14 us (9%)
  local copies, waits for them, and re-layouts  2.88 us (4%)
  other arithmetic  1.27 us (2%)
    ppermute x10, starting transfers between devices, swap(): return lax.ppermute(array, ('segment', 'rows'), pairs)  21.1 us
    all_to_all x1, blocking collectives, body(): mine = lax.all_to_all(mine, 'rows', 0, 0, axis_index_groups=groups)  18.4 us
    all_to_all x1, blocking collectives, body(): lax.all_to_all(mine, 'rows', 0, 0, axis_index_groups=groups).reshape(taps)  12.9 us
    pallas_call x3, Pallas kernels, call(): pl.pallas_call(kernel, out_shape=outs, in_specs=[pl.BlockSpec(memory_spac...  7.23 us
    ppermute x10, waiting for transfers between devices, swap(): return lax.ppermute(array, ('segment', 'rows'), pairs)  6.14 us
    unnamed x12, local copies, waits for them, and re-layouts  2.84 us
  transfers between devices with their start and end apart: 10, of which 5 were waited for; matrix products, arithmetic and copies ran while one was open for 0% of the time, Pallas kernels for 0%

profile of v2, /device:TPU:0, one launch (start us, length us, event | category | flops | bytes accessed | tf_op | source)
XLA Modules:
  0.0 70.6 jit_solution(3158505737772128272)
XLA Ops:
  0.6 0.5 collective-permute-start
  1.1 1.6 %collective-permute-start.1 = (bf16[4,128,128]{2,1,0:T(8,128)(2,1)}, bf16[4,128,128]{2,1,0:T(8,128)(2,1)S(1)}, u32[]{:S(2)}, u32[]{:S(2)}) collective-permute-start(bf16[4,128,128]{2,1,0:T(8,128)(2,1)} %bitcast.22), channel_id=1, source_target_pairs={{0,0},{1,2},{2,1},{3,4},{4,3},{5,6},{6,5},{7,8},{8,7},{9,10},{10,9... | collective-permute-start | bytes 393224 | tf_op jit(solution)/shard_map/ppermute | solution.py:233
  2.7 0.0 collective-permute-done.x_core
  2.7 0.0 collective-permute-done.1.x_other
  2.7 1.0 %copy-done = bf16[1,3,3,128,128]{4,3,2,1,0:T(8,128)(2,1)S(1)} copy-done((bf16[1,3,3,128,128]{4,3,2,1,0:T(8,128)(2,1)S(1)}, bf16[1,3,3,128,128]{4,3,2,1,0:T(8,128)(2,1)}, u32[]{:S(2)}) %copy-start) | copy-done | bytes 294936
  3.7 1.0 %copy-done.3 = bf16[1,3,3,128,128]{4,3,2,1,0:T(8,128)(2,1)S(1)} copy-done((bf16[1,3,3,128,128]{4,3,2,1,0:T(8,128)(2,1)S(1)}, bf16[1,3,3,128,128]{4,3,2,1,0:T(8,128)(2,1)}, u32[]{:S(2)}) %copy-start.3) | copy-done | bytes 294936
  4.6 0.9 %copy-done.5 = bf16[1,4,128,128]{3,2,1,0:T(8,128)(2,1)S(1)} copy-done((bf16[1,4,128,128]{3,2,1,0:T(8,128)(2,1)S(1)}, bf16[1,4,128,128]{3,2,1,0:T(8,128)(2,1)}, u32[]{:S(2)}) %copy-start.5) | copy-done | bytes 131096
  5.5 3.1 %shard_map.75 = (f32[6,128,128]{2,1,0:T(8,128)S(1)}, f32[8,128,128]{2,1,0:T(8,128)S(1)}, bf16[4,128,128]{2,1,0:T(8,128)(2,1)S(1)}, bf16[8,128,128]{2,1,0:T(8,128)(2,1)S(1)}) custom-call(bf16[4,128,128]{2,1,0:T(8,128)(2,1)S(1)} %bitcast.23, bf16[4,128,128]{2,1,0:T(8,128)(2,1)S(1)} %collective-permute-done.x_core, ...), custom_call_target="tpu_custom_call" | custom-call | flops 679477248 | bytes 2293760 | tf_op jit(solution)/shard_map/pallas_call | solution.py:199
  8.7 0.3 collective-permute-start.2
  9.0 5.6 %collective-permute-start.3 = (bf16[4,128,128]{2,1,0:T(8,128)(2,1)S(1)}, bf16[4,128,128]{2,1,0:T(8,128)(2,1)S(1)}, u32[]{:S(2)}, u32[]{:S(2)}) collective-permute-start(bf16[4,128,128]{2,1,0:T(8,128)(2,1)S(1)} %bitcast.15), channel_id=1, source_target_pairs={{0,1},{1,0},{2,3},{3,2},{4,5},{5,4},{6,7},{7,6},{8,9},{9,8},{10,11... | collective-permute-start | bytes 393224 | tf_op jit(solution)/shard_map/ppermute | solution.py:233
  14.7 0.7 collective-permute-start.4
  15.3 0.3 collective-permute-done.3.g_core
  15.6 0.0 collective-permute-done.4.g_other
  15.6 0.0 collective-permute-done.2.skip_there
  15.7 0.0 copy-done.1
  15.7 0.0 copy-start.4
  15.7 0.7 shard_map.76
  16.4 3.2 %collective-permute-start.5 = (bf16[4,128,128]{2,1,0:T(8,128)(2,1)S(1)}, bf16[4,128,128]{2,1,0:T(8,128)(2,1)S(1)}, u32[]{:S(2)}, u32[]{:S(2)}) collective-permute-start(bf16[4,128,128]{2,1,0:T(8,128)(2,1)S(1)} %get-tuple-element.19), channel_id=1, source_target_pairs={{0,16},{1,17},{2,18},{3,19},{4,20},{5,21},{6,22},{7,23},{8,24},{9,... | collective-permute-start | bytes 393224 | tf_op jit(solution)/shard_map/ppermute | solution.py:233
  19.6 6.9 %collective-permute-start.6 = (bf16[2,128,128]{2,1,0:T(8,128)(2,1)S(1)}, bf16[2,128,128]{2,1,0:T(8,128)(2,1)S(1)}, u32[]{:S(2)}, u32[]{:S(2)}) collective-permute-start(bf16[2,128,128]{2,1,0:T(8,128)(2,1)S(1)} %get-tuple-element.20), channel_id=1, source_target_pairs={{0,17},{1,16},{2,19},{3,18},{4,21},{5,20},{6,23},{7,22},{8,25},{9,... | collective-permute-start | bytes 196616 | tf_op jit(solution)/shard_map/ppermute | solution.py:233
  26.5 1.7 %collective-permute-start.7 = (bf16[2,128,128]{2,1,0:T(8,128)(2,1)S(1)}, bf16[2,128,128]{2,1,0:T(8,128)(2,1)S(1)}, u32[]{:S(2)}, u32[]{:S(2)}) collective-permute-start(bf16[2,128,128]{2,1,0:T(8,128)(2,1)S(1)} %get-tuple-element.21), channel_id=1, source_target_pairs={{0,16},{1,18},{2,17},{3,20},{4,19},{5,22},{6,21},{7,24},{8,23},{9,... | collective-permute-start | bytes 196616 | tf_op jit(solution)/shard_map/ppermute | solution.py:233
  28.2 1.6 %collective-permute-done.6.back_core = bf16[2,128,128]{2,1,0:T(8,128)(2,1)S(1)} collective-permute-done((bf16[2,128,128]{2,1,0:T(8,128)(2,1)S(1)}, bf16[2,128,128]{2,1,0:T(8,128)(2,1)S(1)}, u32[]{:S(2)}, u32[]{:S(2)}) %collective-permute-start.6) | collective-permute-done | bytes 65568 | tf_op jit(solution)/shard_map/ppermute | solution.py:233
  29.9 1.4 %collective-permute-done.7.back_other = bf16[2,128,128]{2,1,0:T(8,128)(2,1)S(1)} collective-permute-done((bf16[2,128,128]{2,1,0:T(8,128)(2,1)S(1)}, bf16[2,128,128]{2,1,0:T(8,128)(2,1)S(1)}, u32[]{:S(2)}, u32[]{:S(2)}) %collective-permute-start.7) | collective-permute-done | bytes 65568 | tf_op jit(solution)/shard_map/ppermute | solution.py:233
  31.3 0.0 collective-permute-done.5.back
  31.3 3.4 %shard_map.77 = (bf16[4,128,128]{2,1,0:T(8,128)(2,1)}, f32[3,3,128,128]{3,2,1,0:T(8,128)S(1)}, bf16[3,3,128,128]{3,2,1,0:T(8,128)(2,1)S(1)}) custom-call(bf16[4,128,128]{2,1,0:T(8,128)(2,1)S(1)} %bitcast.24, bf16[4,128,128]{2,1,0:T(8,128)(2,1)S(1)} %bitcast.18, bf16[4,128,128]{2,1,0:T(8,128)(2,1)S(1)} %collective-permute-done.3.g_core, ...), custom_call_target="tpu_custom_call" | custom-call | flops 679477248 | bytes 3899392 | tf_op jit(solution)/shard_map/pallas_call | solution.py:199
  34.7 0.5 collective-permute-start.8
  35.2 1.2 %collective-permute-done.8 = bf16[3,3,128,128]{3,2,1,0:T(8,128)(2,1)S(1)} collective-permute-done((bf16[3,3,128,128]{3,2,1,0:T(8,128)(2,1)S(1)}, bf16[3,3,128,128]{3,2,1,0:T(8,128)(2,1)S(1)}, u32[]{:S(2)}, u32[]{:S(2)}) %collective-permute-start.8) | collective-permute-done | bytes 294944 | tf_op jit(solution)/shard_map/ppermute | solution.py:233
  36.4 0.1 add_convert_fusion
  36.5 18.4 %all_to_all.10 = bf16[8,144,128]{2,1,0:T(8,128)(2,1)S(1)} all-to-all(bf16[8,144,128]{2,1,0:T(8,128)(2,1)S(1)} %bitcast.27), channel_id=1, replica_groups={{0,2,4,6,8,10,12,14},{1,3,5,7,9,11,13,15},{16,18,20,22,24,26,28,30},{17..., dimensions={0} | all-to-all | bytes 589824 | tf_op jit(solution)/shard_map/all_to_all | solution.py:276
  55.0 12.9 %all_to_all.11 = bf16[8,144,128]{2,1,0:T(8,128)(2,1)S(1)} all-to-all(bf16[8,144,128]{2,1,0:T(8,128)(2,1)S(1)} %broadcast_in_dim.20), channel_id=1, replica_groups={{0,2,4,6,8,10,12,14},{1,3,5,7,9,11,13,15},{16,18,20,22,24,26,28,30},{17..., dimensions={0} | all-to-all | bytes 589824 | tf_op jit(solution)/shard_map/all_to_all | solution.py:279
  67.9 0.0 collective-permute-start.9
  67.9 1.6 %collective-permute-done.9 = bf16[3,3,128,128]{3,2,1,0:T(8,128)(2,1)S(1)} collective-permute-done((bf16[3,3,128,128]{3,2,1,0:T(8,128)(2,1)S(1)}, bf16[3,3,128,128]{3,2,1,0:T(8,128)(2,1)S(1)}, u32[]{:S(2)}, u32[]{:S(2)}) %collective-permute-start.9) | collective-permute-done | bytes 294944 | tf_op jit(solution)/shard_map/ppermute | solution.py:233
  69.5 1.2 %multiply_bitcast_fusion = (f32[1,3,3,128,128]{4,3,2,1,0:T(8,128)}, f32[1,3,3,128,128]{4,3,2,1,0:T(8,128)}) fusion(bf16[3,3,128,128]{3,2,1,0:T(8,128)(2,1)S(1)} %collective-permute-done.9, bf16[3,3,128,128]{3,2,1,0:T(8,128)(2,1)S(1)} %bitcast.26, pred[]{:T(512)S(6)} %eq.5), kind=kLoop, calls=%fused_computation | loop fusion | flops 884736 | bytes 1769473 | tf_op jit(solution)/shard_map/broadcast_in_dim | solution.py:284
  (9 shorter events, 0.1 us)
Async XLA Ops:
  0.6 2.1 %collective-permute-start = (bf16[4,128,128]{2,1,0:T(8,128)(2,1)}, bf16[4,128,128]{2,1,0:T(8,128)(2,1)S(1)}, u32[]{:S(2)}, u32[]{:S(2)}) collective-permute-start(bf16[4,128,128]{2,1,0:T(8,128)(2,1)} %bitcast.21), channel_id=1, source_target_pairs={{0,1},{1,0},{2,3},{3,2},{4,5},{5,4},{6,7},{7,6},{8,9},{9,8},{10,11... | collective-permute-start | bytes 393224 | tf_op jit(solution)/shard_map/ppermute | solution.py:233
  1.1 1.6 %collective-permute-start.1 = (bf16[4,128,128]{2,1,0:T(8,128)(2,1)}, bf16[4,128,128]{2,1,0:T(8,128)(2,1)S(1)}, u32[]{:S(2)}, u32[]{:S(2)}) collective-permute-start(bf16[4,128,128]{2,1,0:T(8,128)(2,1)} %bitcast.22), channel_id=1, source_target_pairs={{0,0},{1,2},{2,1},{3,4},{4,3},{5,6},{6,5},{7,8},{8,7},{9,10},{10,9... | collective-permute-start | bytes 393224 | tf_op jit(solution)/shard_map/ppermute | solution.py:233
  2.7 1.0 %copy-start = (bf16[1,3,3,128,128]{4,3,2,1,0:T(8,128)(2,1)S(1)}, bf16[1,3,3,128,128]{4,3,2,1,0:T(8,128)(2,1)}, u32[]{:S(2)}) copy-start(bf16[1,3,3,128,128]{4,3,2,1,0:T(8,128)(2,1)} %param.7) | copy-start | bytes 884740
  3.7 1.0 %copy-start.3 = (bf16[1,3,3,128,128]{4,3,2,1,0:T(8,128)(2,1)S(1)}, bf16[1,3,3,128,128]{4,3,2,1,0:T(8,128)(2,1)}, u32[]{:S(2)}) copy-start(bf16[1,3,3,128,128]{4,3,2,1,0:T(8,128)(2,1)} %param.6) | copy-start | bytes 884740
  4.6 0.9 %copy-start.5 = (bf16[1,4,128,128]{3,2,1,0:T(8,128)(2,1)S(1)}, bf16[1,4,128,128]{3,2,1,0:T(8,128)(2,1)}, u32[]{:S(2)}) copy-start(bf16[1,4,128,128]{3,2,1,0:T(8,128)(2,1)} %param.4) | copy-start | bytes 393220
  5.5 3.5 %copy-start.2 = (bf16[1,4,128,128]{3,2,1,0:T(8,128)(2,1)S(1)}, bf16[1,4,128,128]{3,2,1,0:T(8,128)(2,1)}, u32[]{:S(2)}) copy-start(bf16[1,4,128,128]{3,2,1,0:T(8,128)(2,1)} %param.5) | copy-start | bytes 393220
  5.5 10.1 %copy-start.1 = (bf16[1,3,3,128,128]{4,3,2,1,0:T(8,128)(2,1)S(1)}, bf16[1,3,3,128,128]{4,3,2,1,0:T(8,128)(2,1)}, u32[]{:S(2)}) copy-start(bf16[1,3,3,128,128]{4,3,2,1,0:T(8,128)(2,1)} %param.7) | copy-start | bytes 884740
  8.7 7.0 %collective-permute-start.2 = (bf16[8,128,128]{2,1,0:T(8,128)(2,1)S(1)}, bf16[8,128,128]{2,1,0:T(8,128)(2,1)S(1)}, u32[]{:S(2)}, u32[]{:S(2)}) collective-permute-start(bf16[8,128,128]{2,1,0:T(8,128)(2,1)S(1)} %get-tuple-element.16.skip_here), channel_id=1, source_target_pairs={{0,16},{1,17},{2,18},{3,19},{4,20},{5,21},{6,22},{7,23},{8,24},{9,... | collective-permute-start | bytes 786440 | tf_op jit(solution)/shard_map/ppermute | solution.py:233
  9.0 6.6 %collective-permute-start.3 = (bf16[4,128,128]{2,1,0:T(8,128)(2,1)S(1)}, bf16[4,128,128]{2,1,0:T(8,128)(2,1)S(1)}, u32[]{:S(2)}, u32[]{:S(2)}) collective-permute-start(bf16[4,128,128]{2,1,0:T(8,128)(2,1)S(1)} %bitcast.15), channel_id=1, source_target_pairs={{0,1},{1,0},{2,3},{3,2},{4,5},{5,4},{6,7},{7,6},{8,9},{9,8},{10,11... | collective-permute-start | bytes 393224 | tf_op jit(solution)/shard_map/ppermute | solution.py:233
  14.7 1.0 %collective-permute-start.4 = (bf16[4,128,128]{2,1,0:T(8,128)(2,1)S(1)}, bf16[4,128,128]{2,1,0:T(8,128)(2,1)S(1)}, u32[]{:S(2)}, u32[]{:S(2)}) collective-permute-start(bf16[4,128,128]{2,1,0:T(8,128)(2,1)S(1)} %bitcast.16), channel_id=1, source_target_pairs={{0,0},{1,2},{2,1},{3,4},{4,3},{5,6},{6,5},{7,8},{8,7},{9,10},{10,9... | collective-permute-start | bytes 393224 | tf_op jit(solution)/shard_map/ppermute | solution.py:233
  15.7 15.6 %copy-start.4 = (bf16[1,3,3,128,128]{4,3,2,1,0:T(8,128)(2,1)S(1)}, bf16[1,3,3,128,128]{4,3,2,1,0:T(8,128)(2,1)}, u32[]{:S(2)}) copy-start(bf16[1,3,3,128,128]{4,3,2,1,0:T(8,128)(2,1)} %param.6) | copy-start | bytes 884740
  16.4 14.9 %collective-permute-start.5 = (bf16[4,128,128]{2,1,0:T(8,128)(2,1)S(1)}, bf16[4,128,128]{2,1,0:T(8,128)(2,1)S(1)}, u32[]{:S(2)}, u32[]{:S(2)}) collective-permute-start(bf16[4,128,128]{2,1,0:T(8,128)(2,1)S(1)} %get-tuple-element.19), channel_id=1, source_target_pairs={{0,16},{1,17},{2,18},{3,19},{4,20},{5,21},{6,22},{7,23},{8,24},{9,... | collective-permute-start | bytes 393224 | tf_op jit(solution)/shard_map/ppermute | solution.py:233
  19.6 10.3 %collective-permute-start.6 = (bf16[2,128,128]{2,1,0:T(8,128)(2,1)S(1)}, bf16[2,128,128]{2,1,0:T(8,128)(2,1)S(1)}, u32[]{:S(2)}, u32[]{:S(2)}) collective-permute-start(bf16[2,128,128]{2,1,0:T(8,128)(2,1)S(1)} %get-tuple-element.20), channel_id=1, source_target_pairs={{0,17},{1,16},{2,19},{3,18},{4,21},{5,20},{6,23},{7,22},{8,25},{9,... | collective-permute-start | bytes 196616 | tf_op jit(solution)/shard_map/ppermute | solution.py:233
  26.5 4.7 %collective-permute-start.7 = (bf16[2,128,128]{2,1,0:T(8,128)(2,1)S(1)}, bf16[2,128,128]{2,1,0:T(8,128)(2,1)S(1)}, u32[]{:S(2)}, u32[]{:S(2)}) collective-permute-start(bf16[2,128,128]{2,1,0:T(8,128)(2,1)S(1)} %get-tuple-element.21), channel_id=1, source_target_pairs={{0,16},{1,18},{2,17},{3,20},{4,19},{5,22},{6,21},{7,24},{8,23},{9,... | collective-permute-start | bytes 196616 | tf_op jit(solution)/shard_map/ppermute | solution.py:233
  34.7 1.7 %collective-permute-start.8 = (bf16[3,3,128,128]{3,2,1,0:T(8,128)(2,1)S(1)}, bf16[3,3,128,128]{3,2,1,0:T(8,128)(2,1)S(1)}, u32[]{:S(2)}, u32[]{:S(2)}) collective-permute-start(bf16[3,3,128,128]{3,2,1,0:T(8,128)(2,1)S(1)} %get-tuple-element.27), channel_id=1, source_target_pairs={{0,1},{1,0},{2,3},{3,2},{4,5},{5,4},{6,7},{7,6},{8,9},{9,8},{10,11... | collective-permute-start | bytes 884744 | tf_op jit(solution)/shard_map/ppermute | solution.py:233
  67.9 1.6 %collective-permute-start.9 = (bf16[3,3,128,128]{3,2,1,0:T(8,128)(2,1)S(1)}, bf16[3,3,128,128]{3,2,1,0:T(8,128)(2,1)S(1)}, u32[]{:S(2)}, u32[]{:S(2)}) collective-permute-start(bf16[3,3,128,128]{3,2,1,0:T(8,128)(2,1)S(1)} %bitcast.25), channel_id=1, source_target_pairs={{0,1},{1,0},{2,3},{3,2},{4,5},{5,4},{6,7},{7,6},{8,9},{9,8},{10,11... | collective-permute-start | bytes 884744 | tf_op jit(solution)/shard_map/ppermute | solution.py:233

commit v3 on v2

--- a/solution.py
+++ b/solution.py
@@ -79,24 +79,35 @@
     return values if keep is None else jnp.where(keep, values, 0.0)
 
 
-def front_kernel(segments, strips, x, x_core, x_other, main, second, pre1, pre2, hid, skip, xw, hw):
+def early_kernel(x, main, second, xw, mid):
+    own = x.shape[0]
+    for i in range(own):
+        place(xw, i, x[i].astype(F32))
+    mid[...] = conv(xw, 0, own - 2, main)
+
+
+def front_kernel(segments, strips, xo, mid, x_core, x_other, main, second, pre1, pre2, hid, skip, xw, hw):
     encoder, row, even = here(segments)
-    own = x.shape[0]
+    own = xo.shape[0]
     core_at = jnp.where(even, 2 * own, 0)
     other_at = jnp.where(even, 0, 2 * own)
     core_in = jnp.where(even, row < strips - 1, row > 0)
     other_in = jnp.where(even, row > 0, row < strips - 1)
+    xw[own : 2 * own] = xo[...]
     for i in range(own):
-        place(xw, own + i, x[i].astype(F32))
         place(xw, core_at + i, masked(x_core[i].astype(F32), core_in))
         place(xw, other_at + i, masked(x_other[i].astype(F32), other_in))
 
     @pl.when(encoder)
     def _():
-        first = conv(xw, 0, own + 6, main)
-        pre1[...] = first[2 : own + 4]
+        above = conv(xw, 0, 4, main)
+        below = conv(xw, own + 2, 4, main)
+        pre1[0:2] = above[2:4]
+        pre1[2:own] = mid[...]
+        pre1[own : own + 2] = below[0:2]
         for i in range(own + 6):
-            value = masked(silu(first[i]), inside(row, strips, own, i - 3))
+            first = above[i] if i < 4 else below[i - own - 2] if i >= own + 2 else mid[i - 4]
+            value = masked(silu(first), inside(row, strips, own, i - 3))
             place(hw, i, value)
             if 3 <= i < own + 3:
                 hid[i - 3] = value.astype(BF16)
@@ -107,7 +118,9 @@
 
     @pl.when(jnp.logical_not(encoder))
     def _():
-        pre1[...] = conv(xw, 2, own + 2, main)
+        pre1[0:2] = conv(xw, 2, 2, main)
+        pre1[2:own] = mid[...]
+        pre1[own : own + 2] = conv(xw, own + 2, 2, main)
 
 
 def middle_kernel(
@@ -127,7 +140,7 @@
         pre = pre1[...] + conv(yw, 0, own + 4 - 2, second)
         for i in range(own + 2):
             if i == 0:
-                upstream = jnp.where(even, g_other[own - 1].astype(F32), g_core[own - 1].astype(F32))
+                upstream = jnp.where(even, g_other[1].astype(F32), g_core[1].astype(F32))
             elif i == own + 1:
                 upstream = jnp.where(even, g_core[0].astype(F32), g_other[0].astype(F32))
             else:
@@ -142,8 +155,8 @@
 
 
 def end_kernel(
-    segments, strips, x, g, g_core, g_other, back, back_core, back_other, pre1, pre2, hid, skip_there, grad, main, second,
-    input_grad, kept, sent, ew, hw,
+    segments, strips, x, g, g_core, g_other, back, back_core, back_other, pre1, pre2, hid, skip_there, grad, second,
+    kept, sent, hw, ew,
 ):
     encoder, row, even = here(segments)
     own = x.shape[0]
@@ -166,7 +179,7 @@
     def _():
         for i in range(own + 4):
             if i < 2:
-                upstream = jnp.where(even, g_other[own - 2 + i].astype(F32), g_core[own - 2 + i].astype(F32))
+                upstream = jnp.where(even, g_other[i].astype(F32), g_core[i].astype(F32))
                 returned = jnp.where(even, back_other[i].astype(F32), back_core[i].astype(F32))
             elif i >= own + 2:
                 upstream = jnp.where(even, g_core[i - own - 2].astype(F32), g_other[i - own - 2].astype(F32))
@@ -191,7 +204,26 @@
         conv_weight(skip_there[2 : own + 2], hw, 0, store(False))
 
     conv_weight(x[...], hw, 0, store(True))
-    input_grad[...] = conv_back(hw, 0, own, main).astype(BF16)
+
+
+def input_kernel(hw, main, input_grad):
+    input_grad[...] = conv_back(hw, 0, input_grad.shape[0], main).astype(BF16)
+
+
+def pack_kernel(strips, kept, got, mine, *sends):
+    chip = lax.axis_index("rows") // 2
+    mine[...] = kept[chip] + got[chip].astype(F32)
+    for k, send in enumerate(sends):
+        at = jnp.bitwise_xor(chip, k + 1)
+        send[...] = (kept[at] + got[at].astype(F32)).astype(BF16)
+
+
+def unpack_kernel(strips, mine, *rest):
+    gots, out = rest[:-1], rest[-1]
+    chip = lax.axis_index("rows") // 2
+    out[chip] = mine[...]
+    for k, got in enumerate(gots):
+        out[jnp.bitwise_xor(chip, k + 1)] = got[...]
 
 
 def call(kernel, outs, scratch, args, flops):
@@ -238,18 +270,28 @@
     def wide(rows):
         return pltpu.VMEM((rows, columns, 3 * channels), BF16)
 
+    def wide_out(rows):
+        return jax.ShapeDtypeStruct((rows, columns, 3 * channels), BF16)
+
     work = 2 * columns * 9 * channels * channels
     x_other = swap(x, False, other)
     x_core = swap(x, False, core)
-    g_other = swap(g, False, other)
-    g_core = swap(g, False, core)
+    xo, mid = call(
+        early_kernel,
+        [wide_out(own), like(own - 2, F32)],
+        [],
+        (x, main, second),
+        work * (own - 2),
+    )
     pre1, pre2, hid, skip_here = call(
         functools.partial(front_kernel, segments, strips),
         [like(own + 2, F32), like(own + 4, F32), like(own, BF16), like(own + 4, BF16)],
         [wide(3 * own), wide(own + 6)],
-        (x, x_core, x_other, main, second),
-        work * (2 * own + 10),
-    )
+        (xo, mid, x_core, x_other, main, second),
+        work * (2 * own + 8),
+    )
+    g_core = swap(jnp.where(even, g[own - 2 :], g[:2]), False, core)
+    g_other = swap(jnp.where(even, g[:2], g[own - 2 :]), False, other)
     skip_there = swap(skip_here, True, same)
     output, grad, back, edge_core, edge_other = call(
         functools.partial(middle_kernel, segments, strips),
@@ -262,21 +304,36 @@
     back_other = swap(edge_other, True, other)
     back_core = swap(edge_core, True, core)
     taps = (3, 3, channels, channels)
-    input_grad, kept, sent = call(
+    kept, sent, last = call(
         functools.partial(end_kernel, segments, strips),
-        [like(own, BF16), jax.ShapeDtypeStruct(taps, F32), jax.ShapeDtypeStruct(taps, BF16)],
-        [wide(own + 4), wide(own + 2)],
-        (x, g, g_core, g_other, back_own, back_core, back_other, pre1, pre2, hid, skip_there, grad, main, second),
-        work * (4 * own + 2),
-    )
+        [jax.ShapeDtypeStruct(taps, F32), jax.ShapeDtypeStruct(taps, BF16), wide_out(own + 2)],
+        [wide(own + 4)],
+        (x, g, g_core, g_other, back_own, back_core, back_other, pre1, pre2, hid, skip_there, grad, second),
+        work * (3 * own + 2),
+    )
+    (input_grad,) = call(input_kernel, [like(own, BF16)], [], (last, main), work * own)
     chips = strips // 2
-    groups = [list(range(0, strips, 2)), list(range(1, strips, 2))]
-    mine = (kept + swap(sent, False, core).astype(F32)).astype(BF16)
-    mine = mine.reshape(chips, -1, channels)
-    mine = lax.all_to_all(mine, "rows", 0, 0, axis_index_groups=groups)
-    mine = jnp.sum(mine.astype(F32), axis=0).astype(BF16)
-    mine = jnp.broadcast_to(mine[None], (chips,) + mine.shape)
-    mine = lax.all_to_all(mine, "rows", 0, 0, axis_index_groups=groups).reshape(taps)
+    chunk = (9 * channels // chips, channels)
+    jumps = range(1, chips)
+    got = swap(sent, False, core)
+    mine, *sends = call(
+        functools.partial(pack_kernel, strips),
+        [jax.ShapeDtypeStruct(chunk, F32)] + [jax.ShapeDtypeStruct(chunk, BF16) for _ in jumps],
+        [],
+        (kept.reshape((chips,) + chunk), got.reshape((chips,) + chunk)),
+        kept.size,
+    )
+    gots = [swap(send, False, lambda r, k=k: r ^ (2 * k)) for k, send in zip(jumps, sends)]
+    mine = sum((got.astype(F32) for got in gots), mine).astype(BF16)
+    gots = [swap(mine, False, lambda r, k=k: r ^ (2 * k)) for k in jumps]
+    (mine,) = call(
+        functools.partial(unpack_kernel, strips),
+        [jax.ShapeDtypeStruct((chips,) + chunk, BF16)],
+        [],
+        (mine, *gots),
+        kept.size,
+    )
+    mine = mine.reshape(taps)
     theirs = swap(mine, False, core)
     factor = 1.0 / math.sqrt(own * strips * columns)
     first_sum = jnp.where(even, mine, theirs).astype(F32) * factor

time: 70.9 us -> 67 us (0.945)
  blocking collectives: 31.3 us -> 0 us
  starting transfers between devices: 21.1 us -> 35.1 us
  waiting for transfers between devices: 6.14 us -> 19.9 us
  Pallas kernels: 7.23 us -> 6.21 us
    all_to_all x2 -> x0, blocking collectives: 31.3 us -> none  [the longest x1 18.4 us: body(): mine = lax.all_to_all(mine, 'rows', 0, 0, axis_index_groups=groups)]
    ppermute x10 -> x24, starting transfers between devices: 21.1 us -> 35.1 us  [swap(): return lax.ppermute(array, ('segment', 'rows'), pairs)]
    ppermute x10 -> x24, waiting for transfers between devices: 6.14 us -> 19.9 us  [swap(): return lax.ppermute(array, ('segment', 'rows'), pairs)]
    pallas_call x3 -> x7, Pallas kernels: 7.23 us -> 6.21 us  [call(): pl.pallas_call(kernel, out_shape=outs, in_specs=[pl.BlockSpec(memory_spac...]
  transfers between devices with their start and end apart: 10 -> 24, of which waited for: 5 -> 13; matrix products, arithmetic and copies ran while one was open for 0% -> 0% of each run, Pallas kernels for 0% -> 2%
where the time goes in v3:
time: 67 us; the launch traced here: 66.7 us
  starting transfers between devices  35.1 us (52%)
  waiting for transfers between devices  19.9 us (30%)
  Pallas kernels  6.21 us (9%)
  local copies, waits for them, and re-layouts  3.54 us (5%)
  other arithmetic  1.22 us (2%)
  between operations  0.74 us (1%)
    ppermute x24, starting transfers between devices, swap(): return lax.ppermute(array, ('segment', 'rows'), pairs)  35.1 us
    ppermute x24, waiting for transfers between devices, swap(): return lax.ppermute(array, ('segment', 'rows'), pairs)  19.9 us
    pallas_call x7, Pallas kernels, call(): pl.pallas_call(kernel, out_shape=outs, in_specs=[pl.BlockSpec(memory_spac...  6.21 us
    unnamed x12, local copies, waits for them, and re-layouts  3.54 us
  transfers between devices with their start and end apart: 24, of which 13 were waited for; matrix products, arithmetic and copies ran while one was open for 0% of the time, Pallas kernels for 2%

profile of v3, /device:TPU:0, one launch (start us, length us, event | category | flops | bytes accessed | tf_op | source)
XLA Modules:
  0.0 66.7 jit_solution(7379406091006742157)
XLA Ops:
  0.6 1.6 %collective-permute-start.1 = (bf16[4,128,128]{2,1,0:T(8,128)(2,1)}, bf16[4,128,128]{2,1,0:T(8,128)(2,1)S(1)}, u32[]{:S(2)}, u32[]{:S(2)}) collective-permute-start(bf16[4,128,128]{2,1,0:T(8,128)(2,1)} %bitcast.29), channel_id=1, source_target_pairs={{0,0},{1,2},{2,1},{3,4},{4,3},{5,6},{6,5},{7,8},{8,7},{9,10},{10,9... | collective-permute-start | bytes 393224 | tf_op jit(solution)/shard_map/ppermute | solution.py:265
  2.2 3.5 %collective-permute-start = (bf16[4,128,128]{2,1,0:T(8,128)(2,1)}, bf16[4,128,128]{2,1,0:T(8,128)(2,1)S(1)}, u32[]{:S(2)}, u32[]{:S(2)}) collective-permute-start(bf16[4,128,128]{2,1,0:T(8,128)(2,1)} %bitcast.30), channel_id=1, source_target_pairs={{0,1},{1,0},{2,3},{3,2},{4,5},{5,4},{6,7},{7,6},{8,9},{9,8},{10,11... | collective-permute-start | bytes 393224 | tf_op jit(solution)/shard_map/ppermute | solution.py:265
  5.7 1.0 %copy-done = bf16[1,3,3,128,128]{4,3,2,1,0:T(8,128)(2,1)S(1)} copy-done((bf16[1,3,3,128,128]{4,3,2,1,0:T(8,128)(2,1)S(1)}, bf16[1,3,3,128,128]{4,3,2,1,0:T(8,128)(2,1)}, u32[]{:S(2)}) %copy-start) | copy-done | bytes 294936
  6.6 1.0 %copy-done.3 = bf16[1,3,3,128,128]{4,3,2,1,0:T(8,128)(2,1)S(1)} copy-done((bf16[1,3,3,128,128]{4,3,2,1,0:T(8,128)(2,1)S(1)}, bf16[1,3,3,128,128]{4,3,2,1,0:T(8,128)(2,1)}, u32[]{:S(2)}) %copy-start.3) | copy-done | bytes 294936
  7.6 0.9 %copy-done.5 = bf16[1,4,128,128]{3,2,1,0:T(8,128)(2,1)S(1)} copy-done((bf16[1,4,128,128]{3,2,1,0:T(8,128)(2,1)S(1)}, bf16[1,4,128,128]{3,2,1,0:T(8,128)(2,1)}, u32[]{:S(2)}) %copy-start.5) | copy-done | bytes 131096
  9.5 1.7 %shard_map.76 = (f32[6,128,128]{2,1,0:T(8,128)S(1)}, f32[8,128,128]{2,1,0:T(8,128)S(1)}, bf16[4,128,128]{2,1,0:T(8,128)(2,1)S(1)}, bf16[8,128,128]{2,1,0:T(8,128)(2,1)S(1)}) custom-call(bf16[4,128,384]{2,1,0:T(8,128)(2,1)S(1)} %get-tuple-element.26.xo, f32[2,128,128]{2,1,0:T(8,128)S(1)} %get-tuple-element.27.mid, ...), custom_call_target="tpu_custom_call" | custom-call | flops 603979776 | bytes 2686976 | tf_op jit(solution)/shard_map/pallas_call | solution.py:231
  12.5 3.4 %collective-permute-start.3 = (bf16[2,128,128]{2,1,0:T(8,128)(2,1)S(1)}, bf16[2,128,128]{2,1,0:T(8,128)(2,1)S(1)}, u32[]{:S(2)}, u32[]{:S(2)}) collective-permute-start(bf16[2,128,128]{2,1,0:T(8,128)(2,1)S(1)} %get-tuple-element.51), channel_id=1, source_target_pairs={{0,1},{1,0},{2,3},{3,2},{4,5},{5,4},{6,7},{7,6},{8,9},{9,8},{10,11... | collective-permute-start | bytes 196616 | tf_op jit(solution)/shard_map/ppermute | solution.py:265
  15.9 0.9 %collective-permute-done.3.g_core = bf16[2,128,128]{2,1,0:T(8,128)(2,1)S(1)} collective-permute-done((bf16[2,128,128]{2,1,0:T(8,128)(2,1)S(1)}, bf16[2,128,128]{2,1,0:T(8,128)(2,1)S(1)}, u32[]{:S(2)}, u32[]{:S(2)}) %collective-permute-start.3) | collective-permute-done | bytes 65568 | tf_op jit(solution)/shard_map/ppermute | solution.py:265
  16.8 2.8 %collective-permute-done.2.skip_there = bf16[8,128,128]{2,1,0:T(8,128)(2,1)S(1)} collective-permute-done((bf16[8,128,128]{2,1,0:T(8,128)(2,1)S(1)}, bf16[8,128,128]{2,1,0:T(8,128)(2,1)S(1)}, u32[]{:S(2)}, u32[]{:S(2)}) %collective-permute-start.2) | collective-permute-done | bytes 262176 | tf_op jit(solution)/shard_map/ppermute | solution.py:265
  20.3 2.0 %collective-permute-start.5 = (bf16[4,128,128]{2,1,0:T(8,128)(2,1)S(1)}, bf16[4,128,128]{2,1,0:T(8,128)(2,1)S(1)}, u32[]{:S(2)}, u32[]{:S(2)}) collective-permute-start(bf16[4,128,128]{2,1,0:T(8,128)(2,1)S(1)} %get-tuple-element.31), channel_id=1, source_target_pairs={{0,16},{1,17},{2,18},{3,19},{4,20},{5,21},{6,22},{7,23},{8,24},{9,... | collective-permute-start | bytes 393224 | tf_op jit(solution)/shard_map/ppermute | solution.py:265
  22.3 0.9 %collective-permute-start.7 = (bf16[2,128,128]{2,1,0:T(8,128)(2,1)S(1)}, bf16[2,128,128]{2,1,0:T(8,128)(2,1)S(1)}, u32[]{:S(2)}, u32[]{:S(2)}) collective-permute-start(bf16[2,128,128]{2,1,0:T(8,128)(2,1)S(1)} %get-tuple-element.33), channel_id=1, source_target_pairs={{0,16},{1,18},{2,17},{3,20},{4,19},{5,22},{6,21},{7,24},{8,23},{9,... | collective-permute-start | bytes 196616 | tf_op jit(solution)/shard_map/ppermute | solution.py:265
  23.2 4.2 %collective-permute-done.6.back_core = bf16[2,128,128]{2,1,0:T(8,128)(2,1)S(1)} collective-permute-done((bf16[2,128,128]{2,1,0:T(8,128)(2,1)S(1)}, bf16[2,128,128]{2,1,0:T(8,128)(2,1)S(1)}, u32[]{:S(2)}, u32[]{:S(2)}) %collective-permute-start.6) | collective-permute-done | bytes 65568 | tf_op jit(solution)/shard_map/ppermute | solution.py:265
  27.4 0.9 %collective-permute-done.7.back_other = bf16[2,128,128]{2,1,0:T(8,128)(2,1)S(1)} collective-permute-done((bf16[2,128,128]{2,1,0:T(8,128)(2,1)S(1)}, bf16[2,128,128]{2,1,0:T(8,128)(2,1)S(1)}, u32[]{:S(2)}, u32[]{:S(2)}) %collective-permute-start.7) | collective-permute-done | bytes 65568 | tf_op jit(solution)/shard_map/ppermute | solution.py:265
  28.3 2.3 %shard_map.78 = (f32[3,3,128,128]{3,2,1,0:T(8,128)S(1)}, bf16[3,3,128,128]{3,2,1,0:T(8,128)(2,1)S(1)}, bf16[6,128,384]{2,1,0:T(8,128)(2,1)S(1)}) custom-call(bf16[4,128,128]{2,1,0:T(8,128)(2,1)S(1)} %bitcast.32, bf16[4,128,128]{2,1,0:T(8,128)(2,1)S(1)} %bitcast.22, bf16[2,128,128]{2,1,0:T(8,128)(2,1)S(1)} %collective-permute-done.3.g_core, ...), custom_call_target="tpu_custom_call" | custom-call | flops 528482304 | bytes 3932160 | tf_op jit(solution)/shard_map/pallas_call | solution.py:231
  30.7 1.6 %collective-permute-done.8 = bf16[3,3,128,128]{3,2,1,0:T(8,128)(2,1)S(1)} collective-permute-done((bf16[3,3,128,128]{3,2,1,0:T(8,128)(2,1)S(1)}, bf16[3,3,128,128]{3,2,1,0:T(8,128)(2,1)S(1)}, u32[]{:S(2)}, u32[]{:S(2)}) %collective-permute-start.8) | collective-permute-done | bytes 294944 | tf_op jit(solution)/shard_map/ppermute | solution.py:265
  32.3 1.2 %collective-permute-start.9 = (bf16[144,128]{1,0:T(8,128)(2,1)S(1)}, bf16[144,128]{1,0:T(8,128)(2,1)S(1)}, u32[]{:S(2)}, u32[]{:S(2)}) collective-permute-start(bf16[144,128]{1,0:T(8,128)(2,1)S(1)} %get-tuple-element.41), channel_id=1, source_target_pairs={{0,2},{1,3},{2,0},{3,1},{4,6},{5,7},{6,4},{7,5},{8,10},{9,11},{10,... | collective-permute-start | bytes 110600 | tf_op jit(solution)/shard_map/ppermute | solution.py:265
  33.5 1.6 %collective-permute-start.10 = (bf16[144,128]{1,0:T(8,128)(2,1)S(1)}, bf16[144,128]{1,0:T(8,128)(2,1)S(1)}, u32[]{:S(2)}, u32[]{:S(2)}) collective-permute-start(bf16[144,128]{1,0:T(8,128)(2,1)S(1)} %get-tuple-element.42), channel_id=1, source_target_pairs={{0,4},{1,5},{2,6},{3,7},{4,0},{5,1},{6,2},{7,3},{8,12},{9,13},{10,... | collective-permute-start | bytes 110600 | tf_op jit(solution)/shard_map/ppermute | solution.py:265
  35.1 0.8 %collective-permute-start.11 = (bf16[144,128]{1,0:T(8,128)(2,1)S(1)}, bf16[144,128]{1,0:T(8,128)(2,1)S(1)}, u32[]{:S(2)}, u32[]{:S(2)}) collective-permute-start(bf16[144,128]{1,0:T(8,128)(2,1)S(1)} %get-tuple-element.43), channel_id=1, source_target_pairs={{0,6},{1,7},{2,4},{3,5},{4,2},{5,3},{6,0},{7,1},{8,14},{9,15},{10,... | collective-permute-start | bytes 110600 | tf_op jit(solution)/shard_map/ppermute | solution.py:265
  35.9 2.8 %collective-permute-start.12 = (bf16[144,128]{1,0:T(8,128)(2,1)S(1)}, bf16[144,128]{1,0:T(8,128)(2,1)S(1)}, u32[]{:S(2)}, u32[]{:S(2)}) collective-permute-start(bf16[144,128]{1,0:T(8,128)(2,1)S(1)} %get-tuple-element.44), channel_id=1, source_target_pairs={{0,8},{1,9},{2,10},{3,11},{4,12},{5,13},{6,14},{7,15},{8,0},{9,1},... | collective-permute-start | bytes 110600 | tf_op jit(solution)/shard_map/ppermute | solution.py:265
  39.4 2.6 %collective-permute-start.14 = (bf16[144,128]{1,0:T(8,128)(2,1)S(1)}, bf16[144,128]{1,0:T(8,128)(2,1)S(1)}, u32[]{:S(2)}, u32[]{:S(2)}) collective-permute-start(bf16[144,128]{1,0:T(8,128)(2,1)S(1)} %get-tuple-element.46), channel_id=1, source_target_pairs={{0,12},{1,13},{2,14},{3,15},{4,8},{5,9},{6,10},{7,11},{8,4},{9,5},... | collective-permute-start | bytes 110600 | tf_op jit(solution)/shard_map/ppermute | solution.py:265
  42.1 1.5 %collective-permute-start.15 = (bf16[144,128]{1,0:T(8,128)(2,1)S(1)}, bf16[144,128]{1,0:T(8,128)(2,1)S(1)}, u32[]{:S(2)}, u32[]{:S(2)}) collective-permute-start(bf16[144,128]{1,0:T(8,128)(2,1)S(1)} %get-tuple-element.47), channel_id=1, source_target_pairs={{0,14},{1,15},{2,12},{3,13},{4,10},{5,11},{6,8},{7,9},{8,6},{9,7},... | collective-permute-start | bytes 110600 | tf_op jit(solution)/shard_map/ppermute | solution.py:265
  43.6 1.1 %collective-permute-done.13 = bf16[144,128]{1,0:T(8,128)(2,1)S(1)} collective-permute-done((bf16[144,128]{1,0:T(8,128)(2,1)S(1)}, bf16[144,128]{1,0:T(8,128)(2,1)S(1)}, u32[]{:S(2)}, u32[]{:S(2)}) %collective-permute-start.13) | collective-permute-done | bytes 36896 | tf_op jit(solution)/shard_map/ppermute | solution.py:265
  45.3 3.4 %collective-permute-done.15 = bf16[144,128]{1,0:T(8,128)(2,1)S(1)} collective-permute-done((bf16[144,128]{1,0:T(8,128)(2,1)S(1)}, bf16[144,128]{1,0:T(8,128)(2,1)S(1)}, u32[]{:S(2)}, u32[]{:S(2)}) %collective-permute-start.15) | collective-permute-done | bytes 36896 | tf_op jit(solution)/shard_map/ppermute | solution.py:265
  48.8 1.6 %collective-permute-start.22 = (bf16[144,128]{1,0:T(8,128)(2,1)S(1)}, bf16[144,128]{1,0:T(8,128)(2,1)S(1)}, u32[]{:S(2)}, u32[]{:S(2)}) collective-permute-start(bf16[144,128]{1,0:T(8,128)(2,1)S(1)} %add_convert_fusion.mine), channel_id=1, source_target_pairs={{0,14},{1,15},{2,12},{3,13},{4,10},{5,11},{6,8},{7,9},{8,6},{9,7},... | collective-permute-start | bytes 110600 | tf_op jit(solution)/shard_map/ppermute | solution.py:265
  50.3 3.7 %collective-permute-start.21 = (bf16[144,128]{1,0:T(8,128)(2,1)S(1)}, bf16[144,128]{1,0:T(8,128)(2,1)S(1)}, u32[]{:S(2)}, u32[]{:S(2)}) collective-permute-start(bf16[144,128]{1,0:T(8,128)(2,1)S(1)} %add_convert_fusion.mine), channel_id=1, source_target_pairs={{0,12},{1,13},{2,14},{3,15},{4,8},{5,9},{6,10},{7,11},{8,4},{9,5},... | collective-permute-start | bytes 110600 | tf_op jit(solution)/shard_map/ppermute | solution.py:265
  54.0 2.4 %collective-permute-start.19 = (bf16[144,128]{1,0:T(8,128)(2,1)S(1)}, bf16[144,128]{1,0:T(8,128)(2,1)S(1)}, u32[]{:S(2)}, u32[]{:S(2)}) collective-permute-start(bf16[144,128]{1,0:T(8,128)(2,1)S(1)} %add_convert_fusion.mine), channel_id=1, source_target_pairs={{0,8},{1,9},{2,10},{3,11},{4,12},{5,13},{6,14},{7,15},{8,0},{9,1},... | collective-permute-start | bytes 110600 | tf_op jit(solution)/shard_map/ppermute | solution.py:265
  56.5 3.4 %collective-permute-start.17 = (bf16[144,128]{1,0:T(8,128)(2,1)S(1)}, bf16[144,128]{1,0:T(8,128)(2,1)S(1)}, u32[]{:S(2)}, u32[]{:S(2)}) collective-permute-start(bf16[144,128]{1,0:T(8,128)(2,1)S(1)} %add_convert_fusion.mine), channel_id=1, source_target_pairs={{0,4},{1,5},{2,6},{3,7},{4,0},{5,1},{6,2},{7,3},{8,12},{9,13},{10,... | collective-permute-start | bytes 110600 | tf_op jit(solution)/shard_map/ppermute | solution.py:265
  60.2 1.1 %collective-permute-done.18.rest_2_ = bf16[144,128]{1,0:T(8,128)(2,1)S(1)} collective-permute-done((bf16[144,128]{1,0:T(8,128)(2,1)S(1)}, bf16[144,128]{1,0:T(8,128)(2,1)S(1)}, u32[]{:S(2)}, u32[]{:S(2)}) %collective-permute-start.18) | collective-permute-done | bytes 36896 | tf_op jit(solution)/shard_map/ppermute | solution.py:265
  61.3 0.9 %collective-permute-done.17.rest_1_ = bf16[144,128]{1,0:T(8,128)(2,1)S(1)} collective-permute-done((bf16[144,128]{1,0:T(8,128)(2,1)S(1)}, bf16[144,128]{1,0:T(8,128)(2,1)S(1)}, u32[]{:S(2)}, u32[]{:S(2)}) %collective-permute-start.17) | collective-permute-done | bytes 36896 | tf_op jit(solution)/shard_map/ppermute | solution.py:265
  62.2 1.6 %collective-permute-done.16.rest_0_ = bf16[144,128]{1,0:T(8,128)(2,1)S(1)} collective-permute-done((bf16[144,128]{1,0:T(8,128)(2,1)S(1)}, bf16[144,128]{1,0:T(8,128)(2,1)S(1)}, u32[]{:S(2)}, u32[]{:S(2)}) %collective-permute-start.16) | collective-permute-done | bytes 36896 | tf_op jit(solution)/shard_map/ppermute | solution.py:265
  64.0 1.1 %shard_map.79 = bf16[4,128,128]{2,1,0:T(8,128)(2,1)} custom-call(bf16[6,128,384]{2,1,0:T(8,128)(2,1)S(1)} %get-tuple-element.37.hw, bf16[3,3,128,128]{3,2,1,0:T(8,128)(2,1)S(1)} %bitcast.25), custom_call_target="tpu_custom_call" | custom-call | flops 150994944 | bytes 1015808 | tf_op jit(solution)/shard_map/pallas_call | solution.py:231
  65.5 1.2 %multiply_bitcast_fusion = (f32[1,3,3,128,128]{4,3,2,1,0:T(8,128)}, f32[1,3,3,128,128]{4,3,2,1,0:T(8,128)}) fusion(bf16[3,3,128,128]{3,2,1,0:T(8,128)(2,1)S(1)} %collective-permute-done.23, bf16[3,3,128,128]{3,2,1,0:T(8,128)(2,1)S(1)} %bitcast.27, pred[]{:T(512)S(6)} %eq.5), kind=kLoop, calls=%fused_computation | loop fusion | flops 884736 | bytes 1769473 | tf_op jit(solution)/shard_map/broadcast_in_dim | solution.py:341
  (38 shorter events, 5.3 us)
Async XLA Ops:
  0.6 8.2 %collective-permute-start.1 = (bf16[4,128,128]{2,1,0:T(8,128)(2,1)}, bf16[4,128,128]{2,1,0:T(8,128)(2,1)S(1)}, u32[]{:S(2)}, u32[]{:S(2)}) collective-permute-start(bf16[4,128,128]{2,1,0:T(8,128)(2,1)} %bitcast.29), channel_id=1, source_target_pairs={{0,0},{1,2},{2,1},{3,4},{4,3},{5,6},{6,5},{7,8},{8,7},{9,10},{10,9... | collective-permute-start | bytes 393224 | tf_op jit(solution)/shard_map/ppermute | solution.py:265
  2.2 6.6 %collective-permute-start = (bf16[4,128,128]{2,1,0:T(8,128)(2,1)}, bf16[4,128,128]{2,1,0:T(8,128)(2,1)S(1)}, u32[]{:S(2)}, u32[]{:S(2)}) collective-permute-start(bf16[4,128,128]{2,1,0:T(8,128)(2,1)} %bitcast.30), channel_id=1, source_target_pairs={{0,1},{1,0},{2,3},{3,2},{4,5},{5,4},{6,7},{7,6},{8,9},{9,8},{10,11... | collective-permute-start | bytes 393224 | tf_op jit(solution)/shard_map/ppermute | solution.py:265
  5.7 1.0 %copy-start = (bf16[1,3,3,128,128]{4,3,2,1,0:T(8,128)(2,1)S(1)}, bf16[1,3,3,128,128]{4,3,2,1,0:T(8,128)(2,1)}, u32[]{:S(2)}) copy-start(bf16[1,3,3,128,128]{4,3,2,1,0:T(8,128)(2,1)} %param.7) | copy-start | bytes 884740
  6.6 1.0 %copy-start.3 = (bf16[1,3,3,128,128]{4,3,2,1,0:T(8,128)(2,1)S(1)}, bf16[1,3,3,128,128]{4,3,2,1,0:T(8,128)(2,1)}, u32[]{:S(2)}) copy-start(bf16[1,3,3,128,128]{4,3,2,1,0:T(8,128)(2,1)} %param.6) | copy-start | bytes 884740
  7.6 0.9 %copy-start.5 = (bf16[1,4,128,128]{3,2,1,0:T(8,128)(2,1)S(1)}, bf16[1,4,128,128]{3,2,1,0:T(8,128)(2,1)}, u32[]{:S(2)}) copy-start(bf16[1,4,128,128]{3,2,1,0:T(8,128)(2,1)} %param.4) | copy-start | bytes 393220
  8.5 1.0 %copy-start.1 = (bf16[1,3,3,128,128]{4,3,2,1,0:T(8,128)(2,1)S(1)}, bf16[1,3,3,128,128]{4,3,2,1,0:T(8,128)(2,1)}, u32[]{:S(2)}) copy-start(bf16[1,3,3,128,128]{4,3,2,1,0:T(8,128)(2,1)} %param.7) | copy-start | bytes 884740
  8.5 1.0 %copy-start.4 = (bf16[1,3,3,128,128]{4,3,2,1,0:T(8,128)(2,1)S(1)}, bf16[1,3,3,128,128]{4,3,2,1,0:T(8,128)(2,1)}, u32[]{:S(2)}) copy-start(bf16[1,3,3,128,128]{4,3,2,1,0:T(8,128)(2,1)} %param.6) | copy-start | bytes 884740
  9.5 2.3 %copy-start.2 = (bf16[1,4,128,128]{3,2,1,0:T(8,128)(2,1)S(1)}, bf16[1,4,128,128]{3,2,1,0:T(8,128)(2,1)}, u32[]{:S(2)}) copy-start(bf16[1,4,128,128]{3,2,1,0:T(8,128)(2,1)} %param.5) | copy-start | bytes 393220
  11.3 8.3 %collective-permute-start.2 = (bf16[8,128,128]{2,1,0:T(8,128)(2,1)S(1)}, bf16[8,128,128]{2,1,0:T(8,128)(2,1)S(1)}, u32[]{:S(2)}, u32[]{:S(2)}) collective-permute-start(bf16[8,128,128]{2,1,0:T(8,128)(2,1)S(1)} %get-tuple-element.28.skip_here), channel_id=1, source_target_pairs={{0,16},{1,17},{2,18},{3,19},{4,20},{5,21},{6,22},{7,23},{8,24},{9,... | collective-permute-start | bytes 786440 | tf_op jit(solution)/shard_map/ppermute | solution.py:265
  11.8 4.1 %collective-permute-start.4 = (bf16[2,128,128]{2,1,0:T(8,128)(2,1)S(1)}, bf16[2,128,128]{2,1,0:T(8,128)(2,1)S(1)}, u32[]{:S(2)}, u32[]{:S(2)}) collective-permute-start(bf16[2,128,128]{2,1,0:T(8,128)(2,1)S(1)} %get-tuple-element.50), channel_id=1, source_target_pairs={{0,0},{1,2},{2,1},{3,4},{4,3},{5,6},{6,5},{7,8},{8,7},{9,10},{10,9... | collective-permute-start | bytes 196616 | tf_op jit(solution)/shard_map/ppermute | solution.py:265
  12.5 4.3 %collective-permute-start.3 = (bf16[2,128,128]{2,1,0:T(8,128)(2,1)S(1)}, bf16[2,128,128]{2,1,0:T(8,128)(2,1)S(1)}, u32[]{:S(2)}, u32[]{:S(2)}) collective-permute-start(bf16[2,128,128]{2,1,0:T(8,128)(2,1)S(1)} %get-tuple-element.51), channel_id=1, source_target_pairs={{0,1},{1,0},{2,3},{3,2},{4,5},{5,4},{6,7},{7,6},{8,9},{9,8},{10,11... | collective-permute-start | bytes 196616 | tf_op jit(solution)/shard_map/ppermute | solution.py:265
  20.3 8.1 %collective-permute-start.5 = (bf16[4,128,128]{2,1,0:T(8,128)(2,1)S(1)}, bf16[4,128,128]{2,1,0:T(8,128)(2,1)S(1)}, u32[]{:S(2)}, u32[]{:S(2)}) collective-permute-start(bf16[4,128,128]{2,1,0:T(8,128)(2,1)S(1)} %get-tuple-element.31), channel_id=1, source_target_pairs={{0,16},{1,17},{2,18},{3,19},{4,20},{5,21},{6,22},{7,23},{8,24},{9,... | collective-permute-start | bytes 393224 | tf_op jit(solution)/shard_map/ppermute | solution.py:265
  22.3 5.2 %collective-permute-start.6 = (bf16[2,128,128]{2,1,0:T(8,128)(2,1)S(1)}, bf16[2,128,128]{2,1,0:T(8,128)(2,1)S(1)}, u32[]{:S(2)}, u32[]{:S(2)}) collective-permute-start(bf16[2,128,128]{2,1,0:T(8,128)(2,1)S(1)} %get-tuple-element.32), channel_id=1, source_target_pairs={{0,17},{1,16},{2,19},{3,18},{4,21},{5,20},{6,23},{7,22},{8,25},{9,... | collective-permute-start | bytes 196616 | tf_op jit(solution)/shard_map/ppermute | solution.py:265
  22.3 6.1 %collective-permute-start.7 = (bf16[2,128,128]{2,1,0:T(8,128)(2,1)S(1)}, bf16[2,128,128]{2,1,0:T(8,128)(2,1)S(1)}, u32[]{:S(2)}, u32[]{:S(2)}) collective-permute-start(bf16[2,128,128]{2,1,0:T(8,128)(2,1)S(1)} %get-tuple-element.33), channel_id=1, source_target_pairs={{0,16},{1,18},{2,17},{3,20},{4,19},{5,22},{6,21},{7,24},{8,23},{9,... | collective-permute-start | bytes 196616 | tf_op jit(solution)/shard_map/ppermute | solution.py:265
  30.6 1.6 %collective-permute-start.8 = (bf16[3,3,128,128]{3,2,1,0:T(8,128)(2,1)S(1)}, bf16[3,3,128,128]{3,2,1,0:T(8,128)(2,1)S(1)}, u32[]{:S(2)}, u32[]{:S(2)}) collective-permute-start(bf16[3,3,128,128]{3,2,1,0:T(8,128)(2,1)S(1)} %get-tuple-element.39), channel_id=1, source_target_pairs={{0,1},{1,0},{2,3},{3,2},{4,5},{5,4},{6,7},{7,6},{8,9},{9,8},{10,11... | collective-permute-start | bytes 884744 | tf_op jit(solution)/shard_map/ppermute | solution.py:265
  32.3 7.1 %collective-permute-start.9 = (bf16[144,128]{1,0:T(8,128)(2,1)S(1)}, bf16[144,128]{1,0:T(8,128)(2,1)S(1)}, u32[]{:S(2)}, u32[]{:S(2)}) collective-permute-start(bf16[144,128]{1,0:T(8,128)(2,1)S(1)} %get-tuple-element.41), channel_id=1, source_target_pairs={{0,2},{1,3},{2,0},{3,1},{4,6},{5,7},{6,4},{7,5},{8,10},{9,11},{10,... | collective-permute-start | bytes 110600 | tf_op jit(solution)/shard_map/ppermute | solution.py:265
  33.5 8.5 %collective-permute-start.10 = (bf16[144,128]{1,0:T(8,128)(2,1)S(1)}, bf16[144,128]{1,0:T(8,128)(2,1)S(1)}, u32[]{:S(2)}, u32[]{:S(2)}) collective-permute-start(bf16[144,128]{1,0:T(8,128)(2,1)S(1)} %get-tuple-element.42), channel_id=1, source_target_pairs={{0,4},{1,5},{2,6},{3,7},{4,0},{5,1},{6,2},{7,3},{8,12},{9,13},{10,... | collective-permute-start | bytes 110600 | tf_op jit(solution)/shard_map/ppermute | solution.py:265
  35.1 8.4 %collective-permute-start.11 = (bf16[144,128]{1,0:T(8,128)(2,1)S(1)}, bf16[144,128]{1,0:T(8,128)(2,1)S(1)}, u32[]{:S(2)}, u32[]{:S(2)}) collective-permute-start(bf16[144,128]{1,0:T(8,128)(2,1)S(1)} %get-tuple-element.43), channel_id=1, source_target_pairs={{0,6},{1,7},{2,4},{3,5},{4,2},{5,3},{6,0},{7,1},{8,14},{9,15},{10,... | collective-permute-start | bytes 110600 | tf_op jit(solution)/shard_map/ppermute | solution.py:265
  35.9 7.7 %collective-permute-start.12 = (bf16[144,128]{1,0:T(8,128)(2,1)S(1)}, bf16[144,128]{1,0:T(8,128)(2,1)S(1)}, u32[]{:S(2)}, u32[]{:S(2)}) collective-permute-start(bf16[144,128]{1,0:T(8,128)(2,1)S(1)} %get-tuple-element.44), channel_id=1, source_target_pairs={{0,8},{1,9},{2,10},{3,11},{4,12},{5,13},{6,14},{7,15},{8,0},{9,1},... | collective-permute-start | bytes 110600 | tf_op jit(solution)/shard_map/ppermute | solution.py:265
  38.7 6.0 %collective-permute-start.13 = (bf16[144,128]{1,0:T(8,128)(2,1)S(1)}, bf16[144,128]{1,0:T(8,128)(2,1)S(1)}, u32[]{:S(2)}, u32[]{:S(2)}) collective-permute-start(bf16[144,128]{1,0:T(8,128)(2,1)S(1)} %get-tuple-element.45), channel_id=1, source_target_pairs={{0,10},{1,11},{2,8},{3,9},{4,14},{5,15},{6,12},{7,13},{8,2},{9,3},... | collective-permute-start | bytes 110600 | tf_op jit(solution)/shard_map/ppermute | solution.py:265
  39.4 5.9 %collective-permute-start.14 = (bf16[144,128]{1,0:T(8,128)(2,1)S(1)}, bf16[144,128]{1,0:T(8,128)(2,1)S(1)}, u32[]{:S(2)}, u32[]{:S(2)}) collective-permute-start(bf16[144,128]{1,0:T(8,128)(2,1)S(1)} %get-tuple-element.46), channel_id=1, source_target_pairs={{0,12},{1,13},{2,14},{3,15},{4,8},{5,9},{6,10},{7,11},{8,4},{9,5},... | collective-permute-start | bytes 110600 | tf_op jit(solution)/shard_map/ppermute | solution.py:265
  42.1 6.7 %collective-permute-start.15 = (bf16[144,128]{1,0:T(8,128)(2,1)S(1)}, bf16[144,128]{1,0:T(8,128)(2,1)S(1)}, u32[]{:S(2)}, u32[]{:S(2)}) collective-permute-start(bf16[144,128]{1,0:T(8,128)(2,1)S(1)} %get-tuple-element.47), channel_id=1, source_target_pairs={{0,14},{1,15},{2,12},{3,13},{4,10},{5,11},{6,8},{7,9},{8,6},{9,7},... | collective-permute-start | bytes 110600 | tf_op jit(solution)/shard_map/ppermute | solution.py:265
  48.8 7.7 %collective-permute-start.22 = (bf16[144,128]{1,0:T(8,128)(2,1)S(1)}, bf16[144,128]{1,0:T(8,128)(2,1)S(1)}, u32[]{:S(2)}, u32[]{:S(2)}) collective-permute-start(bf16[144,128]{1,0:T(8,128)(2,1)S(1)} %add_convert_fusion.mine), channel_id=1, source_target_pairs={{0,14},{1,15},{2,12},{3,13},{4,10},{5,11},{6,8},{7,9},{8,6},{9,7},... | collective-permute-start | bytes 110600 | tf_op jit(solution)/shard_map/ppermute | solution.py:265
  50.3 9.6 %collective-permute-start.21 = (bf16[144,128]{1,0:T(8,128)(2,1)S(1)}, bf16[144,128]{1,0:T(8,128)(2,1)S(1)}, u32[]{:S(2)}, u32[]{:S(2)}) collective-permute-start(bf16[144,128]{1,0:T(8,128)(2,1)S(1)} %add_convert_fusion.mine), channel_id=1, source_target_pairs={{0,12},{1,13},{2,14},{3,15},{4,8},{5,9},{6,10},{7,11},{8,4},{9,5},... | collective-permute-start | bytes 110600 | tf_op jit(solution)/shard_map/ppermute | solution.py:265
  54.0 6.2 %collective-permute-start.20 = (bf16[144,128]{1,0:T(8,128)(2,1)S(1)}, bf16[144,128]{1,0:T(8,128)(2,1)S(1)}, u32[]{:S(2)}, u32[]{:S(2)}) collective-permute-start(bf16[144,128]{1,0:T(8,128)(2,1)S(1)} %add_convert_fusion.mine), channel_id=1, source_target_pairs={{0,10},{1,11},{2,8},{3,9},{4,14},{5,15},{6,12},{7,13},{8,2},{9,3},... | collective-permute-start | bytes 110600 | tf_op jit(solution)/shard_map/ppermute | solution.py:265
  54.0 6.2 %collective-permute-start.19 = (bf16[144,128]{1,0:T(8,128)(2,1)S(1)}, bf16[144,128]{1,0:T(8,128)(2,1)S(1)}, u32[]{:S(2)}, u32[]{:S(2)}) collective-permute-start(bf16[144,128]{1,0:T(8,128)(2,1)S(1)} %add_convert_fusion.mine), channel_id=1, source_target_pairs={{0,8},{1,9},{2,10},{3,11},{4,12},{5,13},{6,14},{7,15},{8,0},{9,1},... | collective-permute-start | bytes 110600 | tf_op jit(solution)/shard_map/ppermute | solution.py:265
  56.5 4.9 %collective-permute-start.18 = (bf16[144,128]{1,0:T(8,128)(2,1)S(1)}, bf16[144,128]{1,0:T(8,128)(2,1)S(1)}, u32[]{:S(2)}, u32[]{:S(2)}) collective-permute-start(bf16[144,128]{1,0:T(8,128)(2,1)S(1)} %add_convert_fusion.mine), channel_id=1, source_target_pairs={{0,6},{1,7},{2,4},{3,5},{4,2},{5,3},{6,0},{7,1},{8,14},{9,15},{10,... | collective-permute-start | bytes 110600 | tf_op jit(solution)/shard_map/ppermute | solution.py:265
  56.5 5.7 %collective-permute-start.17 = (bf16[144,128]{1,0:T(8,128)(2,1)S(1)}, bf16[144,128]{1,0:T(8,128)(2,1)S(1)}, u32[]{:S(2)}, u32[]{:S(2)}) collective-permute-start(bf16[144,128]{1,0:T(8,128)(2,1)S(1)} %add_convert_fusion.mine), channel_id=1, source_target_pairs={{0,4},{1,5},{2,6},{3,7},{4,0},{5,1},{6,2},{7,3},{8,12},{9,13},{10,... | collective-permute-start | bytes 110600 | tf_op jit(solution)/shard_map/ppermute | solution.py:265
  59.9 4.0 %collective-permute-start.16 = (bf16[144,128]{1,0:T(8,128)(2,1)S(1)}, bf16[144,128]{1,0:T(8,128)(2,1)S(1)}, u32[]{:S(2)}, u32[]{:S(2)}) collective-permute-start(bf16[144,128]{1,0:T(8,128)(2,1)S(1)} %add_convert_fusion.mine), channel_id=1, source_target_pairs={{0,2},{1,3},{2,0},{3,1},{4,6},{5,7},{6,4},{7,5},{8,10},{9,11},{10,... | collective-permute-start | bytes 110600 | tf_op jit(solution)/shard_map/ppermute | solution.py:265
  63.9 1.6 %collective-permute-start.23 = (bf16[3,3,128,128]{3,2,1,0:T(8,128)(2,1)S(1)}, bf16[3,3,128,128]{3,2,1,0:T(8,128)(2,1)S(1)}, u32[]{:S(2)}, u32[]{:S(2)}) collective-permute-start(bf16[3,3,128,128]{3,2,1,0:T(8,128)(2,1)S(1)} %bitcast.26), channel_id=1, source_target_pairs={{0,1},{1,0},{2,3},{3,2},{4,5},{5,4},{6,7},{7,6},{8,9},{9,8},{10,11... | collective-permute-start | bytes 884744 | tf_op jit(solution)/shard_map/ppermute | solution.py:265

commit v4 on v3

--- a/solution.py
+++ b/solution.py
@@ -124,7 +124,7 @@
 
 
 def middle_kernel(
-    segments, strips, skip_here, skip_there, pre1, g, g_core, g_other, second, out, grad, back, edge_core, edge_other, yw, gw
+    segments, strips, skip_here, skip_there, pre1, g, g_core, g_other, second, out, gw, back, edge_core, edge_other, yw
 ):
     encoder, row, even = here(segments)
     own = g.shape[0]
@@ -148,32 +148,25 @@
                 out[i - 1] = silu(pre[i]).astype(BF16)
             value = masked(upstream * slope(pre[i]), inside(row, strips, own, i - 1))
             place(gw, i, value)
-            grad[i] = value.astype(BF16)
         back[...] = conv_back(gw, 0, own, second).astype(BF16)
         edge_core[...] = jnp.where(even, back[own - 2 : own], back[0:2])
         edge_other[...] = jnp.where(even, back[0:2], back[own - 2 : own])
 
 
-def end_kernel(
-    segments, strips, x, g, g_core, g_other, back, back_core, back_other, pre1, pre2, hid, skip_there, grad, second,
-    kept, sent, hw, ew,
+def store(even, kept, sent):
+    def put(ty, tx, values):
+        half = values.shape[0] // 2
+        kept[ty, tx] = jnp.where(even, values[:half], values[half:])
+        sent[ty, tx] = jnp.where(even, values[half:], values[:half]).astype(BF16)
+
+    return put
+
+
+def second_kernel(
+    segments, strips, g, g_core, g_other, back, back_core, back_other, pre2, hid, skip_there, gw, kept, sent, ew
 ):
     encoder, row, even = here(segments)
-    own = x.shape[0]
-
-    def store(first):
-        keep = jnp.logical_xor(even, not first)
-
-        def put(ty, tx, values):
-            @pl.when(keep)
-            def _():
-                kept[ty, tx] = values
-
-            @pl.when(jnp.logical_not(keep))
-            def _():
-                sent[ty, tx] = values.astype(BF16)
-
-        return put
+    own = g.shape[0]
 
     @pl.when(encoder)
     def _():
@@ -182,48 +175,41 @@
                 upstream = jnp.where(even, g_other[i].astype(F32), g_core[i].astype(F32))
                 returned = jnp.where(even, back_other[i].astype(F32), back_core[i].astype(F32))
             elif i >= own + 2:
-                upstream = jnp.where(even, g_core[i - own - 2].astype(F32), g_other[i - own - 2].astype(F32))
-                returned = jnp.where(
-                    even, back_core[i - own - 2].astype(F32), back_other[i - own - 2].astype(F32)
-                )
+                k = i - own - 2
+                upstream = jnp.where(even, g_core[k].astype(F32), g_other[k].astype(F32))
+                returned = jnp.where(even, back_core[k].astype(F32), back_other[k].astype(F32))
             else:
                 upstream = g[i - 2].astype(F32)
                 returned = back[i - 2].astype(F32)
             value = (upstream + returned) * slope(pre2[i])
             place(ew, i, masked(value, inside(row, strips, own, i - 2)))
+        conv_weight(hid[...], ew, 1, store(even, kept, sent))
+
+    @pl.when(jnp.logical_not(encoder))
+    def _():
+        conv_weight(skip_there[2 : own + 2], gw, 0, store(even, kept, sent))
+
+
+def main_kernel(segments, strips, x, pre1, ew, gw, second, kept, sent, hw):
+    encoder, row, even = here(segments)
+    own = x.shape[0]
+
+    @pl.when(encoder)
+    def _():
         hidden_back = conv_back(ew, 0, own + 2, second)
         for i in range(own + 2):
             value = hidden_back[i] * slope(pre1[i])
             place(hw, i, masked(value, inside(row, strips, own, i - 1)))
-        conv_weight(hid[...], ew, 1, store(False))
 
     @pl.when(jnp.logical_not(encoder))
     def _():
-        for i in range(own + 2):
-            place(hw, i, grad[i].astype(F32))
-        conv_weight(skip_there[2 : own + 2], hw, 0, store(False))
-
-    conv_weight(x[...], hw, 0, store(True))
+        hw[...] = gw[...]
+
+    conv_weight(x[...], hw, 0, store(even, kept, sent))
 
 
 def input_kernel(hw, main, input_grad):
     input_grad[...] = conv_back(hw, 0, input_grad.shape[0], main).astype(BF16)
-
-
-def pack_kernel(strips, kept, got, mine, *sends):
-    chip = lax.axis_index("rows") // 2
-    mine[...] = kept[chip] + got[chip].astype(F32)
-    for k, send in enumerate(sends):
-        at = jnp.bitwise_xor(chip, k + 1)
-        send[...] = (kept[at] + got[at].astype(F32)).astype(BF16)
-
-
-def unpack_kernel(strips, mine, *rest):
-    gots, out = rest[:-1], rest[-1]
-    chip = lax.axis_index("rows") // 2
-    out[chip] = mine[...]
-    for k, got in enumerate(gots):
-        out[jnp.bitwise_xor(chip, k + 1)] = got[...]
 
 
 def call(kernel, outs, scratch, args, flops):
@@ -293,51 +279,62 @@
     g_core = swap(jnp.where(even, g[own - 2 :], g[:2]), False, core)
     g_other = swap(jnp.where(even, g[:2], g[own - 2 :]), False, other)
     skip_there = swap(skip_here, True, same)
-    output, grad, back, edge_core, edge_other = call(
+    output, gw, back, edge_core, edge_other = call(
         functools.partial(middle_kernel, segments, strips),
-        [like(own, BF16), like(own + 2, BF16), like(own, BF16), like(2, BF16), like(2, BF16)],
-        [wide(own + 4), wide(own + 2)],
+        [like(own, BF16), wide_out(own + 2), like(own, BF16), like(2, BF16), like(2, BF16)],
+        [wide(own + 4)],
         (skip_here, skip_there, pre1, g, g_core, g_other, second),
         work * (2 * own + 2),
     )
     back_own = swap(back, True, same)
     back_other = swap(edge_other, True, other)
     back_core = swap(edge_core, True, core)
-    taps = (3, 3, channels, channels)
-    kept, sent, last = call(
-        functools.partial(end_kernel, segments, strips),
-        [jax.ShapeDtypeStruct(taps, F32), jax.ShapeDtypeStruct(taps, BF16), wide_out(own + 2)],
-        [wide(own + 4)],
-        (x, g, g_core, g_other, back_own, back_core, back_other, pre1, pre2, hid, skip_there, grad, second),
-        work * (3 * own + 2),
-    )
-    (input_grad,) = call(input_kernel, [like(own, BF16)], [], (last, main), work * own)
-    chips = strips // 2
-    chunk = (9 * channels // chips, channels)
-    jumps = range(1, chips)
-    got = swap(sent, False, core)
-    mine, *sends = call(
-        functools.partial(pack_kernel, strips),
-        [jax.ShapeDtypeStruct(chunk, F32)] + [jax.ShapeDtypeStruct(chunk, BF16) for _ in jumps],
+    halves = (3, 3, channels // 2, channels)
+    terms = [jax.ShapeDtypeStruct(halves, F32), jax.ShapeDtypeStruct(halves, BF16)]
+    kept2, sent2, ew = call(
+        functools.partial(second_kernel, segments, strips),
+        terms + [wide_out(own + 4)],
         [],
-        (kept.reshape((chips,) + chunk), got.reshape((chips,) + chunk)),
-        kept.size,
-    )
-    gots = [swap(send, False, lambda r, k=k: r ^ (2 * k)) for k, send in zip(jumps, sends)]
-    mine = sum((got.astype(F32) for got in gots), mine).astype(BF16)
-    gots = [swap(mine, False, lambda r, k=k: r ^ (2 * k)) for k in jumps]
-    (mine,) = call(
-        functools.partial(unpack_kernel, strips),
-        [jax.ShapeDtypeStruct((chips,) + chunk, BF16)],
+        (g, g_core, g_other, back_own, back_core, back_other, pre2, hid, skip_there, gw),
+        work * own,
+    )
+    kept1, sent1, hw = call(
+        functools.partial(main_kernel, segments, strips),
+        terms + [wide_out(own + 2)],
         [],
-        (mine, *gots),
-        kept.size,
-    )
-    mine = mine.reshape(taps)
-    theirs = swap(mine, False, core)
+        (x, pre1, ew, gw, second),
+        work * (2 * own + 2),
+    )
+    (input_grad,) = call(input_kernel, [like(own, BF16)], [], (hw, main), work * own)
     factor = 1.0 / math.sqrt(own * strips * columns)
-    first_sum = jnp.where(even, mine, theirs).astype(F32) * factor
-    second_sum = jnp.where(even, theirs, mine).astype(F32) * factor
+
+    def jump(array, bit):
+        return swap(array, False, lambda r: r ^ (1 << bit))
+
+    def total(kept, sent):
+        bits = strips.bit_length() - 1
+        current = kept + jump(sent, 0).astype(F32)
+        split = [0]
+        for bit in range(1, bits):
+            half = current.shape[2] // 2
+            if half >= 16:
+                upper = (row >> bit) & 1
+                mine = lax.dynamic_slice_in_dim(current, upper * half, half, 2)
+                sent = lax.dynamic_slice_in_dim(current, (1 - upper) * half, half, 2).astype(BF16)
+                current = mine + jump(sent, bit).astype(F32)
+                split.append(bit)
+            else:
+                mine = lax.optimization_barrier(current.astype(BF16))
+                current = mine.astype(F32) + jump(mine, bit).astype(F32)
+        mine = lax.optimization_barrier(current.astype(BF16))
+        for bit in reversed(split):
+            upper = ((row >> bit) & 1) == 1
+            got = jump(mine, bit)
+            mine = jnp.concatenate([jnp.where(upper, got, mine), jnp.where(upper, mine, got)], axis=2)
+        return mine.astype(F32) * factor
+
+    second_sum = total(kept2, sent2)
+    first_sum = total(kept1, sent1)
     return (output[None], input_grad[None], first_sum[None], second_sum[None])
 
 

time: 67 us -> 61 us (0.910)
  starting transfers between devices: 35.1 us -> 31.5 us
  waiting for transfers between devices: 19.9 us -> 16.8 us
  other arithmetic: 1.22 us -> 2.17 us
    ppermute x24 -> x22, starting transfers between devices: 35.1 us -> 31.5 us  [swap(): return lax.ppermute(array, ('segment', 'rows'), pairs)]
    ppermute x24 -> x22, waiting for transfers between devices: 19.9 us -> 16.8 us  [swap(): return lax.ppermute(array, ('segment', 'rows'), pairs)]
    mul x0 -> x2, other arithmetic: none -> 1.74 us  [total(): return mine.astype(F32) * factor]
    broadcast_in_dim x1 -> x0, other arithmetic: 1.16 us -> none  [body(): return (output[None], input_grad[None], first_sum[None], second_sum[None])]
    pallas_call x7 -> x6, Pallas kernels: 6.21 us -> 5.65 us  [call(): pl.pallas_call(kernel, out_shape=outs, in_specs=[pl.BlockSpec(memory_spac...]
    unnamed x12 -> x14, local copies, waits for them, and re-layouts: 3.54 us -> 3.57 us
  transfers between devices with their start and end apart: 24 -> 22, of which waited for: 13 -> 13; matrix products, arithmetic and copies ran while one was open for 0% -> 2% of each run, Pallas kernels for 2% -> 4%
where the time goes in v4:
time: 61 us; the launch traced here: 60.7 us
  starting transfers between devices  31.5 us (52%)
  waiting for transfers between devices  16.8 us (28%)
  Pallas kernels  5.65 us (9%)
  local copies, waits for them, and re-layouts  3.64 us (6%)
  other arithmetic  2.17 us (4%)
  between operations  0.87 us (1%)
    ppermute x22, starting transfers between devices, swap(): return lax.ppermute(array, ('segment', 'rows'), pairs)  31.5 us
    ppermute x22, waiting for transfers between devices, swap(): return lax.ppermute(array, ('segment', 'rows'), pairs)  16.8 us
    pallas_call x6, Pallas kernels, call(): pl.pallas_call(kernel, out_shape=outs, in_specs=[pl.BlockSpec(memory_spac...  5.65 us
    unnamed x14, local copies, waits for them, and re-layouts  3.57 us
    mul x2, other arithmetic, total(): return mine.astype(F32) * factor  1.74 us
  transfers between devices with their start and end apart: 22, of which 13 were waited for; matrix products, arithmetic and copies ran while one was open for 2% of the time, Pallas kernels for 4%

profile of v4, /device:TPU:0, one launch (start us, length us, event | category | flops | bytes accessed | tf_op | source)
XLA Modules:
  0.0 60.7 jit_solution(8321404429804950688)
XLA Ops:
  1.1 1.6 %collective-permute-start.1 = (bf16[4,128,128]{2,1,0:T(8,128)(2,1)}, bf16[4,128,128]{2,1,0:T(8,128)(2,1)S(1)}, u32[]{:S(2)}, u32[]{:S(2)}) collective-permute-start(bf16[4,128,128]{2,1,0:T(8,128)(2,1)} %bitcast.28), channel_id=1, source_target_pairs={{0,0},{1,2},{2,1},{3,4},{4,3},{5,6},{6,5},{7,8},{8,7},{9,10},{10,9... | collective-permute-start | bytes 393224 | tf_op jit(solution)/shard_map/ppermute | solution.py:251
  2.7 1.0 %copy-done = bf16[1,3,3,128,128]{4,3,2,1,0:T(8,128)(2,1)S(1)} copy-done((bf16[1,3,3,128,128]{4,3,2,1,0:T(8,128)(2,1)S(1)}, bf16[1,3,3,128,128]{4,3,2,1,0:T(8,128)(2,1)}, u32[]{:S(2)}) %copy-start) | copy-done | bytes 294936
  3.7 1.0 %copy-done.3 = bf16[1,3,3,128,128]{4,3,2,1,0:T(8,128)(2,1)S(1)} copy-done((bf16[1,3,3,128,128]{4,3,2,1,0:T(8,128)(2,1)S(1)}, bf16[1,3,3,128,128]{4,3,2,1,0:T(8,128)(2,1)}, u32[]{:S(2)}) %copy-start.3) | copy-done | bytes 294936
  4.6 0.9 %copy-done.5 = bf16[1,4,128,128]{3,2,1,0:T(8,128)(2,1)S(1)} copy-done((bf16[1,4,128,128]{3,2,1,0:T(8,128)(2,1)S(1)}, bf16[1,4,128,128]{3,2,1,0:T(8,128)(2,1)}, u32[]{:S(2)}) %copy-start.5) | copy-done | bytes 131096
  6.5 1.7 %shard_map.76 = (f32[6,128,128]{2,1,0:T(8,128)S(1)}, f32[8,128,128]{2,1,0:T(8,128)S(1)}, bf16[4,128,128]{2,1,0:T(8,128)(2,1)S(1)}, bf16[8,128,128]{2,1,0:T(8,128)(2,1)S(1)}) custom-call(bf16[4,128,384]{2,1,0:T(8,128)(2,1)S(1)} %get-tuple-element.21.xo, f32[2,128,128]{2,1,0:T(8,128)S(1)} %get-tuple-element.22.mid, ...), custom_call_target="tpu_custom_call" | custom-call | flops 603979776 | bytes 2686976 | tf_op jit(solution)/shard_map/pallas_call | solution.py:217
  8.2 1.5 %collective-permute-start.2 = (bf16[8,128,128]{2,1,0:T(8,128)(2,1)S(1)}, bf16[8,128,128]{2,1,0:T(8,128)(2,1)S(1)}, u32[]{:S(2)}, u32[]{:S(2)}) collective-permute-start(bf16[8,128,128]{2,1,0:T(8,128)(2,1)S(1)} %get-tuple-element.23.skip_here), channel_id=1, source_target_pairs={{0,16},{1,17},{2,18},{3,19},{4,20},{5,21},{6,22},{7,23},{8,24},{9,... | collective-permute-start | bytes 786440 | tf_op jit(solution)/shard_map/ppermute | solution.py:251
  9.8 1.8 %collective-permute-start.3 = (bf16[2,128,128]{2,1,0:T(8,128)(2,1)S(1)}, bf16[2,128,128]{2,1,0:T(8,128)(2,1)S(1)}, u32[]{:S(2)}, u32[]{:S(2)}) collective-permute-start(bf16[2,128,128]{2,1,0:T(8,128)(2,1)S(1)} %get-tuple-element.47), channel_id=1, source_target_pairs={{0,1},{1,0},{2,3},{3,2},{4,5},{5,4},{6,7},{7,6},{8,9},{9,8},{10,11... | collective-permute-start | bytes 196616 | tf_op jit(solution)/shard_map/ppermute | solution.py:251
  12.4 3.0 %collective-permute-done.2.skip_there = bf16[8,128,128]{2,1,0:T(8,128)(2,1)S(1)} collective-permute-done((bf16[8,128,128]{2,1,0:T(8,128)(2,1)S(1)}, bf16[8,128,128]{2,1,0:T(8,128)(2,1)S(1)}, u32[]{:S(2)}, u32[]{:S(2)}) %collective-permute-start.2) | collective-permute-done | bytes 262176 | tf_op jit(solution)/shard_map/ppermute | solution.py:251
  16.1 4.0 %collective-permute-start.5 = (bf16[4,128,128]{2,1,0:T(8,128)(2,1)S(1)}, bf16[4,128,128]{2,1,0:T(8,128)(2,1)S(1)}, u32[]{:S(2)}, u32[]{:S(2)}) collective-permute-start(bf16[4,128,128]{2,1,0:T(8,128)(2,1)S(1)} %get-tuple-element.26), channel_id=1, source_target_pairs={{0,16},{1,17},{2,18},{3,19},{4,20},{5,21},{6,22},{7,23},{8,24},{9,... | collective-permute-start | bytes 393224 | tf_op jit(solution)/shard_map/ppermute | solution.py:251
  21.0 1.7 %collective-permute-start.7 = (bf16[2,128,128]{2,1,0:T(8,128)(2,1)S(1)}, bf16[2,128,128]{2,1,0:T(8,128)(2,1)S(1)}, u32[]{:S(2)}, u32[]{:S(2)}) collective-permute-start(bf16[2,128,128]{2,1,0:T(8,128)(2,1)S(1)} %get-tuple-element.28), channel_id=1, source_target_pairs={{0,16},{1,18},{2,17},{3,20},{4,19},{5,22},{6,21},{7,24},{8,23},{9,... | collective-permute-start | bytes 196616 | tf_op jit(solution)/shard_map/ppermute | solution.py:251
  22.7 3.4 %collective-permute-done.6.back_core = bf16[2,128,128]{2,1,0:T(8,128)(2,1)S(1)} collective-permute-done((bf16[2,128,128]{2,1,0:T(8,128)(2,1)S(1)}, bf16[2,128,128]{2,1,0:T(8,128)(2,1)S(1)}, u32[]{:S(2)}, u32[]{:S(2)}) %collective-permute-start.6) | collective-permute-done | bytes 65568 | tf_op jit(solution)/shard_map/ppermute | solution.py:251
  26.1 1.2 %collective-permute-done.7.back_other = bf16[2,128,128]{2,1,0:T(8,128)(2,1)S(1)} collective-permute-done((bf16[2,128,128]{2,1,0:T(8,128)(2,1)S(1)}, bf16[2,128,128]{2,1,0:T(8,128)(2,1)S(1)}, u32[]{:S(2)}, u32[]{:S(2)}) %collective-permute-start.7) | collective-permute-done | bytes 65568 | tf_op jit(solution)/shard_map/ppermute | solution.py:251
  28.2 1.1 %shard_map.79 = (f32[3,3,64,128]{3,2,1,0:T(8,128)S(1)}, bf16[3,3,64,128]{3,2,1,0:T(8,128)(2,1)S(1)}, bf16[6,128,384]{2,1,0:T(8,128)(2,1)S(1)}) custom-call(bf16[4,128,128]{2,1,0:T(8,128)(2,1)S(1)} %bitcast.30, f32[6,128,128]{2,1,0:T(8,128)S(1)} %get-tuple-element.24.pre1, bf16[8,128,384]{2,1,0:T(8,128)(2,1)S(1)} %get-tuple-element.32.ew, ...), custom_call_target="tpu_custom_call" | custom-call | flops 377487360 | bytes 3227648 | tf_op jit(solution)/shard_map/pallas_call | solution.py:217
  29.8 2.8 %collective-permute-start.16 = (bf16[3,3,32,128]{3,2,1,0:T(8,128)(2,1)S(1)}, bf16[3,3,32,128]{3,2,1,0:T(8,128)(2,1)S(1)}, u32[]{:S(2)}, u32[]{:S(2)}) collective-permute-start(bf16[3,3,32,128]{3,2,1,0:T(8,128)(2,1)S(1)} %dynamic-slice_convert_fusion), channel_id=1, source_target_pairs={{0,2},{1,3},{2,0},{3,1},{4,6},{5,7},{6,4},{7,5},{8,10},{9,11},{10,... | collective-permute-start | bytes 221192 | tf_op jit(solution)/shard_map/ppermute | solution.py:251
  32.8 1.0 %collective-permute-start.9 = (bf16[3,3,32,128]{3,2,1,0:T(8,128)(2,1)S(1)}, bf16[3,3,32,128]{3,2,1,0:T(8,128)(2,1)S(1)}, u32[]{:S(2)}, u32[]{:S(2)}) collective-permute-start(bf16[3,3,32,128]{3,2,1,0:T(8,128)(2,1)S(1)} %dynamic-slice_convert_fusion.1), channel_id=1, source_target_pairs={{0,2},{1,3},{2,0},{3,1},{4,6},{5,7},{6,4},{7,5},{8,10},{9,11},{10,... | collective-permute-start | bytes 221192 | tf_op jit(solution)/shard_map/ppermute | solution.py:251
  33.7 1.5 %collective-permute-done.16 = bf16[3,3,32,128]{3,2,1,0:T(8,128)(2,1)S(1)} collective-permute-done((bf16[3,3,32,128]{3,2,1,0:T(8,128)(2,1)S(1)}, bf16[3,3,32,128]{3,2,1,0:T(8,128)(2,1)S(1)}, u32[]{:S(2)}, u32[]{:S(2)}) %collective-permute-start.16) | collective-permute-done | bytes 73760 | tf_op jit(solution)/shard_map/ppermute | solution.py:251
  35.3 3.3 %collective-permute-start.17 = (bf16[3,3,16,128]{3,2,1,0:T(8,128)(2,1)S(1)}, bf16[3,3,16,128]{3,2,1,0:T(8,128)(2,1)S(1)}, u32[]{:S(2)}, u32[]{:S(2)}) collective-permute-start(bf16[3,3,16,128]{3,2,1,0:T(8,128)(2,1)S(1)} %dynamic-slice_convert_fusion.2), channel_id=1, source_target_pairs={{0,4},{1,5},{2,6},{3,7},{4,0},{5,1},{6,2},{7,3},{8,12},{9,13},{10,... | collective-permute-start | bytes 110600 | tf_op jit(solution)/shard_map/ppermute | solution.py:251
  38.6 1.0 %collective-permute-start.10 = (bf16[3,3,16,128]{3,2,1,0:T(8,128)(2,1)S(1)}, bf16[3,3,16,128]{3,2,1,0:T(8,128)(2,1)S(1)}, u32[]{:S(2)}, u32[]{:S(2)}) collective-permute-start(bf16[3,3,16,128]{3,2,1,0:T(8,128)(2,1)S(1)} %dynamic-slice_convert_fusion.3), channel_id=1, source_target_pairs={{0,4},{1,5},{2,6},{3,7},{4,0},{5,1},{6,2},{7,3},{8,12},{9,13},{10,... | collective-permute-start | bytes 110600 | tf_op jit(solution)/shard_map/ppermute | solution.py:251
  39.6 1.2 %collective-permute-done.17 = bf16[3,3,16,128]{3,2,1,0:T(8,128)(2,1)S(1)} collective-permute-done((bf16[3,3,16,128]{3,2,1,0:T(8,128)(2,1)S(1)}, bf16[3,3,16,128]{3,2,1,0:T(8,128)(2,1)S(1)}, u32[]{:S(2)}, u32[]{:S(2)}) %collective-permute-start.17) | collective-permute-done | bytes 36896 | tf_op jit(solution)/shard_map/ppermute | solution.py:251
  40.8 2.8 %collective-permute-start.18 = (bf16[3,3,16,128]{3,2,1,0:T(8,128)(2,1)S(1)}, bf16[3,3,16,128]{3,2,1,0:T(8,128)(2,1)S(1)}, u32[]{:S(2)}, u32[]{:S(2)}) collective-permute-start(bf16[3,3,16,128]{3,2,1,0:T(8,128)(2,1)S(1)} %add_convert_fusion.1), channel_id=1, source_target_pairs={{0,8},{1,9},{2,10},{3,11},{4,12},{5,13},{6,14},{7,15},{8,0},{9,1},... | collective-permute-start | bytes 110600 | tf_op jit(solution)/shard_map/ppermute | solution.py:251
  43.6 1.7 %collective-permute-start.11 = (bf16[3,3,16,128]{3,2,1,0:T(8,128)(2,1)S(1)}, bf16[3,3,16,128]{3,2,1,0:T(8,128)(2,1)S(1)}, u32[]{:S(2)}, u32[]{:S(2)}) collective-permute-start(bf16[3,3,16,128]{3,2,1,0:T(8,128)(2,1)S(1)} %add_convert_fusion.3), channel_id=1, source_target_pairs={{0,8},{1,9},{2,10},{3,11},{4,12},{5,13},{6,14},{7,15},{8,0},{9,1},... | collective-permute-start | bytes 110600 | tf_op jit(solution)/shard_map/ppermute | solution.py:251
  45.7 1.8 %collective-permute-start.19 = (bf16[3,3,16,128]{3,2,1,0:T(8,128)(2,1)S(1)}, bf16[3,3,16,128]{3,2,1,0:T(8,128)(2,1)S(1)}, u32[]{:S(2)}, u32[]{:S(2)}) collective-permute-start(bf16[3,3,16,128]{3,2,1,0:T(8,128)(2,1)S(1)} %add_convert_fusion), channel_id=1, source_target_pairs={{0,4},{1,5},{2,6},{3,7},{4,0},{5,1},{6,2},{7,3},{8,12},{9,13},{10,... | collective-permute-start | bytes 110600 | tf_op jit(solution)/shard_map/ppermute | solution.py:251
  47.6 1.0 %collective-permute-done.11 = bf16[3,3,16,128]{3,2,1,0:T(8,128)(2,1)S(1)} collective-permute-done((bf16[3,3,16,128]{3,2,1,0:T(8,128)(2,1)S(1)}, bf16[3,3,16,128]{3,2,1,0:T(8,128)(2,1)S(1)}, u32[]{:S(2)}, u32[]{:S(2)}) %collective-permute-start.11) | collective-permute-done | bytes 36896 | tf_op jit(solution)/shard_map/ppermute | solution.py:251
  48.6 1.8 %collective-permute-start.12 = (bf16[3,3,16,128]{3,2,1,0:T(8,128)(2,1)S(1)}, bf16[3,3,16,128]{3,2,1,0:T(8,128)(2,1)S(1)}, u32[]{:S(2)}, u32[]{:S(2)}) collective-permute-start(bf16[3,3,16,128]{3,2,1,0:T(8,128)(2,1)S(1)} %add_convert_fusion.2), channel_id=1, source_target_pairs={{0,4},{1,5},{2,6},{3,7},{4,0},{5,1},{6,2},{7,3},{8,12},{9,13},{10,... | collective-permute-start | bytes 110600 | tf_op jit(solution)/shard_map/ppermute | solution.py:251
  50.4 1.1 %shard_map.80 = bf16[4,128,128]{2,1,0:T(8,128)(2,1)} custom-call(bf16[6,128,384]{2,1,0:T(8,128)(2,1)S(1)} %get-tuple-element.33.hw, bf16[3,3,128,128]{3,2,1,0:T(8,128)(2,1)S(1)} %bitcast.26), custom_call_target="tpu_custom_call" | custom-call | flops 150994944 | bytes 1015808 | tf_op jit(solution)/shard_map/pallas_call | solution.py:217
  51.6 1.0 %collective-permute-done.12 = bf16[3,3,16,128]{3,2,1,0:T(8,128)(2,1)S(1)} collective-permute-done((bf16[3,3,16,128]{3,2,1,0:T(8,128)(2,1)S(1)}, bf16[3,3,16,128]{3,2,1,0:T(8,128)(2,1)S(1)}, u32[]{:S(2)}, u32[]{:S(2)}) %collective-permute-start.12) | collective-permute-done | bytes 36896 | tf_op jit(solution)/shard_map/ppermute | solution.py:251
  52.6 1.2 %collective-permute-start.13 = (bf16[3,3,32,128]{3,2,1,0:T(8,128)(2,1)S(1)}, bf16[3,3,32,128]{3,2,1,0:T(8,128)(2,1)S(1)}, u32[]{:S(2)}, u32[]{:S(2)}) collective-permute-start(bf16[3,3,32,128]{3,2,1,0:T(8,128)(2,1)S(1)} %pad_maximum_fusion.2), channel_id=1, source_target_pairs={{0,2},{1,3},{2,0},{3,1},{4,6},{5,7},{6,4},{7,5},{8,10},{9,11},{10,... | collective-permute-start | bytes 221192 | tf_op jit(solution)/shard_map/ppermute | solution.py:251
  53.9 0.9 %collective-permute-start.20 = (bf16[3,3,32,128]{3,2,1,0:T(8,128)(2,1)S(1)}, bf16[3,3,32,128]{3,2,1,0:T(8,128)(2,1)S(1)}, u32[]{:S(2)}, u32[]{:S(2)}) collective-permute-start(bf16[3,3,32,128]{3,2,1,0:T(8,128)(2,1)S(1)} %pad_maximum_fusion.3), channel_id=1, source_target_pairs={{0,2},{1,3},{2,0},{3,1},{4,6},{5,7},{6,4},{7,5},{8,10},{9,11},{10,... | collective-permute-start | bytes 221192 | tf_op jit(solution)/shard_map/ppermute | solution.py:251
  54.7 2.3 %collective-permute-done.13 = bf16[3,3,32,128]{3,2,1,0:T(8,128)(2,1)S(1)} collective-permute-done((bf16[3,3,32,128]{3,2,1,0:T(8,128)(2,1)S(1)}, bf16[3,3,32,128]{3,2,1,0:T(8,128)(2,1)S(1)}, u32[]{:S(2)}, u32[]{:S(2)}) %collective-permute-start.13) | collective-permute-done | bytes 73760 | tf_op jit(solution)/shard_map/ppermute | solution.py:251
  57.2 1.0 %collective-permute-done.20 = bf16[3,3,32,128]{3,2,1,0:T(8,128)(2,1)S(1)} collective-permute-done((bf16[3,3,32,128]{3,2,1,0:T(8,128)(2,1)S(1)}, bf16[3,3,32,128]{3,2,1,0:T(8,128)(2,1)S(1)}, u32[]{:S(2)}, u32[]{:S(2)}) %collective-permute-start.20) | collective-permute-done | bytes 73760 | tf_op jit(solution)/shard_map/ppermute | solution.py:251
  58.6 0.9 %convert_multiply_fusion.1 = f32[1,3,3,128,128]{4,3,2,1,0:T(8,128)} fusion(bf16[1,3,3,64,128]{4,3,2,1,0:T(8,128)(2,1)S(1)} %get-tuple-element.41, bf16[1,3,3,64,128]{4,3,2,1,0:T(8,128)(2,1)S(1)} %get-tuple-element.40), kind=kLoop, calls=%fused_computation.1 | loop fusion | flops 737280 | bytes 884736 | tf_op jit(solution)/shard_map/mul | solution.py:334
  59.8 0.9 %convert_multiply_fusion = f32[1,3,3,128,128]{4,3,2,1,0:T(8,128)} fusion(bf16[1,3,3,64,128]{4,3,2,1,0:T(8,128)(2,1)S(1)} %get-tuple-element.39, bf16[1,3,3,64,128]{4,3,2,1,0:T(8,128)(2,1)S(1)} %get-tuple-element.38), kind=kLoop, calls=%fused_computation | loop fusion | flops 737280 | bytes 884736 | tf_op jit(solution)/shard_map/mul | solution.py:334
  (56 shorter events, 6.6 us)
Async XLA Ops:
  0.6 5.2 %collective-permute-start = (bf16[4,128,128]{2,1,0:T(8,128)(2,1)}, bf16[4,128,128]{2,1,0:T(8,128)(2,1)S(1)}, u32[]{:S(2)}, u32[]{:S(2)}) collective-permute-start(bf16[4,128,128]{2,1,0:T(8,128)(2,1)} %bitcast.27), channel_id=1, source_target_pairs={{0,1},{1,0},{2,3},{3,2},{4,5},{5,4},{6,7},{7,6},{8,9},{9,8},{10,11... | collective-permute-start | bytes 393224 | tf_op jit(solution)/shard_map/ppermute | solution.py:251
  1.1 4.7 %collective-permute-start.1 = (bf16[4,128,128]{2,1,0:T(8,128)(2,1)}, bf16[4,128,128]{2,1,0:T(8,128)(2,1)S(1)}, u32[]{:S(2)}, u32[]{:S(2)}) collective-permute-start(bf16[4,128,128]{2,1,0:T(8,128)(2,1)} %bitcast.28), channel_id=1, source_target_pairs={{0,0},{1,2},{2,1},{3,4},{4,3},{5,6},{6,5},{7,8},{8,7},{9,10},{10,9... | collective-permute-start | bytes 393224 | tf_op jit(solution)/shard_map/ppermute | solution.py:251
  2.7 1.0 %copy-start = (bf16[1,3,3,128,128]{4,3,2,1,0:T(8,128)(2,1)S(1)}, bf16[1,3,3,128,128]{4,3,2,1,0:T(8,128)(2,1)}, u32[]{:S(2)}) copy-start(bf16[1,3,3,128,128]{4,3,2,1,0:T(8,128)(2,1)} %param.7) | copy-start | bytes 884740
  3.7 1.0 %copy-start.3 = (bf16[1,3,3,128,128]{4,3,2,1,0:T(8,128)(2,1)S(1)}, bf16[1,3,3,128,128]{4,3,2,1,0:T(8,128)(2,1)}, u32[]{:S(2)}) copy-start(bf16[1,3,3,128,128]{4,3,2,1,0:T(8,128)(2,1)} %param.6) | copy-start | bytes 884740
  4.6 0.9 %copy-start.5 = (bf16[1,4,128,128]{3,2,1,0:T(8,128)(2,1)S(1)}, bf16[1,4,128,128]{3,2,1,0:T(8,128)(2,1)}, u32[]{:S(2)}) copy-start(bf16[1,4,128,128]{3,2,1,0:T(8,128)(2,1)} %param.4) | copy-start | bytes 393220
  5.5 1.0 %copy-start.1 = (bf16[1,3,3,128,128]{4,3,2,1,0:T(8,128)(2,1)S(1)}, bf16[1,3,3,128,128]{4,3,2,1,0:T(8,128)(2,1)}, u32[]{:S(2)}) copy-start(bf16[1,3,3,128,128]{4,3,2,1,0:T(8,128)(2,1)} %param.7) | copy-start | bytes 884740
  6.5 3.3 %copy-start.2 = (bf16[1,4,128,128]{3,2,1,0:T(8,128)(2,1)S(1)}, bf16[1,4,128,128]{3,2,1,0:T(8,128)(2,1)}, u32[]{:S(2)}) copy-start(bf16[1,4,128,128]{3,2,1,0:T(8,128)(2,1)} %param.5) | copy-start | bytes 393220
  8.2 7.2 %collective-permute-start.2 = (bf16[8,128,128]{2,1,0:T(8,128)(2,1)S(1)}, bf16[8,128,128]{2,1,0:T(8,128)(2,1)S(1)}, u32[]{:S(2)}, u32[]{:S(2)}) collective-permute-start(bf16[8,128,128]{2,1,0:T(8,128)(2,1)S(1)} %get-tuple-element.23.skip_here), channel_id=1, source_target_pairs={{0,16},{1,17},{2,18},{3,19},{4,20},{5,21},{6,22},{7,23},{8,24},{9,... | collective-permute-start | bytes 786440 | tf_op jit(solution)/shard_map/ppermute | solution.py:251
  9.8 2.7 %collective-permute-start.3 = (bf16[2,128,128]{2,1,0:T(8,128)(2,1)S(1)}, bf16[2,128,128]{2,1,0:T(8,128)(2,1)S(1)}, u32[]{:S(2)}, u32[]{:S(2)}) collective-permute-start(bf16[2,128,128]{2,1,0:T(8,128)(2,1)S(1)} %get-tuple-element.47), channel_id=1, source_target_pairs={{0,1},{1,0},{2,3},{3,2},{4,5},{5,4},{6,7},{7,6},{8,9},{9,8},{10,11... | collective-permute-start | bytes 196616 | tf_op jit(solution)/shard_map/ppermute | solution.py:251
  11.5 0.9 %collective-permute-start.4 = (bf16[2,128,128]{2,1,0:T(8,128)(2,1)S(1)}, bf16[2,128,128]{2,1,0:T(8,128)(2,1)S(1)}, u32[]{:S(2)}, u32[]{:S(2)}) collective-permute-start(bf16[2,128,128]{2,1,0:T(8,128)(2,1)S(1)} %get-tuple-element.46), channel_id=1, source_target_pairs={{0,0},{1,2},{2,1},{3,4},{4,3},{5,6},{6,5},{7,8},{8,7},{9,10},{10,9... | collective-permute-start | bytes 196616 | tf_op jit(solution)/shard_map/ppermute | solution.py:251
  16.1 11.2 %collective-permute-start.5 = (bf16[4,128,128]{2,1,0:T(8,128)(2,1)S(1)}, bf16[4,128,128]{2,1,0:T(8,128)(2,1)S(1)}, u32[]{:S(2)}, u32[]{:S(2)}) collective-permute-start(bf16[4,128,128]{2,1,0:T(8,128)(2,1)S(1)} %get-tuple-element.26), channel_id=1, source_target_pairs={{0,16},{1,17},{2,18},{3,19},{4,20},{5,21},{6,22},{7,23},{8,24},{9,... | collective-permute-start | bytes 393224 | tf_op jit(solution)/shard_map/ppermute | solution.py:251
  20.2 5.9 %collective-permute-start.6 = (bf16[2,128,128]{2,1,0:T(8,128)(2,1)S(1)}, bf16[2,128,128]{2,1,0:T(8,128)(2,1)S(1)}, u32[]{:S(2)}, u32[]{:S(2)}) collective-permute-start(bf16[2,128,128]{2,1,0:T(8,128)(2,1)S(1)} %get-tuple-element.27), channel_id=1, source_target_pairs={{0,17},{1,16},{2,19},{3,18},{4,21},{5,20},{6,23},{7,22},{8,25},{9,... | collective-permute-start | bytes 196616 | tf_op jit(solution)/shard_map/ppermute | solution.py:251
  21.0 6.3 %collective-permute-start.7 = (bf16[2,128,128]{2,1,0:T(8,128)(2,1)S(1)}, bf16[2,128,128]{2,1,0:T(8,128)(2,1)S(1)}, u32[]{:S(2)}, u32[]{:S(2)}) collective-permute-start(bf16[2,128,128]{2,1,0:T(8,128)(2,1)S(1)} %get-tuple-element.28), channel_id=1, source_target_pairs={{0,16},{1,18},{2,17},{3,20},{4,19},{5,22},{6,21},{7,24},{8,23},{9,... | collective-permute-start | bytes 196616 | tf_op jit(solution)/shard_map/ppermute | solution.py:251
  27.3 0.9 %copy-start.6 = (bf16[1,4,128,128]{3,2,1,0:T(8,128)(2,1)S(1)}, bf16[1,4,128,128]{3,2,1,0:T(8,128)(2,1)}, u32[]{:S(2)}) copy-start(bf16[1,4,128,128]{3,2,1,0:T(8,128)(2,1)} %param.4) | copy-start | bytes 393220
  28.0 1.8 %collective-permute-start.15 = (bf16[3,3,64,128]{3,2,1,0:T(8,128)(2,1)S(1)}, bf16[3,3,64,128]{3,2,1,0:T(8,128)(2,1)S(1)}, u32[]{:S(2)}, u32[]{:S(2)}) collective-permute-start(bf16[3,3,64,128]{3,2,1,0:T(8,128)(2,1)S(1)} %get-tuple-element.37), channel_id=1, source_target_pairs={{0,1},{1,0},{2,3},{3,2},{4,5},{5,4},{6,7},{7,6},{8,9},{9,8},{10,11... | collective-permute-start | bytes 442376 | tf_op jit(solution)/shard_map/ppermute | solution.py:251
  29.4 3.3 %collective-permute-start.8 = (bf16[3,3,64,128]{3,2,1,0:T(8,128)(2,1)S(1)}, bf16[3,3,64,128]{3,2,1,0:T(8,128)(2,1)S(1)}, u32[]{:S(2)}, u32[]{:S(2)}) collective-permute-start(bf16[3,3,64,128]{3,2,1,0:T(8,128)(2,1)S(1)} %get-tuple-element.35), channel_id=1, source_target_pairs={{0,1},{1,0},{2,3},{3,2},{4,5},{5,4},{6,7},{7,6},{8,9},{9,8},{10,11... | collective-permute-start | bytes 442376 | tf_op jit(solution)/shard_map/ppermute | solution.py:251
  29.8 5.4 %collective-permute-start.16 = (bf16[3,3,32,128]{3,2,1,0:T(8,128)(2,1)S(1)}, bf16[3,3,32,128]{3,2,1,0:T(8,128)(2,1)S(1)}, u32[]{:S(2)}, u32[]{:S(2)}) collective-permute-start(bf16[3,3,32,128]{3,2,1,0:T(8,128)(2,1)S(1)} %dynamic-slice_convert_fusion), channel_id=1, source_target_pairs={{0,2},{1,3},{2,0},{3,1},{4,6},{5,7},{6,4},{7,5},{8,10},{9,11},{10,... | collective-permute-start | bytes 221192 | tf_op jit(solution)/shard_map/ppermute | solution.py:251
  32.8 5.8 %collective-permute-start.9 = (bf16[3,3,32,128]{3,2,1,0:T(8,128)(2,1)S(1)}, bf16[3,3,32,128]{3,2,1,0:T(8,128)(2,1)S(1)}, u32[]{:S(2)}, u32[]{:S(2)}) collective-permute-start(bf16[3,3,32,128]{3,2,1,0:T(8,128)(2,1)S(1)} %dynamic-slice_convert_fusion.1), channel_id=1, source_target_pairs={{0,2},{1,3},{2,0},{3,1},{4,6},{5,7},{6,4},{7,5},{8,10},{9,11},{10,... | collective-permute-start | bytes 221192 | tf_op jit(solution)/shard_map/ppermute | solution.py:251
  35.3 5.5 %collective-permute-start.17 = (bf16[3,3,16,128]{3,2,1,0:T(8,128)(2,1)S(1)}, bf16[3,3,16,128]{3,2,1,0:T(8,128)(2,1)S(1)}, u32[]{:S(2)}, u32[]{:S(2)}) collective-permute-start(bf16[3,3,16,128]{3,2,1,0:T(8,128)(2,1)S(1)} %dynamic-slice_convert_fusion.2), channel_id=1, source_target_pairs={{0,4},{1,5},{2,6},{3,7},{4,0},{5,1},{6,2},{7,3},{8,12},{9,13},{10,... | collective-permute-start | bytes 110600 | tf_op jit(solution)/shard_map/ppermute | solution.py:251
  38.6 11.8 %copy-start.4 = (bf16[1,3,3,128,128]{4,3,2,1,0:T(8,128)(2,1)S(1)}, bf16[1,3,3,128,128]{4,3,2,1,0:T(8,128)(2,1)}, u32[]{:S(2)}) copy-start(bf16[1,3,3,128,128]{4,3,2,1,0:T(8,128)(2,1)} %param.6) | copy-start | bytes 884740
  38.6 5.0 %collective-permute-start.10 = (bf16[3,3,16,128]{3,2,1,0:T(8,128)(2,1)S(1)}, bf16[3,3,16,128]{3,2,1,0:T(8,128)(2,1)S(1)}, u32[]{:S(2)}, u32[]{:S(2)}) collective-permute-start(bf16[3,3,16,128]{3,2,1,0:T(8,128)(2,1)S(1)} %dynamic-slice_convert_fusion.3), channel_id=1, source_target_pairs={{0,4},{1,5},{2,6},{3,7},{4,0},{5,1},{6,2},{7,3},{8,12},{9,13},{10,... | collective-permute-start | bytes 110600 | tf_op jit(solution)/shard_map/ppermute | solution.py:251
  40.8 4.9 %collective-permute-start.18 = (bf16[3,3,16,128]{3,2,1,0:T(8,128)(2,1)S(1)}, bf16[3,3,16,128]{3,2,1,0:T(8,128)(2,1)S(1)}, u32[]{:S(2)}, u32[]{:S(2)}) collective-permute-start(bf16[3,3,16,128]{3,2,1,0:T(8,128)(2,1)S(1)} %add_convert_fusion.1), channel_id=1, source_target_pairs={{0,8},{1,9},{2,10},{3,11},{4,12},{5,13},{6,14},{7,15},{8,0},{9,1},... | collective-permute-start | bytes 110600 | tf_op jit(solution)/shard_map/ppermute | solution.py:251
  43.6 4.9 %collective-permute-start.11 = (bf16[3,3,16,128]{3,2,1,0:T(8,128)(2,1)S(1)}, bf16[3,3,16,128]{3,2,1,0:T(8,128)(2,1)S(1)}, u32[]{:S(2)}, u32[]{:S(2)}) collective-permute-start(bf16[3,3,16,128]{3,2,1,0:T(8,128)(2,1)S(1)} %add_convert_fusion.3), channel_id=1, source_target_pairs={{0,8},{1,9},{2,10},{3,11},{4,12},{5,13},{6,14},{7,15},{8,0},{9,1},... | collective-permute-start | bytes 110600 | tf_op jit(solution)/shard_map/ppermute | solution.py:251
  45.7 5.8 %collective-permute-start.19 = (bf16[3,3,16,128]{3,2,1,0:T(8,128)(2,1)S(1)}, bf16[3,3,16,128]{3,2,1,0:T(8,128)(2,1)S(1)}, u32[]{:S(2)}, u32[]{:S(2)}) collective-permute-start(bf16[3,3,16,128]{3,2,1,0:T(8,128)(2,1)S(1)} %add_convert_fusion), channel_id=1, source_target_pairs={{0,4},{1,5},{2,6},{3,7},{4,0},{5,1},{6,2},{7,3},{8,12},{9,13},{10,... | collective-permute-start | bytes 110600 | tf_op jit(solution)/shard_map/ppermute | solution.py:251
  48.6 4.0 %collective-permute-start.12 = (bf16[3,3,16,128]{3,2,1,0:T(8,128)(2,1)S(1)}, bf16[3,3,16,128]{3,2,1,0:T(8,128)(2,1)S(1)}, u32[]{:S(2)}, u32[]{:S(2)}) collective-permute-start(bf16[3,3,16,128]{3,2,1,0:T(8,128)(2,1)S(1)} %add_convert_fusion.2), channel_id=1, source_target_pairs={{0,4},{1,5},{2,6},{3,7},{4,0},{5,1},{6,2},{7,3},{8,12},{9,13},{10,... | collective-permute-start | bytes 110600 | tf_op jit(solution)/shard_map/ppermute | solution.py:251
  52.6 4.4 %collective-permute-start.13 = (bf16[3,3,32,128]{3,2,1,0:T(8,128)(2,1)S(1)}, bf16[3,3,32,128]{3,2,1,0:T(8,128)(2,1)S(1)}, u32[]{:S(2)}, u32[]{:S(2)}) collective-permute-start(bf16[3,3,32,128]{3,2,1,0:T(8,128)(2,1)S(1)} %pad_maximum_fusion.2), channel_id=1, source_target_pairs={{0,2},{1,3},{2,0},{3,1},{4,6},{5,7},{6,4},{7,5},{8,10},{9,11},{10,... | collective-permute-start | bytes 221192 | tf_op jit(solution)/shard_map/ppermute | solution.py:251
  53.9 4.4 %collective-permute-start.20 = (bf16[3,3,32,128]{3,2,1,0:T(8,128)(2,1)S(1)}, bf16[3,3,32,128]{3,2,1,0:T(8,128)(2,1)S(1)}, u32[]{:S(2)}, u32[]{:S(2)}) collective-permute-start(bf16[3,3,32,128]{3,2,1,0:T(8,128)(2,1)S(1)} %pad_maximum_fusion.3), channel_id=1, source_target_pairs={{0,2},{1,3},{2,0},{3,1},{4,6},{5,7},{6,4},{7,5},{8,10},{9,11},{10,... | collective-permute-start | bytes 221192 | tf_op jit(solution)/shard_map/ppermute | solution.py:251
  57.1 1.4 %collective-permute-start.14 = (bf16[3,3,64,128]{3,2,1,0:T(8,128)(2,1)S(1)}, bf16[3,3,64,128]{3,2,1,0:T(8,128)(2,1)S(1)}, u32[]{:S(2)}, u32[]{:S(2)}) collective-permute-start(bf16[3,3,64,128]{3,2,1,0:T(8,128)(2,1)S(1)} %pad_maximum_fusion), channel_id=1, source_target_pairs={{0,1},{1,0},{2,3},{3,2},{4,5},{5,4},{6,7},{7,6},{8,9},{9,8},{10,11... | collective-permute-start | bytes 442376 | tf_op jit(solution)/shard_map/ppermute | solution.py:251
  58.3 1.4 %collective-permute-start.21 = (bf16[3,3,64,128]{3,2,1,0:T(8,128)(2,1)S(1)}, bf16[3,3,64,128]{3,2,1,0:T(8,128)(2,1)S(1)}, u32[]{:S(2)}, u32[]{:S(2)}) collective-permute-start(bf16[3,3,64,128]{3,2,1,0:T(8,128)(2,1)S(1)} %pad_maximum_fusion.1), channel_id=1, source_target_pairs={{0,1},{1,0},{2,3},{3,2},{4,5},{5,4},{6,7},{7,6},{8,9},{9,8},{10,11... | collective-permute-start | bytes 442376 | tf_op jit(solution)/shard_map/ppermute | solution.py:251

commit v5 on v4

--- a/solution.py
+++ b/solution.py
@@ -212,6 +212,37 @@
     input_grad[...] = conv_back(hw, 0, input_grad.shape[0], main).astype(BF16)
 
 
+def quarters(rows):
+    quad = lax.rem(lax.axis_index("rows") // 2, 4)
+    return [pl.ds(pl.multiple_of(jnp.bitwise_xor(quad, k) * rows, rows), rows) for k in range(4)]
+
+
+def pack_kernel(kept1, got1, kept2, got2, mine, *sends):
+    for k, rows in enumerate(quarters(mine.shape[3])):
+        for t, (kept, got) in enumerate(((kept1, got1), (kept2, got2))):
+            value = kept[:, :, rows, :] + got[:, :, rows, :].astype(F32)
+            if k == 0:
+                mine[t] = value
+            else:
+                sends[k - 1][t] = value.astype(BF16)
+
+
+def unpack_kernel(mine, *rest):
+    out = rest[-1]
+    for got, rows in zip((mine,) + rest[:-1], quarters(mine.shape[3])):
+        out[:, :, :, rows, :] = got[...]
+
+
+def last_kernel(factor, mine, theirs, *outs):
+    even = lax.rem(lax.axis_index("rows"), 2) == 0
+    rows = mine.shape[3]
+    own_at = pl.ds(pl.multiple_of(jnp.where(even, 0, rows), rows), rows)
+    their_at = pl.ds(pl.multiple_of(jnp.where(even, rows, 0), rows), rows)
+    for t, out in enumerate(outs):
+        out[:, :, own_at, :] = mine[t].astype(F32) * factor
+        out[:, :, their_at, :] = theirs[t].astype(F32) * factor
+
+
 def call(kernel, outs, scratch, args, flops):
     moved = sum(math.prod(a.shape) * a.dtype.itemsize for a in list(args) + outs)
     return pl.pallas_call(
@@ -289,6 +320,7 @@
     back_own = swap(back, True, same)
     back_other = swap(edge_other, True, other)
     back_core = swap(edge_core, True, core)
+    taps = (3, 3, channels, channels)
     halves = (3, 3, channels // 2, channels)
     terms = [jax.ShapeDtypeStruct(halves, F32), jax.ShapeDtypeStruct(halves, BF16)]
     kept2, sent2, ew = call(
@@ -308,33 +340,37 @@
     (input_grad,) = call(input_kernel, [like(own, BF16)], [], (hw, main), work * own)
     factor = 1.0 / math.sqrt(own * strips * columns)
 
-    def jump(array, bit):
-        return swap(array, False, lambda r: r ^ (1 << bit))
-
-    def total(kept, sent):
-        bits = strips.bit_length() - 1
-        current = kept + jump(sent, 0).astype(F32)
-        split = [0]
-        for bit in range(1, bits):
-            half = current.shape[2] // 2
-            if half >= 16:
-                upper = (row >> bit) & 1
-                mine = lax.dynamic_slice_in_dim(current, upper * half, half, 2)
-                sent = lax.dynamic_slice_in_dim(current, (1 - upper) * half, half, 2).astype(BF16)
-                current = mine + jump(sent, bit).astype(F32)
-                split.append(bit)
-            else:
-                mine = lax.optimization_barrier(current.astype(BF16))
-                current = mine.astype(F32) + jump(mine, bit).astype(F32)
-        mine = lax.optimization_barrier(current.astype(BF16))
-        for bit in reversed(split):
-            upper = ((row >> bit) & 1) == 1
-            got = jump(mine, bit)
-            mine = jnp.concatenate([jnp.where(upper, got, mine), jnp.where(upper, mine, got)], axis=2)
-        return mine.astype(F32) * factor
-
-    second_sum = total(kept2, sent2)
-    first_sum = total(kept1, sent1)
+    def jump(array, bit, times=1):
+        return swap(array, False, lambda r: r ^ (times << bit))
+
+    bits = strips.bit_length() - 1
+    quarter = (2, 3, 3, channels // 8, channels)
+    got2, got1 = jump(sent2, 0), jump(sent1, 0)
+    mine, *sends = call(
+        pack_kernel,
+        [jax.ShapeDtypeStruct(quarter, F32)] + [jax.ShapeDtypeStruct(quarter, BF16)] * 3,
+        [],
+        (kept1, got1, kept2, got2),
+        kept1.size,
+    )
+    for k, send in enumerate(sends):
+        mine = mine + jump(send, 1, k + 1).astype(F32)
+    for bit in range(3, bits):
+        rounded = lax.optimization_barrier(mine.astype(BF16))
+        mine = rounded.astype(F32) + jump(rounded, bit).astype(F32)
+    mine = lax.optimization_barrier(mine.astype(BF16))
+    gots = [jump(mine, 1, k) for k in range(1, 4)]
+    (mine,) = call(
+        unpack_kernel,
+        [jax.ShapeDtypeStruct((2,) + halves, BF16)],
+        [],
+        (mine, *gots),
+        kept1.size,
+    )
+    theirs = jump(mine, 0)
+    first_sum, second_sum = call(
+        functools.partial(last_kernel, factor), [jax.ShapeDtypeStruct(taps, F32)] * 2, [], (mine, theirs), kept1.size
+    )
     return (output[None], input_grad[None], first_sum[None], second_sum[None])
 
 

time: 61 us -> 56.5 us (0.926)
  starting transfers between devices: 31.5 us -> 22.7 us
  waiting for transfers between devices: 16.8 us -> 22.2 us
  other arithmetic: 2.17 us -> 0.08 us
  Pallas kernels: 5.65 us -> 6.84 us
    ppermute x22 -> x18, starting transfers between devices: 31.5 us -> 22.7 us  [swap(): return lax.ppermute(array, ('segment', 'rows'), pairs)]
    ppermute x22 -> x18, waiting for transfers between devices: 16.8 us -> 22.2 us  [swap(): return lax.ppermute(array, ('segment', 'rows'), pairs)]
    mul x2 -> x0, other arithmetic: 1.74 us -> none  [total(): return mine.astype(F32) * factor]
    pallas_call x6 -> x9, Pallas kernels: 5.65 us -> 6.84 us  [call(): pl.pallas_call(kernel, out_shape=outs, in_specs=[pl.BlockSpec(memory_spac...]
  transfers between devices with their start and end apart: 22 -> 18, of which waited for: 13 -> 14; matrix products, arithmetic and copies ran while one was open for 2% -> 0% of each run, Pallas kernels for 4% -> 3%
where the time goes in v5:
time: 56.5 us; the launch traced here: 56.2 us
  starting transfers between devices  22.7 us (40%)
  waiting for transfers between devices  22.2 us (39%)
  Pallas kernels  6.84 us (12%)
  local copies, waits for them, and re-layouts  3.67 us (6%)
  between operations  0.76 us (1%)
    ppermute x18, starting transfers between devices, swap(): return lax.ppermute(array, ('segment', 'rows'), pairs)  22.7 us
    ppermute x18, waiting for transfers between devices, swap(): return lax.ppermute(array, ('segment', 'rows'), pairs)  22.2 us
    pallas_call x9, Pallas kernels, call(): pl.pallas_call(kernel, out_shape=outs, in_specs=[pl.BlockSpec(memory_spac...  6.84 us
    unnamed x14, local copies, waits for them, and re-layouts  3.67 us
  transfers between devices with their start and end apart: 18, of which 14 were waited for; matrix products, arithmetic and copies ran while one was open for 0% of the time, Pallas kernels for 3%

profile of v5, /device:TPU:0, one launch (start us, length us, event | category | flops | bytes accessed | tf_op | source)
XLA Modules:
  0.0 56.2 jit_solution(12031499608480546578)
XLA Ops:
  0.6 1.6 %collective-permute-start.1 = (bf16[4,128,128]{2,1,0:T(8,128)(2,1)}, bf16[4,128,128]{2,1,0:T(8,128)(2,1)S(1)}, u32[]{:S(2)}, u32[]{:S(2)}) collective-permute-start(bf16[4,128,128]{2,1,0:T(8,128)(2,1)} %bitcast.21), channel_id=1, source_target_pairs={{0,0},{1,2},{2,1},{3,4},{4,3},{5,6},{6,5},{7,8},{8,7},{9,10},{10,9... | collective-permute-start | bytes 393224 | tf_op jit(solution)/shard_map/ppermute | solution.py:282
  2.2 3.5 %collective-permute-start = (bf16[4,128,128]{2,1,0:T(8,128)(2,1)}, bf16[4,128,128]{2,1,0:T(8,128)(2,1)S(1)}, u32[]{:S(2)}, u32[]{:S(2)}) collective-permute-start(bf16[4,128,128]{2,1,0:T(8,128)(2,1)} %bitcast.22), channel_id=1, source_target_pairs={{0,1},{1,0},{2,3},{3,2},{4,5},{5,4},{6,7},{7,6},{8,9},{9,8},{10,11... | collective-permute-start | bytes 393224 | tf_op jit(solution)/shard_map/ppermute | solution.py:282
  5.7 1.0 %copy-done = bf16[1,3,3,128,128]{4,3,2,1,0:T(8,128)(2,1)S(1)} copy-done((bf16[1,3,3,128,128]{4,3,2,1,0:T(8,128)(2,1)S(1)}, bf16[1,3,3,128,128]{4,3,2,1,0:T(8,128)(2,1)}, u32[]{:S(2)}) %copy-start) | copy-done | bytes 294936
  6.6 1.0 %copy-done.3 = bf16[1,3,3,128,128]{4,3,2,1,0:T(8,128)(2,1)S(1)} copy-done((bf16[1,3,3,128,128]{4,3,2,1,0:T(8,128)(2,1)S(1)}, bf16[1,3,3,128,128]{4,3,2,1,0:T(8,128)(2,1)}, u32[]{:S(2)}) %copy-start.3) | copy-done | bytes 294936
  7.6 0.9 %copy-done.5 = bf16[1,4,128,128]{3,2,1,0:T(8,128)(2,1)S(1)} copy-done((bf16[1,4,128,128]{3,2,1,0:T(8,128)(2,1)S(1)}, bf16[1,4,128,128]{3,2,1,0:T(8,128)(2,1)}, u32[]{:S(2)}) %copy-start.5) | copy-done | bytes 131096
  9.5 1.7 %shard_map.76 = (f32[6,128,128]{2,1,0:T(8,128)S(1)}, f32[8,128,128]{2,1,0:T(8,128)S(1)}, bf16[4,128,128]{2,1,0:T(8,128)(2,1)S(1)}, bf16[8,128,128]{2,1,0:T(8,128)(2,1)S(1)}) custom-call(bf16[4,128,384]{2,1,0:T(8,128)(2,1)S(1)} %get-tuple-element.27.xo, f32[2,128,128]{2,1,0:T(8,128)S(1)} %get-tuple-element.28.mid, ...), custom_call_target="tpu_custom_call" | custom-call | flops 603979776 | bytes 2686976 | tf_op jit(solution)/shard_map/pallas_call | solution.py:248
  12.4 3.5 %collective-permute-start.3 = (bf16[2,128,128]{2,1,0:T(8,128)(2,1)S(1)}, bf16[2,128,128]{2,1,0:T(8,128)(2,1)S(1)}, u32[]{:S(2)}, u32[]{:S(2)}) collective-permute-start(bf16[2,128,128]{2,1,0:T(8,128)(2,1)S(1)} %get-tuple-element.51), channel_id=1, source_target_pairs={{0,1},{1,0},{2,3},{3,2},{4,5},{5,4},{6,7},{7,6},{8,9},{9,8},{10,11... | collective-permute-start | bytes 196616 | tf_op jit(solution)/shard_map/ppermute | solution.py:282
  15.9 0.9 %collective-permute-done.3.g_core = bf16[2,128,128]{2,1,0:T(8,128)(2,1)S(1)} collective-permute-done((bf16[2,128,128]{2,1,0:T(8,128)(2,1)S(1)}, bf16[2,128,128]{2,1,0:T(8,128)(2,1)S(1)}, u32[]{:S(2)}, u32[]{:S(2)}) %collective-permute-start.3) | collective-permute-done | bytes 65568 | tf_op jit(solution)/shard_map/ppermute | solution.py:282
  16.8 2.7 %collective-permute-done.2.skip_there = bf16[8,128,128]{2,1,0:T(8,128)(2,1)S(1)} collective-permute-done((bf16[8,128,128]{2,1,0:T(8,128)(2,1)S(1)}, bf16[8,128,128]{2,1,0:T(8,128)(2,1)S(1)}, u32[]{:S(2)}, u32[]{:S(2)}) %collective-permute-start.2) | collective-permute-done | bytes 262176 | tf_op jit(solution)/shard_map/ppermute | solution.py:282
  19.5 0.7 %shard_map.77 = (bf16[4,128,128]{2,1,0:T(8,128)(2,1)}, bf16[6,128,384]{2,1,0:T(8,128)(2,1)S(1)}, bf16[4,128,128]{2,1,0:T(8,128)(2,1)S(1)}, bf16[2,128,128]{2,1,0:T(8,128)(2,1)S(1)}, bf16[2,128,128]{2,1,0:T(8,128)(2,1)S(1)}) custom-call(bf16[8,128,128]{2,1,0:T(8,128)(2,1)S(1)} %get-tuple-element.29.skip_here, ...), custom_call_target="tpu_custom_call" | custom-call | flops 377487360 | bytes 2457600 | tf_op jit(solution)/shard_map/pallas_call | solution.py:248
  20.2 2.0 %collective-permute-start.5 = (bf16[4,128,128]{2,1,0:T(8,128)(2,1)S(1)}, bf16[4,128,128]{2,1,0:T(8,128)(2,1)S(1)}, u32[]{:S(2)}, u32[]{:S(2)}) collective-permute-start(bf16[4,128,128]{2,1,0:T(8,128)(2,1)S(1)} %get-tuple-element.32), channel_id=1, source_target_pairs={{0,16},{1,17},{2,18},{3,19},{4,20},{5,21},{6,22},{7,23},{8,24},{9,... | collective-permute-start | bytes 393224 | tf_op jit(solution)/shard_map/ppermute | solution.py:282
  22.2 1.0 %collective-permute-start.7 = (bf16[2,128,128]{2,1,0:T(8,128)(2,1)S(1)}, bf16[2,128,128]{2,1,0:T(8,128)(2,1)S(1)}, u32[]{:S(2)}, u32[]{:S(2)}) collective-permute-start(bf16[2,128,128]{2,1,0:T(8,128)(2,1)S(1)} %get-tuple-element.34), channel_id=1, source_target_pairs={{0,16},{1,18},{2,17},{3,20},{4,19},{5,22},{6,21},{7,24},{8,23},{9,... | collective-permute-start | bytes 196616 | tf_op jit(solution)/shard_map/ppermute | solution.py:282
  23.2 4.1 %collective-permute-done.6.back_core = bf16[2,128,128]{2,1,0:T(8,128)(2,1)S(1)} collective-permute-done((bf16[2,128,128]{2,1,0:T(8,128)(2,1)S(1)}, bf16[2,128,128]{2,1,0:T(8,128)(2,1)S(1)}, u32[]{:S(2)}, u32[]{:S(2)}) %collective-permute-start.6) | collective-permute-done | bytes 65568 | tf_op jit(solution)/shard_map/ppermute | solution.py:282
  27.3 1.0 %collective-permute-done.7.back_other = bf16[2,128,128]{2,1,0:T(8,128)(2,1)S(1)} collective-permute-done((bf16[2,128,128]{2,1,0:T(8,128)(2,1)S(1)}, bf16[2,128,128]{2,1,0:T(8,128)(2,1)S(1)}, u32[]{:S(2)}, u32[]{:S(2)}) %collective-permute-start.7) | collective-permute-done | bytes 65568 | tf_op jit(solution)/shard_map/ppermute | solution.py:282
  28.3 0.7 %shard_map.78 = (f32[3,3,64,128]{3,2,1,0:T(8,128)S(1)}, bf16[3,3,64,128]{3,2,1,0:T(8,128)(2,1)S(1)}, bf16[8,128,384]{2,1,0:T(8,128)(2,1)S(1)}) custom-call(bf16[4,128,128]{2,1,0:T(8,128)(2,1)S(1)} %bitcast.17, bf16[2,128,128]{2,1,0:T(8,128)(2,1)S(1)} %collective-permute-done.3.g_core, bf16[2,128,128]{2,1,0:T(8,128)(2,1)S(1)} %collective-permute-done.4.g_other, ...), custom_call_target="tpu_custom_call" | custom-call | flops 150994944 | bytes 3260416 | tf_op jit(solution)/shard_map/pallas_call | solution.py:248
  29.2 1.1 %shard_map.79 = (f32[3,3,64,128]{3,2,1,0:T(8,128)S(1)}, bf16[3,3,64,128]{3,2,1,0:T(8,128)(2,1)S(1)}, bf16[6,128,384]{2,1,0:T(8,128)(2,1)S(1)}) custom-call(bf16[4,128,128]{2,1,0:T(8,128)(2,1)S(1)} %bitcast.24, f32[6,128,128]{2,1,0:T(8,128)S(1)} %get-tuple-element.30.pre1, bf16[8,128,384]{2,1,0:T(8,128)(2,1)S(1)} %get-tuple-element.38.ew, ...), custom_call_target="tpu_custom_call" | custom-call | flops 377487360 | bytes 3227648 | tf_op jit(solution)/shard_map/pallas_call | solution.py:248
  30.9 0.9 %collective-permute-done.8.got1 = bf16[3,3,64,128]{3,2,1,0:T(8,128)(2,1)S(1)} collective-permute-done((bf16[3,3,64,128]{3,2,1,0:T(8,128)(2,1)S(1)}, bf16[3,3,64,128]{3,2,1,0:T(8,128)(2,1)S(1)}, u32[]{:S(2)}, u32[]{:S(2)}) %collective-permute-start.8) | collective-permute-done | bytes 147488 | tf_op jit(solution)/shard_map/ppermute | solution.py:282
  32.1 1.3 %collective-permute-start.10 = (bf16[2,3,3,16,128]{4,3,2,1,0:T(8,128)(2,1)S(1)}, bf16[2,3,3,16,128]{4,3,2,1,0:T(8,128)(2,1)S(1)}, u32[]{:S(2)}, u32[]{:S(2)}) collective-permute-start(bf16[2,3,3,16,128]{4,3,2,1,0:T(8,128)(2,1)S(1)} %get-tuple-element.45), channel_id=1, source_target_pairs={{0,2},{1,3},{2,0},{3,1},{4,6},{5,7},{6,4},{7,5},{8,10},{9,11},{10,... | collective-permute-start | bytes 221192 | tf_op jit(solution)/shard_map/ppermute | solution.py:282
  33.3 1.6 %collective-permute-start.11 = (bf16[2,3,3,16,128]{4,3,2,1,0:T(8,128)(2,1)S(1)}, bf16[2,3,3,16,128]{4,3,2,1,0:T(8,128)(2,1)S(1)}, u32[]{:S(2)}, u32[]{:S(2)}) collective-permute-start(bf16[2,3,3,16,128]{4,3,2,1,0:T(8,128)(2,1)S(1)} %get-tuple-element.46), channel_id=1, source_target_pairs={{0,4},{1,5},{2,6},{3,7},{4,0},{5,1},{6,2},{7,3},{8,12},{9,13},{10,... | collective-permute-start | bytes 221192 | tf_op jit(solution)/shard_map/ppermute | solution.py:282
  34.9 0.7 %collective-permute-start.12 = (bf16[2,3,3,16,128]{4,3,2,1,0:T(8,128)(2,1)S(1)}, bf16[2,3,3,16,128]{4,3,2,1,0:T(8,128)(2,1)S(1)}, u32[]{:S(2)}, u32[]{:S(2)}) collective-permute-start(bf16[2,3,3,16,128]{4,3,2,1,0:T(8,128)(2,1)S(1)} %get-tuple-element.47), channel_id=1, source_target_pairs={{0,6},{1,7},{2,4},{3,5},{4,2},{5,3},{6,0},{7,1},{8,14},{9,15},{10,... | collective-permute-start | bytes 221192 | tf_op jit(solution)/shard_map/ppermute | solution.py:282
  35.6 1.0 %collective-permute-done.10 = bf16[2,3,3,16,128]{4,3,2,1,0:T(8,128)(2,1)S(1)} collective-permute-done((bf16[2,3,3,16,128]{4,3,2,1,0:T(8,128)(2,1)S(1)}, bf16[2,3,3,16,128]{4,3,2,1,0:T(8,128)(2,1)S(1)}, u32[]{:S(2)}, u32[]{:S(2)}) %collective-permute-start.10) | collective-permute-done | bytes 73760 | tf_op jit(solution)/shard_map/ppermute | solution.py:282
  36.6 1.1 %collective-permute-done.11 = bf16[2,3,3,16,128]{4,3,2,1,0:T(8,128)(2,1)S(1)} collective-permute-done((bf16[2,3,3,16,128]{4,3,2,1,0:T(8,128)(2,1)S(1)}, bf16[2,3,3,16,128]{4,3,2,1,0:T(8,128)(2,1)S(1)}, u32[]{:S(2)}, u32[]{:S(2)}) %collective-permute-start.11) | collective-permute-done | bytes 73760 | tf_op jit(solution)/shard_map/ppermute | solution.py:282
  37.7 2.5 %collective-permute-done.12 = bf16[2,3,3,16,128]{4,3,2,1,0:T(8,128)(2,1)S(1)} collective-permute-done((bf16[2,3,3,16,128]{4,3,2,1,0:T(8,128)(2,1)S(1)}, bf16[2,3,3,16,128]{4,3,2,1,0:T(8,128)(2,1)S(1)}, u32[]{:S(2)}, u32[]{:S(2)}) %collective-permute-start.12) | collective-permute-done | bytes 73760 | tf_op jit(solution)/shard_map/ppermute | solution.py:282
  40.2 2.3 %collective-permute-start.13 = (bf16[2,3,3,16,128]{4,3,2,1,0:T(8,128)(2,1)S(1)}, bf16[2,3,3,16,128]{4,3,2,1,0:T(8,128)(2,1)S(1)}, u32[]{:S(2)}, u32[]{:S(2)}) collective-permute-start(bf16[2,3,3,16,128]{4,3,2,1,0:T(8,128)(2,1)S(1)} %add_convert_fusion.1), channel_id=1, source_target_pairs={{0,8},{1,9},{2,10},{3,11},{4,12},{5,13},{6,14},{7,15},{8,0},{9,1},... | collective-permute-start | bytes 221192 | tf_op jit(solution)/shard_map/ppermute | solution.py:282
  42.5 3.9 %collective-permute-done.13 = bf16[2,3,3,16,128]{4,3,2,1,0:T(8,128)(2,1)S(1)} collective-permute-done((bf16[2,3,3,16,128]{4,3,2,1,0:T(8,128)(2,1)S(1)}, bf16[2,3,3,16,128]{4,3,2,1,0:T(8,128)(2,1)S(1)}, u32[]{:S(2)}, u32[]{:S(2)}) %collective-permute-start.13) | collective-permute-done | bytes 73760 | tf_op jit(solution)/shard_map/ppermute | solution.py:282
  46.4 0.7 %collective-permute-start.16 = (bf16[2,3,3,16,128]{4,3,2,1,0:T(8,128)(2,1)S(1)}, bf16[2,3,3,16,128]{4,3,2,1,0:T(8,128)(2,1)S(1)}, u32[]{:S(2)}, u32[]{:S(2)}) collective-permute-start(bf16[2,3,3,16,128]{4,3,2,1,0:T(8,128)(2,1)S(1)} %add_convert_fusion.mine), channel_id=1, source_target_pairs={{0,6},{1,7},{2,4},{3,5},{4,2},{5,3},{6,0},{7,1},{8,14},{9,15},{10,... | collective-permute-start | bytes 221192 | tf_op jit(solution)/shard_map/ppermute | solution.py:282
  47.1 2.0 %collective-permute-start.15 = (bf16[2,3,3,16,128]{4,3,2,1,0:T(8,128)(2,1)S(1)}, bf16[2,3,3,16,128]{4,3,2,1,0:T(8,128)(2,1)S(1)}, u32[]{:S(2)}, u32[]{:S(2)}) collective-permute-start(bf16[2,3,3,16,128]{4,3,2,1,0:T(8,128)(2,1)S(1)} %add_convert_fusion.mine), channel_id=1, source_target_pairs={{0,4},{1,5},{2,6},{3,7},{4,0},{5,1},{6,2},{7,3},{8,12},{9,13},{10,... | collective-permute-start | bytes 221192 | tf_op jit(solution)/shard_map/ppermute | solution.py:282
  49.1 0.9 %collective-permute-start.14 = (bf16[2,3,3,16,128]{4,3,2,1,0:T(8,128)(2,1)S(1)}, bf16[2,3,3,16,128]{4,3,2,1,0:T(8,128)(2,1)S(1)}, u32[]{:S(2)}, u32[]{:S(2)}) collective-permute-start(bf16[2,3,3,16,128]{4,3,2,1,0:T(8,128)(2,1)S(1)} %add_convert_fusion.mine), channel_id=1, source_target_pairs={{0,2},{1,3},{2,0},{3,1},{4,6},{5,7},{6,4},{7,5},{8,10},{9,11},{10,... | collective-permute-start | bytes 221192 | tf_op jit(solution)/shard_map/ppermute | solution.py:282
  49.9 1.8 %collective-permute-done.16.rest_2_ = bf16[2,3,3,16,128]{4,3,2,1,0:T(8,128)(2,1)S(1)} collective-permute-done((bf16[2,3,3,16,128]{4,3,2,1,0:T(8,128)(2,1)S(1)}, bf16[2,3,3,16,128]{4,3,2,1,0:T(8,128)(2,1)S(1)}, u32[]{:S(2)}, u32[]{:S(2)}) %collective-permute-start.16) | collective-permute-done | bytes 73760 | tf_op jit(solution)/shard_map/ppermute | solution.py:282
  52.2 1.2 %collective-permute-done.14.rest_0_ = bf16[2,3,3,16,128]{4,3,2,1,0:T(8,128)(2,1)S(1)} collective-permute-done((bf16[2,3,3,16,128]{4,3,2,1,0:T(8,128)(2,1)S(1)}, bf16[2,3,3,16,128]{4,3,2,1,0:T(8,128)(2,1)S(1)}, u32[]{:S(2)}, u32[]{:S(2)}) %collective-permute-start.14) | collective-permute-done | bytes 73760 | tf_op jit(solution)/shard_map/ppermute | solution.py:282
  53.6 1.1 %shard_map.80 = bf16[4,128,128]{2,1,0:T(8,128)(2,1)} custom-call(bf16[6,128,384]{2,1,0:T(8,128)(2,1)S(1)} %get-tuple-element.39.hw, bf16[3,3,128,128]{3,2,1,0:T(8,128)(2,1)S(1)} %bitcast.20), custom_call_target="tpu_custom_call" | custom-call | flops 150994944 | bytes 1015808 | tf_op jit(solution)/shard_map/pallas_call | solution.py:248
  55.1 1.1 %shard_map.83 = (f32[3,3,128,128]{3,2,1,0:T(8,128)}, f32[3,3,128,128]{3,2,1,0:T(8,128)}) custom-call(bf16[2,3,3,64,128]{4,3,2,1,0:T(8,128)(2,1)S(1)} %shard_map.82.mine, bf16[2,3,3,64,128]{4,3,2,1,0:T(8,128)(2,1)S(1)} %collective-permute-done.17.theirs), custom_call_target="tpu_custom_call" | custom-call | flops 73728 | bytes 1769472 | tf_op jit(solution)/shard_map/pallas_call | solution.py:248
  (30 shorter events, 4.3 us)
Async XLA Ops:
  0.6 8.2 %collective-permute-start.1 = (bf16[4,128,128]{2,1,0:T(8,128)(2,1)}, bf16[4,128,128]{2,1,0:T(8,128)(2,1)S(1)}, u32[]{:S(2)}, u32[]{:S(2)}) collective-permute-start(bf16[4,128,128]{2,1,0:T(8,128)(2,1)} %bitcast.21), channel_id=1, source_target_pairs={{0,0},{1,2},{2,1},{3,4},{4,3},{5,6},{6,5},{7,8},{8,7},{9,10},{10,9... | collective-permute-start | bytes 393224 | tf_op jit(solution)/shard_map/ppermute | solution.py:282
  2.2 6.6 %collective-permute-start = (bf16[4,128,128]{2,1,0:T(8,128)(2,1)}, bf16[4,128,128]{2,1,0:T(8,128)(2,1)S(1)}, u32[]{:S(2)}, u32[]{:S(2)}) collective-permute-start(bf16[4,128,128]{2,1,0:T(8,128)(2,1)} %bitcast.22), channel_id=1, source_target_pairs={{0,1},{1,0},{2,3},{3,2},{4,5},{5,4},{6,7},{7,6},{8,9},{9,8},{10,11... | collective-permute-start | bytes 393224 | tf_op jit(solution)/shard_map/ppermute | solution.py:282
  5.7 1.0 %copy-start = (bf16[1,3,3,128,128]{4,3,2,1,0:T(8,128)(2,1)S(1)}, bf16[1,3,3,128,128]{4,3,2,1,0:T(8,128)(2,1)}, u32[]{:S(2)}) copy-start(bf16[1,3,3,128,128]{4,3,2,1,0:T(8,128)(2,1)} %param.7) | copy-start | bytes 884740
  6.6 1.0 %copy-start.3 = (bf16[1,3,3,128,128]{4,3,2,1,0:T(8,128)(2,1)S(1)}, bf16[1,3,3,128,128]{4,3,2,1,0:T(8,128)(2,1)}, u32[]{:S(2)}) copy-start(bf16[1,3,3,128,128]{4,3,2,1,0:T(8,128)(2,1)} %param.6) | copy-start | bytes 884740
  7.6 0.9 %copy-start.5 = (bf16[1,4,128,128]{3,2,1,0:T(8,128)(2,1)S(1)}, bf16[1,4,128,128]{3,2,1,0:T(8,128)(2,1)}, u32[]{:S(2)}) copy-start(bf16[1,4,128,128]{3,2,1,0:T(8,128)(2,1)} %param.4) | copy-start | bytes 393220
  8.5 1.0 %copy-start.1 = (bf16[1,3,3,128,128]{4,3,2,1,0:T(8,128)(2,1)S(1)}, bf16[1,3,3,128,128]{4,3,2,1,0:T(8,128)(2,1)}, u32[]{:S(2)}) copy-start(bf16[1,3,3,128,128]{4,3,2,1,0:T(8,128)(2,1)} %param.7) | copy-start | bytes 884740
  9.5 2.3 %copy-start.2 = (bf16[1,4,128,128]{3,2,1,0:T(8,128)(2,1)S(1)}, bf16[1,4,128,128]{3,2,1,0:T(8,128)(2,1)}, u32[]{:S(2)}) copy-start(bf16[1,4,128,128]{3,2,1,0:T(8,128)(2,1)} %param.5) | copy-start | bytes 393220
  11.2 8.3 %collective-permute-start.2 = (bf16[8,128,128]{2,1,0:T(8,128)(2,1)S(1)}, bf16[8,128,128]{2,1,0:T(8,128)(2,1)S(1)}, u32[]{:S(2)}, u32[]{:S(2)}) collective-permute-start(bf16[8,128,128]{2,1,0:T(8,128)(2,1)S(1)} %get-tuple-element.29.skip_here), channel_id=1, source_target_pairs={{0,16},{1,17},{2,18},{3,19},{4,20},{5,21},{6,22},{7,23},{8,24},{9,... | collective-permute-start | bytes 786440 | tf_op jit(solution)/shard_map/ppermute | solution.py:282
  11.7 4.1 %collective-permute-start.4 = (bf16[2,128,128]{2,1,0:T(8,128)(2,1)S(1)}, bf16[2,128,128]{2,1,0:T(8,128)(2,1)S(1)}, u32[]{:S(2)}, u32[]{:S(2)}) collective-permute-start(bf16[2,128,128]{2,1,0:T(8,128)(2,1)S(1)} %get-tuple-element.50), channel_id=1, source_target_pairs={{0,0},{1,2},{2,1},{3,4},{4,3},{5,6},{6,5},{7,8},{8,7},{9,10},{10,9... | collective-permute-start | bytes 196616 | tf_op jit(solution)/shard_map/ppermute | solution.py:282
  12.4 4.4 %collective-permute-start.3 = (bf16[2,128,128]{2,1,0:T(8,128)(2,1)S(1)}, bf16[2,128,128]{2,1,0:T(8,128)(2,1)S(1)}, u32[]{:S(2)}, u32[]{:S(2)}) collective-permute-start(bf16[2,128,128]{2,1,0:T(8,128)(2,1)S(1)} %get-tuple-element.51), channel_id=1, source_target_pairs={{0,1},{1,0},{2,3},{3,2},{4,5},{5,4},{6,7},{7,6},{8,9},{9,8},{10,11... | collective-permute-start | bytes 196616 | tf_op jit(solution)/shard_map/ppermute | solution.py:282
  20.2 8.1 %collective-permute-start.5 = (bf16[4,128,128]{2,1,0:T(8,128)(2,1)S(1)}, bf16[4,128,128]{2,1,0:T(8,128)(2,1)S(1)}, u32[]{:S(2)}, u32[]{:S(2)}) collective-permute-start(bf16[4,128,128]{2,1,0:T(8,128)(2,1)S(1)} %get-tuple-element.32), channel_id=1, source_target_pairs={{0,16},{1,17},{2,18},{3,19},{4,20},{5,21},{6,22},{7,23},{8,24},{9,... | collective-permute-start | bytes 393224 | tf_op jit(solution)/shard_map/ppermute | solution.py:282
  22.2 5.1 %collective-permute-start.6 = (bf16[2,128,128]{2,1,0:T(8,128)(2,1)S(1)}, bf16[2,128,128]{2,1,0:T(8,128)(2,1)S(1)}, u32[]{:S(2)}, u32[]{:S(2)}) collective-permute-start(bf16[2,128,128]{2,1,0:T(8,128)(2,1)S(1)} %get-tuple-element.33), channel_id=1, source_target_pairs={{0,17},{1,16},{2,19},{3,18},{4,21},{5,20},{6,23},{7,22},{8,25},{9,... | collective-permute-start | bytes 196616 | tf_op jit(solution)/shard_map/ppermute | solution.py:282
  22.2 6.1 %collective-permute-start.7 = (bf16[2,128,128]{2,1,0:T(8,128)(2,1)S(1)}, bf16[2,128,128]{2,1,0:T(8,128)(2,1)S(1)}, u32[]{:S(2)}, u32[]{:S(2)}) collective-permute-start(bf16[2,128,128]{2,1,0:T(8,128)(2,1)S(1)} %get-tuple-element.34), channel_id=1, source_target_pairs={{0,16},{1,18},{2,17},{3,20},{4,19},{5,22},{6,21},{7,24},{8,23},{9,... | collective-permute-start | bytes 196616 | tf_op jit(solution)/shard_map/ppermute | solution.py:282
  28.3 0.9 %copy-start.6 = (bf16[1,4,128,128]{3,2,1,0:T(8,128)(2,1)S(1)}, bf16[1,4,128,128]{3,2,1,0:T(8,128)(2,1)}, u32[]{:S(2)}) copy-start(bf16[1,4,128,128]{3,2,1,0:T(8,128)(2,1)} %param.4) | copy-start | bytes 393220
  30.3 1.4 %collective-permute-start.8 = (bf16[3,3,64,128]{3,2,1,0:T(8,128)(2,1)S(1)}, bf16[3,3,64,128]{3,2,1,0:T(8,128)(2,1)S(1)}, u32[]{:S(2)}, u32[]{:S(2)}) collective-permute-start(bf16[3,3,64,128]{3,2,1,0:T(8,128)(2,1)S(1)} %get-tuple-element.41), channel_id=1, source_target_pairs={{0,1},{1,0},{2,3},{3,2},{4,5},{5,4},{6,7},{7,6},{8,9},{9,8},{10,11... | collective-permute-start | bytes 442376 | tf_op jit(solution)/shard_map/ppermute | solution.py:282
  30.4 1.6 %collective-permute-start.9 = (bf16[3,3,64,128]{3,2,1,0:T(8,128)(2,1)S(1)}, bf16[3,3,64,128]{3,2,1,0:T(8,128)(2,1)S(1)}, u32[]{:S(2)}, u32[]{:S(2)}) collective-permute-start(bf16[3,3,64,128]{3,2,1,0:T(8,128)(2,1)S(1)} %get-tuple-element.43), channel_id=1, source_target_pairs={{0,1},{1,0},{2,3},{3,2},{4,5},{5,4},{6,7},{7,6},{8,9},{9,8},{10,11... | collective-permute-start | bytes 442376 | tf_op jit(solution)/shard_map/ppermute | solution.py:282
  32.1 4.5 %collective-permute-start.10 = (bf16[2,3,3,16,128]{4,3,2,1,0:T(8,128)(2,1)S(1)}, bf16[2,3,3,16,128]{4,3,2,1,0:T(8,128)(2,1)S(1)}, u32[]{:S(2)}, u32[]{:S(2)}) collective-permute-start(bf16[2,3,3,16,128]{4,3,2,1,0:T(8,128)(2,1)S(1)} %get-tuple-element.45), channel_id=1, source_target_pairs={{0,2},{1,3},{2,0},{3,1},{4,6},{5,7},{6,4},{7,5},{8,10},{9,11},{10,... | collective-permute-start | bytes 221192 | tf_op jit(solution)/shard_map/ppermute | solution.py:282
  33.3 4.4 %collective-permute-start.11 = (bf16[2,3,3,16,128]{4,3,2,1,0:T(8,128)(2,1)S(1)}, bf16[2,3,3,16,128]{4,3,2,1,0:T(8,128)(2,1)S(1)}, u32[]{:S(2)}, u32[]{:S(2)}) collective-permute-start(bf16[2,3,3,16,128]{4,3,2,1,0:T(8,128)(2,1)S(1)} %get-tuple-element.46), channel_id=1, source_target_pairs={{0,4},{1,5},{2,6},{3,7},{4,0},{5,1},{6,2},{7,3},{8,12},{9,13},{10,... | collective-permute-start | bytes 221192 | tf_op jit(solution)/shard_map/ppermute | solution.py:282
  34.9 5.3 %collective-permute-start.12 = (bf16[2,3,3,16,128]{4,3,2,1,0:T(8,128)(2,1)S(1)}, bf16[2,3,3,16,128]{4,3,2,1,0:T(8,128)(2,1)S(1)}, u32[]{:S(2)}, u32[]{:S(2)}) collective-permute-start(bf16[2,3,3,16,128]{4,3,2,1,0:T(8,128)(2,1)S(1)} %get-tuple-element.47), channel_id=1, source_target_pairs={{0,6},{1,7},{2,4},{3,5},{4,2},{5,3},{6,0},{7,1},{8,14},{9,15},{10,... | collective-permute-start | bytes 221192 | tf_op jit(solution)/shard_map/ppermute | solution.py:282
  40.2 6.1 %collective-permute-start.13 = (bf16[2,3,3,16,128]{4,3,2,1,0:T(8,128)(2,1)S(1)}, bf16[2,3,3,16,128]{4,3,2,1,0:T(8,128)(2,1)S(1)}, u32[]{:S(2)}, u32[]{:S(2)}) collective-permute-start(bf16[2,3,3,16,128]{4,3,2,1,0:T(8,128)(2,1)S(1)} %add_convert_fusion.1), channel_id=1, source_target_pairs={{0,8},{1,9},{2,10},{3,11},{4,12},{5,13},{6,14},{7,15},{8,0},{9,1},... | collective-permute-start | bytes 221192 | tf_op jit(solution)/shard_map/ppermute | solution.py:282
  46.4 7.2 %copy-start.4 = (bf16[1,3,3,128,128]{4,3,2,1,0:T(8,128)(2,1)S(1)}, bf16[1,3,3,128,128]{4,3,2,1,0:T(8,128)(2,1)}, u32[]{:S(2)}) copy-start(bf16[1,3,3,128,128]{4,3,2,1,0:T(8,128)(2,1)} %param.6) | copy-start | bytes 884740
  46.4 5.3 %collective-permute-start.16 = (bf16[2,3,3,16,128]{4,3,2,1,0:T(8,128)(2,1)S(1)}, bf16[2,3,3,16,128]{4,3,2,1,0:T(8,128)(2,1)S(1)}, u32[]{:S(2)}, u32[]{:S(2)}) collective-permute-start(bf16[2,3,3,16,128]{4,3,2,1,0:T(8,128)(2,1)S(1)} %add_convert_fusion.mine), channel_id=1, source_target_pairs={{0,6},{1,7},{2,4},{3,5},{4,2},{5,3},{6,0},{7,1},{8,14},{9,15},{10,... | collective-permute-start | bytes 221192 | tf_op jit(solution)/shard_map/ppermute | solution.py:282
  47.1 5.1 %collective-permute-start.15 = (bf16[2,3,3,16,128]{4,3,2,1,0:T(8,128)(2,1)S(1)}, bf16[2,3,3,16,128]{4,3,2,1,0:T(8,128)(2,1)S(1)}, u32[]{:S(2)}, u32[]{:S(2)}) collective-permute-start(bf16[2,3,3,16,128]{4,3,2,1,0:T(8,128)(2,1)S(1)} %add_convert_fusion.mine), channel_id=1, source_target_pairs={{0,4},{1,5},{2,6},{3,7},{4,0},{5,1},{6,2},{7,3},{8,12},{9,13},{10,... | collective-permute-start | bytes 221192 | tf_op jit(solution)/shard_map/ppermute | solution.py:282
  49.1 4.4 %collective-permute-start.14 = (bf16[2,3,3,16,128]{4,3,2,1,0:T(8,128)(2,1)S(1)}, bf16[2,3,3,16,128]{4,3,2,1,0:T(8,128)(2,1)S(1)}, u32[]{:S(2)}, u32[]{:S(2)}) collective-permute-start(bf16[2,3,3,16,128]{4,3,2,1,0:T(8,128)(2,1)S(1)} %add_convert_fusion.mine), channel_id=1, source_target_pairs={{0,2},{1,3},{2,0},{3,1},{4,6},{5,7},{6,4},{7,5},{8,10},{9,11},{10,... | collective-permute-start | bytes 221192 | tf_op jit(solution)/shard_map/ppermute | solution.py:282
  53.5 1.6 %collective-permute-start.17 = (bf16[2,3,3,64,128]{4,3,2,1,0:T(8,128)(2,1)S(1)}, bf16[2,3,3,64,128]{4,3,2,1,0:T(8,128)(2,1)S(1)}, u32[]{:S(2)}, u32[]{:S(2)}) collective-permute-start(bf16[2,3,3,64,128]{4,3,2,1,0:T(8,128)(2,1)S(1)} %shard_map.82.mine), channel_id=1, source_target_pairs={{0,1},{1,0},{2,3},{3,2},{4,5},{5,4},{6,7},{7,6},{8,9},{9,8},{10,11... | collective-permute-start | bytes 884744 | tf_op jit(solution)/shard_map/ppermute | solution.py:282

commit v6 on v5

--- a/solution.py
+++ b/solution.py
@@ -275,10 +275,16 @@
     def same(r):
         return r
 
-    def swap(array, across, to):
-        pairs = [
-            (s * strips + r, ((s + half) % segments if across else s) * strips + to(r)) for s, r in everyone
-        ]
+    def swap(array, to):
+        pairs = [(s * strips + r, s * strips + to(r)) for s, r in everyone]
+        return lax.ppermute(array, ("segment", "rows"), pairs)
+
+    def down(array):
+        pairs = [(s * strips + r, (s + half) * strips + r) for s, r in everyone if s < half]
+        return lax.ppermute(array, ("segment", "rows"), pairs)
+
+    def up(array, to):
+        pairs = [(s * strips + r, (s - half) * strips + to(r)) for s, r in everyone if s >= half]
         return lax.ppermute(array, ("segment", "rows"), pairs)
 
     def like(rows, dtype):
@@ -291,8 +297,8 @@
         return jax.ShapeDtypeStruct((rows, columns, 3 * channels), BF16)
 
     work = 2 * columns * 9 * channels * channels
-    x_other = swap(x, False, other)
-    x_core = swap(x, False, core)
+    x_other = swap(x, other)
+    x_core = swap(x, core)
     xo, mid = call(
         early_kernel,
         [wide_out(own), like(own - 2, F32)],
@@ -307,9 +313,9 @@
         (xo, mid, x_core, x_other, main, second),
         work * (2 * own + 8),
     )
-    g_core = swap(jnp.where(even, g[own - 2 :], g[:2]), False, core)
-    g_other = swap(jnp.where(even, g[:2], g[own - 2 :]), False, other)
-    skip_there = swap(skip_here, True, same)
+    g_core = swap(jnp.where(even, g[own - 2 :], g[:2]), core)
+    g_other = swap(jnp.where(even, g[:2], g[own - 2 :]), other)
+    skip_there = down(skip_here)
     output, gw, back, edge_core, edge_other = call(
         functools.partial(middle_kernel, segments, strips),
         [like(own, BF16), wide_out(own + 2), like(own, BF16), like(2, BF16), like(2, BF16)],
@@ -317,9 +323,9 @@
         (skip_here, skip_there, pre1, g, g_core, g_other, second),
         work * (2 * own + 2),
     )
-    back_own = swap(back, True, same)
-    back_other = swap(edge_other, True, other)
-    back_core = swap(edge_core, True, core)
+    back_own = up(back, same)
+    back_other = up(edge_other, other)
+    back_core = up(edge_core, core)
     taps = (3, 3, channels, channels)
     halves = (3, 3, channels // 2, channels)
     terms = [jax.ShapeDtypeStruct(halves, F32), jax.ShapeDtypeStruct(halves, BF16)]
@@ -341,7 +347,7 @@
     factor = 1.0 / math.sqrt(own * strips * columns)
 
     def jump(array, bit, times=1):
-        return swap(array, False, lambda r: r ^ (times << bit))
+        return swap(array, lambda r: r ^ (times << bit))
 
     bits = strips.bit_length() - 1
     quarter = (2, 3, 3, channels // 8, channels)

time: 56.5 us -> 59.2 us (1.048)
  starting transfers between devices: 22.7 us -> 25.4 us
    ppermute x18 -> x14, waiting for transfers between devices: 22.2 us -> 15 us  [swap(): return lax.ppermute(array, ('segment', 'rows'), pairs)]
    ppermute x0 -> x4, waiting for transfers between devices: none -> 7.03 us  [the longest x3 6.36 us: up(): return lax.ppermute(array, ('segment', 'rows'), pairs)]
    ppermute x0 -> x4, starting transfers between devices: none -> 6.22 us  [the longest x3 3.86 us: up(): return lax.ppermute(array, ('segment', 'rows'), pairs)]
    ppermute x18 -> x14, starting transfers between devices: 22.7 us -> 19.2 us  [swap(): return lax.ppermute(array, ('segment', 'rows'), pairs)]
  transfers between devices with their start and end apart: 18 -> 18, of which waited for: 14 -> 14; matrix products, arithmetic and copies ran while one was open for 0% -> 0% of each run, Pallas kernels for 3% -> 2%
where the time goes in v6:
time: 59.2 us; the launch traced here: 58.8 us
  starting transfers between devices  25.4 us (43%)
  waiting for transfers between devices  22 us (37%)
  Pallas kernels  6.85 us (12%)
  local copies, waits for them, and re-layouts  3.67 us (6%)
  between operations  0.79 us (1%)
    ppermute x14, starting transfers between devices, swap(): return lax.ppermute(array, ('segment', 'rows'), pairs)  19.2 us
    ppermute x14, waiting for transfers between devices, swap(): return lax.ppermute(array, ('segment', 'rows'), pairs)  15 us
    pallas_call x9, Pallas kernels, call(): pl.pallas_call(kernel, out_shape=outs, in_specs=[pl.BlockSpec(memory_spac...  6.85 us
    ppermute x3, waiting for transfers between devices, up(): return lax.ppermute(array, ('segment', 'rows'), pairs)  6.36 us
    ppermute x3, starting transfers between devices, up(): return lax.ppermute(array, ('segment', 'rows'), pairs)  3.86 us
    unnamed x14, local copies, waits for them, and re-layouts  3.67 us
    ppermute x1, starting transfers between devices, down(): return lax.ppermute(array, ('segment', 'rows'), pairs)  2.36 us
  transfers between devices with their start and end apart: 18, of which 14 were waited for; matrix products, arithmetic and copies ran while one was open for 0% of the time, Pallas kernels for 2%

profile of v6, /device:TPU:0, one launch (start us, length us, event | category | flops | bytes accessed | tf_op | source)
XLA Modules:
  0.0 58.8 jit_solution(13446392440008017891)
XLA Ops:
  0.6 1.6 %collective-permute-start.1 = (bf16[4,128,128]{2,1,0:T(8,128)(2,1)}, bf16[4,128,128]{2,1,0:T(8,128)(2,1)S(1)}, u32[]{:S(2)}, u32[]{:S(2)}) collective-permute-start(bf16[4,128,128]{2,1,0:T(8,128)(2,1)} %bitcast.21), channel_id=1, source_target_pairs={{0,0},{1,2},{2,1},{3,4},{4,3},{5,6},{6,5},{7,8},{8,7},{9,10},{10,9... | collective-permute-start | bytes 393224 | tf_op jit(solution)/shard_map/ppermute | solution.py:280
  2.2 3.5 %collective-permute-start = (bf16[4,128,128]{2,1,0:T(8,128)(2,1)}, bf16[4,128,128]{2,1,0:T(8,128)(2,1)S(1)}, u32[]{:S(2)}, u32[]{:S(2)}) collective-permute-start(bf16[4,128,128]{2,1,0:T(8,128)(2,1)} %bitcast.22), channel_id=1, source_target_pairs={{0,1},{1,0},{2,3},{3,2},{4,5},{5,4},{6,7},{7,6},{8,9},{9,8},{10,11... | collective-permute-start | bytes 393224 | tf_op jit(solution)/shard_map/ppermute | solution.py:280
  5.7 1.0 %copy-done = bf16[1,3,3,128,128]{4,3,2,1,0:T(8,128)(2,1)S(1)} copy-done((bf16[1,3,3,128,128]{4,3,2,1,0:T(8,128)(2,1)S(1)}, bf16[1,3,3,128,128]{4,3,2,1,0:T(8,128)(2,1)}, u32[]{:S(2)}) %copy-start) | copy-done | bytes 294936
  6.6 1.0 %copy-done.3 = bf16[1,3,3,128,128]{4,3,2,1,0:T(8,128)(2,1)S(1)} copy-done((bf16[1,3,3,128,128]{4,3,2,1,0:T(8,128)(2,1)S(1)}, bf16[1,3,3,128,128]{4,3,2,1,0:T(8,128)(2,1)}, u32[]{:S(2)}) %copy-start.3) | copy-done | bytes 294936
  7.6 0.9 %copy-done.5 = bf16[1,4,128,128]{3,2,1,0:T(8,128)(2,1)S(1)} copy-done((bf16[1,4,128,128]{3,2,1,0:T(8,128)(2,1)S(1)}, bf16[1,4,128,128]{3,2,1,0:T(8,128)(2,1)}, u32[]{:S(2)}) %copy-start.5) | copy-done | bytes 131096
  9.5 1.7 %shard_map.76 = (f32[6,128,128]{2,1,0:T(8,128)S(1)}, f32[8,128,128]{2,1,0:T(8,128)S(1)}, bf16[4,128,128]{2,1,0:T(8,128)(2,1)S(1)}, bf16[8,128,128]{2,1,0:T(8,128)(2,1)S(1)}) custom-call(bf16[4,128,384]{2,1,0:T(8,128)(2,1)S(1)} %get-tuple-element.27.xo, f32[2,128,128]{2,1,0:T(8,128)S(1)} %get-tuple-element.28.mid, ...), custom_call_target="tpu_custom_call" | custom-call | flops 603979776 | bytes 2686976 | tf_op jit(solution)/shard_map/pallas_call | solution.py:248
  11.2 2.4 %collective-permute-start.2 = (bf16[8,128,128]{2,1,0:T(8,128)(2,1)S(1)}, bf16[8,128,128]{2,1,0:T(8,128)(2,1)S(1)}, u32[]{:S(2)}, u32[]{:S(2)}) collective-permute-start(bf16[8,128,128]{2,1,0:T(8,128)(2,1)S(1)} %get-tuple-element.29.skip_here), channel_id=1, source_target_pairs={{0,16},{1,17},{2,18},{3,19},{4,20},{5,21},{6,22},{7,23},{8,24},{9,... | collective-permute-start | bytes 786440 | tf_op jit(solution)/shard_map/ppermute | solution.py:284
  14.3 3.5 %collective-permute-start.3 = (bf16[2,128,128]{2,1,0:T(8,128)(2,1)S(1)}, bf16[2,128,128]{2,1,0:T(8,128)(2,1)S(1)}, u32[]{:S(2)}, u32[]{:S(2)}) collective-permute-start(bf16[2,128,128]{2,1,0:T(8,128)(2,1)S(1)} %get-tuple-element.51), channel_id=1, source_target_pairs={{0,1},{1,0},{2,3},{3,2},{4,5},{5,4},{6,7},{7,6},{8,9},{9,8},{10,11... | collective-permute-start | bytes 196616 | tf_op jit(solution)/shard_map/ppermute | solution.py:280
  17.7 0.9 %collective-permute-done.3.g_core = bf16[2,128,128]{2,1,0:T(8,128)(2,1)S(1)} collective-permute-done((bf16[2,128,128]{2,1,0:T(8,128)(2,1)S(1)}, bf16[2,128,128]{2,1,0:T(8,128)(2,1)S(1)}, u32[]{:S(2)}, u32[]{:S(2)}) %collective-permute-start.3) | collective-permute-done | bytes 65568 | tf_op jit(solution)/shard_map/ppermute | solution.py:280
  20.0 1.3 %collective-permute-start.5 = (bf16[4,128,128]{2,1,0:T(8,128)(2,1)S(1)}, bf16[4,128,128]{2,1,0:T(8,128)(2,1)S(1)}, u32[]{:S(2)}, u32[]{:S(2)}) collective-permute-start(bf16[4,128,128]{2,1,0:T(8,128)(2,1)S(1)} %get-tuple-element.32), channel_id=1, source_target_pairs={{16,0},{17,1},{18,2},{19,3},{20,4},{21,5},{22,6},{23,7},{24,8},{25... | collective-permute-start | bytes 393224 | tf_op jit(solution)/shard_map/ppermute | solution.py:288
  21.2 1.3 %collective-permute-start.6 = (bf16[2,128,128]{2,1,0:T(8,128)(2,1)S(1)}, bf16[2,128,128]{2,1,0:T(8,128)(2,1)S(1)}, u32[]{:S(2)}, u32[]{:S(2)}) collective-permute-start(bf16[2,128,128]{2,1,0:T(8,128)(2,1)S(1)} %get-tuple-element.33), channel_id=1, source_target_pairs={{16,1},{17,0},{18,3},{19,2},{20,5},{21,4},{22,7},{23,6},{24,9},{25... | collective-permute-start | bytes 196616 | tf_op jit(solution)/shard_map/ppermute | solution.py:288
  22.5 1.3 %collective-permute-start.7 = (bf16[2,128,128]{2,1,0:T(8,128)(2,1)S(1)}, bf16[2,128,128]{2,1,0:T(8,128)(2,1)S(1)}, u32[]{:S(2)}, u32[]{:S(2)}) collective-permute-start(bf16[2,128,128]{2,1,0:T(8,128)(2,1)S(1)} %get-tuple-element.34), channel_id=1, source_target_pairs={{16,0},{17,2},{18,1},{19,4},{20,3},{21,6},{22,5},{23,8},{24,7},{25... | collective-permute-start | bytes 196616 | tf_op jit(solution)/shard_map/ppermute | solution.py:288
  23.8 4.1 %collective-permute-done.6.back_core = bf16[2,128,128]{2,1,0:T(8,128)(2,1)S(1)} collective-permute-done((bf16[2,128,128]{2,1,0:T(8,128)(2,1)S(1)}, bf16[2,128,128]{2,1,0:T(8,128)(2,1)S(1)}, u32[]{:S(2)}, u32[]{:S(2)}) %collective-permute-start.6) | collective-permute-done | bytes 65568 | tf_op jit(solution)/shard_map/ppermute | solution.py:288
  27.9 2.3 %collective-permute-done.7.back_other = bf16[2,128,128]{2,1,0:T(8,128)(2,1)S(1)} collective-permute-done((bf16[2,128,128]{2,1,0:T(8,128)(2,1)S(1)}, bf16[2,128,128]{2,1,0:T(8,128)(2,1)S(1)}, u32[]{:S(2)}, u32[]{:S(2)}) %collective-permute-start.7) | collective-permute-done | bytes 65568 | tf_op jit(solution)/shard_map/ppermute | solution.py:288
  30.2 0.7 %shard_map.78 = (f32[3,3,64,128]{3,2,1,0:T(8,128)S(1)}, bf16[3,3,64,128]{3,2,1,0:T(8,128)(2,1)S(1)}, bf16[8,128,384]{2,1,0:T(8,128)(2,1)S(1)}) custom-call(bf16[4,128,128]{2,1,0:T(8,128)(2,1)S(1)} %bitcast.17, bf16[2,128,128]{2,1,0:T(8,128)(2,1)S(1)} %collective-permute-done.3.g_core, bf16[2,128,128]{2,1,0:T(8,128)(2,1)S(1)} %collective-permute-done.4.g_other, ...), custom_call_target="tpu_custom_call" | custom-call | flops 150994944 | bytes 3260416 | tf_op jit(solution)/shard_map/pallas_call | solution.py:248
  31.1 1.1 %shard_map.79 = (f32[3,3,64,128]{3,2,1,0:T(8,128)S(1)}, bf16[3,3,64,128]{3,2,1,0:T(8,128)(2,1)S(1)}, bf16[6,128,384]{2,1,0:T(8,128)(2,1)S(1)}) custom-call(bf16[4,128,128]{2,1,0:T(8,128)(2,1)S(1)} %bitcast.24, f32[6,128,128]{2,1,0:T(8,128)S(1)} %get-tuple-element.30.pre1, bf16[8,128,384]{2,1,0:T(8,128)(2,1)S(1)} %get-tuple-element.38.ew, ...), custom_call_target="tpu_custom_call" | custom-call | flops 377487360 | bytes 3227648 | tf_op jit(solution)/shard_map/pallas_call | solution.py:248
  32.2 0.8 %collective-permute-start.8 = (bf16[3,3,64,128]{3,2,1,0:T(8,128)(2,1)S(1)}, bf16[3,3,64,128]{3,2,1,0:T(8,128)(2,1)S(1)}, u32[]{:S(2)}, u32[]{:S(2)}) collective-permute-start(bf16[3,3,64,128]{3,2,1,0:T(8,128)(2,1)S(1)} %get-tuple-element.41), channel_id=1, source_target_pairs={{0,1},{1,0},{2,3},{3,2},{4,5},{5,4},{6,7},{7,6},{8,9},{9,8},{10,11... | collective-permute-start | bytes 442376 | tf_op jit(solution)/shard_map/ppermute | solution.py:280
  33.1 0.9 %collective-permute-done.8.got1 = bf16[3,3,64,128]{3,2,1,0:T(8,128)(2,1)S(1)} collective-permute-done((bf16[3,3,64,128]{3,2,1,0:T(8,128)(2,1)S(1)}, bf16[3,3,64,128]{3,2,1,0:T(8,128)(2,1)S(1)}, u32[]{:S(2)}, u32[]{:S(2)}) %collective-permute-start.8) | collective-permute-done | bytes 147488 | tf_op jit(solution)/shard_map/ppermute | solution.py:280
  34.5 1.9 %collective-permute-start.10 = (bf16[2,3,3,16,128]{4,3,2,1,0:T(8,128)(2,1)S(1)}, bf16[2,3,3,16,128]{4,3,2,1,0:T(8,128)(2,1)S(1)}, u32[]{:S(2)}, u32[]{:S(2)}) collective-permute-start(bf16[2,3,3,16,128]{4,3,2,1,0:T(8,128)(2,1)S(1)} %get-tuple-element.45), channel_id=1, source_target_pairs={{0,2},{1,3},{2,0},{3,1},{4,6},{5,7},{6,4},{7,5},{8,10},{9,11},{10,... | collective-permute-start | bytes 221192 | tf_op jit(solution)/shard_map/ppermute | solution.py:280
  36.4 1.6 %collective-permute-start.11 = (bf16[2,3,3,16,128]{4,3,2,1,0:T(8,128)(2,1)S(1)}, bf16[2,3,3,16,128]{4,3,2,1,0:T(8,128)(2,1)S(1)}, u32[]{:S(2)}, u32[]{:S(2)}) collective-permute-start(bf16[2,3,3,16,128]{4,3,2,1,0:T(8,128)(2,1)S(1)} %get-tuple-element.46), channel_id=1, source_target_pairs={{0,4},{1,5},{2,6},{3,7},{4,0},{5,1},{6,2},{7,3},{8,12},{9,13},{10,... | collective-permute-start | bytes 221192 | tf_op jit(solution)/shard_map/ppermute | solution.py:280
  38.2 0.9 %collective-permute-done.10 = bf16[2,3,3,16,128]{4,3,2,1,0:T(8,128)(2,1)S(1)} collective-permute-done((bf16[2,3,3,16,128]{4,3,2,1,0:T(8,128)(2,1)S(1)}, bf16[2,3,3,16,128]{4,3,2,1,0:T(8,128)(2,1)S(1)}, u32[]{:S(2)}, u32[]{:S(2)}) %collective-permute-start.10) | collective-permute-done | bytes 73760 | tf_op jit(solution)/shard_map/ppermute | solution.py:280
  39.1 2.1 %collective-permute-done.11 = bf16[2,3,3,16,128]{4,3,2,1,0:T(8,128)(2,1)S(1)} collective-permute-done((bf16[2,3,3,16,128]{4,3,2,1,0:T(8,128)(2,1)S(1)}, bf16[2,3,3,16,128]{4,3,2,1,0:T(8,128)(2,1)S(1)}, u32[]{:S(2)}, u32[]{:S(2)}) %collective-permute-start.11) | collective-permute-done | bytes 73760 | tf_op jit(solution)/shard_map/ppermute | solution.py:280
  41.2 2.1 %collective-permute-done.12 = bf16[2,3,3,16,128]{4,3,2,1,0:T(8,128)(2,1)S(1)} collective-permute-done((bf16[2,3,3,16,128]{4,3,2,1,0:T(8,128)(2,1)S(1)}, bf16[2,3,3,16,128]{4,3,2,1,0:T(8,128)(2,1)S(1)}, u32[]{:S(2)}, u32[]{:S(2)}) %collective-permute-start.12) | collective-permute-done | bytes 73760 | tf_op jit(solution)/shard_map/ppermute | solution.py:280
  43.3 1.9 %collective-permute-start.13 = (bf16[2,3,3,16,128]{4,3,2,1,0:T(8,128)(2,1)S(1)}, bf16[2,3,3,16,128]{4,3,2,1,0:T(8,128)(2,1)S(1)}, u32[]{:S(2)}, u32[]{:S(2)}) collective-permute-start(bf16[2,3,3,16,128]{4,3,2,1,0:T(8,128)(2,1)S(1)} %add_convert_fusion.1), channel_id=1, source_target_pairs={{0,8},{1,9},{2,10},{3,11},{4,12},{5,13},{6,14},{7,15},{8,0},{9,1},... | collective-permute-start | bytes 221192 | tf_op jit(solution)/shard_map/ppermute | solution.py:280
  45.2 4.2 %collective-permute-done.13 = bf16[2,3,3,16,128]{4,3,2,1,0:T(8,128)(2,1)S(1)} collective-permute-done((bf16[2,3,3,16,128]{4,3,2,1,0:T(8,128)(2,1)S(1)}, bf16[2,3,3,16,128]{4,3,2,1,0:T(8,128)(2,1)S(1)}, u32[]{:S(2)}, u32[]{:S(2)}) %collective-permute-start.13) | collective-permute-done | bytes 73760 | tf_op jit(solution)/shard_map/ppermute | solution.py:280
  49.4 0.7 %collective-permute-start.16 = (bf16[2,3,3,16,128]{4,3,2,1,0:T(8,128)(2,1)S(1)}, bf16[2,3,3,16,128]{4,3,2,1,0:T(8,128)(2,1)S(1)}, u32[]{:S(2)}, u32[]{:S(2)}) collective-permute-start(bf16[2,3,3,16,128]{4,3,2,1,0:T(8,128)(2,1)S(1)} %add_convert_fusion.mine), channel_id=1, source_target_pairs={{0,6},{1,7},{2,4},{3,5},{4,2},{5,3},{6,0},{7,1},{8,14},{9,15},{10,... | collective-permute-start | bytes 221192 | tf_op jit(solution)/shard_map/ppermute | solution.py:280
  50.1 1.6 %collective-permute-start.15 = (bf16[2,3,3,16,128]{4,3,2,1,0:T(8,128)(2,1)S(1)}, bf16[2,3,3,16,128]{4,3,2,1,0:T(8,128)(2,1)S(1)}, u32[]{:S(2)}, u32[]{:S(2)}) collective-permute-start(bf16[2,3,3,16,128]{4,3,2,1,0:T(8,128)(2,1)S(1)} %add_convert_fusion.mine), channel_id=1, source_target_pairs={{0,4},{1,5},{2,6},{3,7},{4,0},{5,1},{6,2},{7,3},{8,12},{9,13},{10,... | collective-permute-start | bytes 221192 | tf_op jit(solution)/shard_map/ppermute | solution.py:280
  51.7 1.3 %collective-permute-start.14 = (bf16[2,3,3,16,128]{4,3,2,1,0:T(8,128)(2,1)S(1)}, bf16[2,3,3,16,128]{4,3,2,1,0:T(8,128)(2,1)S(1)}, u32[]{:S(2)}, u32[]{:S(2)}) collective-permute-start(bf16[2,3,3,16,128]{4,3,2,1,0:T(8,128)(2,1)S(1)} %add_convert_fusion.mine), channel_id=1, source_target_pairs={{0,2},{1,3},{2,0},{3,1},{4,6},{5,7},{6,4},{7,5},{8,10},{9,11},{10,... | collective-permute-start | bytes 221192 | tf_op jit(solution)/shard_map/ppermute | solution.py:280
  53.0 1.8 %collective-permute-done.16.rest_2_ = bf16[2,3,3,16,128]{4,3,2,1,0:T(8,128)(2,1)S(1)} collective-permute-done((bf16[2,3,3,16,128]{4,3,2,1,0:T(8,128)(2,1)S(1)}, bf16[2,3,3,16,128]{4,3,2,1,0:T(8,128)(2,1)S(1)}, u32[]{:S(2)}, u32[]{:S(2)}) %collective-permute-start.16) | collective-permute-done | bytes 73760 | tf_op jit(solution)/shard_map/ppermute | solution.py:280
  54.8 1.2 %collective-permute-done.14.rest_0_ = bf16[2,3,3,16,128]{4,3,2,1,0:T(8,128)(2,1)S(1)} collective-permute-done((bf16[2,3,3,16,128]{4,3,2,1,0:T(8,128)(2,1)S(1)}, bf16[2,3,3,16,128]{4,3,2,1,0:T(8,128)(2,1)S(1)}, u32[]{:S(2)}, u32[]{:S(2)}) %collective-permute-start.14) | collective-permute-done | bytes 73760 | tf_op jit(solution)/shard_map/ppermute | solution.py:280
  56.2 1.1 %shard_map.80 = bf16[4,128,128]{2,1,0:T(8,128)(2,1)} custom-call(bf16[6,128,384]{2,1,0:T(8,128)(2,1)S(1)} %get-tuple-element.39.hw, bf16[3,3,128,128]{3,2,1,0:T(8,128)(2,1)S(1)} %bitcast.20), custom_call_target="tpu_custom_call" | custom-call | flops 150994944 | bytes 1015808 | tf_op jit(solution)/shard_map/pallas_call | solution.py:248
  57.8 1.1 %shard_map.83 = (f32[3,3,128,128]{3,2,1,0:T(8,128)}, f32[3,3,128,128]{3,2,1,0:T(8,128)}) custom-call(bf16[2,3,3,64,128]{4,3,2,1,0:T(8,128)(2,1)S(1)} %shard_map.82.mine, bf16[2,3,3,64,128]{4,3,2,1,0:T(8,128)(2,1)S(1)} %collective-permute-done.17.theirs), custom_call_target="tpu_custom_call" | custom-call | flops 73728 | bytes 1769472 | tf_op jit(solution)/shard_map/pallas_call | solution.py:248
  (30 shorter events, 4.6 us)
Async XLA Ops:
  0.6 8.2 %collective-permute-start.1 = (bf16[4,128,128]{2,1,0:T(8,128)(2,1)}, bf16[4,128,128]{2,1,0:T(8,128)(2,1)S(1)}, u32[]{:S(2)}, u32[]{:S(2)}) collective-permute-start(bf16[4,128,128]{2,1,0:T(8,128)(2,1)} %bitcast.21), channel_id=1, source_target_pairs={{0,0},{1,2},{2,1},{3,4},{4,3},{5,6},{6,5},{7,8},{8,7},{9,10},{10,9... | collective-permute-start | bytes 393224 | tf_op jit(solution)/shard_map/ppermute | solution.py:280
  2.2 6.6 %collective-permute-start = (bf16[4,128,128]{2,1,0:T(8,128)(2,1)}, bf16[4,128,128]{2,1,0:T(8,128)(2,1)S(1)}, u32[]{:S(2)}, u32[]{:S(2)}) collective-permute-start(bf16[4,128,128]{2,1,0:T(8,128)(2,1)} %bitcast.22), channel_id=1, source_target_pairs={{0,1},{1,0},{2,3},{3,2},{4,5},{5,4},{6,7},{7,6},{8,9},{9,8},{10,11... | collective-permute-start | bytes 393224 | tf_op jit(solution)/shard_map/ppermute | solution.py:280
  5.7 1.0 %copy-start = (bf16[1,3,3,128,128]{4,3,2,1,0:T(8,128)(2,1)S(1)}, bf16[1,3,3,128,128]{4,3,2,1,0:T(8,128)(2,1)}, u32[]{:S(2)}) copy-start(bf16[1,3,3,128,128]{4,3,2,1,0:T(8,128)(2,1)} %param.7) | copy-start | bytes 884740
  6.6 1.0 %copy-start.3 = (bf16[1,3,3,128,128]{4,3,2,1,0:T(8,128)(2,1)S(1)}, bf16[1,3,3,128,128]{4,3,2,1,0:T(8,128)(2,1)}, u32[]{:S(2)}) copy-start(bf16[1,3,3,128,128]{4,3,2,1,0:T(8,128)(2,1)} %param.6) | copy-start | bytes 884740
  7.6 0.9 %copy-start.5 = (bf16[1,4,128,128]{3,2,1,0:T(8,128)(2,1)S(1)}, bf16[1,4,128,128]{3,2,1,0:T(8,128)(2,1)}, u32[]{:S(2)}) copy-start(bf16[1,4,128,128]{3,2,1,0:T(8,128)(2,1)} %param.4) | copy-start | bytes 393220
  8.5 1.0 %copy-start.1 = (bf16[1,3,3,128,128]{4,3,2,1,0:T(8,128)(2,1)S(1)}, bf16[1,3,3,128,128]{4,3,2,1,0:T(8,128)(2,1)}, u32[]{:S(2)}) copy-start(bf16[1,3,3,128,128]{4,3,2,1,0:T(8,128)(2,1)} %param.7) | copy-start | bytes 884740
  9.5 4.1 %copy-start.2 = (bf16[1,4,128,128]{3,2,1,0:T(8,128)(2,1)S(1)}, bf16[1,4,128,128]{3,2,1,0:T(8,128)(2,1)}, u32[]{:S(2)}) copy-start(bf16[1,4,128,128]{3,2,1,0:T(8,128)(2,1)} %param.5) | copy-start | bytes 393220
  11.2 8.1 %collective-permute-start.2 = (bf16[8,128,128]{2,1,0:T(8,128)(2,1)S(1)}, bf16[8,128,128]{2,1,0:T(8,128)(2,1)S(1)}, u32[]{:S(2)}, u32[]{:S(2)}) collective-permute-start(bf16[8,128,128]{2,1,0:T(8,128)(2,1)S(1)} %get-tuple-element.29.skip_here), channel_id=1, source_target_pairs={{0,16},{1,17},{2,18},{3,19},{4,20},{5,21},{6,22},{7,23},{8,24},{9,... | collective-permute-start | bytes 786440 | tf_op jit(solution)/shard_map/ppermute | solution.py:284
  13.6 4.1 %collective-permute-start.4 = (bf16[2,128,128]{2,1,0:T(8,128)(2,1)S(1)}, bf16[2,128,128]{2,1,0:T(8,128)(2,1)S(1)}, u32[]{:S(2)}, u32[]{:S(2)}) collective-permute-start(bf16[2,128,128]{2,1,0:T(8,128)(2,1)S(1)} %get-tuple-element.50), channel_id=1, source_target_pairs={{0,0},{1,2},{2,1},{3,4},{4,3},{5,6},{6,5},{7,8},{8,7},{9,10},{10,9... | collective-permute-start | bytes 196616 | tf_op jit(solution)/shard_map/ppermute | solution.py:280
  14.3 4.4 %collective-permute-start.3 = (bf16[2,128,128]{2,1,0:T(8,128)(2,1)S(1)}, bf16[2,128,128]{2,1,0:T(8,128)(2,1)S(1)}, u32[]{:S(2)}, u32[]{:S(2)}) collective-permute-start(bf16[2,128,128]{2,1,0:T(8,128)(2,1)S(1)} %get-tuple-element.51), channel_id=1, source_target_pairs={{0,1},{1,0},{2,3},{3,2},{4,5},{5,4},{6,7},{7,6},{8,9},{9,8},{10,11... | collective-permute-start | bytes 196616 | tf_op jit(solution)/shard_map/ppermute | solution.py:280
  20.0 10.3 %collective-permute-start.5 = (bf16[4,128,128]{2,1,0:T(8,128)(2,1)S(1)}, bf16[4,128,128]{2,1,0:T(8,128)(2,1)S(1)}, u32[]{:S(2)}, u32[]{:S(2)}) collective-permute-start(bf16[4,128,128]{2,1,0:T(8,128)(2,1)S(1)} %get-tuple-element.32), channel_id=1, source_target_pairs={{16,0},{17,1},{18,2},{19,3},{20,4},{21,5},{22,6},{23,7},{24,8},{25... | collective-permute-start | bytes 393224 | tf_op jit(solution)/shard_map/ppermute | solution.py:288
  21.2 6.7 %collective-permute-start.6 = (bf16[2,128,128]{2,1,0:T(8,128)(2,1)S(1)}, bf16[2,128,128]{2,1,0:T(8,128)(2,1)S(1)}, u32[]{:S(2)}, u32[]{:S(2)}) collective-permute-start(bf16[2,128,128]{2,1,0:T(8,128)(2,1)S(1)} %get-tuple-element.33), channel_id=1, source_target_pairs={{16,1},{17,0},{18,3},{19,2},{20,5},{21,4},{22,7},{23,6},{24,9},{25... | collective-permute-start | bytes 196616 | tf_op jit(solution)/shard_map/ppermute | solution.py:288
  22.5 7.7 %collective-permute-start.7 = (bf16[2,128,128]{2,1,0:T(8,128)(2,1)S(1)}, bf16[2,128,128]{2,1,0:T(8,128)(2,1)S(1)}, u32[]{:S(2)}, u32[]{:S(2)}) collective-permute-start(bf16[2,128,128]{2,1,0:T(8,128)(2,1)S(1)} %get-tuple-element.34), channel_id=1, source_target_pairs={{16,0},{17,2},{18,1},{19,4},{20,3},{21,6},{22,5},{23,8},{24,7},{25... | collective-permute-start | bytes 196616 | tf_op jit(solution)/shard_map/ppermute | solution.py:288
  30.2 0.9 %copy-start.6 = (bf16[1,4,128,128]{3,2,1,0:T(8,128)(2,1)S(1)}, bf16[1,4,128,128]{3,2,1,0:T(8,128)(2,1)}, u32[]{:S(2)}) copy-start(bf16[1,4,128,128]{3,2,1,0:T(8,128)(2,1)} %param.4) | copy-start | bytes 393220
  32.2 1.8 %collective-permute-start.8 = (bf16[3,3,64,128]{3,2,1,0:T(8,128)(2,1)S(1)}, bf16[3,3,64,128]{3,2,1,0:T(8,128)(2,1)S(1)}, u32[]{:S(2)}, u32[]{:S(2)}) collective-permute-start(bf16[3,3,64,128]{3,2,1,0:T(8,128)(2,1)S(1)} %get-tuple-element.41), channel_id=1, source_target_pairs={{0,1},{1,0},{2,3},{3,2},{4,5},{5,4},{6,7},{7,6},{8,9},{9,8},{10,11... | collective-permute-start | bytes 442376 | tf_op jit(solution)/shard_map/ppermute | solution.py:280
  33.0 1.4 %collective-permute-start.9 = (bf16[3,3,64,128]{3,2,1,0:T(8,128)(2,1)S(1)}, bf16[3,3,64,128]{3,2,1,0:T(8,128)(2,1)S(1)}, u32[]{:S(2)}, u32[]{:S(2)}) collective-permute-start(bf16[3,3,64,128]{3,2,1,0:T(8,128)(2,1)S(1)} %get-tuple-element.43), channel_id=1, source_target_pairs={{0,1},{1,0},{2,3},{3,2},{4,5},{5,4},{6,7},{7,6},{8,9},{9,8},{10,11... | collective-permute-start | bytes 442376 | tf_op jit(solution)/shard_map/ppermute | solution.py:280
  34.5 4.6 %collective-permute-start.10 = (bf16[2,3,3,16,128]{4,3,2,1,0:T(8,128)(2,1)S(1)}, bf16[2,3,3,16,128]{4,3,2,1,0:T(8,128)(2,1)S(1)}, u32[]{:S(2)}, u32[]{:S(2)}) collective-permute-start(bf16[2,3,3,16,128]{4,3,2,1,0:T(8,128)(2,1)S(1)} %get-tuple-element.45), channel_id=1, source_target_pairs={{0,2},{1,3},{2,0},{3,1},{4,6},{5,7},{6,4},{7,5},{8,10},{9,11},{10,... | collective-permute-start | bytes 221192 | tf_op jit(solution)/shard_map/ppermute | solution.py:280
  36.4 4.8 %collective-permute-start.11 = (bf16[2,3,3,16,128]{4,3,2,1,0:T(8,128)(2,1)S(1)}, bf16[2,3,3,16,128]{4,3,2,1,0:T(8,128)(2,1)S(1)}, u32[]{:S(2)}, u32[]{:S(2)}) collective-permute-start(bf16[2,3,3,16,128]{4,3,2,1,0:T(8,128)(2,1)S(1)} %get-tuple-element.46), channel_id=1, source_target_pairs={{0,4},{1,5},{2,6},{3,7},{4,0},{5,1},{6,2},{7,3},{8,12},{9,13},{10,... | collective-permute-start | bytes 221192 | tf_op jit(solution)/shard_map/ppermute | solution.py:280
  38.0 5.3 %collective-permute-start.12 = (bf16[2,3,3,16,128]{4,3,2,1,0:T(8,128)(2,1)S(1)}, bf16[2,3,3,16,128]{4,3,2,1,0:T(8,128)(2,1)S(1)}, u32[]{:S(2)}, u32[]{:S(2)}) collective-permute-start(bf16[2,3,3,16,128]{4,3,2,1,0:T(8,128)(2,1)S(1)} %get-tuple-element.47), channel_id=1, source_target_pairs={{0,6},{1,7},{2,4},{3,5},{4,2},{5,3},{6,0},{7,1},{8,14},{9,15},{10,... | collective-permute-start | bytes 221192 | tf_op jit(solution)/shard_map/ppermute | solution.py:280
  43.3 6.1 %collective-permute-start.13 = (bf16[2,3,3,16,128]{4,3,2,1,0:T(8,128)(2,1)S(1)}, bf16[2,3,3,16,128]{4,3,2,1,0:T(8,128)(2,1)S(1)}, u32[]{:S(2)}, u32[]{:S(2)}) collective-permute-start(bf16[2,3,3,16,128]{4,3,2,1,0:T(8,128)(2,1)S(1)} %add_convert_fusion.1), channel_id=1, source_target_pairs={{0,8},{1,9},{2,10},{3,11},{4,12},{5,13},{6,14},{7,15},{8,0},{9,1},... | collective-permute-start | bytes 221192 | tf_op jit(solution)/shard_map/ppermute | solution.py:280
  49.4 6.8 %copy-start.4 = (bf16[1,3,3,128,128]{4,3,2,1,0:T(8,128)(2,1)S(1)}, bf16[1,3,3,128,128]{4,3,2,1,0:T(8,128)(2,1)}, u32[]{:S(2)}) copy-start(bf16[1,3,3,128,128]{4,3,2,1,0:T(8,128)(2,1)} %param.6) | copy-start | bytes 884740
  49.4 5.3 %collective-permute-start.16 = (bf16[2,3,3,16,128]{4,3,2,1,0:T(8,128)(2,1)S(1)}, bf16[2,3,3,16,128]{4,3,2,1,0:T(8,128)(2,1)S(1)}, u32[]{:S(2)}, u32[]{:S(2)}) collective-permute-start(bf16[2,3,3,16,128]{4,3,2,1,0:T(8,128)(2,1)S(1)} %add_convert_fusion.mine), channel_id=1, source_target_pairs={{0,6},{1,7},{2,4},{3,5},{4,2},{5,3},{6,0},{7,1},{8,14},{9,15},{10,... | collective-permute-start | bytes 221192 | tf_op jit(solution)/shard_map/ppermute | solution.py:280
  50.1 4.7 %collective-permute-start.15 = (bf16[2,3,3,16,128]{4,3,2,1,0:T(8,128)(2,1)S(1)}, bf16[2,3,3,16,128]{4,3,2,1,0:T(8,128)(2,1)S(1)}, u32[]{:S(2)}, u32[]{:S(2)}) collective-permute-start(bf16[2,3,3,16,128]{4,3,2,1,0:T(8,128)(2,1)S(1)} %add_convert_fusion.mine), channel_id=1, source_target_pairs={{0,4},{1,5},{2,6},{3,7},{4,0},{5,1},{6,2},{7,3},{8,12},{9,13},{10,... | collective-permute-start | bytes 221192 | tf_op jit(solution)/shard_map/ppermute | solution.py:280
  51.7 4.4 %collective-permute-start.14 = (bf16[2,3,3,16,128]{4,3,2,1,0:T(8,128)(2,1)S(1)}, bf16[2,3,3,16,128]{4,3,2,1,0:T(8,128)(2,1)S(1)}, u32[]{:S(2)}, u32[]{:S(2)}) collective-permute-start(bf16[2,3,3,16,128]{4,3,2,1,0:T(8,128)(2,1)S(1)} %add_convert_fusion.mine), channel_id=1, source_target_pairs={{0,2},{1,3},{2,0},{3,1},{4,6},{5,7},{6,4},{7,5},{8,10},{9,11},{10,... | collective-permute-start | bytes 221192 | tf_op jit(solution)/shard_map/ppermute | solution.py:280
  56.1 1.6 %collective-permute-start.17 = (bf16[2,3,3,64,128]{4,3,2,1,0:T(8,128)(2,1)S(1)}, bf16[2,3,3,64,128]{4,3,2,1,0:T(8,128)(2,1)S(1)}, u32[]{:S(2)}, u32[]{:S(2)}) collective-permute-start(bf16[2,3,3,64,128]{4,3,2,1,0:T(8,128)(2,1)S(1)} %shard_map.82.mine), channel_id=1, source_target_pairs={{0,1},{1,0},{2,3},{3,2},{4,5},{5,4},{6,7},{7,6},{8,9},{9,8},{10,11... | collective-permute-start | bytes 884744 | tf_op jit(solution)/shard_map/ppermute | solution.py:280

commit v7 on v5

--- a/solution.py
+++ b/solution.py
@@ -11,6 +11,9 @@
 BF16 = jnp.bfloat16
 F32 = jnp.float32
 TAPS = [(ty, tx) for ty in range(3) for tx in range(3)]
+
+
+TURNS = ((1, 2), (2, 1), (3, 3))
 
 
 def silu(values):
@@ -140,7 +143,7 @@
         pre = pre1[...] + conv(yw, 0, own + 4 - 2, second)
         for i in range(own + 2):
             if i == 0:
-                upstream = jnp.where(even, g_other[1].astype(F32), g_core[1].astype(F32))
+                upstream = jnp.where(even, g_other[own - 1].astype(F32), g_core[own - 1].astype(F32))
             elif i == own + 1:
                 upstream = jnp.where(even, g_core[0].astype(F32), g_other[0].astype(F32))
             else:
@@ -172,7 +175,7 @@
     def _():
         for i in range(own + 4):
             if i < 2:
-                upstream = jnp.where(even, g_other[i].astype(F32), g_core[i].astype(F32))
+                upstream = jnp.where(even, g_other[own - 2 + i].astype(F32), g_core[own - 2 + i].astype(F32))
                 returned = jnp.where(even, back_other[i].astype(F32), back_core[i].astype(F32))
             elif i >= own + 2:
                 k = i - own - 2
@@ -208,13 +211,16 @@
     conv_weight(x[...], hw, 0, store(even, kept, sent))
 
 
-def input_kernel(hw, main, input_grad):
+def input_kernel(hw, main, out, input_grad, output):
+    output[...] = out[...]
     input_grad[...] = conv_back(hw, 0, input_grad.shape[0], main).astype(BF16)
 
 
 def quarters(rows):
-    quad = lax.rem(lax.axis_index("rows") // 2, 4)
-    return [pl.ds(pl.multiple_of(jnp.bitwise_xor(quad, k) * rows, rows), rows) for k in range(4)]
+    at = lax.axis_index("rows")
+    quad = lax.rem(at // 2, 4)
+    partners = [jnp.bitwise_xor(quad, jnp.where(lax.rem(at, 2) == 0, *turn)) for turn in TURNS]
+    return [pl.ds(pl.multiple_of(partner * rows, rows), rows) for partner in [quad] + partners]
 
 
 def pack_kernel(kept1, got1, kept2, got2, mine, *sends):
@@ -293,6 +299,8 @@
     work = 2 * columns * 9 * channels * channels
     x_other = swap(x, False, other)
     x_core = swap(x, False, core)
+    g_other = swap(g, False, other)
+    g_core = swap(g, False, core)
     xo, mid = call(
         early_kernel,
         [wide_out(own), like(own - 2, F32)],
@@ -307,10 +315,9 @@
         (xo, mid, x_core, x_other, main, second),
         work * (2 * own + 8),
     )
-    g_core = swap(jnp.where(even, g[own - 2 :], g[:2]), False, core)
-    g_other = swap(jnp.where(even, g[:2], g[own - 2 :]), False, other)
+    skip_here, g_core, g_other = lax.optimization_barrier((skip_here, g_core, g_other))
     skip_there = swap(skip_here, True, same)
-    output, gw, back, edge_core, edge_other = call(
+    out, gw, back, edge_core, edge_other = call(
         functools.partial(middle_kernel, segments, strips),
         [like(own, BF16), wide_out(own + 2), like(own, BF16), like(2, BF16), like(2, BF16)],
         [wide(own + 4)],
@@ -337,11 +344,14 @@
         (x, pre1, ew, gw, second),
         work * (2 * own + 2),
     )
-    (input_grad,) = call(input_kernel, [like(own, BF16)], [], (hw, main), work * own)
+    input_grad, output = call(input_kernel, [like(own, BF16)] * 2, [], (hw, main, out), work * own)
     factor = 1.0 / math.sqrt(own * strips * columns)
 
-    def jump(array, bit, times=1):
-        return swap(array, False, lambda r: r ^ (times << bit))
+    def jump(array, bit):
+        return swap(array, False, lambda r: r ^ (1 << bit))
+
+    def meet(array, turn):
+        return swap(array, False, lambda r: r ^ (turn[r % 2] << 1))
 
     bits = strips.bit_length() - 1
     quarter = (2, 3, 3, channels // 8, channels)
@@ -353,13 +363,13 @@
         (kept1, got1, kept2, got2),
         kept1.size,
     )
-    for k, send in enumerate(sends):
-        mine = mine + jump(send, 1, k + 1).astype(F32)
+    for turn, send in zip(TURNS, sends):
+        mine = mine + meet(send, turn).astype(F32)
     for bit in range(3, bits):
         rounded = lax.optimization_barrier(mine.astype(BF16))
         mine = rounded.astype(F32) + jump(rounded, bit).astype(F32)
     mine = lax.optimization_barrier(mine.astype(BF16))
-    gots = [jump(mine, 1, k) for k in range(1, 4)]
+    gots = [meet(mine, turn) for turn in TURNS]
     (mine,) = call(
         unpack_kernel,
         [jax.ShapeDtypeStruct((2,) + halves, BF16)],

time: 56.5 us -> 58.9 us (1.042)
  waiting for transfers between devices: 22.2 us -> 26.3 us
  starting transfers between devices: 22.7 us -> 21.5 us
  Pallas kernels: 6.84 us -> 6.19 us
    ppermute x18, waiting for transfers between devices: 22.2 us -> 26.3 us  [swap(): return lax.ppermute(array, ('segment', 'rows'), pairs)]
    ppermute x18, starting transfers between devices: 22.7 us -> 21.5 us  [swap(): return lax.ppermute(array, ('segment', 'rows'), pairs)]
    pallas_call x9, Pallas kernels: 6.84 us -> 6.19 us  [call(): pl.pallas_call(kernel, out_shape=outs, in_specs=[pl.BlockSpec(memory_spac...]
  transfers between devices with their start and end apart: 18 -> 18, of which waited for: 14 -> 13; matrix products, arithmetic and copies ran while one was open for 0% -> 0% of each run, Pallas kernels for 3% -> 5%
where the time goes in v7:
time: 58.9 us; the launch traced here: 58.6 us
  waiting for transfers between devices  26.3 us (45%)
  starting transfers between devices  21.5 us (37%)
  Pallas kernels  6.19 us (11%)
  local copies, waits for them, and re-layouts  3.67 us (6%)
  between operations  0.77 us (1%)
    ppermute x18, waiting for transfers between devices, swap(): return lax.ppermute(array, ('segment', 'rows'), pairs)  26.3 us
    ppermute x18, starting transfers between devices, swap(): return lax.ppermute(array, ('segment', 'rows'), pairs)  21.5 us
    pallas_call x9, Pallas kernels, call(): pl.pallas_call(kernel, out_shape=outs, in_specs=[pl.BlockSpec(memory_spac...  6.19 us
    unnamed x14, local copies, waits for them, and re-layouts  3.67 us
  transfers between devices with their start and end apart: 18, of which 13 were waited for; matrix products, arithmetic and copies ran while one was open for 0% of the time, Pallas kernels for 5%

profile of v7, /device:TPU:0, one launch (start us, length us, event | category | flops | bytes accessed | tf_op | source)
XLA Modules:
  0.0 58.6 jit_solution(4617074764737180948)
XLA Ops:
  0.6 1.6 %collective-permute-start.1 = (bf16[4,128,128]{2,1,0:T(8,128)(2,1)}, bf16[4,128,128]{2,1,0:T(8,128)(2,1)S(1)}, u32[]{:S(2)}, u32[]{:S(2)}) collective-permute-start(bf16[4,128,128]{2,1,0:T(8,128)(2,1)} %bitcast.19), channel_id=1, source_target_pairs={{0,0},{1,2},{2,1},{3,4},{4,3},{5,6},{6,5},{7,8},{8,7},{9,10},{10,9... | collective-permute-start | bytes 393224 | tf_op jit(solution)/shard_map/ppermute | solution.py:288
  2.2 3.5 %collective-permute-start = (bf16[4,128,128]{2,1,0:T(8,128)(2,1)}, bf16[4,128,128]{2,1,0:T(8,128)(2,1)S(1)}, u32[]{:S(2)}, u32[]{:S(2)}) collective-permute-start(bf16[4,128,128]{2,1,0:T(8,128)(2,1)} %bitcast.20), channel_id=1, source_target_pairs={{0,1},{1,0},{2,3},{3,2},{4,5},{5,4},{6,7},{7,6},{8,9},{9,8},{10,11... | collective-permute-start | bytes 393224 | tf_op jit(solution)/shard_map/ppermute | solution.py:288
  5.7 1.6 %collective-permute-start.3 = (bf16[4,128,128]{2,1,0:T(8,128)(2,1)}, bf16[4,128,128]{2,1,0:T(8,128)(2,1)S(1)}, u32[]{:S(2)}, u32[]{:S(2)}) collective-permute-start(bf16[4,128,128]{2,1,0:T(8,128)(2,1)} %bitcast.15), channel_id=1, source_target_pairs={{0,0},{1,2},{2,1},{3,4},{4,3},{5,6},{6,5},{7,8},{8,7},{9,10},{10,9... | collective-permute-start | bytes 393224 | tf_op jit(solution)/shard_map/ppermute | solution.py:288
  7.2 2.1 %collective-permute-start.2 = (bf16[4,128,128]{2,1,0:T(8,128)(2,1)}, bf16[4,128,128]{2,1,0:T(8,128)(2,1)S(1)}, u32[]{:S(2)}, u32[]{:S(2)}) collective-permute-start(bf16[4,128,128]{2,1,0:T(8,128)(2,1)} %bitcast.16), channel_id=1, source_target_pairs={{0,1},{1,0},{2,3},{3,2},{4,5},{5,4},{6,7},{7,6},{8,9},{9,8},{10,11... | collective-permute-start | bytes 393224 | tf_op jit(solution)/shard_map/ppermute | solution.py:288
  9.3 1.0 %copy-done = bf16[1,3,3,128,128]{4,3,2,1,0:T(8,128)(2,1)S(1)} copy-done((bf16[1,3,3,128,128]{4,3,2,1,0:T(8,128)(2,1)S(1)}, bf16[1,3,3,128,128]{4,3,2,1,0:T(8,128)(2,1)}, u32[]{:S(2)}) %copy-start) | copy-done | bytes 294936
  10.3 1.0 %copy-done.2 = bf16[1,3,3,128,128]{4,3,2,1,0:T(8,128)(2,1)S(1)} copy-done((bf16[1,3,3,128,128]{4,3,2,1,0:T(8,128)(2,1)S(1)}, bf16[1,3,3,128,128]{4,3,2,1,0:T(8,128)(2,1)}, u32[]{:S(2)}) %copy-start.2) | copy-done | bytes 294936
  11.2 0.9 %copy-done.5 = bf16[1,4,128,128]{3,2,1,0:T(8,128)(2,1)S(1)} copy-done((bf16[1,4,128,128]{3,2,1,0:T(8,128)(2,1)S(1)}, bf16[1,4,128,128]{3,2,1,0:T(8,128)(2,1)}, u32[]{:S(2)}) %copy-start.5) | copy-done | bytes 131096
  12.5 0.6 %copy-done.1 = bf16[1,3,3,128,128]{4,3,2,1,0:T(8,128)(2,1)S(1)} copy-done((bf16[1,3,3,128,128]{4,3,2,1,0:T(8,128)(2,1)S(1)}, bf16[1,3,3,128,128]{4,3,2,1,0:T(8,128)(2,1)}, u32[]{:S(2)}) %copy-start.1) | copy-done | bytes 294936
  13.1 1.7 %shard_map.76 = (f32[6,128,128]{2,1,0:T(8,128)S(1)}, f32[8,128,128]{2,1,0:T(8,128)S(1)}, bf16[4,128,128]{2,1,0:T(8,128)(2,1)S(1)}, bf16[8,128,128]{2,1,0:T(8,128)(2,1)S(1)}) custom-call(bf16[4,128,384]{2,1,0:T(8,128)(2,1)S(1)} %get-tuple-element.32.xo, f32[2,128,128]{2,1,0:T(8,128)S(1)} %get-tuple-element.33.mid, ...), custom_call_target="tpu_custom_call" | custom-call | flops 603979776 | bytes 2686976 | tf_op jit(solution)/shard_map/pallas_call | solution.py:254
  14.9 0.5 collective-permute-start.4
  15.4 7.8 %collective-permute-done.4.skip_there = bf16[8,128,128]{2,1,0:T(8,128)(2,1)S(1)} collective-permute-done((bf16[8,128,128]{2,1,0:T(8,128)(2,1)S(1)}, bf16[8,128,128]{2,1,0:T(8,128)(2,1)S(1)}, u32[]{:S(2)}, u32[]{:S(2)}) %collective-permute-start.4) | collective-permute-done | bytes 262176 | tf_op jit(solution)/shard_map/ppermute | solution.py:288
  23.2 2.1 %collective-permute-start.5 = (bf16[4,128,128]{2,1,0:T(8,128)(2,1)S(1)}, bf16[4,128,128]{2,1,0:T(8,128)(2,1)S(1)}, u32[]{:S(2)}, u32[]{:S(2)}) collective-permute-start(bf16[4,128,128]{2,1,0:T(8,128)(2,1)S(1)} %get-tuple-element.39), channel_id=1, source_target_pairs={{0,16},{1,17},{2,18},{3,19},{4,20},{5,21},{6,22},{7,23},{8,24},{9,... | collective-permute-start | bytes 393224 | tf_op jit(solution)/shard_map/ppermute | solution.py:288
  25.2 0.5 collective-permute-start.7
  25.8 4.6 %collective-permute-done.6.back_core = bf16[2,128,128]{2,1,0:T(8,128)(2,1)S(1)} collective-permute-done((bf16[2,128,128]{2,1,0:T(8,128)(2,1)S(1)}, bf16[2,128,128]{2,1,0:T(8,128)(2,1)S(1)}, u32[]{:S(2)}, u32[]{:S(2)}) %collective-permute-start.6) | collective-permute-done | bytes 65568 | tf_op jit(solution)/shard_map/ppermute | solution.py:288
  30.4 0.6 %collective-permute-done.7.back_other = bf16[2,128,128]{2,1,0:T(8,128)(2,1)S(1)} collective-permute-done((bf16[2,128,128]{2,1,0:T(8,128)(2,1)S(1)}, bf16[2,128,128]{2,1,0:T(8,128)(2,1)S(1)}, u32[]{:S(2)}, u32[]{:S(2)}) %collective-permute-start.7) | collective-permute-done | bytes 65568 | tf_op jit(solution)/shard_map/ppermute | solution.py:288
  31.0 0.7 %shard_map.78 = (f32[3,3,64,128]{3,2,1,0:T(8,128)S(1)}, bf16[3,3,64,128]{3,2,1,0:T(8,128)(2,1)S(1)}, bf16[8,128,384]{2,1,0:T(8,128)(2,1)S(1)}) custom-call(bf16[4,128,128]{2,1,0:T(8,128)(2,1)S(1)} %bitcast.18, bf16[4,128,128]{2,1,0:T(8,128)(2,1)S(1)} %collective-permute-done.2.g_core, bf16[4,128,128]{2,1,0:T(8,128)(2,1)S(1)} %collective-permute-done.3.g_other, ...), custom_call_target="tpu_custom_call" | custom-call | flops 150994944 | bytes 3391488 | tf_op jit(solution)/shard_map/pallas_call | solution.py:254
  31.9 1.1 %shard_map.79 = (f32[3,3,64,128]{3,2,1,0:T(8,128)S(1)}, bf16[3,3,64,128]{3,2,1,0:T(8,128)(2,1)S(1)}, bf16[6,128,384]{2,1,0:T(8,128)(2,1)S(1)}) custom-call(bf16[4,128,128]{2,1,0:T(8,128)(2,1)S(1)} %bitcast.22, f32[6,128,128]{2,1,0:T(8,128)S(1)} %get-tuple-element.34.pre1, bf16[8,128,384]{2,1,0:T(8,128)(2,1)S(1)} %get-tuple-element.45.ew, ...), custom_call_target="tpu_custom_call" | custom-call | flops 377487360 | bytes 3227648 | tf_op jit(solution)/shard_map/pallas_call | solution.py:254
  33.6 0.9 %collective-permute-done.8.got1 = bf16[3,3,64,128]{3,2,1,0:T(8,128)(2,1)S(1)} collective-permute-done((bf16[3,3,64,128]{3,2,1,0:T(8,128)(2,1)S(1)}, bf16[3,3,64,128]{3,2,1,0:T(8,128)(2,1)S(1)}, u32[]{:S(2)}, u32[]{:S(2)}) %collective-permute-start.8) | collective-permute-done | bytes 147488 | tf_op jit(solution)/shard_map/ppermute | solution.py:288
  34.8 1.3 %collective-permute-start.10 = (bf16[2,3,3,16,128]{4,3,2,1,0:T(8,128)(2,1)S(1)}, bf16[2,3,3,16,128]{4,3,2,1,0:T(8,128)(2,1)S(1)}, u32[]{:S(2)}, u32[]{:S(2)}) collective-permute-start(bf16[2,3,3,16,128]{4,3,2,1,0:T(8,128)(2,1)S(1)} %get-tuple-element.55), channel_id=1, source_target_pairs={{0,2},{1,5},{2,0},{3,7},{4,6},{5,1},{6,4},{7,3},{8,10},{9,13},{10,... | collective-permute-start | bytes 221192 | tf_op jit(solution)/shard_map/ppermute | solution.py:288
  36.0 1.6 %collective-permute-start.11 = (bf16[2,3,3,16,128]{4,3,2,1,0:T(8,128)(2,1)S(1)}, bf16[2,3,3,16,128]{4,3,2,1,0:T(8,128)(2,1)S(1)}, u32[]{:S(2)}, u32[]{:S(2)}) collective-permute-start(bf16[2,3,3,16,128]{4,3,2,1,0:T(8,128)(2,1)S(1)} %get-tuple-element.56), channel_id=1, source_target_pairs={{0,4},{1,3},{2,6},{3,1},{4,0},{5,7},{6,2},{7,5},{8,12},{9,11},{10,... | collective-permute-start | bytes 221192 | tf_op jit(solution)/shard_map/ppermute | solution.py:288
  37.6 0.7 %collective-permute-start.12 = (bf16[2,3,3,16,128]{4,3,2,1,0:T(8,128)(2,1)S(1)}, bf16[2,3,3,16,128]{4,3,2,1,0:T(8,128)(2,1)S(1)}, u32[]{:S(2)}, u32[]{:S(2)}) collective-permute-start(bf16[2,3,3,16,128]{4,3,2,1,0:T(8,128)(2,1)S(1)} %get-tuple-element.57), channel_id=1, source_target_pairs={{0,6},{1,7},{2,4},{3,5},{4,2},{5,3},{6,0},{7,1},{8,14},{9,15},{10,... | collective-permute-start | bytes 221192 | tf_op jit(solution)/shard_map/ppermute | solution.py:288
  38.3 1.1 %collective-permute-done.10 = bf16[2,3,3,16,128]{4,3,2,1,0:T(8,128)(2,1)S(1)} collective-permute-done((bf16[2,3,3,16,128]{4,3,2,1,0:T(8,128)(2,1)S(1)}, bf16[2,3,3,16,128]{4,3,2,1,0:T(8,128)(2,1)S(1)}, u32[]{:S(2)}, u32[]{:S(2)}) %collective-permute-start.10) | collective-permute-done | bytes 73760 | tf_op jit(solution)/shard_map/ppermute | solution.py:288
  39.4 1.2 %collective-permute-done.11 = bf16[2,3,3,16,128]{4,3,2,1,0:T(8,128)(2,1)S(1)} collective-permute-done((bf16[2,3,3,16,128]{4,3,2,1,0:T(8,128)(2,1)S(1)}, bf16[2,3,3,16,128]{4,3,2,1,0:T(8,128)(2,1)S(1)}, u32[]{:S(2)}, u32[]{:S(2)}) %collective-permute-start.11) | collective-permute-done | bytes 73760 | tf_op jit(solution)/shard_map/ppermute | solution.py:288
  40.6 2.3 %collective-permute-done.12 = bf16[2,3,3,16,128]{4,3,2,1,0:T(8,128)(2,1)S(1)} collective-permute-done((bf16[2,3,3,16,128]{4,3,2,1,0:T(8,128)(2,1)S(1)}, bf16[2,3,3,16,128]{4,3,2,1,0:T(8,128)(2,1)S(1)}, u32[]{:S(2)}, u32[]{:S(2)}) %collective-permute-start.12) | collective-permute-done | bytes 73760 | tf_op jit(solution)/shard_map/ppermute | solution.py:288
  42.9 2.0 %collective-permute-start.13 = (bf16[2,3,3,16,128]{4,3,2,1,0:T(8,128)(2,1)S(1)}, bf16[2,3,3,16,128]{4,3,2,1,0:T(8,128)(2,1)S(1)}, u32[]{:S(2)}, u32[]{:S(2)}) collective-permute-start(bf16[2,3,3,16,128]{4,3,2,1,0:T(8,128)(2,1)S(1)} %add_convert_fusion.1), channel_id=1, source_target_pairs={{0,8},{1,9},{2,10},{3,11},{4,12},{5,13},{6,14},{7,15},{8,0},{9,1},... | collective-permute-start | bytes 221192 | tf_op jit(solution)/shard_map/ppermute | solution.py:288
  45.0 4.1 %collective-permute-done.13 = bf16[2,3,3,16,128]{4,3,2,1,0:T(8,128)(2,1)S(1)} collective-permute-done((bf16[2,3,3,16,128]{4,3,2,1,0:T(8,128)(2,1)S(1)}, bf16[2,3,3,16,128]{4,3,2,1,0:T(8,128)(2,1)S(1)}, u32[]{:S(2)}, u32[]{:S(2)}) %collective-permute-start.13) | collective-permute-done | bytes 73760 | tf_op jit(solution)/shard_map/ppermute | solution.py:288
  49.5 1.9 %collective-permute-start.15 = (bf16[2,3,3,16,128]{4,3,2,1,0:T(8,128)(2,1)S(1)}, bf16[2,3,3,16,128]{4,3,2,1,0:T(8,128)(2,1)S(1)}, u32[]{:S(2)}, u32[]{:S(2)}) collective-permute-start(bf16[2,3,3,16,128]{4,3,2,1,0:T(8,128)(2,1)S(1)} %add_convert_fusion.mine), channel_id=1, source_target_pairs={{0,4},{1,3},{2,6},{3,1},{4,0},{5,7},{6,2},{7,5},{8,12},{9,11},{10,... | collective-permute-start | bytes 221192 | tf_op jit(solution)/shard_map/ppermute | solution.py:288
  51.4 1.2 %collective-permute-start.14 = (bf16[2,3,3,16,128]{4,3,2,1,0:T(8,128)(2,1)S(1)}, bf16[2,3,3,16,128]{4,3,2,1,0:T(8,128)(2,1)S(1)}, u32[]{:S(2)}, u32[]{:S(2)}) collective-permute-start(bf16[2,3,3,16,128]{4,3,2,1,0:T(8,128)(2,1)S(1)} %add_convert_fusion.mine), channel_id=1, source_target_pairs={{0,2},{1,5},{2,0},{3,7},{4,6},{5,1},{6,4},{7,3},{8,10},{9,13},{10,... | collective-permute-start | bytes 221192 | tf_op jit(solution)/shard_map/ppermute | solution.py:288
  52.7 1.8 %collective-permute-done.16.rest_2_ = bf16[2,3,3,16,128]{4,3,2,1,0:T(8,128)(2,1)S(1)} collective-permute-done((bf16[2,3,3,16,128]{4,3,2,1,0:T(8,128)(2,1)S(1)}, bf16[2,3,3,16,128]{4,3,2,1,0:T(8,128)(2,1)S(1)}, u32[]{:S(2)}, u32[]{:S(2)}) %collective-permute-start.16) | collective-permute-done | bytes 73760 | tf_op jit(solution)/shard_map/ppermute | solution.py:288
  54.5 1.2 %collective-permute-done.14.rest_0_ = bf16[2,3,3,16,128]{4,3,2,1,0:T(8,128)(2,1)S(1)} collective-permute-done((bf16[2,3,3,16,128]{4,3,2,1,0:T(8,128)(2,1)S(1)}, bf16[2,3,3,16,128]{4,3,2,1,0:T(8,128)(2,1)S(1)}, u32[]{:S(2)}, u32[]{:S(2)}) %collective-permute-start.14) | collective-permute-done | bytes 73760 | tf_op jit(solution)/shard_map/ppermute | solution.py:288
  55.9 1.1 %shard_map.80 = (bf16[4,128,128]{2,1,0:T(8,128)(2,1)}, bf16[4,128,128]{2,1,0:T(8,128)(2,1)}) custom-call(bf16[6,128,384]{2,1,0:T(8,128)(2,1)S(1)} %get-tuple-element.46.hw, bf16[3,3,128,128]{3,2,1,0:T(8,128)(2,1)S(1)} %bitcast.14, bf16[4,128,128]{2,1,0:T(8,128)(2,1)S(1)} %get-tuple-element.47.out), custom_call_target="tpu_custom_call" | custom-call | flops 150994944 | bytes 1277952 | tf_op jit(solution)/shard_map/pallas_call | solution.py:254
  57.5 1.1 %shard_map.83 = (f32[3,3,128,128]{3,2,1,0:T(8,128)}, f32[3,3,128,128]{3,2,1,0:T(8,128)}) custom-call(bf16[2,3,3,64,128]{4,3,2,1,0:T(8,128)(2,1)S(1)} %shard_map.82.mine, bf16[2,3,3,64,128]{4,3,2,1,0:T(8,128)(2,1)S(1)} %collective-permute-done.17.theirs), custom_call_target="tpu_custom_call" | custom-call | flops 73728 | bytes 1769472 | tf_op jit(solution)/shard_map/pallas_call | solution.py:254
  (29 shorter events, 2.6 us)
Async XLA Ops:
  0.6 11.8 %collective-permute-start.1 = (bf16[4,128,128]{2,1,0:T(8,128)(2,1)}, bf16[4,128,128]{2,1,0:T(8,128)(2,1)S(1)}, u32[]{:S(2)}, u32[]{:S(2)}) collective-permute-start(bf16[4,128,128]{2,1,0:T(8,128)(2,1)} %bitcast.19), channel_id=1, source_target_pairs={{0,0},{1,2},{2,1},{3,4},{4,3},{5,6},{6,5},{7,8},{8,7},{9,10},{10,9... | collective-permute-start | bytes 393224 | tf_op jit(solution)/shard_map/ppermute | solution.py:288
  2.2 10.3 %collective-permute-start = (bf16[4,128,128]{2,1,0:T(8,128)(2,1)}, bf16[4,128,128]{2,1,0:T(8,128)(2,1)S(1)}, u32[]{:S(2)}, u32[]{:S(2)}) collective-permute-start(bf16[4,128,128]{2,1,0:T(8,128)(2,1)} %bitcast.20), channel_id=1, source_target_pairs={{0,1},{1,0},{2,3},{3,2},{4,5},{5,4},{6,7},{7,6},{8,9},{9,8},{10,11... | collective-permute-start | bytes 393224 | tf_op jit(solution)/shard_map/ppermute | solution.py:288
  5.7 9.2 %collective-permute-start.3 = (bf16[4,128,128]{2,1,0:T(8,128)(2,1)}, bf16[4,128,128]{2,1,0:T(8,128)(2,1)S(1)}, u32[]{:S(2)}, u32[]{:S(2)}) collective-permute-start(bf16[4,128,128]{2,1,0:T(8,128)(2,1)} %bitcast.15), channel_id=1, source_target_pairs={{0,0},{1,2},{2,1},{3,4},{4,3},{5,6},{6,5},{7,8},{8,7},{9,10},{10,9... | collective-permute-start | bytes 393224 | tf_op jit(solution)/shard_map/ppermute | solution.py:288
  7.2 7.6 %collective-permute-start.2 = (bf16[4,128,128]{2,1,0:T(8,128)(2,1)}, bf16[4,128,128]{2,1,0:T(8,128)(2,1)S(1)}, u32[]{:S(2)}, u32[]{:S(2)}) collective-permute-start(bf16[4,128,128]{2,1,0:T(8,128)(2,1)} %bitcast.16), channel_id=1, source_target_pairs={{0,1},{1,0},{2,3},{3,2},{4,5},{5,4},{6,7},{7,6},{8,9},{9,8},{10,11... | collective-permute-start | bytes 393224 | tf_op jit(solution)/shard_map/ppermute | solution.py:288
  9.3 1.0 %copy-start = (bf16[1,3,3,128,128]{4,3,2,1,0:T(8,128)(2,1)S(1)}, bf16[1,3,3,128,128]{4,3,2,1,0:T(8,128)(2,1)}, u32[]{:S(2)}) copy-start(bf16[1,3,3,128,128]{4,3,2,1,0:T(8,128)(2,1)} %param.7) | copy-start | bytes 884740
  10.3 1.0 %copy-start.2 = (bf16[1,3,3,128,128]{4,3,2,1,0:T(8,128)(2,1)S(1)}, bf16[1,3,3,128,128]{4,3,2,1,0:T(8,128)(2,1)}, u32[]{:S(2)}) copy-start(bf16[1,3,3,128,128]{4,3,2,1,0:T(8,128)(2,1)} %param.6) | copy-start | bytes 884740
  11.2 0.9 %copy-start.5 = (bf16[1,4,128,128]{3,2,1,0:T(8,128)(2,1)S(1)}, bf16[1,4,128,128]{3,2,1,0:T(8,128)(2,1)}, u32[]{:S(2)}) copy-start(bf16[1,4,128,128]{3,2,1,0:T(8,128)(2,1)} %param.4) | copy-start | bytes 393220
  12.1 1.0 %copy-start.1 = (bf16[1,3,3,128,128]{4,3,2,1,0:T(8,128)(2,1)S(1)}, bf16[1,3,3,128,128]{4,3,2,1,0:T(8,128)(2,1)}, u32[]{:S(2)}) copy-start(bf16[1,3,3,128,128]{4,3,2,1,0:T(8,128)(2,1)} %param.7) | copy-start | bytes 884740
  13.1 10.1 %copy-start.4 = (bf16[1,4,128,128]{3,2,1,0:T(8,128)(2,1)S(1)}, bf16[1,4,128,128]{3,2,1,0:T(8,128)(2,1)}, u32[]{:S(2)}) copy-start(bf16[1,4,128,128]{3,2,1,0:T(8,128)(2,1)} %param.5) | copy-start | bytes 393220
  14.9 8.3 %collective-permute-start.4 = (bf16[8,128,128]{2,1,0:T(8,128)(2,1)S(1)}, bf16[8,128,128]{2,1,0:T(8,128)(2,1)S(1)}, u32[]{:S(2)}, u32[]{:S(2)}) collective-permute-start(bf16[8,128,128]{2,1,0:T(8,128)(2,1)S(1)} %get-tuple-element.38.skip_here), channel_id=1, source_target_pairs={{0,16},{1,17},{2,18},{3,19},{4,20},{5,21},{6,22},{7,23},{8,24},{9,... | collective-permute-start | bytes 786440 | tf_op jit(solution)/shard_map/ppermute | solution.py:288
  23.2 7.8 %collective-permute-start.5 = (bf16[4,128,128]{2,1,0:T(8,128)(2,1)S(1)}, bf16[4,128,128]{2,1,0:T(8,128)(2,1)S(1)}, u32[]{:S(2)}, u32[]{:S(2)}) collective-permute-start(bf16[4,128,128]{2,1,0:T(8,128)(2,1)S(1)} %get-tuple-element.39), channel_id=1, source_target_pairs={{0,16},{1,17},{2,18},{3,19},{4,20},{5,21},{6,22},{7,23},{8,24},{9,... | collective-permute-start | bytes 393224 | tf_op jit(solution)/shard_map/ppermute | solution.py:288
  25.2 5.1 %collective-permute-start.6 = (bf16[2,128,128]{2,1,0:T(8,128)(2,1)S(1)}, bf16[2,128,128]{2,1,0:T(8,128)(2,1)S(1)}, u32[]{:S(2)}, u32[]{:S(2)}) collective-permute-start(bf16[2,128,128]{2,1,0:T(8,128)(2,1)S(1)} %get-tuple-element.40), channel_id=1, source_target_pairs={{0,17},{1,16},{2,19},{3,18},{4,21},{5,20},{6,23},{7,22},{8,25},{9,... | collective-permute-start | bytes 196616 | tf_op jit(solution)/shard_map/ppermute | solution.py:288
  25.2 5.8 %collective-permute-start.7 = (bf16[2,128,128]{2,1,0:T(8,128)(2,1)S(1)}, bf16[2,128,128]{2,1,0:T(8,128)(2,1)S(1)}, u32[]{:S(2)}, u32[]{:S(2)}) collective-permute-start(bf16[2,128,128]{2,1,0:T(8,128)(2,1)S(1)} %get-tuple-element.41), channel_id=1, source_target_pairs={{0,16},{1,18},{2,17},{3,20},{4,19},{5,22},{6,21},{7,24},{8,23},{9,... | collective-permute-start | bytes 196616 | tf_op jit(solution)/shard_map/ppermute | solution.py:288
  31.0 0.9 %copy-start.6 = (bf16[1,4,128,128]{3,2,1,0:T(8,128)(2,1)S(1)}, bf16[1,4,128,128]{3,2,1,0:T(8,128)(2,1)}, u32[]{:S(2)}) copy-start(bf16[1,4,128,128]{3,2,1,0:T(8,128)(2,1)} %param.4) | copy-start | bytes 393220
  33.1 1.4 %collective-permute-start.8 = (bf16[3,3,64,128]{3,2,1,0:T(8,128)(2,1)S(1)}, bf16[3,3,64,128]{3,2,1,0:T(8,128)(2,1)S(1)}, u32[]{:S(2)}, u32[]{:S(2)}) collective-permute-start(bf16[3,3,64,128]{3,2,1,0:T(8,128)(2,1)S(1)} %get-tuple-element.51), channel_id=1, source_target_pairs={{0,1},{1,0},{2,3},{3,2},{4,5},{5,4},{6,7},{7,6},{8,9},{9,8},{10,11... | collective-permute-start | bytes 442376 | tf_op jit(solution)/shard_map/ppermute | solution.py:288
  33.1 1.6 %collective-permute-start.9 = (bf16[3,3,64,128]{3,2,1,0:T(8,128)(2,1)S(1)}, bf16[3,3,64,128]{3,2,1,0:T(8,128)(2,1)S(1)}, u32[]{:S(2)}, u32[]{:S(2)}) collective-permute-start(bf16[3,3,64,128]{3,2,1,0:T(8,128)(2,1)S(1)} %get-tuple-element.53), channel_id=1, source_target_pairs={{0,1},{1,0},{2,3},{3,2},{4,5},{5,4},{6,7},{7,6},{8,9},{9,8},{10,11... | collective-permute-start | bytes 442376 | tf_op jit(solution)/shard_map/ppermute | solution.py:288
  34.8 4.6 %collective-permute-start.10 = (bf16[2,3,3,16,128]{4,3,2,1,0:T(8,128)(2,1)S(1)}, bf16[2,3,3,16,128]{4,3,2,1,0:T(8,128)(2,1)S(1)}, u32[]{:S(2)}, u32[]{:S(2)}) collective-permute-start(bf16[2,3,3,16,128]{4,3,2,1,0:T(8,128)(2,1)S(1)} %get-tuple-element.55), channel_id=1, source_target_pairs={{0,2},{1,5},{2,0},{3,7},{4,6},{5,1},{6,4},{7,3},{8,10},{9,13},{10,... | collective-permute-start | bytes 221192 | tf_op jit(solution)/shard_map/ppermute | solution.py:288
  36.0 4.6 %collective-permute-start.11 = (bf16[2,3,3,16,128]{4,3,2,1,0:T(8,128)(2,1)S(1)}, bf16[2,3,3,16,128]{4,3,2,1,0:T(8,128)(2,1)S(1)}, u32[]{:S(2)}, u32[]{:S(2)}) collective-permute-start(bf16[2,3,3,16,128]{4,3,2,1,0:T(8,128)(2,1)S(1)} %get-tuple-element.56), channel_id=1, source_target_pairs={{0,4},{1,3},{2,6},{3,1},{4,0},{5,7},{6,2},{7,5},{8,12},{9,11},{10,... | collective-permute-start | bytes 221192 | tf_op jit(solution)/shard_map/ppermute | solution.py:288
  37.6 5.3 %collective-permute-start.12 = (bf16[2,3,3,16,128]{4,3,2,1,0:T(8,128)(2,1)S(1)}, bf16[2,3,3,16,128]{4,3,2,1,0:T(8,128)(2,1)S(1)}, u32[]{:S(2)}, u32[]{:S(2)}) collective-permute-start(bf16[2,3,3,16,128]{4,3,2,1,0:T(8,128)(2,1)S(1)} %get-tuple-element.57), channel_id=1, source_target_pairs={{0,6},{1,7},{2,4},{3,5},{4,2},{5,3},{6,0},{7,1},{8,14},{9,15},{10,... | collective-permute-start | bytes 221192 | tf_op jit(solution)/shard_map/ppermute | solution.py:288
  42.9 6.1 %collective-permute-start.13 = (bf16[2,3,3,16,128]{4,3,2,1,0:T(8,128)(2,1)S(1)}, bf16[2,3,3,16,128]{4,3,2,1,0:T(8,128)(2,1)S(1)}, u32[]{:S(2)}, u32[]{:S(2)}) collective-permute-start(bf16[2,3,3,16,128]{4,3,2,1,0:T(8,128)(2,1)S(1)} %add_convert_fusion.1), channel_id=1, source_target_pairs={{0,8},{1,9},{2,10},{3,11},{4,12},{5,13},{6,14},{7,15},{8,0},{9,1},... | collective-permute-start | bytes 221192 | tf_op jit(solution)/shard_map/ppermute | solution.py:288
  49.1 6.8 %copy-start.3 = (bf16[1,3,3,128,128]{4,3,2,1,0:T(8,128)(2,1)S(1)}, bf16[1,3,3,128,128]{4,3,2,1,0:T(8,128)(2,1)}, u32[]{:S(2)}) copy-start(bf16[1,3,3,128,128]{4,3,2,1,0:T(8,128)(2,1)} %param.6) | copy-start | bytes 884740
  49.1 5.3 %collective-permute-start.16 = (bf16[2,3,3,16,128]{4,3,2,1,0:T(8,128)(2,1)S(1)}, bf16[2,3,3,16,128]{4,3,2,1,0:T(8,128)(2,1)S(1)}, u32[]{:S(2)}, u32[]{:S(2)}) collective-permute-start(bf16[2,3,3,16,128]{4,3,2,1,0:T(8,128)(2,1)S(1)} %add_convert_fusion.mine), channel_id=1, source_target_pairs={{0,6},{1,7},{2,4},{3,5},{4,2},{5,3},{6,0},{7,1},{8,14},{9,15},{10,... | collective-permute-start | bytes 221192 | tf_op jit(solution)/shard_map/ppermute | solution.py:288
  49.5 5.0 %collective-permute-start.15 = (bf16[2,3,3,16,128]{4,3,2,1,0:T(8,128)(2,1)S(1)}, bf16[2,3,3,16,128]{4,3,2,1,0:T(8,128)(2,1)S(1)}, u32[]{:S(2)}, u32[]{:S(2)}) collective-permute-start(bf16[2,3,3,16,128]{4,3,2,1,0:T(8,128)(2,1)S(1)} %add_convert_fusion.mine), channel_id=1, source_target_pairs={{0,4},{1,3},{2,6},{3,1},{4,0},{5,7},{6,2},{7,5},{8,12},{9,11},{10,... | collective-permute-start | bytes 221192 | tf_op jit(solution)/shard_map/ppermute | solution.py:288
  51.4 4.4 %collective-permute-start.14 = (bf16[2,3,3,16,128]{4,3,2,1,0:T(8,128)(2,1)S(1)}, bf16[2,3,3,16,128]{4,3,2,1,0:T(8,128)(2,1)S(1)}, u32[]{:S(2)}, u32[]{:S(2)}) collective-permute-start(bf16[2,3,3,16,128]{4,3,2,1,0:T(8,128)(2,1)S(1)} %add_convert_fusion.mine), channel_id=1, source_target_pairs={{0,2},{1,5},{2,0},{3,7},{4,6},{5,1},{6,4},{7,3},{8,10},{9,13},{10,... | collective-permute-start | bytes 221192 | tf_op jit(solution)/shard_map/ppermute | solution.py:288
  55.8 1.6 %collective-permute-start.17 = (bf16[2,3,3,64,128]{4,3,2,1,0:T(8,128)(2,1)S(1)}, bf16[2,3,3,64,128]{4,3,2,1,0:T(8,128)(2,1)S(1)}, u32[]{:S(2)}, u32[]{:S(2)}) collective-permute-start(bf16[2,3,3,64,128]{4,3,2,1,0:T(8,128)(2,1)S(1)} %shard_map.82.mine), channel_id=1, source_target_pairs={{0,1},{1,0},{2,3},{3,2},{4,5},{5,4},{6,7},{7,6},{8,9},{9,8},{10,11... | collective-permute-start | bytes 884744 | tf_op jit(solution)/shard_map/ppermute | solution.py:288

commit v8 on v7

--- a/solution.py
+++ b/solution.py
@@ -82,7 +82,11 @@
     return values if keep is None else jnp.where(keep, values, 0.0)
 
 
-def early_kernel(x, main, second, xw, mid):
+def first_kernel(token):
+    token[...] = jnp.zeros_like(token)
+
+
+def early_kernel(token, x, main, second, xw, mid):
     own = x.shape[0]
     for i in range(own):
         place(xw, i, x[i].astype(F32))
@@ -143,7 +147,7 @@
         pre = pre1[...] + conv(yw, 0, own + 4 - 2, second)
         for i in range(own + 2):
             if i == 0:
-                upstream = jnp.where(even, g_other[own - 1].astype(F32), g_core[own - 1].astype(F32))
+                upstream = jnp.where(even, g_other[1].astype(F32), g_core[own - 1].astype(F32))
             elif i == own + 1:
                 upstream = jnp.where(even, g_core[0].astype(F32), g_other[0].astype(F32))
             else:
@@ -175,7 +179,7 @@
     def _():
         for i in range(own + 4):
             if i < 2:
-                upstream = jnp.where(even, g_other[own - 2 + i].astype(F32), g_core[own - 2 + i].astype(F32))
+                upstream = jnp.where(even, g_other[i].astype(F32), g_core[own - 2 + i].astype(F32))
                 returned = jnp.where(even, back_other[i].astype(F32), back_core[i].astype(F32))
             elif i >= own + 2:
                 k = i - own - 2
@@ -278,6 +282,9 @@
         neighbour = r - 1 if r % 2 == 0 else r + 1
         return neighbour if 0 <= neighbour < strips else r
 
+    def far(r):
+        return other(core(r))
+
     def same(r):
         return r
 
@@ -297,15 +304,17 @@
         return jax.ShapeDtypeStruct((rows, columns, 3 * channels), BF16)
 
     work = 2 * columns * 9 * channels * channels
-    x_other = swap(x, False, other)
+    (token,) = call(first_kernel, [jax.ShapeDtypeStruct((8, 128), F32)], [], (), 5 * 10**9)
     x_core = swap(x, False, core)
-    g_other = swap(g, False, other)
     g_core = swap(g, False, core)
+    x_core, token = lax.optimization_barrier((x_core, token))
+    x_other = swap(x_core, False, far)
+    g_other = swap(jnp.where(even, g_core[own - 2 :], g_core[:2]), False, far)
     xo, mid = call(
         early_kernel,
         [wide_out(own), like(own - 2, F32)],
         [],
-        (x, main, second),
+        (token, x, main, second),
         work * (own - 2),
     )
     pre1, pre2, hid, skip_here = call(

time: 58.9 us -> 55.1 us (0.935)
  local copies, waits for them, and re-layouts: 3.67 us -> 0.01 us
  waiting for transfers between devices: 26.3 us -> 28.8 us
  starting transfers between devices: 21.5 us -> 19.1 us
    unnamed x14 -> x8, local copies, waits for them, and re-layouts: 3.67 us -> 0.01 us
    ppermute x18, waiting for transfers between devices: 26.3 us -> 28.8 us  [swap(): return lax.ppermute(array, ('segment', 'rows'), pairs)]
    ppermute x18, starting transfers between devices: 21.5 us -> 19.1 us  [swap(): return lax.ppermute(array, ('segment', 'rows'), pairs)]
    pallas_call x9 -> x10, Pallas kernels: 6.19 us -> 6.21 us  [call(): pl.pallas_call(kernel, out_shape=outs, in_specs=[pl.BlockSpec(memory_spac...]
  transfers between devices with their start and end apart: 18 -> 18, of which waited for: 13 -> 14; matrix products, arithmetic and copies ran while one was open for 0% -> 0% of each run, Pallas kernels for 5% -> 6%
where the time goes in v8:
time: 55.1 us; the launch traced here: 54.9 us
  waiting for transfers between devices  28.8 us (52%)
  starting transfers between devices  19.1 us (35%)
  Pallas kernels  6.21 us (11%)
  between operations  0.75 us (1%)
    ppermute x18, waiting for transfers between devices, swap(): return lax.ppermute(array, ('segment', 'rows'), pairs)  28.8 us
    ppermute x18, starting transfers between devices, swap(): return lax.ppermute(array, ('segment', 'rows'), pairs)  19.1 us
    pallas_call x10, Pallas kernels, call(): pl.pallas_call(kernel, out_shape=outs, in_specs=[pl.BlockSpec(memory_spac...  6.21 us
  transfers between devices with their start and end apart: 18, of which 14 were waited for; matrix products, arithmetic and copies ran while one was open for 0% of the time, Pallas kernels for 6%

profile of v8, /device:TPU:0, one launch (start us, length us, event | category | flops | bytes accessed | tf_op | source)
XLA Modules:
  0.0 54.9 jit_solution(7881009678685016608)
XLA Ops:
  0.6 0.5 collective-permute-start
  1.3 1.1 %collective-permute-done.x_core = bf16[4,128,128]{2,1,0:T(8,128)(2,1)S(1)} collective-permute-done((bf16[4,128,128]{2,1,0:T(8,128)(2,1)}, bf16[4,128,128]{2,1,0:T(8,128)(2,1)S(1)}, u32[]{:S(2)}, u32[]{:S(2)}) %collective-permute-start) | collective-permute-done | bytes 131104 | tf_op jit(solution)/shard_map/ppermute | solution.py:295
  2.3 2.8 %collective-permute-start.1 = (bf16[4,128,128]{2,1,0:T(8,128)(2,1)S(1)}, bf16[4,128,128]{2,1,0:T(8,128)(2,1)S(1)}, u32[]{:S(2)}, u32[]{:S(2)}) collective-permute-start(bf16[4,128,128]{2,1,0:T(8,128)(2,1)S(1)} %collective-permute-done.x_core), channel_id=1, source_target_pairs={{0,2},{1,0},{2,4},{3,1},{4,6},{5,3},{6,8},{7,5},{8,10},{9,7},{10,1... | collective-permute-start | bytes 393224 | tf_op jit(solution)/shard_map/ppermute | solution.py:295
  5.2 1.6 %collective-permute-start.3 = (bf16[2,128,128]{2,1,0:T(8,128)(2,1)S(1)}, bf16[2,128,128]{2,1,0:T(8,128)(2,1)S(1)}, u32[]{:S(2)}, u32[]{:S(2)}) collective-permute-start(bf16[2,128,128]{2,1,0:T(8,128)(2,1)S(1)} %slice_select_fusion), channel_id=1, source_target_pairs={{0,2},{1,0},{2,4},{3,1},{4,6},{5,3},{6,8},{7,5},{8,10},{9,7},{10,1... | collective-permute-start | bytes 196616 | tf_op jit(solution)/shard_map/ppermute | solution.py:295
  7.2 2.6 %collective-permute-done.1.x_other = bf16[4,128,128]{2,1,0:T(8,128)(2,1)S(1)} collective-permute-done((bf16[4,128,128]{2,1,0:T(8,128)(2,1)S(1)}, bf16[4,128,128]{2,1,0:T(8,128)(2,1)S(1)}, u32[]{:S(2)}, u32[]{:S(2)}) %collective-permute-start.1) | collective-permute-done | bytes 131104 | tf_op jit(solution)/shard_map/ppermute | solution.py:295
  9.8 1.7 %shard_map.77 = (f32[6,128,128]{2,1,0:T(8,128)S(1)}, f32[8,128,128]{2,1,0:T(8,128)S(1)}, bf16[4,128,128]{2,1,0:T(8,128)(2,1)S(1)}, bf16[8,128,128]{2,1,0:T(8,128)(2,1)S(1)}) custom-call(bf16[4,128,384]{2,1,0:T(8,128)(2,1)S(1)} %get-tuple-element.35.xo, f32[2,128,128]{2,1,0:T(8,128)S(1)} %get-tuple-element.36.mid, ...), custom_call_target="tpu_custom_call" | custom-call | flops 603979776 | bytes 2686976 | tf_op jit(solution)/shard_map/pallas_call | solution.py:258
  11.5 0.5 collective-permute-start.4
  12.0 6.2 %collective-permute-done.4.skip_there = bf16[8,128,128]{2,1,0:T(8,128)(2,1)S(1)} collective-permute-done((bf16[8,128,128]{2,1,0:T(8,128)(2,1)S(1)}, bf16[8,128,128]{2,1,0:T(8,128)(2,1)S(1)}, u32[]{:S(2)}, u32[]{:S(2)}) %collective-permute-start.4) | collective-permute-done | bytes 262176 | tf_op jit(solution)/shard_map/ppermute | solution.py:295
  18.3 1.8 %collective-permute-start.5 = (bf16[4,128,128]{2,1,0:T(8,128)(2,1)S(1)}, bf16[4,128,128]{2,1,0:T(8,128)(2,1)S(1)}, u32[]{:S(2)}, u32[]{:S(2)}) collective-permute-start(bf16[4,128,128]{2,1,0:T(8,128)(2,1)S(1)} %get-tuple-element.43), channel_id=1, source_target_pairs={{0,16},{1,17},{2,18},{3,19},{4,20},{5,21},{6,22},{7,23},{8,24},{9,... | collective-permute-start | bytes 393224 | tf_op jit(solution)/shard_map/ppermute | solution.py:295
  20.1 0.3 collective-permute-start.7
  20.4 4.1 %collective-permute-done.6.back_core = bf16[2,128,128]{2,1,0:T(8,128)(2,1)S(1)} collective-permute-done((bf16[2,128,128]{2,1,0:T(8,128)(2,1)S(1)}, bf16[2,128,128]{2,1,0:T(8,128)(2,1)S(1)}, u32[]{:S(2)}, u32[]{:S(2)}) %collective-permute-start.6) | collective-permute-done | bytes 65568 | tf_op jit(solution)/shard_map/ppermute | solution.py:295
  24.5 1.7 %collective-permute-done.7.back_other = bf16[2,128,128]{2,1,0:T(8,128)(2,1)S(1)} collective-permute-done((bf16[2,128,128]{2,1,0:T(8,128)(2,1)S(1)}, bf16[2,128,128]{2,1,0:T(8,128)(2,1)S(1)}, u32[]{:S(2)}, u32[]{:S(2)}) %collective-permute-start.7) | collective-permute-done | bytes 65568 | tf_op jit(solution)/shard_map/ppermute | solution.py:295
  26.1 0.7 %shard_map.79 = (f32[3,3,64,128]{3,2,1,0:T(8,128)S(1)}, bf16[3,3,64,128]{3,2,1,0:T(8,128)(2,1)S(1)}, bf16[8,128,384]{2,1,0:T(8,128)(2,1)S(1)}) custom-call(bf16[4,128,128]{2,1,0:T(8,128)(2,1)S(1)} %bitcast.17, bf16[4,128,128]{2,1,0:T(8,128)(2,1)S(1)} %collective-permute-done.2.g_core, bf16[2,128,128]{2,1,0:T(8,128)(2,1)S(1)} %collective-permute-done.3.g_other, ...), custom_call_target="tpu_custom_call" | custom-call | flops 150994944 | bytes 3325952 | tf_op jit(solution)/shard_map/pallas_call | solution.py:258
  26.8 1.1 %shard_map.80 = (f32[3,3,64,128]{3,2,1,0:T(8,128)S(1)}, bf16[3,3,64,128]{3,2,1,0:T(8,128)(2,1)S(1)}, bf16[6,128,384]{2,1,0:T(8,128)(2,1)S(1)}) custom-call(bf16[4,128,128]{2,1,0:T(8,128)(2,1)S(1)} %bitcast.20, f32[6,128,128]{2,1,0:T(8,128)S(1)} %get-tuple-element.38.pre1, bf16[8,128,384]{2,1,0:T(8,128)(2,1)S(1)} %get-tuple-element.49.ew, ...), custom_call_target="tpu_custom_call" | custom-call | flops 377487360 | bytes 3227648 | tf_op jit(solution)/shard_map/pallas_call | solution.py:258
  28.0 0.5 collective-permute-start.9
  28.5 0.9 %collective-permute-done.8.got1 = bf16[3,3,64,128]{3,2,1,0:T(8,128)(2,1)S(1)} collective-permute-done((bf16[3,3,64,128]{3,2,1,0:T(8,128)(2,1)S(1)}, bf16[3,3,64,128]{3,2,1,0:T(8,128)(2,1)S(1)}, u32[]{:S(2)}, u32[]{:S(2)}) %collective-permute-start.8) | collective-permute-done | bytes 147488 | tf_op jit(solution)/shard_map/ppermute | solution.py:295
  29.7 2.2 %collective-permute-start.10 = (bf16[2,3,3,16,128]{4,3,2,1,0:T(8,128)(2,1)S(1)}, bf16[2,3,3,16,128]{4,3,2,1,0:T(8,128)(2,1)S(1)}, u32[]{:S(2)}, u32[]{:S(2)}) collective-permute-start(bf16[2,3,3,16,128]{4,3,2,1,0:T(8,128)(2,1)S(1)} %get-tuple-element.59), channel_id=1, source_target_pairs={{0,2},{1,5},{2,0},{3,7},{4,6},{5,1},{6,4},{7,3},{8,10},{9,13},{10,... | collective-permute-start | bytes 221192 | tf_op jit(solution)/shard_map/ppermute | solution.py:295
  31.8 1.6 %collective-permute-start.11 = (bf16[2,3,3,16,128]{4,3,2,1,0:T(8,128)(2,1)S(1)}, bf16[2,3,3,16,128]{4,3,2,1,0:T(8,128)(2,1)S(1)}, u32[]{:S(2)}, u32[]{:S(2)}) collective-permute-start(bf16[2,3,3,16,128]{4,3,2,1,0:T(8,128)(2,1)S(1)} %get-tuple-element.60), channel_id=1, source_target_pairs={{0,4},{1,3},{2,6},{3,1},{4,0},{5,7},{6,2},{7,5},{8,12},{9,11},{10,... | collective-permute-start | bytes 221192 | tf_op jit(solution)/shard_map/ppermute | solution.py:295
  33.4 0.8 %collective-permute-start.12 = (bf16[2,3,3,16,128]{4,3,2,1,0:T(8,128)(2,1)S(1)}, bf16[2,3,3,16,128]{4,3,2,1,0:T(8,128)(2,1)S(1)}, u32[]{:S(2)}, u32[]{:S(2)}) collective-permute-start(bf16[2,3,3,16,128]{4,3,2,1,0:T(8,128)(2,1)S(1)} %get-tuple-element.61), channel_id=1, source_target_pairs={{0,6},{1,7},{2,4},{3,5},{4,2},{5,3},{6,0},{7,1},{8,14},{9,15},{10,... | collective-permute-start | bytes 221192 | tf_op jit(solution)/shard_map/ppermute | solution.py:295
  34.3 1.9 %collective-permute-done.11 = bf16[2,3,3,16,128]{4,3,2,1,0:T(8,128)(2,1)S(1)} collective-permute-done((bf16[2,3,3,16,128]{4,3,2,1,0:T(8,128)(2,1)S(1)}, bf16[2,3,3,16,128]{4,3,2,1,0:T(8,128)(2,1)S(1)}, u32[]{:S(2)}, u32[]{:S(2)}) %collective-permute-start.11) | collective-permute-done | bytes 73760 | tf_op jit(solution)/shard_map/ppermute | solution.py:295
  36.2 2.5 %collective-permute-done.12 = bf16[2,3,3,16,128]{4,3,2,1,0:T(8,128)(2,1)S(1)} collective-permute-done((bf16[2,3,3,16,128]{4,3,2,1,0:T(8,128)(2,1)S(1)}, bf16[2,3,3,16,128]{4,3,2,1,0:T(8,128)(2,1)S(1)}, u32[]{:S(2)}, u32[]{:S(2)}) %collective-permute-start.12) | collective-permute-done | bytes 73760 | tf_op jit(solution)/shard_map/ppermute | solution.py:295
  38.7 2.6 %collective-permute-start.13 = (bf16[2,3,3,16,128]{4,3,2,1,0:T(8,128)(2,1)S(1)}, bf16[2,3,3,16,128]{4,3,2,1,0:T(8,128)(2,1)S(1)}, u32[]{:S(2)}, u32[]{:S(2)}) collective-permute-start(bf16[2,3,3,16,128]{4,3,2,1,0:T(8,128)(2,1)S(1)} %add_convert_fusion.1), channel_id=1, source_target_pairs={{0,8},{1,9},{2,10},{3,11},{4,12},{5,13},{6,14},{7,15},{8,0},{9,1},... | collective-permute-start | bytes 221192 | tf_op jit(solution)/shard_map/ppermute | solution.py:295
  41.3 3.5 %collective-permute-done.13 = bf16[2,3,3,16,128]{4,3,2,1,0:T(8,128)(2,1)S(1)} collective-permute-done((bf16[2,3,3,16,128]{4,3,2,1,0:T(8,128)(2,1)S(1)}, bf16[2,3,3,16,128]{4,3,2,1,0:T(8,128)(2,1)S(1)}, u32[]{:S(2)}, u32[]{:S(2)}) %collective-permute-start.13) | collective-permute-done | bytes 73760 | tf_op jit(solution)/shard_map/ppermute | solution.py:295
  44.9 0.9 %collective-permute-start.16 = (bf16[2,3,3,16,128]{4,3,2,1,0:T(8,128)(2,1)S(1)}, bf16[2,3,3,16,128]{4,3,2,1,0:T(8,128)(2,1)S(1)}, u32[]{:S(2)}, u32[]{:S(2)}) collective-permute-start(bf16[2,3,3,16,128]{4,3,2,1,0:T(8,128)(2,1)S(1)} %add_convert_fusion.mine), channel_id=1, source_target_pairs={{0,6},{1,7},{2,4},{3,5},{4,2},{5,3},{6,0},{7,1},{8,14},{9,15},{10,... | collective-permute-start | bytes 221192 | tf_op jit(solution)/shard_map/ppermute | solution.py:295
  45.8 2.0 %collective-permute-start.15 = (bf16[2,3,3,16,128]{4,3,2,1,0:T(8,128)(2,1)S(1)}, bf16[2,3,3,16,128]{4,3,2,1,0:T(8,128)(2,1)S(1)}, u32[]{:S(2)}, u32[]{:S(2)}) collective-permute-start(bf16[2,3,3,16,128]{4,3,2,1,0:T(8,128)(2,1)S(1)} %add_convert_fusion.mine), channel_id=1, source_target_pairs={{0,4},{1,3},{2,6},{3,1},{4,0},{5,7},{6,2},{7,5},{8,12},{9,11},{10,... | collective-permute-start | bytes 221192 | tf_op jit(solution)/shard_map/ppermute | solution.py:295
  47.8 0.6 %collective-permute-start.14 = (bf16[2,3,3,16,128]{4,3,2,1,0:T(8,128)(2,1)S(1)}, bf16[2,3,3,16,128]{4,3,2,1,0:T(8,128)(2,1)S(1)}, u32[]{:S(2)}, u32[]{:S(2)}) collective-permute-start(bf16[2,3,3,16,128]{4,3,2,1,0:T(8,128)(2,1)S(1)} %add_convert_fusion.mine), channel_id=1, source_target_pairs={{0,2},{1,5},{2,0},{3,7},{4,6},{5,1},{6,4},{7,3},{8,10},{9,13},{10,... | collective-permute-start | bytes 221192 | tf_op jit(solution)/shard_map/ppermute | solution.py:295
  48.4 1.8 %collective-permute-done.16.rest_2_ = bf16[2,3,3,16,128]{4,3,2,1,0:T(8,128)(2,1)S(1)} collective-permute-done((bf16[2,3,3,16,128]{4,3,2,1,0:T(8,128)(2,1)S(1)}, bf16[2,3,3,16,128]{4,3,2,1,0:T(8,128)(2,1)S(1)}, u32[]{:S(2)}, u32[]{:S(2)}) %collective-permute-start.16) | collective-permute-done | bytes 73760 | tf_op jit(solution)/shard_map/ppermute | solution.py:295
  50.2 0.7 %collective-permute-done.15.rest_1_ = bf16[2,3,3,16,128]{4,3,2,1,0:T(8,128)(2,1)S(1)} collective-permute-done((bf16[2,3,3,16,128]{4,3,2,1,0:T(8,128)(2,1)S(1)}, bf16[2,3,3,16,128]{4,3,2,1,0:T(8,128)(2,1)S(1)}, u32[]{:S(2)}, u32[]{:S(2)}) %collective-permute-start.15) | collective-permute-done | bytes 73760 | tf_op jit(solution)/shard_map/ppermute | solution.py:295
  50.9 1.2 %collective-permute-done.14.rest_0_ = bf16[2,3,3,16,128]{4,3,2,1,0:T(8,128)(2,1)S(1)} collective-permute-done((bf16[2,3,3,16,128]{4,3,2,1,0:T(8,128)(2,1)S(1)}, bf16[2,3,3,16,128]{4,3,2,1,0:T(8,128)(2,1)S(1)}, u32[]{:S(2)}, u32[]{:S(2)}) %collective-permute-start.14) | collective-permute-done | bytes 73760 | tf_op jit(solution)/shard_map/ppermute | solution.py:295
  52.3 1.1 %shard_map.81 = (bf16[4,128,128]{2,1,0:T(8,128)(2,1)}, bf16[4,128,128]{2,1,0:T(8,128)(2,1)}) custom-call(bf16[6,128,384]{2,1,0:T(8,128)(2,1)S(1)} %get-tuple-element.50.hw, bf16[3,3,128,128]{3,2,1,0:T(8,128)(2,1)S(1)} %bitcast.14, bf16[4,128,128]{2,1,0:T(8,128)(2,1)S(1)} %get-tuple-element.51.out), custom_call_target="tpu_custom_call" | custom-call | flops 150994944 | bytes 1277952 | tf_op jit(solution)/shard_map/pallas_call | solution.py:258
  53.4 0.4 collective-permute-done.17.theirs
  53.9 1.1 %shard_map.84 = (f32[3,3,128,128]{3,2,1,0:T(8,128)}, f32[3,3,128,128]{3,2,1,0:T(8,128)}) custom-call(bf16[2,3,3,64,128]{4,3,2,1,0:T(8,128)(2,1)S(1)} %shard_map.83.mine, bf16[2,3,3,64,128]{4,3,2,1,0:T(8,128)(2,1)S(1)} %collective-permute-done.17.theirs), custom_call_target="tpu_custom_call" | custom-call | flops 73728 | bytes 1769472 | tf_op jit(solution)/shard_map/pallas_call | solution.py:258
  (25 shorter events, 1.0 us)
Async XLA Ops:
  0.6 1.7 %collective-permute-start = (bf16[4,128,128]{2,1,0:T(8,128)(2,1)}, bf16[4,128,128]{2,1,0:T(8,128)(2,1)S(1)}, u32[]{:S(2)}, u32[]{:S(2)}) collective-permute-start(bf16[4,128,128]{2,1,0:T(8,128)(2,1)} %bitcast.18), channel_id=1, source_target_pairs={{0,1},{1,0},{2,3},{3,2},{4,5},{5,4},{6,7},{7,6},{8,9},{9,8},{10,11... | collective-permute-start | bytes 393224 | tf_op jit(solution)/shard_map/ppermute | solution.py:295
  1.1 4.0 %collective-permute-start.2 = (bf16[4,128,128]{2,1,0:T(8,128)(2,1)}, bf16[4,128,128]{2,1,0:T(8,128)(2,1)S(1)}, u32[]{:S(2)}, u32[]{:S(2)}) collective-permute-start(bf16[4,128,128]{2,1,0:T(8,128)(2,1)} %bitcast.15), channel_id=1, source_target_pairs={{0,1},{1,0},{2,3},{3,2},{4,5},{5,4},{6,7},{7,6},{8,9},{9,8},{10,11... | collective-permute-start | bytes 393224 | tf_op jit(solution)/shard_map/ppermute | solution.py:295
  1.2 5.6 %copy-start = (bf16[1,3,3,128,128]{4,3,2,1,0:T(8,128)(2,1)S(1)}, bf16[1,3,3,128,128]{4,3,2,1,0:T(8,128)(2,1)}, u32[]{:S(2)}) copy-start(bf16[1,3,3,128,128]{4,3,2,1,0:T(8,128)(2,1)} %param.7) | copy-start | bytes 884740
  1.2 5.6 %copy-start.1 = (bf16[1,3,3,128,128]{4,3,2,1,0:T(8,128)(2,1)S(1)}, bf16[1,3,3,128,128]{4,3,2,1,0:T(8,128)(2,1)}, u32[]{:S(2)}) copy-start(bf16[1,3,3,128,128]{4,3,2,1,0:T(8,128)(2,1)} %param.6) | copy-start | bytes 884740
  1.2 5.6 %copy-start.3 = (bf16[1,4,128,128]{3,2,1,0:T(8,128)(2,1)S(1)}, bf16[1,4,128,128]{3,2,1,0:T(8,128)(2,1)}, u32[]{:S(2)}) copy-start(bf16[1,4,128,128]{3,2,1,0:T(8,128)(2,1)} %param.4) | copy-start | bytes 393220
  2.3 7.4 %collective-permute-start.1 = (bf16[4,128,128]{2,1,0:T(8,128)(2,1)S(1)}, bf16[4,128,128]{2,1,0:T(8,128)(2,1)S(1)}, u32[]{:S(2)}, u32[]{:S(2)}) collective-permute-start(bf16[4,128,128]{2,1,0:T(8,128)(2,1)S(1)} %collective-permute-done.x_core), channel_id=1, source_target_pairs={{0,2},{1,0},{2,4},{3,1},{4,6},{5,3},{6,8},{7,5},{8,10},{9,7},{10,1... | collective-permute-start | bytes 393224 | tf_op jit(solution)/shard_map/ppermute | solution.py:295
  5.2 6.3 %collective-permute-start.3 = (bf16[2,128,128]{2,1,0:T(8,128)(2,1)S(1)}, bf16[2,128,128]{2,1,0:T(8,128)(2,1)S(1)}, u32[]{:S(2)}, u32[]{:S(2)}) collective-permute-start(bf16[2,128,128]{2,1,0:T(8,128)(2,1)S(1)} %slice_select_fusion), channel_id=1, source_target_pairs={{0,2},{1,0},{2,4},{3,1},{4,6},{5,3},{6,8},{7,5},{8,10},{9,7},{10,1... | collective-permute-start | bytes 196616 | tf_op jit(solution)/shard_map/ppermute | solution.py:295
  9.8 8.5 %copy-start.2 = (bf16[1,4,128,128]{3,2,1,0:T(8,128)(2,1)S(1)}, bf16[1,4,128,128]{3,2,1,0:T(8,128)(2,1)}, u32[]{:S(2)}) copy-start(bf16[1,4,128,128]{3,2,1,0:T(8,128)(2,1)} %param.5) | copy-start | bytes 393220
  11.5 6.7 %collective-permute-start.4 = (bf16[8,128,128]{2,1,0:T(8,128)(2,1)S(1)}, bf16[8,128,128]{2,1,0:T(8,128)(2,1)S(1)}, u32[]{:S(2)}, u32[]{:S(2)}) collective-permute-start(bf16[8,128,128]{2,1,0:T(8,128)(2,1)S(1)} %get-tuple-element.42.skip_here), channel_id=1, source_target_pairs={{0,16},{1,17},{2,18},{3,19},{4,20},{5,21},{6,22},{7,23},{8,24},{9,... | collective-permute-start | bytes 786440 | tf_op jit(solution)/shard_map/ppermute | solution.py:295
  18.3 7.8 %collective-permute-start.5 = (bf16[4,128,128]{2,1,0:T(8,128)(2,1)S(1)}, bf16[4,128,128]{2,1,0:T(8,128)(2,1)S(1)}, u32[]{:S(2)}, u32[]{:S(2)}) collective-permute-start(bf16[4,128,128]{2,1,0:T(8,128)(2,1)S(1)} %get-tuple-element.43), channel_id=1, source_target_pairs={{0,16},{1,17},{2,18},{3,19},{4,20},{5,21},{6,22},{7,23},{8,24},{9,... | collective-permute-start | bytes 393224 | tf_op jit(solution)/shard_map/ppermute | solution.py:295
  20.1 4.4 %collective-permute-start.6 = (bf16[2,128,128]{2,1,0:T(8,128)(2,1)S(1)}, bf16[2,128,128]{2,1,0:T(8,128)(2,1)S(1)}, u32[]{:S(2)}, u32[]{:S(2)}) collective-permute-start(bf16[2,128,128]{2,1,0:T(8,128)(2,1)S(1)} %get-tuple-element.44), channel_id=1, source_target_pairs={{0,17},{1,16},{2,19},{3,18},{4,21},{5,20},{6,23},{7,22},{8,25},{9,... | collective-permute-start | bytes 196616 | tf_op jit(solution)/shard_map/ppermute | solution.py:295
  20.1 6.1 %collective-permute-start.7 = (bf16[2,128,128]{2,1,0:T(8,128)(2,1)S(1)}, bf16[2,128,128]{2,1,0:T(8,128)(2,1)S(1)}, u32[]{:S(2)}, u32[]{:S(2)}) collective-permute-start(bf16[2,128,128]{2,1,0:T(8,128)(2,1)S(1)} %get-tuple-element.45), channel_id=1, source_target_pairs={{0,16},{1,18},{2,17},{3,20},{4,19},{5,22},{6,21},{7,24},{8,23},{9,... | collective-permute-start | bytes 196616 | tf_op jit(solution)/shard_map/ppermute | solution.py:295
  27.9 1.4 %collective-permute-start.8 = (bf16[3,3,64,128]{3,2,1,0:T(8,128)(2,1)S(1)}, bf16[3,3,64,128]{3,2,1,0:T(8,128)(2,1)S(1)}, u32[]{:S(2)}, u32[]{:S(2)}) collective-permute-start(bf16[3,3,64,128]{3,2,1,0:T(8,128)(2,1)S(1)} %get-tuple-element.55), channel_id=1, source_target_pairs={{0,1},{1,0},{2,3},{3,2},{4,5},{5,4},{6,7},{7,6},{8,9},{9,8},{10,11... | collective-permute-start | bytes 442376 | tf_op jit(solution)/shard_map/ppermute | solution.py:295
  28.0 1.6 %collective-permute-start.9 = (bf16[3,3,64,128]{3,2,1,0:T(8,128)(2,1)S(1)}, bf16[3,3,64,128]{3,2,1,0:T(8,128)(2,1)S(1)}, u32[]{:S(2)}, u32[]{:S(2)}) collective-permute-start(bf16[3,3,64,128]{3,2,1,0:T(8,128)(2,1)S(1)} %get-tuple-element.57), channel_id=1, source_target_pairs={{0,1},{1,0},{2,3},{3,2},{4,5},{5,4},{6,7},{7,6},{8,9},{9,8},{10,11... | collective-permute-start | bytes 442376 | tf_op jit(solution)/shard_map/ppermute | solution.py:295
  29.7 4.6 %collective-permute-start.10 = (bf16[2,3,3,16,128]{4,3,2,1,0:T(8,128)(2,1)S(1)}, bf16[2,3,3,16,128]{4,3,2,1,0:T(8,128)(2,1)S(1)}, u32[]{:S(2)}, u32[]{:S(2)}) collective-permute-start(bf16[2,3,3,16,128]{4,3,2,1,0:T(8,128)(2,1)S(1)} %get-tuple-element.59), channel_id=1, source_target_pairs={{0,2},{1,5},{2,0},{3,7},{4,6},{5,1},{6,4},{7,3},{8,10},{9,13},{10,... | collective-permute-start | bytes 221192 | tf_op jit(solution)/shard_map/ppermute | solution.py:295
  31.8 4.4 %collective-permute-start.11 = (bf16[2,3,3,16,128]{4,3,2,1,0:T(8,128)(2,1)S(1)}, bf16[2,3,3,16,128]{4,3,2,1,0:T(8,128)(2,1)S(1)}, u32[]{:S(2)}, u32[]{:S(2)}) collective-permute-start(bf16[2,3,3,16,128]{4,3,2,1,0:T(8,128)(2,1)S(1)} %get-tuple-element.60), channel_id=1, source_target_pairs={{0,4},{1,3},{2,6},{3,1},{4,0},{5,7},{6,2},{7,5},{8,12},{9,11},{10,... | collective-permute-start | bytes 221192 | tf_op jit(solution)/shard_map/ppermute | solution.py:295
  33.4 5.3 %collective-permute-start.12 = (bf16[2,3,3,16,128]{4,3,2,1,0:T(8,128)(2,1)S(1)}, bf16[2,3,3,16,128]{4,3,2,1,0:T(8,128)(2,1)S(1)}, u32[]{:S(2)}, u32[]{:S(2)}) collective-permute-start(bf16[2,3,3,16,128]{4,3,2,1,0:T(8,128)(2,1)S(1)} %get-tuple-element.61), channel_id=1, source_target_pairs={{0,6},{1,7},{2,4},{3,5},{4,2},{5,3},{6,0},{7,1},{8,14},{9,15},{10,... | collective-permute-start | bytes 221192 | tf_op jit(solution)/shard_map/ppermute | solution.py:295
  38.7 6.1 %collective-permute-start.13 = (bf16[2,3,3,16,128]{4,3,2,1,0:T(8,128)(2,1)S(1)}, bf16[2,3,3,16,128]{4,3,2,1,0:T(8,128)(2,1)S(1)}, u32[]{:S(2)}, u32[]{:S(2)}) collective-permute-start(bf16[2,3,3,16,128]{4,3,2,1,0:T(8,128)(2,1)S(1)} %add_convert_fusion.1), channel_id=1, source_target_pairs={{0,8},{1,9},{2,10},{3,11},{4,12},{5,13},{6,14},{7,15},{8,0},{9,1},... | collective-permute-start | bytes 221192 | tf_op jit(solution)/shard_map/ppermute | solution.py:295
  44.9 5.3 %collective-permute-start.16 = (bf16[2,3,3,16,128]{4,3,2,1,0:T(8,128)(2,1)S(1)}, bf16[2,3,3,16,128]{4,3,2,1,0:T(8,128)(2,1)S(1)}, u32[]{:S(2)}, u32[]{:S(2)}) collective-permute-start(bf16[2,3,3,16,128]{4,3,2,1,0:T(8,128)(2,1)S(1)} %add_convert_fusion.mine), channel_id=1, source_target_pairs={{0,6},{1,7},{2,4},{3,5},{4,2},{5,3},{6,0},{7,1},{8,14},{9,15},{10,... | collective-permute-start | bytes 221192 | tf_op jit(solution)/shard_map/ppermute | solution.py:295
  45.8 5.1 %collective-permute-start.15 = (bf16[2,3,3,16,128]{4,3,2,1,0:T(8,128)(2,1)S(1)}, bf16[2,3,3,16,128]{4,3,2,1,0:T(8,128)(2,1)S(1)}, u32[]{:S(2)}, u32[]{:S(2)}) collective-permute-start(bf16[2,3,3,16,128]{4,3,2,1,0:T(8,128)(2,1)S(1)} %add_convert_fusion.mine), channel_id=1, source_target_pairs={{0,4},{1,3},{2,6},{3,1},{4,0},{5,7},{6,2},{7,5},{8,12},{9,11},{10,... | collective-permute-start | bytes 221192 | tf_op jit(solution)/shard_map/ppermute | solution.py:295
  47.8 4.4 %collective-permute-start.14 = (bf16[2,3,3,16,128]{4,3,2,1,0:T(8,128)(2,1)S(1)}, bf16[2,3,3,16,128]{4,3,2,1,0:T(8,128)(2,1)S(1)}, u32[]{:S(2)}, u32[]{:S(2)}) collective-permute-start(bf16[2,3,3,16,128]{4,3,2,1,0:T(8,128)(2,1)S(1)} %add_convert_fusion.mine), channel_id=1, source_target_pairs={{0,2},{1,5},{2,0},{3,7},{4,6},{5,1},{6,4},{7,3},{8,10},{9,13},{10,... | collective-permute-start | bytes 221192 | tf_op jit(solution)/shard_map/ppermute | solution.py:295
  52.2 1.6 %collective-permute-start.17 = (bf16[2,3,3,64,128]{4,3,2,1,0:T(8,128)(2,1)S(1)}, bf16[2,3,3,64,128]{4,3,2,1,0:T(8,128)(2,1)S(1)}, u32[]{:S(2)}, u32[]{:S(2)}) collective-permute-start(bf16[2,3,3,64,128]{4,3,2,1,0:T(8,128)(2,1)S(1)} %shard_map.83.mine), channel_id=1, source_target_pairs={{0,1},{1,0},{2,3},{3,2},{4,5},{5,4},{6,7},{7,6},{8,9},{9,8},{10,11... | collective-permute-start | bytes 884744 | tf_op jit(solution)/shard_map/ppermute | solution.py:295

commit v9 on v8

--- a/solution.py
+++ b/solution.py
@@ -86,74 +86,100 @@
     token[...] = jnp.zeros_like(token)
 
 
-def early_kernel(token, x, main, second, xw, mid):
+def near_kernel(segments, token, x, x_core, main, second, xa, first, ha, pre, skip):
+    encoder, _, even = here(segments)
     own = x.shape[0]
     for i in range(own):
-        place(xw, i, x[i].astype(F32))
-    mid[...] = conv(xw, 0, own - 2, main)
-
-
-def front_kernel(segments, strips, xo, mid, x_core, x_other, main, second, pre1, pre2, hid, skip, xw, hw):
+        place(xa, jnp.where(even, 0, own) + i, x[i].astype(F32))
+        place(xa, jnp.where(even, own, 0) + i, x_core[i].astype(F32))
+    first[...] = conv(xa, 0, 2 * own - 2, main)
+
+    @pl.when(encoder)
+    def _():
+        for i in range(2 * own - 2):
+            place(ha, i, silu(first[i]))
+        pre[...] = conv(ha, 0, 2 * own - 4, second)
+        for i in range(2 * own - 4):
+            skip[i] = silu(pre[i]).astype(BF16)
+
+
+def far_kernel(segments, strips, xa, ha, x_far, main, second, first, pre, hid, skip, xb, hb):
     encoder, row, even = here(segments)
-    own = xo.shape[0]
-    core_at = jnp.where(even, 2 * own, 0)
-    other_at = jnp.where(even, 0, 2 * own)
-    core_in = jnp.where(even, row < strips - 1, row > 0)
-    other_in = jnp.where(even, row > 0, row < strips - 1)
-    xw[own : 2 * own] = xo[...]
+    own = x_far.shape[0]
+    near = ha.shape[0]
+    columns, channels = x_far.shape[1:]
+    far_in = jnp.where(even, row > 0, row < strips - 1)
     for i in range(own):
-        place(xw, core_at + i, masked(x_core[i].astype(F32), core_in))
-        place(xw, other_at + i, masked(x_other[i].astype(F32), other_in))
+        place(xb, jnp.where(even, 0, 2) + i, masked(x_far[i].astype(F32), far_in))
+    for i in range(2):
+        xb[jnp.where(even, own, 0) + i] = xa[jnp.where(even, 0, 2 * own - 2) + i]
+    first[...] = conv(xb, 0, own, main)
 
     @pl.when(encoder)
     def _():
-        above = conv(xw, 0, 4, main)
-        below = conv(xw, own + 2, 4, main)
-        pre1[0:2] = above[2:4]
-        pre1[2:own] = mid[...]
-        pre1[own : own + 2] = below[0:2]
-        for i in range(own + 6):
-            first = above[i] if i < 4 else below[i - own - 2] if i >= own + 2 else mid[i - 4]
-            value = masked(silu(first), inside(row, strips, own, i - 3))
-            place(hw, i, value)
-            if 3 <= i < own + 3:
-                hid[i - 3] = value.astype(BF16)
-        final = conv(hw, 0, own + 4, second)
-        pre2[...] = final
-        for i in range(own + 4):
-            skip[i] = masked(silu(final[i]), inside(row, strips, own, i - 2)).astype(BF16)
-
-    @pl.when(jnp.logical_not(encoder))
-    def _():
-        pre1[0:2] = conv(xw, 2, 2, main)
-        pre1[2:own] = mid[...]
-        pre1[own : own + 2] = conv(xw, own + 2, 2, main)
+        for i in range(own):
+            keep = far_in
+            if i == 0:
+                keep = jnp.logical_or(far_in, jnp.logical_not(even))
+            elif i == own - 1:
+                keep = jnp.logical_or(far_in, even)
+            place(hb, jnp.where(even, 0, 2) + i, masked(silu(first[i]), keep))
+        for i in range(2):
+            hb[jnp.where(even, own, 0) + i] = ha[jnp.where(even, 0, near - 2) + i]
+        pre[...] = conv(hb, 0, own, second)
+        for i in range(own):
+            keep = jnp.logical_or(far_in, jnp.logical_not(even) if i < 2 else even)
+            skip[i] = masked(silu(pre[i]), keep).astype(BF16)
+        for i in range(own):
+            middle = slice(channels, 2 * channels)
+            at_even = hb[own - 1, :, middle] if i == 0 else ha[i - 1, :, middle]
+            at_odd = hb[2, :, middle] if i == own - 1 else ha[own - 1 + i, :, middle]
+            hid[i] = jnp.where(even, at_even, at_odd)
+
+
+def joined(even, near, far, i):
+    half = near.shape[0]
+    if i < half:
+        return jnp.where(even, far[i], near[i])
+    return jnp.where(even, near[i - half], far[i - half])
+
+
+def joined_first(even, near, far, i):
+    own = far.shape[0]
+    t = own - 1 + i
+    at_even = near[t - own - 1] if t > own else far[t - 1]
+    at_odd = near[t - 1] if t < 2 * own - 1 else far[t - 2 * own + 1]
+    return jnp.where(even, at_even, at_odd)
 
 
 def middle_kernel(
-    segments, strips, skip_here, skip_there, pre1, g, g_core, g_other, second, out, gw, back, edge_core, edge_other, yw
+    segments, strips, near_here, far_here, near, far, near_first, far_first, g, g_core, g_other, second, out, gw, back, edge_core, edge_other, yw
 ):
     encoder, row, even = here(segments)
     own = g.shape[0]
 
     @pl.when(encoder)
     def _():
-        out[...] = skip_here[2 : own + 2]
+        for i in range(own):
+            out[i] = joined(even, near_here, far_here, i + 2)
 
     @pl.when(jnp.logical_not(encoder))
     def _():
-        for i in range(own + 4):
-            place(yw, i, skip_there[i].astype(F32))
-        pre = pre1[...] + conv(yw, 0, own + 4 - 2, second)
+        half = near.shape[0]
+        for i in range(half):
+            place(yw, jnp.where(even, half, 0) + i, near[i].astype(F32))
+            place(yw, jnp.where(even, 0, half) + i, far[i].astype(F32))
+        skip_pre = conv(yw, 0, own + 2, second)
         for i in range(own + 2):
+            pre = skip_pre[i] + joined_first(even, near_first, far_first, i)
             if i == 0:
                 upstream = jnp.where(even, g_other[1].astype(F32), g_core[own - 1].astype(F32))
             elif i == own + 1:
                 upstream = jnp.where(even, g_core[0].astype(F32), g_other[0].astype(F32))
             else:
                 upstream = g[i - 1].astype(F32)
-                out[i - 1] = silu(pre[i]).astype(BF16)
-            value = masked(upstream * slope(pre[i]), inside(row, strips, own, i - 1))
+                out[i - 1] = silu(pre).astype(BF16)
+            value = masked(upstream * slope(pre), inside(row, strips, own, i - 1))
             place(gw, i, value)
         back[...] = conv_back(gw, 0, own, second).astype(BF16)
         edge_core[...] = jnp.where(even, back[own - 2 : own], back[0:2])
@@ -170,7 +196,7 @@
 
 
 def second_kernel(
-    segments, strips, g, g_core, g_other, back, back_core, back_other, pre2, hid, skip_there, gw, kept, sent, ew
+    segments, strips, g, g_core, g_other, back, back_core, back_other, near_pre, far_pre, hid, near, far, gw, kept, sent, ew
 ):
     encoder, row, even = here(segments)
     own = g.shape[0]
@@ -188,16 +214,17 @@
             else:
                 upstream = g[i - 2].astype(F32)
                 returned = back[i - 2].astype(F32)
-            value = (upstream + returned) * slope(pre2[i])
+            value = (upstream + returned) * slope(joined(even, near_pre, far_pre, i))
             place(ew, i, masked(value, inside(row, strips, own, i - 2)))
         conv_weight(hid[...], ew, 1, store(even, kept, sent))
 
     @pl.when(jnp.logical_not(encoder))
     def _():
-        conv_weight(skip_there[2 : own + 2], gw, 0, store(even, kept, sent))
-
-
-def main_kernel(segments, strips, x, pre1, ew, gw, second, kept, sent, hw):
+        skip = jnp.stack([joined(even, near, far, i + 2) for i in range(own)])
+        conv_weight(skip, gw, 0, store(even, kept, sent))
+
+
+def main_kernel(segments, strips, x, near_first, far_first, ew, gw, second, kept, sent, hw):
     encoder, row, even = here(segments)
     own = x.shape[0]
 
@@ -205,7 +232,7 @@
     def _():
         hidden_back = conv_back(ew, 0, own + 2, second)
         for i in range(own + 2):
-            value = hidden_back[i] * slope(pre1[i])
+            value = hidden_back[i] * slope(joined_first(even, near_first, far_first, i))
             place(hw, i, masked(value, inside(row, strips, own, i - 1)))
 
     @pl.when(jnp.logical_not(encoder))
@@ -308,29 +335,30 @@
     x_core = swap(x, False, core)
     g_core = swap(g, False, core)
     x_core, token = lax.optimization_barrier((x_core, token))
-    x_other = swap(x_core, False, far)
-    g_other = swap(jnp.where(even, g_core[own - 2 :], g_core[:2]), False, far)
-    xo, mid = call(
-        early_kernel,
-        [wide_out(own), like(own - 2, F32)],
+    x_far = swap(x_core, False, far)
+    xa, near_first, ha, near_pre, near_here = call(
+        functools.partial(near_kernel, segments),
+        [wide_out(2 * own), like(2 * own - 2, F32), wide_out(2 * own - 2), like(2 * own - 4, F32), like(2 * own - 4, BF16)],
         [],
-        (token, x, main, second),
-        work * (own - 2),
-    )
-    pre1, pre2, hid, skip_here = call(
-        functools.partial(front_kernel, segments, strips),
-        [like(own + 2, F32), like(own + 4, F32), like(own, BF16), like(own + 4, BF16)],
-        [wide(3 * own), wide(own + 6)],
-        (xo, mid, x_core, x_other, main, second),
-        work * (2 * own + 8),
-    )
-    skip_here, g_core, g_other = lax.optimization_barrier((skip_here, g_core, g_other))
-    skip_there = swap(skip_here, True, same)
+        (token, x, x_core, main, second),
+        work * (4 * own - 6),
+    )
+    near_here, edge = lax.optimization_barrier((near_here, jnp.where(even, g_core[own - 2 :], g_core[:2])))
+    near_there = swap(near_here, True, same)
+    g_other = swap(edge, False, far)
+    far_first, far_pre, hid, far_here = call(
+        functools.partial(far_kernel, segments, strips),
+        [like(own, F32), like(own, F32), like(own, BF16), like(own, BF16)],
+        [wide(own + 2), wide(own + 2)],
+        (xa, ha, x_far, main, second),
+        work * 2 * own,
+    )
+    far_there = swap(far_here, True, same)
     out, gw, back, edge_core, edge_other = call(
         functools.partial(middle_kernel, segments, strips),
         [like(own, BF16), wide_out(own + 2), like(own, BF16), like(2, BF16), like(2, BF16)],
         [wide(own + 4)],
-        (skip_here, skip_there, pre1, g, g_core, g_other, second),
+        (near_here, far_here, near_there, far_there, near_first, far_first, g, g_core, g_other, second),
         work * (2 * own + 2),
     )
     back_own = swap(back, True, same)
@@ -343,14 +371,14 @@
         functools.partial(second_kernel, segments, strips),
         terms + [wide_out(own + 4)],
         [],
-        (g, g_core, g_other, back_own, back_core, back_other, pre2, hid, skip_there, gw),
+        (g, g_core, g_other, back_own, back_core, back_other, near_pre, far_pre, hid, near_there, far_there, gw),
         work * own,
     )
     kept1, sent1, hw = call(
         functools.partial(main_kernel, segments, strips),
         terms + [wide_out(own + 2)],
         [],
-        (x, pre1, ew, gw, second),
+        (x, near_first, far_first, ew, gw, second),
         work * (2 * own + 2),
     )
     input_grad, output = call(input_kernel, [like(own, BF16)] * 2, [], (hw, main, out), work * own)

time: 55.1 us -> 53 us (0.962)
  waiting for transfers between devices: 28.8 us -> 23.5 us
  starting transfers between devices: 19.1 us -> 21.8 us
  Pallas kernels: 6.21 us -> 6.77 us
    ppermute x18 -> x19, waiting for transfers between devices: 28.8 us -> 23.5 us  [swap(): return lax.ppermute(array, ('segment', 'rows'), pairs)]
    ppermute x18 -> x19, starting transfers between devices: 19.1 us -> 21.8 us  [swap(): return lax.ppermute(array, ('segment', 'rows'), pairs)]
    pallas_call x10, Pallas kernels: 6.21 us -> 6.77 us  [call(): pl.pallas_call(kernel, out_shape=outs, in_specs=[pl.BlockSpec(memory_spac...]
  transfers between devices with their start and end apart: 18 -> 19, of which waited for: 14 -> 15; matrix products, arithmetic and copies ran while one was open for 0% -> 0% of each run, Pallas kernels for 6% -> 7%
where the time goes in v9:
time: 53 us; the launch traced here: 52.9 us
  waiting for transfers between devices  23.5 us (44%)
  starting transfers between devices  21.8 us (41%)
  Pallas kernels  6.77 us (13%)
  between operations  0.75 us (1%)
    ppermute x19, waiting for transfers between devices, swap(): return lax.ppermute(array, ('segment', 'rows'), pairs)  23.5 us
    ppermute x19, starting transfers between devices, swap(): return lax.ppermute(array, ('segment', 'rows'), pairs)  21.8 us
    pallas_call x10, Pallas kernels, call(): pl.pallas_call(kernel, out_shape=outs, in_specs=[pl.BlockSpec(memory_spac...  6.77 us
  transfers between devices with their start and end apart: 19, of which 15 were waited for; matrix products, arithmetic and copies ran while one was open for 0% of the time, Pallas kernels for 7%

profile of v9, /device:TPU:0, one launch (start us, length us, event | category | flops | bytes accessed | tf_op | source)
XLA Modules:
  0.0 52.9 jit_solution(10403826013011650367)
XLA Ops:
  0.6 0.5 collective-permute-start
  1.3 1.1 %collective-permute-done.x_core = bf16[4,128,128]{2,1,0:T(8,128)(2,1)S(1)} collective-permute-done((bf16[4,128,128]{2,1,0:T(8,128)(2,1)}, bf16[4,128,128]{2,1,0:T(8,128)(2,1)S(1)}, u32[]{:S(2)}, u32[]{:S(2)}) %collective-permute-start) | collective-permute-done | bytes 131104 | tf_op jit(solution)/shard_map/ppermute | solution.py:322
  2.3 2.8 %collective-permute-start.1 = (bf16[4,128,128]{2,1,0:T(8,128)(2,1)S(1)}, bf16[4,128,128]{2,1,0:T(8,128)(2,1)S(1)}, u32[]{:S(2)}, u32[]{:S(2)}) collective-permute-start(bf16[4,128,128]{2,1,0:T(8,128)(2,1)S(1)} %collective-permute-done.x_core), channel_id=1, source_target_pairs={{0,2},{1,0},{2,4},{3,1},{4,6},{5,3},{6,8},{7,5},{8,10},{9,7},{10,1... | collective-permute-start | bytes 393224 | tf_op jit(solution)/shard_map/ppermute | solution.py:322
  5.2 1.3 %shard_map.76 = (bf16[8,128,384]{2,1,0:T(8,128)(2,1)S(1)}, f32[6,128,128]{2,1,0:T(8,128)S(1)}, bf16[6,128,384]{2,1,0:T(8,128)(2,1)S(1)}, f32[4,128,128]{2,1,0:T(8,128)S(1)}, bf16[4,128,128]{2,1,0:T(8,128)(2,1)S(1)}) custom-call(f32[8,128]{1,0:T(8,128)S(1)} %shard_map.75.token, bf16[4,128,128]{2,1,0:T(8,128)(2,1)S(1)} %bitcast.19, ...), custom_call_target="tpu_custom_call" | custom-call | flops 377487360 | bytes 3018752 | tf_op jit(solution)/shard_map/pallas_call | solution.py:285
  6.5 1.1 %collective-permute-start.4 = (bf16[4,128,128]{2,1,0:T(8,128)(2,1)S(1)}, bf16[4,128,128]{2,1,0:T(8,128)(2,1)S(1)}, u32[]{:S(2)}, u32[]{:S(2)}) collective-permute-start(bf16[4,128,128]{2,1,0:T(8,128)(2,1)S(1)} %get-tuple-element.44.near_here), channel_id=1, source_target_pairs={{0,16},{1,17},{2,18},{3,19},{4,20},{5,21},{6,22},{7,23},{8,24},{9,... | collective-permute-start | bytes 393224 | tf_op jit(solution)/shard_map/ppermute | solution.py:322
  7.6 1.5 %collective-permute-done.1.x_far = bf16[4,128,128]{2,1,0:T(8,128)(2,1)S(1)} collective-permute-done((bf16[4,128,128]{2,1,0:T(8,128)(2,1)S(1)}, bf16[4,128,128]{2,1,0:T(8,128)(2,1)S(1)}, u32[]{:S(2)}, u32[]{:S(2)}) %collective-permute-start.1) | collective-permute-done | bytes 131104 | tf_op jit(solution)/shard_map/ppermute | solution.py:322
  9.1 1.3 %shard_map.77 = (f32[4,128,128]{2,1,0:T(8,128)S(1)}, f32[4,128,128]{2,1,0:T(8,128)S(1)}, bf16[4,128,128]{2,1,0:T(8,128)(2,1)S(1)}, bf16[4,128,128]{2,1,0:T(8,128)(2,1)S(1)}) custom-call(bf16[8,128,384]{2,1,0:T(8,128)(2,1)S(1)} %get-tuple-element.39.xa, bf16[6,128,384]{2,1,0:T(8,128)(2,1)S(1)} %get-tuple-element.40.ha, ...), custom_call_target="tpu_custom_call" | custom-call | flops 301989888 | bytes 2883584 | tf_op jit(solution)/shard_map/pallas_call | solution.py:285
  10.4 0.9 %collective-permute-start.5 = (bf16[4,128,128]{2,1,0:T(8,128)(2,1)S(1)}, bf16[4,128,128]{2,1,0:T(8,128)(2,1)S(1)}, u32[]{:S(2)}, u32[]{:S(2)}) collective-permute-start(bf16[4,128,128]{2,1,0:T(8,128)(2,1)S(1)} %get-tuple-element.45.far_here), channel_id=1, source_target_pairs={{0,16},{1,17},{2,18},{3,19},{4,20},{5,21},{6,22},{7,23},{8,24},{9,... | collective-permute-start | bytes 393224 | tf_op jit(solution)/shard_map/ppermute | solution.py:322
  11.3 2.5 %collective-permute-start.3 = (bf16[2,128,128]{2,1,0:T(8,128)(2,1)S(1)}, bf16[2,128,128]{2,1,0:T(8,128)(2,1)S(1)}, u32[]{:S(2)}, u32[]{:S(2)}) collective-permute-start(bf16[2,128,128]{2,1,0:T(8,128)(2,1)S(1)} %slice_select_fusion), channel_id=1, source_target_pairs={{0,2},{1,0},{2,4},{3,1},{4,6},{5,3},{6,8},{7,5},{8,10},{9,7},{10,1... | collective-permute-start | bytes 196616 | tf_op jit(solution)/shard_map/ppermute | solution.py:322
  13.7 1.9 %collective-permute-done.3.g_other = bf16[2,128,128]{2,1,0:T(8,128)(2,1)S(1)} collective-permute-done((bf16[2,128,128]{2,1,0:T(8,128)(2,1)S(1)}, bf16[2,128,128]{2,1,0:T(8,128)(2,1)S(1)}, u32[]{:S(2)}, u32[]{:S(2)}) %collective-permute-start.3) | collective-permute-done | bytes 65568 | tf_op jit(solution)/shard_map/ppermute | solution.py:322
  15.7 2.9 %collective-permute-start.6 = (bf16[4,128,128]{2,1,0:T(8,128)(2,1)S(1)}, bf16[4,128,128]{2,1,0:T(8,128)(2,1)S(1)}, u32[]{:S(2)}, u32[]{:S(2)}) collective-permute-start(bf16[4,128,128]{2,1,0:T(8,128)(2,1)S(1)} %get-tuple-element.46), channel_id=1, source_target_pairs={{0,16},{1,17},{2,18},{3,19},{4,20},{5,21},{6,22},{7,23},{8,24},{9,... | collective-permute-start | bytes 393224 | tf_op jit(solution)/shard_map/ppermute | solution.py:322
  18.7 5.0 %collective-permute-done.7.back_core = bf16[2,128,128]{2,1,0:T(8,128)(2,1)S(1)} collective-permute-done((bf16[2,128,128]{2,1,0:T(8,128)(2,1)S(1)}, bf16[2,128,128]{2,1,0:T(8,128)(2,1)S(1)}, u32[]{:S(2)}, u32[]{:S(2)}) %collective-permute-start.7) | collective-permute-done | bytes 65568 | tf_op jit(solution)/shard_map/ppermute | solution.py:322
  23.7 0.6 %collective-permute-done.8.back_other = bf16[2,128,128]{2,1,0:T(8,128)(2,1)S(1)} collective-permute-done((bf16[2,128,128]{2,1,0:T(8,128)(2,1)S(1)}, bf16[2,128,128]{2,1,0:T(8,128)(2,1)S(1)}, u32[]{:S(2)}, u32[]{:S(2)}) %collective-permute-start.8) | collective-permute-done | bytes 65568 | tf_op jit(solution)/shard_map/ppermute | solution.py:322
  24.3 0.7 %shard_map.79 = (f32[3,3,64,128]{3,2,1,0:T(8,128)S(1)}, bf16[3,3,64,128]{3,2,1,0:T(8,128)(2,1)S(1)}, bf16[8,128,384]{2,1,0:T(8,128)(2,1)S(1)}) custom-call(bf16[4,128,128]{2,1,0:T(8,128)(2,1)S(1)} %bitcast.17, bf16[4,128,128]{2,1,0:T(8,128)(2,1)S(1)} %collective-permute-done.2.g_core, bf16[2,128,128]{2,1,0:T(8,128)(2,1)S(1)} %collective-permute-done.3.g_other, ...), custom_call_target="tpu_custom_call" | custom-call | flops 150994944 | bytes 3325952 | tf_op jit(solution)/shard_map/pallas_call | solution.py:285
  25.0 1.1 %shard_map.80 = (f32[3,3,64,128]{3,2,1,0:T(8,128)S(1)}, bf16[3,3,64,128]{3,2,1,0:T(8,128)(2,1)S(1)}, bf16[6,128,384]{2,1,0:T(8,128)(2,1)S(1)}) custom-call(bf16[4,128,128]{2,1,0:T(8,128)(2,1)S(1)} %bitcast.20, f32[6,128,128]{2,1,0:T(8,128)S(1)} %get-tuple-element.38.near_first, f32[4,128,128]{2,1,0:T(8,128)S(1)} %get-tuple-element.41.far_first, ...), custom_call_target="tpu_custom_call" | custom-call | flops 377487360 | bytes 3489792 | tf_op jit(solution)/shard_map/pallas_call | solution.py:285
  26.3 0.5 collective-permute-start.10
  26.8 0.9 %collective-permute-done.9.got1 = bf16[3,3,64,128]{3,2,1,0:T(8,128)(2,1)S(1)} collective-permute-done((bf16[3,3,64,128]{3,2,1,0:T(8,128)(2,1)S(1)}, bf16[3,3,64,128]{3,2,1,0:T(8,128)(2,1)S(1)}, u32[]{:S(2)}, u32[]{:S(2)}) %collective-permute-start.9) | collective-permute-done | bytes 147488 | tf_op jit(solution)/shard_map/ppermute | solution.py:322
  27.9 2.1 %collective-permute-start.11 = (bf16[2,3,3,16,128]{4,3,2,1,0:T(8,128)(2,1)S(1)}, bf16[2,3,3,16,128]{4,3,2,1,0:T(8,128)(2,1)S(1)}, u32[]{:S(2)}, u32[]{:S(2)}) collective-permute-start(bf16[2,3,3,16,128]{4,3,2,1,0:T(8,128)(2,1)S(1)} %get-tuple-element.63), channel_id=1, source_target_pairs={{0,2},{1,5},{2,0},{3,7},{4,6},{5,1},{6,4},{7,3},{8,10},{9,13},{10,... | collective-permute-start | bytes 221192 | tf_op jit(solution)/shard_map/ppermute | solution.py:322
  30.1 1.6 %collective-permute-start.12 = (bf16[2,3,3,16,128]{4,3,2,1,0:T(8,128)(2,1)S(1)}, bf16[2,3,3,16,128]{4,3,2,1,0:T(8,128)(2,1)S(1)}, u32[]{:S(2)}, u32[]{:S(2)}) collective-permute-start(bf16[2,3,3,16,128]{4,3,2,1,0:T(8,128)(2,1)S(1)} %get-tuple-element.64), channel_id=1, source_target_pairs={{0,4},{1,3},{2,6},{3,1},{4,0},{5,7},{6,2},{7,5},{8,12},{9,11},{10,... | collective-permute-start | bytes 221192 | tf_op jit(solution)/shard_map/ppermute | solution.py:322
  31.7 0.6 %collective-permute-start.13 = (bf16[2,3,3,16,128]{4,3,2,1,0:T(8,128)(2,1)S(1)}, bf16[2,3,3,16,128]{4,3,2,1,0:T(8,128)(2,1)S(1)}, u32[]{:S(2)}, u32[]{:S(2)}) collective-permute-start(bf16[2,3,3,16,128]{4,3,2,1,0:T(8,128)(2,1)S(1)} %get-tuple-element.65), channel_id=1, source_target_pairs={{0,6},{1,7},{2,4},{3,5},{4,2},{5,3},{6,0},{7,1},{8,14},{9,15},{10,... | collective-permute-start | bytes 221192 | tf_op jit(solution)/shard_map/ppermute | solution.py:322
  32.4 2.0 %collective-permute-done.12 = bf16[2,3,3,16,128]{4,3,2,1,0:T(8,128)(2,1)S(1)} collective-permute-done((bf16[2,3,3,16,128]{4,3,2,1,0:T(8,128)(2,1)S(1)}, bf16[2,3,3,16,128]{4,3,2,1,0:T(8,128)(2,1)S(1)}, u32[]{:S(2)}, u32[]{:S(2)}) %collective-permute-start.12) | collective-permute-done | bytes 73760 | tf_op jit(solution)/shard_map/ppermute | solution.py:322
  34.4 2.5 %collective-permute-done.13 = bf16[2,3,3,16,128]{4,3,2,1,0:T(8,128)(2,1)S(1)} collective-permute-done((bf16[2,3,3,16,128]{4,3,2,1,0:T(8,128)(2,1)S(1)}, bf16[2,3,3,16,128]{4,3,2,1,0:T(8,128)(2,1)S(1)}, u32[]{:S(2)}, u32[]{:S(2)}) %collective-permute-start.13) | collective-permute-done | bytes 73760 | tf_op jit(solution)/shard_map/ppermute | solution.py:322
  37.0 2.3 %collective-permute-start.14 = (bf16[2,3,3,16,128]{4,3,2,1,0:T(8,128)(2,1)S(1)}, bf16[2,3,3,16,128]{4,3,2,1,0:T(8,128)(2,1)S(1)}, u32[]{:S(2)}, u32[]{:S(2)}) collective-permute-start(bf16[2,3,3,16,128]{4,3,2,1,0:T(8,128)(2,1)S(1)} %add_convert_fusion.1), channel_id=1, source_target_pairs={{0,8},{1,9},{2,10},{3,11},{4,12},{5,13},{6,14},{7,15},{8,0},{9,1},... | collective-permute-start | bytes 221192 | tf_op jit(solution)/shard_map/ppermute | solution.py:322
  39.3 3.8 %collective-permute-done.14 = bf16[2,3,3,16,128]{4,3,2,1,0:T(8,128)(2,1)S(1)} collective-permute-done((bf16[2,3,3,16,128]{4,3,2,1,0:T(8,128)(2,1)S(1)}, bf16[2,3,3,16,128]{4,3,2,1,0:T(8,128)(2,1)S(1)}, u32[]{:S(2)}, u32[]{:S(2)}) %collective-permute-start.14) | collective-permute-done | bytes 73760 | tf_op jit(solution)/shard_map/ppermute | solution.py:322
  43.1 0.6 %collective-permute-start.17 = (bf16[2,3,3,16,128]{4,3,2,1,0:T(8,128)(2,1)S(1)}, bf16[2,3,3,16,128]{4,3,2,1,0:T(8,128)(2,1)S(1)}, u32[]{:S(2)}, u32[]{:S(2)}) collective-permute-start(bf16[2,3,3,16,128]{4,3,2,1,0:T(8,128)(2,1)S(1)} %add_convert_fusion.mine), channel_id=1, source_target_pairs={{0,6},{1,7},{2,4},{3,5},{4,2},{5,3},{6,0},{7,1},{8,14},{9,15},{10,... | collective-permute-start | bytes 221192 | tf_op jit(solution)/shard_map/ppermute | solution.py:322
  43.7 2.0 %collective-permute-start.16 = (bf16[2,3,3,16,128]{4,3,2,1,0:T(8,128)(2,1)S(1)}, bf16[2,3,3,16,128]{4,3,2,1,0:T(8,128)(2,1)S(1)}, u32[]{:S(2)}, u32[]{:S(2)}) collective-permute-start(bf16[2,3,3,16,128]{4,3,2,1,0:T(8,128)(2,1)S(1)} %add_convert_fusion.mine), channel_id=1, source_target_pairs={{0,4},{1,3},{2,6},{3,1},{4,0},{5,7},{6,2},{7,5},{8,12},{9,11},{10,... | collective-permute-start | bytes 221192 | tf_op jit(solution)/shard_map/ppermute | solution.py:322
  45.8 0.9 %collective-permute-start.15 = (bf16[2,3,3,16,128]{4,3,2,1,0:T(8,128)(2,1)S(1)}, bf16[2,3,3,16,128]{4,3,2,1,0:T(8,128)(2,1)S(1)}, u32[]{:S(2)}, u32[]{:S(2)}) collective-permute-start(bf16[2,3,3,16,128]{4,3,2,1,0:T(8,128)(2,1)S(1)} %add_convert_fusion.mine), channel_id=1, source_target_pairs={{0,2},{1,5},{2,0},{3,7},{4,6},{5,1},{6,4},{7,3},{8,10},{9,13},{10,... | collective-permute-start | bytes 221192 | tf_op jit(solution)/shard_map/ppermute | solution.py:322
  46.7 1.8 %collective-permute-done.17.rest_2_ = bf16[2,3,3,16,128]{4,3,2,1,0:T(8,128)(2,1)S(1)} collective-permute-done((bf16[2,3,3,16,128]{4,3,2,1,0:T(8,128)(2,1)S(1)}, bf16[2,3,3,16,128]{4,3,2,1,0:T(8,128)(2,1)S(1)}, u32[]{:S(2)}, u32[]{:S(2)}) %collective-permute-start.17) | collective-permute-done | bytes 73760 | tf_op jit(solution)/shard_map/ppermute | solution.py:322
  48.4 0.5 collective-permute-done.16.rest_1_
  48.9 1.2 %collective-permute-done.15.rest_0_ = bf16[2,3,3,16,128]{4,3,2,1,0:T(8,128)(2,1)S(1)} collective-permute-done((bf16[2,3,3,16,128]{4,3,2,1,0:T(8,128)(2,1)S(1)}, bf16[2,3,3,16,128]{4,3,2,1,0:T(8,128)(2,1)S(1)}, u32[]{:S(2)}, u32[]{:S(2)}) %collective-permute-start.15) | collective-permute-done | bytes 73760 | tf_op jit(solution)/shard_map/ppermute | solution.py:322
  50.2 1.1 %shard_map.81 = (bf16[4,128,128]{2,1,0:T(8,128)(2,1)}, bf16[4,128,128]{2,1,0:T(8,128)(2,1)}) custom-call(bf16[6,128,384]{2,1,0:T(8,128)(2,1)S(1)} %get-tuple-element.54.hw, bf16[3,3,128,128]{3,2,1,0:T(8,128)(2,1)S(1)} %bitcast.14, bf16[4,128,128]{2,1,0:T(8,128)(2,1)S(1)} %get-tuple-element.55.out), custom_call_target="tpu_custom_call" | custom-call | flops 150994944 | bytes 1277952 | tf_op jit(solution)/shard_map/pallas_call | solution.py:285
  51.8 1.1 %shard_map.84 = (f32[3,3,128,128]{3,2,1,0:T(8,128)}, f32[3,3,128,128]{3,2,1,0:T(8,128)}) custom-call(bf16[2,3,3,64,128]{4,3,2,1,0:T(8,128)(2,1)S(1)} %shard_map.83.mine, bf16[2,3,3,64,128]{4,3,2,1,0:T(8,128)(2,1)S(1)} %collective-permute-done.18.theirs), custom_call_target="tpu_custom_call" | custom-call | flops 73728 | bytes 1769472 | tf_op jit(solution)/shard_map/pallas_call | solution.py:285
  (27 shorter events, 1.5 us)
Async XLA Ops:
  0.6 1.7 %collective-permute-start = (bf16[4,128,128]{2,1,0:T(8,128)(2,1)}, bf16[4,128,128]{2,1,0:T(8,128)(2,1)S(1)}, u32[]{:S(2)}, u32[]{:S(2)}) collective-permute-start(bf16[4,128,128]{2,1,0:T(8,128)(2,1)} %bitcast.18), channel_id=1, source_target_pairs={{0,1},{1,0},{2,3},{3,2},{4,5},{5,4},{6,7},{7,6},{8,9},{9,8},{10,11... | collective-permute-start | bytes 393224 | tf_op jit(solution)/shard_map/ppermute | solution.py:322
  1.1 4.1 %copy-start = (bf16[1,3,3,128,128]{4,3,2,1,0:T(8,128)(2,1)S(1)}, bf16[1,3,3,128,128]{4,3,2,1,0:T(8,128)(2,1)}, u32[]{:S(2)}) copy-start(bf16[1,3,3,128,128]{4,3,2,1,0:T(8,128)(2,1)} %param.7) | copy-start | bytes 884740
  1.2 4.1 %copy-start.1 = (bf16[1,3,3,128,128]{4,3,2,1,0:T(8,128)(2,1)S(1)}, bf16[1,3,3,128,128]{4,3,2,1,0:T(8,128)(2,1)}, u32[]{:S(2)}) copy-start(bf16[1,3,3,128,128]{4,3,2,1,0:T(8,128)(2,1)} %param.6) | copy-start | bytes 884740
  1.2 4.0 %collective-permute-start.2 = (bf16[4,128,128]{2,1,0:T(8,128)(2,1)}, bf16[4,128,128]{2,1,0:T(8,128)(2,1)S(1)}, u32[]{:S(2)}, u32[]{:S(2)}) collective-permute-start(bf16[4,128,128]{2,1,0:T(8,128)(2,1)} %bitcast.15), channel_id=1, source_target_pairs={{0,1},{1,0},{2,3},{3,2},{4,5},{5,4},{6,7},{7,6},{8,9},{9,8},{10,11... | collective-permute-start | bytes 393224 | tf_op jit(solution)/shard_map/ppermute | solution.py:322
  1.3 4.0 %copy-start.3 = (bf16[1,4,128,128]{3,2,1,0:T(8,128)(2,1)S(1)}, bf16[1,4,128,128]{3,2,1,0:T(8,128)(2,1)}, u32[]{:S(2)}) copy-start(bf16[1,4,128,128]{3,2,1,0:T(8,128)(2,1)} %param.4) | copy-start | bytes 393220
  2.3 6.7 %collective-permute-start.1 = (bf16[4,128,128]{2,1,0:T(8,128)(2,1)S(1)}, bf16[4,128,128]{2,1,0:T(8,128)(2,1)S(1)}, u32[]{:S(2)}, u32[]{:S(2)}) collective-permute-start(bf16[4,128,128]{2,1,0:T(8,128)(2,1)S(1)} %collective-permute-done.x_core), channel_id=1, source_target_pairs={{0,2},{1,0},{2,4},{3,1},{4,6},{5,3},{6,8},{7,5},{8,10},{9,7},{10,1... | collective-permute-start | bytes 393224 | tf_op jit(solution)/shard_map/ppermute | solution.py:322
  6.5 9.1 %collective-permute-start.4 = (bf16[4,128,128]{2,1,0:T(8,128)(2,1)S(1)}, bf16[4,128,128]{2,1,0:T(8,128)(2,1)S(1)}, u32[]{:S(2)}, u32[]{:S(2)}) collective-permute-start(bf16[4,128,128]{2,1,0:T(8,128)(2,1)S(1)} %get-tuple-element.44.near_here), channel_id=1, source_target_pairs={{0,16},{1,17},{2,18},{3,19},{4,20},{5,21},{6,22},{7,23},{8,24},{9,... | collective-permute-start | bytes 393224 | tf_op jit(solution)/shard_map/ppermute | solution.py:322
  9.1 6.6 %copy-start.2 = (bf16[1,4,128,128]{3,2,1,0:T(8,128)(2,1)S(1)}, bf16[1,4,128,128]{3,2,1,0:T(8,128)(2,1)}, u32[]{:S(2)}) copy-start(bf16[1,4,128,128]{3,2,1,0:T(8,128)(2,1)} %param.5) | copy-start | bytes 393220
  10.4 5.3 %collective-permute-start.5 = (bf16[4,128,128]{2,1,0:T(8,128)(2,1)S(1)}, bf16[4,128,128]{2,1,0:T(8,128)(2,1)S(1)}, u32[]{:S(2)}, u32[]{:S(2)}) collective-permute-start(bf16[4,128,128]{2,1,0:T(8,128)(2,1)S(1)} %get-tuple-element.45.far_here), channel_id=1, source_target_pairs={{0,16},{1,17},{2,18},{3,19},{4,20},{5,21},{6,22},{7,23},{8,24},{9,... | collective-permute-start | bytes 393224 | tf_op jit(solution)/shard_map/ppermute | solution.py:322
  11.3 4.4 %collective-permute-start.3 = (bf16[2,128,128]{2,1,0:T(8,128)(2,1)S(1)}, bf16[2,128,128]{2,1,0:T(8,128)(2,1)S(1)}, u32[]{:S(2)}, u32[]{:S(2)}) collective-permute-start(bf16[2,128,128]{2,1,0:T(8,128)(2,1)S(1)} %slice_select_fusion), channel_id=1, source_target_pairs={{0,2},{1,0},{2,4},{3,1},{4,6},{5,3},{6,8},{7,5},{8,10},{9,7},{10,1... | collective-permute-start | bytes 196616 | tf_op jit(solution)/shard_map/ppermute | solution.py:322
  15.7 8.6 %collective-permute-start.6 = (bf16[4,128,128]{2,1,0:T(8,128)(2,1)S(1)}, bf16[4,128,128]{2,1,0:T(8,128)(2,1)S(1)}, u32[]{:S(2)}, u32[]{:S(2)}) collective-permute-start(bf16[4,128,128]{2,1,0:T(8,128)(2,1)S(1)} %get-tuple-element.46), channel_id=1, source_target_pairs={{0,16},{1,17},{2,18},{3,19},{4,20},{5,21},{6,22},{7,23},{8,24},{9,... | collective-permute-start | bytes 393224 | tf_op jit(solution)/shard_map/ppermute | solution.py:322
  18.6 5.2 %collective-permute-start.7 = (bf16[2,128,128]{2,1,0:T(8,128)(2,1)S(1)}, bf16[2,128,128]{2,1,0:T(8,128)(2,1)S(1)}, u32[]{:S(2)}, u32[]{:S(2)}) collective-permute-start(bf16[2,128,128]{2,1,0:T(8,128)(2,1)S(1)} %get-tuple-element.47), channel_id=1, source_target_pairs={{0,17},{1,16},{2,19},{3,18},{4,21},{5,20},{6,23},{7,22},{8,25},{9,... | collective-permute-start | bytes 196616 | tf_op jit(solution)/shard_map/ppermute | solution.py:322
  18.6 5.8 %collective-permute-start.8 = (bf16[2,128,128]{2,1,0:T(8,128)(2,1)S(1)}, bf16[2,128,128]{2,1,0:T(8,128)(2,1)S(1)}, u32[]{:S(2)}, u32[]{:S(2)}) collective-permute-start(bf16[2,128,128]{2,1,0:T(8,128)(2,1)S(1)} %get-tuple-element.48), channel_id=1, source_target_pairs={{0,16},{1,18},{2,17},{3,20},{4,19},{5,22},{6,21},{7,24},{8,23},{9,... | collective-permute-start | bytes 196616 | tf_op jit(solution)/shard_map/ppermute | solution.py:322
  26.2 1.4 %collective-permute-start.9 = (bf16[3,3,64,128]{3,2,1,0:T(8,128)(2,1)S(1)}, bf16[3,3,64,128]{3,2,1,0:T(8,128)(2,1)S(1)}, u32[]{:S(2)}, u32[]{:S(2)}) collective-permute-start(bf16[3,3,64,128]{3,2,1,0:T(8,128)(2,1)S(1)} %get-tuple-element.59), channel_id=1, source_target_pairs={{0,1},{1,0},{2,3},{3,2},{4,5},{5,4},{6,7},{7,6},{8,9},{9,8},{10,11... | collective-permute-start | bytes 442376 | tf_op jit(solution)/shard_map/ppermute | solution.py:322
  26.3 1.6 %collective-permute-start.10 = (bf16[3,3,64,128]{3,2,1,0:T(8,128)(2,1)S(1)}, bf16[3,3,64,128]{3,2,1,0:T(8,128)(2,1)S(1)}, u32[]{:S(2)}, u32[]{:S(2)}) collective-permute-start(bf16[3,3,64,128]{3,2,1,0:T(8,128)(2,1)S(1)} %get-tuple-element.61), channel_id=1, source_target_pairs={{0,1},{1,0},{2,3},{3,2},{4,5},{5,4},{6,7},{7,6},{8,9},{9,8},{10,11... | collective-permute-start | bytes 442376 | tf_op jit(solution)/shard_map/ppermute | solution.py:322
  27.9 4.5 %collective-permute-start.11 = (bf16[2,3,3,16,128]{4,3,2,1,0:T(8,128)(2,1)S(1)}, bf16[2,3,3,16,128]{4,3,2,1,0:T(8,128)(2,1)S(1)}, u32[]{:S(2)}, u32[]{:S(2)}) collective-permute-start(bf16[2,3,3,16,128]{4,3,2,1,0:T(8,128)(2,1)S(1)} %get-tuple-element.63), channel_id=1, source_target_pairs={{0,2},{1,5},{2,0},{3,7},{4,6},{5,1},{6,4},{7,3},{8,10},{9,13},{10,... | collective-permute-start | bytes 221192 | tf_op jit(solution)/shard_map/ppermute | solution.py:322
  30.1 4.4 %collective-permute-start.12 = (bf16[2,3,3,16,128]{4,3,2,1,0:T(8,128)(2,1)S(1)}, bf16[2,3,3,16,128]{4,3,2,1,0:T(8,128)(2,1)S(1)}, u32[]{:S(2)}, u32[]{:S(2)}) collective-permute-start(bf16[2,3,3,16,128]{4,3,2,1,0:T(8,128)(2,1)S(1)} %get-tuple-element.64), channel_id=1, source_target_pairs={{0,4},{1,3},{2,6},{3,1},{4,0},{5,7},{6,2},{7,5},{8,12},{9,11},{10,... | collective-permute-start | bytes 221192 | tf_op jit(solution)/shard_map/ppermute | solution.py:322
  31.7 5.3 %collective-permute-start.13 = (bf16[2,3,3,16,128]{4,3,2,1,0:T(8,128)(2,1)S(1)}, bf16[2,3,3,16,128]{4,3,2,1,0:T(8,128)(2,1)S(1)}, u32[]{:S(2)}, u32[]{:S(2)}) collective-permute-start(bf16[2,3,3,16,128]{4,3,2,1,0:T(8,128)(2,1)S(1)} %get-tuple-element.65), channel_id=1, source_target_pairs={{0,6},{1,7},{2,4},{3,5},{4,2},{5,3},{6,0},{7,1},{8,14},{9,15},{10,... | collective-permute-start | bytes 221192 | tf_op jit(solution)/shard_map/ppermute | solution.py:322
  37.0 6.1 %collective-permute-start.14 = (bf16[2,3,3,16,128]{4,3,2,1,0:T(8,128)(2,1)S(1)}, bf16[2,3,3,16,128]{4,3,2,1,0:T(8,128)(2,1)S(1)}, u32[]{:S(2)}, u32[]{:S(2)}) collective-permute-start(bf16[2,3,3,16,128]{4,3,2,1,0:T(8,128)(2,1)S(1)} %add_convert_fusion.1), channel_id=1, source_target_pairs={{0,8},{1,9},{2,10},{3,11},{4,12},{5,13},{6,14},{7,15},{8,0},{9,1},... | collective-permute-start | bytes 221192 | tf_op jit(solution)/shard_map/ppermute | solution.py:322
  43.1 5.3 %collective-permute-start.17 = (bf16[2,3,3,16,128]{4,3,2,1,0:T(8,128)(2,1)S(1)}, bf16[2,3,3,16,128]{4,3,2,1,0:T(8,128)(2,1)S(1)}, u32[]{:S(2)}, u32[]{:S(2)}) collective-permute-start(bf16[2,3,3,16,128]{4,3,2,1,0:T(8,128)(2,1)S(1)} %add_convert_fusion.mine), channel_id=1, source_target_pairs={{0,6},{1,7},{2,4},{3,5},{4,2},{5,3},{6,0},{7,1},{8,14},{9,15},{10,... | collective-permute-start | bytes 221192 | tf_op jit(solution)/shard_map/ppermute | solution.py:322
  43.7 5.1 %collective-permute-start.16 = (bf16[2,3,3,16,128]{4,3,2,1,0:T(8,128)(2,1)S(1)}, bf16[2,3,3,16,128]{4,3,2,1,0:T(8,128)(2,1)S(1)}, u32[]{:S(2)}, u32[]{:S(2)}) collective-permute-start(bf16[2,3,3,16,128]{4,3,2,1,0:T(8,128)(2,1)S(1)} %add_convert_fusion.mine), channel_id=1, source_target_pairs={{0,4},{1,3},{2,6},{3,1},{4,0},{5,7},{6,2},{7,5},{8,12},{9,11},{10,... | collective-permute-start | bytes 221192 | tf_op jit(solution)/shard_map/ppermute | solution.py:322
  45.8 4.4 %collective-permute-start.15 = (bf16[2,3,3,16,128]{4,3,2,1,0:T(8,128)(2,1)S(1)}, bf16[2,3,3,16,128]{4,3,2,1,0:T(8,128)(2,1)S(1)}, u32[]{:S(2)}, u32[]{:S(2)}) collective-permute-start(bf16[2,3,3,16,128]{4,3,2,1,0:T(8,128)(2,1)S(1)} %add_convert_fusion.mine), channel_id=1, source_target_pairs={{0,2},{1,5},{2,0},{3,7},{4,6},{5,1},{6,4},{7,3},{8,10},{9,13},{10,... | collective-permute-start | bytes 221192 | tf_op jit(solution)/shard_map/ppermute | solution.py:322
  50.2 1.6 %collective-permute-start.18 = (bf16[2,3,3,64,128]{4,3,2,1,0:T(8,128)(2,1)S(1)}, bf16[2,3,3,64,128]{4,3,2,1,0:T(8,128)(2,1)S(1)}, u32[]{:S(2)}, u32[]{:S(2)}) collective-permute-start(bf16[2,3,3,64,128]{4,3,2,1,0:T(8,128)(2,1)S(1)} %shard_map.83.mine), channel_id=1, source_target_pairs={{0,1},{1,0},{2,3},{3,2},{4,5},{5,4},{6,7},{7,6},{8,9},{9,8},{10,11... | collective-permute-start | bytes 884744 | tf_op jit(solution)/shard_map/ppermute | solution.py:322

commit v10 on v9

--- a/solution.py
+++ b/solution.py
@@ -13,7 +13,7 @@
 TAPS = [(ty, tx) for ty in range(3) for tx in range(3)]
 
 
-TURNS = ((1, 2), (2, 1), (3, 3))
+TURNS = ((3, 3), (1, 2), (2, 1))
 
 
 def silu(values):
@@ -103,14 +103,14 @@
             skip[i] = silu(pre[i]).astype(BF16)
 
 
-def far_kernel(segments, strips, xa, ha, x_far, main, second, first, pre, hid, skip, xb, hb):
+def far_kernel(segments, strips, xa, ha, from_far, main, second, first, pre, hid, skip, xb, hb):
     encoder, row, even = here(segments)
-    own = x_far.shape[0]
+    own = first.shape[0]
     near = ha.shape[0]
-    columns, channels = x_far.shape[1:]
+    channels = from_far.shape[2]
     far_in = jnp.where(even, row > 0, row < strips - 1)
     for i in range(own):
-        place(xb, jnp.where(even, 0, 2) + i, masked(x_far[i].astype(F32), far_in))
+        place(xb, jnp.where(even, 0, 2) + i, masked(from_far[i].astype(F32), far_in))
     for i in range(2):
         xb[jnp.where(even, own, 0) + i] = xa[jnp.where(even, 0, 2 * own - 2) + i]
     first[...] = conv(xb, 0, own, main)
@@ -153,7 +153,7 @@
 
 
 def middle_kernel(
-    segments, strips, near_here, far_here, near, far, near_first, far_first, g, g_core, g_other, second, out, gw, back, edge_core, edge_other, yw
+    segments, strips, near_here, far_here, near, far, near_first, far_first, g, g_core, from_far, second, out, gw, back, edge_core, edge_other, yw
 ):
     encoder, row, even = here(segments)
     own = g.shape[0]
@@ -173,9 +173,9 @@
         for i in range(own + 2):
             pre = skip_pre[i] + joined_first(even, near_first, far_first, i)
             if i == 0:
-                upstream = jnp.where(even, g_other[1].astype(F32), g_core[own - 1].astype(F32))
+                upstream = jnp.where(even, from_far[own + 1].astype(F32), g_core[own - 1].astype(F32))
             elif i == own + 1:
-                upstream = jnp.where(even, g_core[0].astype(F32), g_other[0].astype(F32))
+                upstream = jnp.where(even, g_core[0].astype(F32), from_far[own].astype(F32))
             else:
                 upstream = g[i - 1].astype(F32)
                 out[i - 1] = silu(pre).astype(BF16)
@@ -196,7 +196,7 @@
 
 
 def second_kernel(
-    segments, strips, g, g_core, g_other, back, back_core, back_other, near_pre, far_pre, hid, near, far, gw, kept, sent, ew
+    segments, strips, g, g_core, from_far, back, back_core, back_other, near_pre, far_pre, hid, near, far, gw, kept, sent, ew
 ):
     encoder, row, even = here(segments)
     own = g.shape[0]
@@ -205,11 +205,11 @@
     def _():
         for i in range(own + 4):
             if i < 2:
-                upstream = jnp.where(even, g_other[i].astype(F32), g_core[own - 2 + i].astype(F32))
+                upstream = jnp.where(even, from_far[own + i].astype(F32), g_core[own - 2 + i].astype(F32))
                 returned = jnp.where(even, back_other[i].astype(F32), back_core[i].astype(F32))
             elif i >= own + 2:
                 k = i - own - 2
-                upstream = jnp.where(even, g_core[k].astype(F32), g_other[k].astype(F32))
+                upstream = jnp.where(even, g_core[k].astype(F32), from_far[own + k].astype(F32))
                 returned = jnp.where(even, back_core[k].astype(F32), back_other[k].astype(F32))
             else:
                 upstream = g[i - 2].astype(F32)
@@ -335,7 +335,8 @@
     x_core = swap(x, False, core)
     g_core = swap(g, False, core)
     x_core, token = lax.optimization_barrier((x_core, token))
-    x_far = swap(x_core, False, far)
+    edge = jnp.where(even, g_core[own - 2 :], g_core[:2])
+    from_far = swap(jnp.concatenate([x_core, edge]), False, far)
     xa, near_first, ha, near_pre, near_here = call(
         functools.partial(near_kernel, segments),
         [wide_out(2 * own), like(2 * own - 2, F32), wide_out(2 * own - 2), like(2 * own - 4, F32), like(2 * own - 4, BF16)],
@@ -343,14 +344,12 @@
         (token, x, x_core, main, second),
         work * (4 * own - 6),
     )
-    near_here, edge = lax.optimization_barrier((near_here, jnp.where(even, g_core[own - 2 :], g_core[:2])))
     near_there = swap(near_here, True, same)
-    g_other = swap(edge, False, far)
     far_first, far_pre, hid, far_here = call(
         functools.partial(far_kernel, segments, strips),
         [like(own, F32), like(own, F32), like(own, BF16), like(own, BF16)],
         [wide(own + 2), wide(own + 2)],
-        (xa, ha, x_far, main, second),
+        (xa, ha, from_far, main, second),
         work * 2 * own,
     )
     far_there = swap(far_here, True, same)
@@ -358,7 +357,7 @@
         functools.partial(middle_kernel, segments, strips),
         [like(own, BF16), wide_out(own + 2), like(own, BF16), like(2, BF16), like(2, BF16)],
         [wide(own + 4)],
-        (near_here, far_here, near_there, far_there, near_first, far_first, g, g_core, g_other, second),
+        (near_here, far_here, near_there, far_there, near_first, far_first, g, g_core, from_far, second),
         work * (2 * own + 2),
     )
     back_own = swap(back, True, same)
@@ -371,7 +370,7 @@
         functools.partial(second_kernel, segments, strips),
         terms + [wide_out(own + 4)],
         [],
-        (g, g_core, g_other, back_own, back_core, back_other, near_pre, far_pre, hid, near_there, far_there, gw),
+        (g, g_core, from_far, back_own, back_core, back_other, near_pre, far_pre, hid, near_there, far_there, gw),
         work * own,
     )
     kept1, sent1, hw = call(

time: 53 us -> 53.4 us (level)
  waiting for transfers between devices: 23.5 us -> 26.6 us
  starting transfers between devices: 21.8 us -> 19 us
    ppermute x19 -> x18, waiting for transfers between devices: 23.5 us -> 26.6 us  [swap(): return lax.ppermute(array, ('segment', 'rows'), pairs)]
    ppermute x19 -> x18, starting transfers between devices: 21.8 us -> 19 us  [swap(): return lax.ppermute(array, ('segment', 'rows'), pairs)]
  transfers between devices with their start and end apart: 19 -> 18, of which waited for: 15 -> 16; matrix products, arithmetic and copies ran while one was open for 0% -> 0% of each run, Pallas kernels for 7% -> 7%
where the time goes in v10:
time: 53.4 us; the launch traced here: 53.2 us
  waiting for transfers between devices  26.6 us (50%)
  starting transfers between devices  19 us (36%)
  Pallas kernels  6.76 us (13%)
  between operations  0.73 us (1%)
    ppermute x18, waiting for transfers between devices, swap(): return lax.ppermute(array, ('segment', 'rows'), pairs)  26.6 us
    ppermute x18, starting transfers between devices, swap(): return lax.ppermute(array, ('segment', 'rows'), pairs)  19 us
    pallas_call x10, Pallas kernels, call(): pl.pallas_call(kernel, out_shape=outs, in_specs=[pl.BlockSpec(memory_spac...  6.76 us
  transfers between devices with their start and end apart: 18, of which 16 were waited for; matrix products, arithmetic and copies ran while one was open for 0% of the time, Pallas kernels for 7%

profile of v10, /device:TPU:0, one launch (start us, length us, event | category | flops | bytes accessed | tf_op | source)
XLA Modules:
  0.0 53.2 jit_solution(13331534252764560249)
XLA Ops:
  0.6 0.5 collective-permute-start
  1.2 1.1 %collective-permute-done.x_core = bf16[4,128,128]{2,1,0:T(8,128)(2,1)S(1)} collective-permute-done((bf16[4,128,128]{2,1,0:T(8,128)(2,1)}, bf16[4,128,128]{2,1,0:T(8,128)(2,1)S(1)}, u32[]{:S(2)}, u32[]{:S(2)}) %collective-permute-start) | collective-permute-done | bytes 131104 | tf_op jit(solution)/shard_map/ppermute | solution.py:322
  2.7 2.7 %collective-permute-start.2 = (bf16[6,128,128]{2,1,0:T(8,128)(2,1)S(1)}, bf16[6,128,128]{2,1,0:T(8,128)(2,1)S(1)}, u32[]{:S(2)}, u32[]{:S(2)}) collective-permute-start(bf16[6,128,128]{2,1,0:T(8,128)(2,1)S(1)} %pad_maximum_fusion), channel_id=1, source_target_pairs={{0,2},{1,0},{2,4},{3,1},{4,6},{5,3},{6,8},{7,5},{8,10},{9,7},{10,1... | collective-permute-start | bytes 589832 | tf_op jit(solution)/shard_map/ppermute | solution.py:322
  5.5 1.3 %shard_map.76 = (bf16[8,128,384]{2,1,0:T(8,128)(2,1)S(1)}, f32[6,128,128]{2,1,0:T(8,128)S(1)}, bf16[6,128,384]{2,1,0:T(8,128)(2,1)S(1)}, f32[4,128,128]{2,1,0:T(8,128)S(1)}, bf16[4,128,128]{2,1,0:T(8,128)(2,1)S(1)}) custom-call(f32[8,128]{1,0:T(8,128)S(1)} %shard_map.75.token, bf16[4,128,128]{2,1,0:T(8,128)(2,1)S(1)} %bitcast.19, ...), custom_call_target="tpu_custom_call" | custom-call | flops 377487360 | bytes 3018752 | tf_op jit(solution)/shard_map/pallas_call | solution.py:285
  6.8 1.1 %collective-permute-start.3 = (bf16[4,128,128]{2,1,0:T(8,128)(2,1)S(1)}, bf16[4,128,128]{2,1,0:T(8,128)(2,1)S(1)}, u32[]{:S(2)}, u32[]{:S(2)}) collective-permute-start(bf16[4,128,128]{2,1,0:T(8,128)(2,1)S(1)} %get-tuple-element.40.near_here), channel_id=1, source_target_pairs={{0,16},{1,17},{2,18},{3,19},{4,20},{5,21},{6,22},{7,23},{8,24},{9,... | collective-permute-start | bytes 393224 | tf_op jit(solution)/shard_map/ppermute | solution.py:322
  7.8 2.9 %collective-permute-done.2.from_far = bf16[6,128,128]{2,1,0:T(8,128)(2,1)S(1)} collective-permute-done((bf16[6,128,128]{2,1,0:T(8,128)(2,1)S(1)}, bf16[6,128,128]{2,1,0:T(8,128)(2,1)S(1)}, u32[]{:S(2)}, u32[]{:S(2)}) %collective-permute-start.2) | collective-permute-done | bytes 196640 | tf_op jit(solution)/shard_map/ppermute | solution.py:322
  10.8 1.3 %shard_map.77 = (f32[4,128,128]{2,1,0:T(8,128)S(1)}, f32[4,128,128]{2,1,0:T(8,128)S(1)}, bf16[4,128,128]{2,1,0:T(8,128)(2,1)S(1)}, bf16[4,128,128]{2,1,0:T(8,128)(2,1)S(1)}) custom-call(bf16[8,128,384]{2,1,0:T(8,128)(2,1)S(1)} %get-tuple-element.37.xa, bf16[6,128,384]{2,1,0:T(8,128)(2,1)S(1)} %get-tuple-element.38.ha, ...), custom_call_target="tpu_custom_call" | custom-call | flops 301989888 | bytes 2949120 | tf_op jit(solution)/shard_map/pallas_call | solution.py:285
  12.0 0.9 %collective-permute-start.4 = (bf16[4,128,128]{2,1,0:T(8,128)(2,1)S(1)}, bf16[4,128,128]{2,1,0:T(8,128)(2,1)S(1)}, u32[]{:S(2)}, u32[]{:S(2)}) collective-permute-start(bf16[4,128,128]{2,1,0:T(8,128)(2,1)S(1)} %get-tuple-element.41.far_here), channel_id=1, source_target_pairs={{0,16},{1,17},{2,18},{3,19},{4,20},{5,21},{6,22},{7,23},{8,24},{9,... | collective-permute-start | bytes 393224 | tf_op jit(solution)/shard_map/ppermute | solution.py:322
  13.0 4.1 %collective-permute-done.4.far = bf16[4,128,128]{2,1,0:T(8,128)(2,1)S(1)} collective-permute-done((bf16[4,128,128]{2,1,0:T(8,128)(2,1)S(1)}, bf16[4,128,128]{2,1,0:T(8,128)(2,1)S(1)}, u32[]{:S(2)}, u32[]{:S(2)}) %collective-permute-start.4) | collective-permute-done | bytes 131104 | tf_op jit(solution)/shard_map/ppermute | solution.py:322
  17.1 2.5 %collective-permute-start.5 = (bf16[4,128,128]{2,1,0:T(8,128)(2,1)S(1)}, bf16[4,128,128]{2,1,0:T(8,128)(2,1)S(1)}, u32[]{:S(2)}, u32[]{:S(2)}) collective-permute-start(bf16[4,128,128]{2,1,0:T(8,128)(2,1)S(1)} %get-tuple-element.42), channel_id=1, source_target_pairs={{0,16},{1,17},{2,18},{3,19},{4,20},{5,21},{6,22},{7,23},{8,24},{9,... | collective-permute-start | bytes 393224 | tf_op jit(solution)/shard_map/ppermute | solution.py:322
  19.8 5.0 %collective-permute-done.6.back_core = bf16[2,128,128]{2,1,0:T(8,128)(2,1)S(1)} collective-permute-done((bf16[2,128,128]{2,1,0:T(8,128)(2,1)S(1)}, bf16[2,128,128]{2,1,0:T(8,128)(2,1)S(1)}, u32[]{:S(2)}, u32[]{:S(2)}) %collective-permute-start.6) | collective-permute-done | bytes 65568 | tf_op jit(solution)/shard_map/ppermute | solution.py:322
  24.8 0.6 %collective-permute-done.7.back_other = bf16[2,128,128]{2,1,0:T(8,128)(2,1)S(1)} collective-permute-done((bf16[2,128,128]{2,1,0:T(8,128)(2,1)S(1)}, bf16[2,128,128]{2,1,0:T(8,128)(2,1)S(1)}, u32[]{:S(2)}, u32[]{:S(2)}) %collective-permute-start.7) | collective-permute-done | bytes 65568 | tf_op jit(solution)/shard_map/ppermute | solution.py:322
  25.4 0.7 %shard_map.79 = (f32[3,3,64,128]{3,2,1,0:T(8,128)S(1)}, bf16[3,3,64,128]{3,2,1,0:T(8,128)(2,1)S(1)}, bf16[8,128,384]{2,1,0:T(8,128)(2,1)S(1)}) custom-call(bf16[4,128,128]{2,1,0:T(8,128)(2,1)S(1)} %bitcast.17, bf16[4,128,128]{2,1,0:T(8,128)(2,1)S(1)} %collective-permute-done.1.g_core, bf16[6,128,128]{2,1,0:T(8,128)(2,1)S(1)} %collective-permute-done.2.from_far, ...), custom_call_target="tpu_custom_call" | custom-call | flops 150994944 | bytes 3457024 | tf_op jit(solution)/shard_map/pallas_call | solution.py:285
  26.1 1.1 %shard_map.80 = (f32[3,3,64,128]{3,2,1,0:T(8,128)S(1)}, bf16[3,3,64,128]{3,2,1,0:T(8,128)(2,1)S(1)}, bf16[6,128,384]{2,1,0:T(8,128)(2,1)S(1)}) custom-call(bf16[4,128,128]{2,1,0:T(8,128)(2,1)S(1)} %bitcast.20, f32[6,128,128]{2,1,0:T(8,128)S(1)} %get-tuple-element.36.near_first, f32[4,128,128]{2,1,0:T(8,128)S(1)} %get-tuple-element.39.far_first, ...), custom_call_target="tpu_custom_call" | custom-call | flops 377487360 | bytes 3489792 | tf_op jit(solution)/shard_map/pallas_call | solution.py:285
  27.4 0.5 collective-permute-start.9
  27.9 0.9 %collective-permute-done.8.got1 = bf16[3,3,64,128]{3,2,1,0:T(8,128)(2,1)S(1)} collective-permute-done((bf16[3,3,64,128]{3,2,1,0:T(8,128)(2,1)S(1)}, bf16[3,3,64,128]{3,2,1,0:T(8,128)(2,1)S(1)}, u32[]{:S(2)}, u32[]{:S(2)}) %collective-permute-start.8) | collective-permute-done | bytes 147488 | tf_op jit(solution)/shard_map/ppermute | solution.py:322
  29.0 3.3 %collective-permute-start.10 = (bf16[2,3,3,16,128]{4,3,2,1,0:T(8,128)(2,1)S(1)}, bf16[2,3,3,16,128]{4,3,2,1,0:T(8,128)(2,1)S(1)}, u32[]{:S(2)}, u32[]{:S(2)}) collective-permute-start(bf16[2,3,3,16,128]{4,3,2,1,0:T(8,128)(2,1)S(1)} %get-tuple-element.59), channel_id=1, source_target_pairs={{0,6},{1,7},{2,4},{3,5},{4,2},{5,3},{6,0},{7,1},{8,14},{9,15},{10,... | collective-permute-start | bytes 221192 | tf_op jit(solution)/shard_map/ppermute | solution.py:322
  32.3 0.8 %collective-permute-start.11 = (bf16[2,3,3,16,128]{4,3,2,1,0:T(8,128)(2,1)S(1)}, bf16[2,3,3,16,128]{4,3,2,1,0:T(8,128)(2,1)S(1)}, u32[]{:S(2)}, u32[]{:S(2)}) collective-permute-start(bf16[2,3,3,16,128]{4,3,2,1,0:T(8,128)(2,1)S(1)} %get-tuple-element.60), channel_id=1, source_target_pairs={{0,2},{1,5},{2,0},{3,7},{4,6},{5,1},{6,4},{7,3},{8,10},{9,13},{10,... | collective-permute-start | bytes 221192 | tf_op jit(solution)/shard_map/ppermute | solution.py:322
  33.1 1.8 %collective-permute-done.10 = bf16[2,3,3,16,128]{4,3,2,1,0:T(8,128)(2,1)S(1)} collective-permute-done((bf16[2,3,3,16,128]{4,3,2,1,0:T(8,128)(2,1)S(1)}, bf16[2,3,3,16,128]{4,3,2,1,0:T(8,128)(2,1)S(1)}, u32[]{:S(2)}, u32[]{:S(2)}) %collective-permute-start.10) | collective-permute-done | bytes 73760 | tf_op jit(solution)/shard_map/ppermute | solution.py:322
  34.9 1.7 %collective-permute-done.11 = bf16[2,3,3,16,128]{4,3,2,1,0:T(8,128)(2,1)S(1)} collective-permute-done((bf16[2,3,3,16,128]{4,3,2,1,0:T(8,128)(2,1)S(1)}, bf16[2,3,3,16,128]{4,3,2,1,0:T(8,128)(2,1)S(1)}, u32[]{:S(2)}, u32[]{:S(2)}) %collective-permute-start.11) | collective-permute-done | bytes 73760 | tf_op jit(solution)/shard_map/ppermute | solution.py:322
  36.6 0.8 %collective-permute-done.12 = bf16[2,3,3,16,128]{4,3,2,1,0:T(8,128)(2,1)S(1)} collective-permute-done((bf16[2,3,3,16,128]{4,3,2,1,0:T(8,128)(2,1)S(1)}, bf16[2,3,3,16,128]{4,3,2,1,0:T(8,128)(2,1)S(1)}, u32[]{:S(2)}, u32[]{:S(2)}) %collective-permute-start.12) | collective-permute-done | bytes 73760 | tf_op jit(solution)/shard_map/ppermute | solution.py:322
  37.5 2.7 %collective-permute-start.13 = (bf16[2,3,3,16,128]{4,3,2,1,0:T(8,128)(2,1)S(1)}, bf16[2,3,3,16,128]{4,3,2,1,0:T(8,128)(2,1)S(1)}, u32[]{:S(2)}, u32[]{:S(2)}) collective-permute-start(bf16[2,3,3,16,128]{4,3,2,1,0:T(8,128)(2,1)S(1)} %add_convert_fusion.1), channel_id=1, source_target_pairs={{0,8},{1,9},{2,10},{3,11},{4,12},{5,13},{6,14},{7,15},{8,0},{9,1},... | collective-permute-start | bytes 221192 | tf_op jit(solution)/shard_map/ppermute | solution.py:322
  40.2 3.9 %collective-permute-done.13 = bf16[2,3,3,16,128]{4,3,2,1,0:T(8,128)(2,1)S(1)} collective-permute-done((bf16[2,3,3,16,128]{4,3,2,1,0:T(8,128)(2,1)S(1)}, bf16[2,3,3,16,128]{4,3,2,1,0:T(8,128)(2,1)S(1)}, u32[]{:S(2)}, u32[]{:S(2)}) %collective-permute-start.13) | collective-permute-done | bytes 73760 | tf_op jit(solution)/shard_map/ppermute | solution.py:322
  44.1 0.6 %collective-permute-start.16 = (bf16[2,3,3,16,128]{4,3,2,1,0:T(8,128)(2,1)S(1)}, bf16[2,3,3,16,128]{4,3,2,1,0:T(8,128)(2,1)S(1)}, u32[]{:S(2)}, u32[]{:S(2)}) collective-permute-start(bf16[2,3,3,16,128]{4,3,2,1,0:T(8,128)(2,1)S(1)} %add_convert_fusion.mine), channel_id=1, source_target_pairs={{0,4},{1,3},{2,6},{3,1},{4,0},{5,7},{6,2},{7,5},{8,12},{9,11},{10,... | collective-permute-start | bytes 221192 | tf_op jit(solution)/shard_map/ppermute | solution.py:322
  44.7 0.5 collective-permute-start.15
  45.2 2.4 %collective-permute-start.14 = (bf16[2,3,3,16,128]{4,3,2,1,0:T(8,128)(2,1)S(1)}, bf16[2,3,3,16,128]{4,3,2,1,0:T(8,128)(2,1)S(1)}, u32[]{:S(2)}, u32[]{:S(2)}) collective-permute-start(bf16[2,3,3,16,128]{4,3,2,1,0:T(8,128)(2,1)S(1)} %add_convert_fusion.mine), channel_id=1, source_target_pairs={{0,6},{1,7},{2,4},{3,5},{4,2},{5,3},{6,0},{7,1},{8,14},{9,15},{10,... | collective-permute-start | bytes 221192 | tf_op jit(solution)/shard_map/ppermute | solution.py:322
  47.6 1.4 %collective-permute-done.16.rest_2_ = bf16[2,3,3,16,128]{4,3,2,1,0:T(8,128)(2,1)S(1)} collective-permute-done((bf16[2,3,3,16,128]{4,3,2,1,0:T(8,128)(2,1)S(1)}, bf16[2,3,3,16,128]{4,3,2,1,0:T(8,128)(2,1)S(1)}, u32[]{:S(2)}, u32[]{:S(2)}) %collective-permute-start.16) | collective-permute-done | bytes 73760 | tf_op jit(solution)/shard_map/ppermute | solution.py:322
  49.0 0.4 collective-permute-done.15.rest_1_
  49.4 1.0 %collective-permute-done.14.rest_0_ = bf16[2,3,3,16,128]{4,3,2,1,0:T(8,128)(2,1)S(1)} collective-permute-done((bf16[2,3,3,16,128]{4,3,2,1,0:T(8,128)(2,1)S(1)}, bf16[2,3,3,16,128]{4,3,2,1,0:T(8,128)(2,1)S(1)}, u32[]{:S(2)}, u32[]{:S(2)}) %collective-permute-start.14) | collective-permute-done | bytes 73760 | tf_op jit(solution)/shard_map/ppermute | solution.py:322
  50.6 1.1 %shard_map.81 = (bf16[4,128,128]{2,1,0:T(8,128)(2,1)}, bf16[4,128,128]{2,1,0:T(8,128)(2,1)}) custom-call(bf16[6,128,384]{2,1,0:T(8,128)(2,1)S(1)} %get-tuple-element.50.hw, bf16[3,3,128,128]{3,2,1,0:T(8,128)(2,1)S(1)} %bitcast.14, bf16[4,128,128]{2,1,0:T(8,128)(2,1)S(1)} %get-tuple-element.51.out), custom_call_target="tpu_custom_call" | custom-call | flops 150994944 | bytes 1277952 | tf_op jit(solution)/shard_map/pallas_call | solution.py:285
  51.7 0.4 collective-permute-done.17.theirs
  52.1 1.1 %shard_map.84 = (f32[3,3,128,128]{3,2,1,0:T(8,128)}, f32[3,3,128,128]{3,2,1,0:T(8,128)}) custom-call(bf16[2,3,3,64,128]{4,3,2,1,0:T(8,128)(2,1)S(1)} %shard_map.83.mine, bf16[2,3,3,64,128]{4,3,2,1,0:T(8,128)(2,1)S(1)} %collective-permute-done.17.theirs), custom_call_target="tpu_custom_call" | custom-call | flops 73728 | bytes 1769472 | tf_op jit(solution)/shard_map/pallas_call | solution.py:285
  (26 shorter events, 1.2 us)
Async XLA Ops:
  0.6 1.7 %collective-permute-start = (bf16[4,128,128]{2,1,0:T(8,128)(2,1)}, bf16[4,128,128]{2,1,0:T(8,128)(2,1)S(1)}, u32[]{:S(2)}, u32[]{:S(2)}) collective-permute-start(bf16[4,128,128]{2,1,0:T(8,128)(2,1)} %bitcast.18), channel_id=1, source_target_pairs={{0,1},{1,0},{2,3},{3,2},{4,5},{5,4},{6,7},{7,6},{8,9},{9,8},{10,11... | collective-permute-start | bytes 393224 | tf_op jit(solution)/shard_map/ppermute | solution.py:322
  1.1 1.6 %collective-permute-start.1 = (bf16[4,128,128]{2,1,0:T(8,128)(2,1)}, bf16[4,128,128]{2,1,0:T(8,128)(2,1)S(1)}, u32[]{:S(2)}, u32[]{:S(2)}) collective-permute-start(bf16[4,128,128]{2,1,0:T(8,128)(2,1)} %bitcast.15), channel_id=1, source_target_pairs={{0,1},{1,0},{2,3},{3,2},{4,5},{5,4},{6,7},{7,6},{8,9},{9,8},{10,11... | collective-permute-start | bytes 393224 | tf_op jit(solution)/shard_map/ppermute | solution.py:322
  1.2 4.3 %copy-start.3 = (bf16[1,4,128,128]{3,2,1,0:T(8,128)(2,1)S(1)}, bf16[1,4,128,128]{3,2,1,0:T(8,128)(2,1)}, u32[]{:S(2)}) copy-start(bf16[1,4,128,128]{3,2,1,0:T(8,128)(2,1)} %param.4) | copy-start | bytes 393220
  1.2 4.3 %copy-start = (bf16[1,3,3,128,128]{4,3,2,1,0:T(8,128)(2,1)S(1)}, bf16[1,3,3,128,128]{4,3,2,1,0:T(8,128)(2,1)}, u32[]{:S(2)}) copy-start(bf16[1,3,3,128,128]{4,3,2,1,0:T(8,128)(2,1)} %param.7) | copy-start | bytes 884740
  1.2 4.3 %copy-start.1 = (bf16[1,3,3,128,128]{4,3,2,1,0:T(8,128)(2,1)S(1)}, bf16[1,3,3,128,128]{4,3,2,1,0:T(8,128)(2,1)}, u32[]{:S(2)}) copy-start(bf16[1,3,3,128,128]{4,3,2,1,0:T(8,128)(2,1)} %param.6) | copy-start | bytes 884740
  2.7 8.0 %collective-permute-start.2 = (bf16[6,128,128]{2,1,0:T(8,128)(2,1)S(1)}, bf16[6,128,128]{2,1,0:T(8,128)(2,1)S(1)}, u32[]{:S(2)}, u32[]{:S(2)}) collective-permute-start(bf16[6,128,128]{2,1,0:T(8,128)(2,1)S(1)} %pad_maximum_fusion), channel_id=1, source_target_pairs={{0,2},{1,0},{2,4},{3,1},{4,6},{5,3},{6,8},{7,5},{8,10},{9,7},{10,1... | collective-permute-start | bytes 589832 | tf_op jit(solution)/shard_map/ppermute | solution.py:322
  6.8 6.2 %collective-permute-start.3 = (bf16[4,128,128]{2,1,0:T(8,128)(2,1)S(1)}, bf16[4,128,128]{2,1,0:T(8,128)(2,1)S(1)}, u32[]{:S(2)}, u32[]{:S(2)}) collective-permute-start(bf16[4,128,128]{2,1,0:T(8,128)(2,1)S(1)} %get-tuple-element.40.near_here), channel_id=1, source_target_pairs={{0,16},{1,17},{2,18},{3,19},{4,20},{5,21},{6,22},{7,23},{8,24},{9,... | collective-permute-start | bytes 393224 | tf_op jit(solution)/shard_map/ppermute | solution.py:322
  10.8 6.3 %copy-start.2 = (bf16[1,4,128,128]{3,2,1,0:T(8,128)(2,1)S(1)}, bf16[1,4,128,128]{3,2,1,0:T(8,128)(2,1)}, u32[]{:S(2)}) copy-start(bf16[1,4,128,128]{3,2,1,0:T(8,128)(2,1)} %param.5) | copy-start | bytes 393220
  12.0 5.0 %collective-permute-start.4 = (bf16[4,128,128]{2,1,0:T(8,128)(2,1)S(1)}, bf16[4,128,128]{2,1,0:T(8,128)(2,1)S(1)}, u32[]{:S(2)}, u32[]{:S(2)}) collective-permute-start(bf16[4,128,128]{2,1,0:T(8,128)(2,1)S(1)} %get-tuple-element.41.far_here), channel_id=1, source_target_pairs={{0,16},{1,17},{2,18},{3,19},{4,20},{5,21},{6,22},{7,23},{8,24},{9,... | collective-permute-start | bytes 393224 | tf_op jit(solution)/shard_map/ppermute | solution.py:322
  17.1 8.3 %collective-permute-start.5 = (bf16[4,128,128]{2,1,0:T(8,128)(2,1)S(1)}, bf16[4,128,128]{2,1,0:T(8,128)(2,1)S(1)}, u32[]{:S(2)}, u32[]{:S(2)}) collective-permute-start(bf16[4,128,128]{2,1,0:T(8,128)(2,1)S(1)} %get-tuple-element.42), channel_id=1, source_target_pairs={{0,16},{1,17},{2,18},{3,19},{4,20},{5,21},{6,22},{7,23},{8,24},{9,... | collective-permute-start | bytes 393224 | tf_op jit(solution)/shard_map/ppermute | solution.py:322
  19.6 5.2 %collective-permute-start.6 = (bf16[2,128,128]{2,1,0:T(8,128)(2,1)S(1)}, bf16[2,128,128]{2,1,0:T(8,128)(2,1)S(1)}, u32[]{:S(2)}, u32[]{:S(2)}) collective-permute-start(bf16[2,128,128]{2,1,0:T(8,128)(2,1)S(1)} %get-tuple-element.43), channel_id=1, source_target_pairs={{0,17},{1,16},{2,19},{3,18},{4,21},{5,20},{6,23},{7,22},{8,25},{9,... | collective-permute-start | bytes 196616 | tf_op jit(solution)/shard_map/ppermute | solution.py:322
  19.6 5.8 %collective-permute-start.7 = (bf16[2,128,128]{2,1,0:T(8,128)(2,1)S(1)}, bf16[2,128,128]{2,1,0:T(8,128)(2,1)S(1)}, u32[]{:S(2)}, u32[]{:S(2)}) collective-permute-start(bf16[2,128,128]{2,1,0:T(8,128)(2,1)S(1)} %get-tuple-element.44), channel_id=1, source_target_pairs={{0,16},{1,18},{2,17},{3,20},{4,19},{5,22},{6,21},{7,24},{8,23},{9,... | collective-permute-start | bytes 196616 | tf_op jit(solution)/shard_map/ppermute | solution.py:322
  27.3 1.4 %collective-permute-start.8 = (bf16[3,3,64,128]{3,2,1,0:T(8,128)(2,1)S(1)}, bf16[3,3,64,128]{3,2,1,0:T(8,128)(2,1)S(1)}, u32[]{:S(2)}, u32[]{:S(2)}) collective-permute-start(bf16[3,3,64,128]{3,2,1,0:T(8,128)(2,1)S(1)} %get-tuple-element.55), channel_id=1, source_target_pairs={{0,1},{1,0},{2,3},{3,2},{4,5},{5,4},{6,7},{7,6},{8,9},{9,8},{10,11... | collective-permute-start | bytes 442376 | tf_op jit(solution)/shard_map/ppermute | solution.py:322
  27.4 1.6 %collective-permute-start.9 = (bf16[3,3,64,128]{3,2,1,0:T(8,128)(2,1)S(1)}, bf16[3,3,64,128]{3,2,1,0:T(8,128)(2,1)S(1)}, u32[]{:S(2)}, u32[]{:S(2)}) collective-permute-start(bf16[3,3,64,128]{3,2,1,0:T(8,128)(2,1)S(1)} %get-tuple-element.57), channel_id=1, source_target_pairs={{0,1},{1,0},{2,3},{3,2},{4,5},{5,4},{6,7},{7,6},{8,9},{9,8},{10,11... | collective-permute-start | bytes 442376 | tf_op jit(solution)/shard_map/ppermute | solution.py:322
  29.0 5.9 %collective-permute-start.10 = (bf16[2,3,3,16,128]{4,3,2,1,0:T(8,128)(2,1)S(1)}, bf16[2,3,3,16,128]{4,3,2,1,0:T(8,128)(2,1)S(1)}, u32[]{:S(2)}, u32[]{:S(2)}) collective-permute-start(bf16[2,3,3,16,128]{4,3,2,1,0:T(8,128)(2,1)S(1)} %get-tuple-element.59), channel_id=1, source_target_pairs={{0,6},{1,7},{2,4},{3,5},{4,2},{5,3},{6,0},{7,1},{8,14},{9,15},{10,... | collective-permute-start | bytes 221192 | tf_op jit(solution)/shard_map/ppermute | solution.py:322
  32.3 4.4 %collective-permute-start.11 = (bf16[2,3,3,16,128]{4,3,2,1,0:T(8,128)(2,1)S(1)}, bf16[2,3,3,16,128]{4,3,2,1,0:T(8,128)(2,1)S(1)}, u32[]{:S(2)}, u32[]{:S(2)}) collective-permute-start(bf16[2,3,3,16,128]{4,3,2,1,0:T(8,128)(2,1)S(1)} %get-tuple-element.60), channel_id=1, source_target_pairs={{0,2},{1,5},{2,0},{3,7},{4,6},{5,1},{6,4},{7,3},{8,10},{9,13},{10,... | collective-permute-start | bytes 221192 | tf_op jit(solution)/shard_map/ppermute | solution.py:322
  33.1 4.4 %collective-permute-start.12 = (bf16[2,3,3,16,128]{4,3,2,1,0:T(8,128)(2,1)S(1)}, bf16[2,3,3,16,128]{4,3,2,1,0:T(8,128)(2,1)S(1)}, u32[]{:S(2)}, u32[]{:S(2)}) collective-permute-start(bf16[2,3,3,16,128]{4,3,2,1,0:T(8,128)(2,1)S(1)} %get-tuple-element.61), channel_id=1, source_target_pairs={{0,4},{1,3},{2,6},{3,1},{4,0},{5,7},{6,2},{7,5},{8,12},{9,11},{10,... | collective-permute-start | bytes 221192 | tf_op jit(solution)/shard_map/ppermute | solution.py:322
  37.5 6.5 %collective-permute-start.13 = (bf16[2,3,3,16,128]{4,3,2,1,0:T(8,128)(2,1)S(1)}, bf16[2,3,3,16,128]{4,3,2,1,0:T(8,128)(2,1)S(1)}, u32[]{:S(2)}, u32[]{:S(2)}) collective-permute-start(bf16[2,3,3,16,128]{4,3,2,1,0:T(8,128)(2,1)S(1)} %add_convert_fusion.1), channel_id=1, source_target_pairs={{0,8},{1,9},{2,10},{3,11},{4,12},{5,13},{6,14},{7,15},{8,0},{9,1},... | collective-permute-start | bytes 221192 | tf_op jit(solution)/shard_map/ppermute | solution.py:322
  44.1 5.0 %collective-permute-start.16 = (bf16[2,3,3,16,128]{4,3,2,1,0:T(8,128)(2,1)S(1)}, bf16[2,3,3,16,128]{4,3,2,1,0:T(8,128)(2,1)S(1)}, u32[]{:S(2)}, u32[]{:S(2)}) collective-permute-start(bf16[2,3,3,16,128]{4,3,2,1,0:T(8,128)(2,1)S(1)} %add_convert_fusion.mine), channel_id=1, source_target_pairs={{0,4},{1,3},{2,6},{3,1},{4,0},{5,7},{6,2},{7,5},{8,12},{9,11},{10,... | collective-permute-start | bytes 221192 | tf_op jit(solution)/shard_map/ppermute | solution.py:322
  44.7 4.8 %collective-permute-start.15 = (bf16[2,3,3,16,128]{4,3,2,1,0:T(8,128)(2,1)S(1)}, bf16[2,3,3,16,128]{4,3,2,1,0:T(8,128)(2,1)S(1)}, u32[]{:S(2)}, u32[]{:S(2)}) collective-permute-start(bf16[2,3,3,16,128]{4,3,2,1,0:T(8,128)(2,1)S(1)} %add_convert_fusion.mine), channel_id=1, source_target_pairs={{0,2},{1,5},{2,0},{3,7},{4,6},{5,1},{6,4},{7,3},{8,10},{9,13},{10,... | collective-permute-start | bytes 221192 | tf_op jit(solution)/shard_map/ppermute | solution.py:322
  45.2 5.3 %collective-permute-start.14 = (bf16[2,3,3,16,128]{4,3,2,1,0:T(8,128)(2,1)S(1)}, bf16[2,3,3,16,128]{4,3,2,1,0:T(8,128)(2,1)S(1)}, u32[]{:S(2)}, u32[]{:S(2)}) collective-permute-start(bf16[2,3,3,16,128]{4,3,2,1,0:T(8,128)(2,1)S(1)} %add_convert_fusion.mine), channel_id=1, source_target_pairs={{0,6},{1,7},{2,4},{3,5},{4,2},{5,3},{6,0},{7,1},{8,14},{9,15},{10,... | collective-permute-start | bytes 221192 | tf_op jit(solution)/shard_map/ppermute | solution.py:322
  50.5 1.6 %collective-permute-start.17 = (bf16[2,3,3,64,128]{4,3,2,1,0:T(8,128)(2,1)S(1)}, bf16[2,3,3,64,128]{4,3,2,1,0:T(8,128)(2,1)S(1)}, u32[]{:S(2)}, u32[]{:S(2)}) collective-permute-start(bf16[2,3,3,64,128]{4,3,2,1,0:T(8,128)(2,1)S(1)} %shard_map.83.mine), channel_id=1, source_target_pairs={{0,1},{1,0},{2,3},{3,2},{4,5},{5,4},{6,7},{7,6},{8,9},{9,8},{10,11... | collective-permute-start | bytes 884744 | tf_op jit(solution)/shard_map/ppermute | solution.py:322

commit v11 on v9

--- a/solution.py
+++ b/solution.py
@@ -13,7 +13,7 @@
 TAPS = [(ty, tx) for ty in range(3) for tx in range(3)]
 
 
-TURNS = ((1, 2), (2, 1), (3, 3))
+TURNS = (3, 1, 2)
 
 
 def silu(values):
@@ -186,11 +186,10 @@
         edge_other[...] = jnp.where(even, back[0:2], back[own - 2 : own])
 
 
-def store(even, kept, sent):
+def store(kept, sent):
     def put(ty, tx, values):
-        half = values.shape[0] // 2
-        kept[ty, tx] = jnp.where(even, values[:half], values[half:])
-        sent[ty, tx] = jnp.where(even, values[half:], values[:half]).astype(BF16)
+        kept[ty, tx] = values
+        sent[ty, tx] = values.astype(BF16)
 
     return put
 
@@ -216,12 +215,12 @@
                 returned = back[i - 2].astype(F32)
             value = (upstream + returned) * slope(joined(even, near_pre, far_pre, i))
             place(ew, i, masked(value, inside(row, strips, own, i - 2)))
-        conv_weight(hid[...], ew, 1, store(even, kept, sent))
+        conv_weight(hid[...], ew, 1, store(kept, sent))
 
     @pl.when(jnp.logical_not(encoder))
     def _():
         skip = jnp.stack([joined(even, near, far, i + 2) for i in range(own)])
-        conv_weight(skip, gw, 0, store(even, kept, sent))
+        conv_weight(skip, gw, 0, store(kept, sent))
 
 
 def main_kernel(segments, strips, x, near_first, far_first, ew, gw, second, kept, sent, hw):
@@ -239,7 +238,7 @@
     def _():
         hw[...] = gw[...]
 
-    conv_weight(x[...], hw, 0, store(even, kept, sent))
+    conv_weight(x[...], hw, 0, store(kept, sent))
 
 
 def input_kernel(hw, main, out, input_grad, output):
@@ -248,10 +247,8 @@
 
 
 def quarters(rows):
-    at = lax.axis_index("rows")
-    quad = lax.rem(at // 2, 4)
-    partners = [jnp.bitwise_xor(quad, jnp.where(lax.rem(at, 2) == 0, *turn)) for turn in TURNS]
-    return [pl.ds(pl.multiple_of(partner * rows, rows), rows) for partner in [quad] + partners]
+    quad = lax.rem(lax.axis_index("rows") // 2, 4)
+    return [pl.ds(pl.multiple_of(jnp.bitwise_xor(quad, k) * rows, rows), rows) for k in (0,) + TURNS]
 
 
 def pack_kernel(kept1, got1, kept2, got2, mine, *sends):
@@ -272,12 +269,13 @@
 
 def last_kernel(factor, mine, theirs, *outs):
     even = lax.rem(lax.axis_index("rows"), 2) == 0
-    rows = mine.shape[3]
-    own_at = pl.ds(pl.multiple_of(jnp.where(even, 0, rows), rows), rows)
-    their_at = pl.ds(pl.multiple_of(jnp.where(even, rows, 0), rows), rows)
-    for t, out in enumerate(outs):
-        out[:, :, own_at, :] = mine[t].astype(F32) * factor
-        out[:, :, their_at, :] = theirs[t].astype(F32) * factor
+
+    def write(sums):
+        for t, out in enumerate(outs):
+            out[...] = sums[t].astype(F32) * factor
+
+    pl.when(even)(lambda: write(theirs))
+    pl.when(jnp.logical_not(even))(lambda: write(mine))
 
 
 def call(kernel, outs, scratch, args, flops):
@@ -353,6 +351,7 @@
         (xa, ha, x_far, main, second),
         work * 2 * own,
     )
+    far_here, g_other = lax.optimization_barrier((far_here, g_other))
     far_there = swap(far_here, True, same)
     out, gw, back, edge_core, edge_other = call(
         functools.partial(middle_kernel, segments, strips),
@@ -365,8 +364,7 @@
     back_other = swap(edge_other, True, other)
     back_core = swap(edge_core, True, core)
     taps = (3, 3, channels, channels)
-    halves = (3, 3, channels // 2, channels)
-    terms = [jax.ShapeDtypeStruct(halves, F32), jax.ShapeDtypeStruct(halves, BF16)]
+    terms = [jax.ShapeDtypeStruct(taps, F32), jax.ShapeDtypeStruct(taps, BF16)]
     kept2, sent2, ew = call(
         functools.partial(second_kernel, segments, strips),
         terms + [wide_out(own + 4)],
@@ -384,15 +382,15 @@
     input_grad, output = call(input_kernel, [like(own, BF16)] * 2, [], (hw, main, out), work * own)
     factor = 1.0 / math.sqrt(own * strips * columns)
 
-    def jump(array, bit):
-        return swap(array, False, lambda r: r ^ (1 << bit))
-
-    def meet(array, turn):
-        return swap(array, False, lambda r: r ^ (turn[r % 2] << 1))
+    def hand(array):
+        return swap(array, False, core)
+
+    def meet(array, chips):
+        return swap(array, False, lambda r: r ^ (chips << 1) if r % 2 else r)
 
     bits = strips.bit_length() - 1
-    quarter = (2, 3, 3, channels // 8, channels)
-    got2, got1 = jump(sent2, 0), jump(sent1, 0)
+    quarter = (2, 3, 3, channels // 4, channels)
+    got2, got1 = hand(sent2), hand(sent1)
     mine, *sends = call(
         pack_kernel,
         [jax.ShapeDtypeStruct(quarter, F32)] + [jax.ShapeDtypeStruct(quarter, BF16)] * 3,
@@ -404,17 +402,17 @@
         mine = mine + meet(send, turn).astype(F32)
     for bit in range(3, bits):
         rounded = lax.optimization_barrier(mine.astype(BF16))
-        mine = rounded.astype(F32) + jump(rounded, bit).astype(F32)
+        mine = rounded.astype(F32) + meet(rounded, 1 << (bit - 1)).astype(F32)
     mine = lax.optimization_barrier(mine.astype(BF16))
     gots = [meet(mine, turn) for turn in TURNS]
     (mine,) = call(
         unpack_kernel,
-        [jax.ShapeDtypeStruct((2,) + halves, BF16)],
+        [jax.ShapeDtypeStruct((2,) + taps, BF16)],
         [],
         (mine, *gots),
         kept1.size,
     )
-    theirs = jump(mine, 0)
+    theirs = hand(mine)
     first_sum, second_sum = call(
         functools.partial(last_kernel, factor), [jax.ShapeDtypeStruct(taps, F32)] * 2, [], (mine, theirs), kept1.size
     )

time: 53 us -> 65 us (1.23)
  starting transfers between devices: 21.8 us -> 43.4 us
  waiting for transfers between devices: 23.5 us -> 13.4 us
    ppermute x19, starting transfers between devices: 21.8 us -> 43.4 us  [swap(): return lax.ppermute(array, ('segment', 'rows'), pairs)]
    ppermute x19, waiting for transfers between devices: 23.5 us -> 13.4 us  [swap(): return lax.ppermute(array, ('segment', 'rows'), pairs)]
  transfers between devices with their start and end apart: 19 -> 19, of which waited for: 15 -> 9; matrix products, arithmetic and copies ran while one was open for 0% -> 0% of each run, Pallas kernels for 7% -> 6%
where the time goes in v11:
time: 65 us; the launch traced here: 64.7 us
  starting transfers between devices  43.4 us (67%)
  waiting for transfers between devices  13.4 us (21%)
  Pallas kernels  6.83 us (11%)
  between operations  0.86 us (1%)
    ppermute x19, starting transfers between devices, swap(): return lax.ppermute(array, ('segment', 'rows'), pairs)  43.4 us
    ppermute x19, waiting for transfers between devices, swap(): return lax.ppermute(array, ('segment', 'rows'), pairs)  13.4 us
    pallas_call x10, Pallas kernels, call(): pl.pallas_call(kernel, out_shape=outs, in_specs=[pl.BlockSpec(memory_spac...  6.83 us
  transfers between devices with their start and end apart: 19, of which 9 were waited for; matrix products, arithmetic and copies ran while one was open for 0% of the time, Pallas kernels for 6%

profile of v11, /device:TPU:0, one launch (start us, length us, event | category | flops | bytes accessed | tf_op | source)
XLA Modules:
  0.0 64.7 jit_solution(11960589447741282769)
XLA Ops:
  0.6 0.5 collective-permute-start
  1.3 1.1 %collective-permute-done.x_core = bf16[4,128,128]{2,1,0:T(8,128)(2,1)S(1)} collective-permute-done((bf16[4,128,128]{2,1,0:T(8,128)(2,1)}, bf16[4,128,128]{2,1,0:T(8,128)(2,1)S(1)}, u32[]{:S(2)}, u32[]{:S(2)}) %collective-permute-start) | collective-permute-done | bytes 131104 | tf_op jit(solution)/shard_map/ppermute | solution.py:320
  2.3 2.8 %collective-permute-start.1 = (bf16[4,128,128]{2,1,0:T(8,128)(2,1)S(1)}, bf16[4,128,128]{2,1,0:T(8,128)(2,1)S(1)}, u32[]{:S(2)}, u32[]{:S(2)}) collective-permute-start(bf16[4,128,128]{2,1,0:T(8,128)(2,1)S(1)} %collective-permute-done.x_core), channel_id=1, source_target_pairs={{0,2},{1,0},{2,4},{3,1},{4,6},{5,3},{6,8},{7,5},{8,10},{9,7},{10,1... | collective-permute-start | bytes 393224 | tf_op jit(solution)/shard_map/ppermute | solution.py:320
  5.2 1.3 %shard_map.76 = (bf16[8,128,384]{2,1,0:T(8,128)(2,1)S(1)}, f32[6,128,128]{2,1,0:T(8,128)S(1)}, bf16[6,128,384]{2,1,0:T(8,128)(2,1)S(1)}, f32[4,128,128]{2,1,0:T(8,128)S(1)}, bf16[4,128,128]{2,1,0:T(8,128)(2,1)S(1)}) custom-call(f32[8,128]{1,0:T(8,128)S(1)} %shard_map.75.token, bf16[4,128,128]{2,1,0:T(8,128)(2,1)S(1)} %bitcast.19, ...), custom_call_target="tpu_custom_call" | custom-call | flops 377487360 | bytes 3018752 | tf_op jit(solution)/shard_map/pallas_call | solution.py:283
  6.5 1.6 %collective-permute-start.3 = (bf16[2,128,128]{2,1,0:T(8,128)(2,1)S(1)}, bf16[2,128,128]{2,1,0:T(8,128)(2,1)S(1)}, u32[]{:S(2)}, u32[]{:S(2)}) collective-permute-start(bf16[2,128,128]{2,1,0:T(8,128)(2,1)S(1)} %slice_select_fusion), channel_id=1, source_target_pairs={{0,2},{1,0},{2,4},{3,1},{4,6},{5,3},{6,8},{7,5},{8,10},{9,7},{10,1... | collective-permute-start | bytes 196616 | tf_op jit(solution)/shard_map/ppermute | solution.py:320
  8.1 1.0 %collective-permute-start.4 = (bf16[4,128,128]{2,1,0:T(8,128)(2,1)S(1)}, bf16[4,128,128]{2,1,0:T(8,128)(2,1)S(1)}, u32[]{:S(2)}, u32[]{:S(2)}) collective-permute-start(bf16[4,128,128]{2,1,0:T(8,128)(2,1)S(1)} %get-tuple-element.48.near_here), channel_id=1, source_target_pairs={{0,16},{1,17},{2,18},{3,19},{4,20},{5,21},{6,22},{7,23},{8,24},{9,... | collective-permute-start | bytes 393224 | tf_op jit(solution)/shard_map/ppermute | solution.py:320
  9.1 0.6 collective-permute-done.1.x_far
  9.8 1.3 %shard_map.77 = (f32[4,128,128]{2,1,0:T(8,128)S(1)}, f32[4,128,128]{2,1,0:T(8,128)S(1)}, bf16[4,128,128]{2,1,0:T(8,128)(2,1)S(1)}, bf16[4,128,128]{2,1,0:T(8,128)(2,1)S(1)}) custom-call(bf16[8,128,384]{2,1,0:T(8,128)(2,1)S(1)} %get-tuple-element.41.xa, bf16[6,128,384]{2,1,0:T(8,128)(2,1)S(1)} %get-tuple-element.42.ha, ...), custom_call_target="tpu_custom_call" | custom-call | flops 301989888 | bytes 2883584 | tf_op jit(solution)/shard_map/pallas_call | solution.py:283
  11.1 0.9 %collective-permute-start.5 = (bf16[4,128,128]{2,1,0:T(8,128)(2,1)S(1)}, bf16[4,128,128]{2,1,0:T(8,128)(2,1)S(1)}, u32[]{:S(2)}, u32[]{:S(2)}) collective-permute-start(bf16[4,128,128]{2,1,0:T(8,128)(2,1)S(1)} %get-tuple-element.49.far_here), channel_id=1, source_target_pairs={{0,16},{1,17},{2,18},{3,19},{4,20},{5,21},{6,22},{7,23},{8,24},{9,... | collective-permute-start | bytes 393224 | tf_op jit(solution)/shard_map/ppermute | solution.py:320
  12.0 2.4 %collective-permute-done.4.near = bf16[4,128,128]{2,1,0:T(8,128)(2,1)S(1)} collective-permute-done((bf16[4,128,128]{2,1,0:T(8,128)(2,1)S(1)}, bf16[4,128,128]{2,1,0:T(8,128)(2,1)S(1)}, u32[]{:S(2)}, u32[]{:S(2)}) %collective-permute-start.4) | collective-permute-done | bytes 131104 | tf_op jit(solution)/shard_map/ppermute | solution.py:320
  14.4 1.7 %collective-permute-done.5.far = bf16[4,128,128]{2,1,0:T(8,128)(2,1)S(1)} collective-permute-done((bf16[4,128,128]{2,1,0:T(8,128)(2,1)S(1)}, bf16[4,128,128]{2,1,0:T(8,128)(2,1)S(1)}, u32[]{:S(2)}, u32[]{:S(2)}) %collective-permute-start.5) | collective-permute-done | bytes 131104 | tf_op jit(solution)/shard_map/ppermute | solution.py:320
  16.1 2.6 %collective-permute-start.6 = (bf16[4,128,128]{2,1,0:T(8,128)(2,1)S(1)}, bf16[4,128,128]{2,1,0:T(8,128)(2,1)S(1)}, u32[]{:S(2)}, u32[]{:S(2)}) collective-permute-start(bf16[4,128,128]{2,1,0:T(8,128)(2,1)S(1)} %get-tuple-element.50), channel_id=1, source_target_pairs={{0,16},{1,17},{2,18},{3,19},{4,20},{5,21},{6,22},{7,23},{8,24},{9,... | collective-permute-start | bytes 393224 | tf_op jit(solution)/shard_map/ppermute | solution.py:320
  18.7 0.2 collective-permute-start.8
  18.9 5.0 %collective-permute-done.7.back_core = bf16[2,128,128]{2,1,0:T(8,128)(2,1)S(1)} collective-permute-done((bf16[2,128,128]{2,1,0:T(8,128)(2,1)S(1)}, bf16[2,128,128]{2,1,0:T(8,128)(2,1)S(1)}, u32[]{:S(2)}, u32[]{:S(2)}) %collective-permute-start.7) | collective-permute-done | bytes 65568 | tf_op jit(solution)/shard_map/ppermute | solution.py:320
  23.8 0.6 collective-permute-done.8.back_other
  24.5 0.7 %shard_map.79 = (f32[3,3,128,128]{3,2,1,0:T(8,128)S(1)}, bf16[3,3,128,128]{3,2,1,0:T(8,128)(2,1)S(1)}, bf16[8,128,384]{2,1,0:T(8,128)(2,1)S(1)}) custom-call(bf16[4,128,128]{2,1,0:T(8,128)(2,1)S(1)} %bitcast.17, bf16[4,128,128]{2,1,0:T(8,128)(2,1)S(1)} %collective-permute-done.2.g_core, bf16[2,128,128]{2,1,0:T(8,128)(2,1)S(1)} %collective-permute-done.3.g_other, ...), custom_call_target="tpu_custom_call" | custom-call | flops 150994944 | bytes 3768320 | tf_op jit(solution)/shard_map/pallas_call | solution.py:283
  25.2 1.1 %shard_map.80 = (f32[3,3,128,128]{3,2,1,0:T(8,128)S(1)}, bf16[3,3,128,128]{3,2,1,0:T(8,128)(2,1)S(1)}, bf16[6,128,384]{2,1,0:T(8,128)(2,1)S(1)}) custom-call(bf16[4,128,128]{2,1,0:T(8,128)(2,1)S(1)} %bitcast.20, f32[6,128,128]{2,1,0:T(8,128)S(1)} %get-tuple-element.40.near_first, f32[4,128,128]{2,1,0:T(8,128)S(1)} %get-tuple-element.43.far_first, ...), custom_call_target="tpu_custom_call" | custom-call | flops 377487360 | bytes 3932160 | tf_op jit(solution)/shard_map/pallas_call | solution.py:283
  26.4 0.5 collective-permute-start.10
  26.9 1.1 %collective-permute-done.9.got1 = bf16[3,3,128,128]{3,2,1,0:T(8,128)(2,1)S(1)} collective-permute-done((bf16[3,3,128,128]{3,2,1,0:T(8,128)(2,1)S(1)}, bf16[3,3,128,128]{3,2,1,0:T(8,128)(2,1)S(1)}, u32[]{:S(2)}, u32[]{:S(2)}) %collective-permute-start.9) | collective-permute-done | bytes 294944 | tf_op jit(solution)/shard_map/ppermute | solution.py:320
  28.0 0.4 collective-permute-done.10.got2
  28.4 0.1 shard_map.82
  28.5 0.7 %collective-permute-start.11 = (bf16[2,3,3,32,128]{4,3,2,1,0:T(8,128)(2,1)S(1)}, bf16[2,3,3,32,128]{4,3,2,1,0:T(8,128)(2,1)S(1)}, u32[]{:S(2)}, u32[]{:S(2)}) collective-permute-start(bf16[2,3,3,32,128]{4,3,2,1,0:T(8,128)(2,1)S(1)} %get-tuple-element.67), channel_id=1, source_target_pairs={{0,0},{1,7},{2,2},{3,5},{4,4},{5,3},{6,6},{7,1},{8,8},{9,15},{10,1... | collective-permute-start | bytes 442376 | tf_op jit(solution)/shard_map/ppermute | solution.py:320
  29.2 0.7 %collective-permute-start.12 = (bf16[2,3,3,32,128]{4,3,2,1,0:T(8,128)(2,1)S(1)}, bf16[2,3,3,32,128]{4,3,2,1,0:T(8,128)(2,1)S(1)}, u32[]{:S(2)}, u32[]{:S(2)}) collective-permute-start(bf16[2,3,3,32,128]{4,3,2,1,0:T(8,128)(2,1)S(1)} %get-tuple-element.68), channel_id=1, source_target_pairs={{0,0},{1,3},{2,2},{3,1},{4,4},{5,7},{6,6},{7,5},{8,8},{9,11},{10,1... | collective-permute-start | bytes 442376 | tf_op jit(solution)/shard_map/ppermute | solution.py:320
  29.9 0.7 %collective-permute-start.13 = (bf16[2,3,3,32,128]{4,3,2,1,0:T(8,128)(2,1)S(1)}, bf16[2,3,3,32,128]{4,3,2,1,0:T(8,128)(2,1)S(1)}, u32[]{:S(2)}, u32[]{:S(2)}) collective-permute-start(bf16[2,3,3,32,128]{4,3,2,1,0:T(8,128)(2,1)S(1)} %get-tuple-element.69), channel_id=1, source_target_pairs={{0,0},{1,5},{2,2},{3,7},{4,4},{5,1},{6,6},{7,3},{8,8},{9,13},{10,1... | collective-permute-start | bytes 442376 | tf_op jit(solution)/shard_map/ppermute | solution.py:320
  30.7 0.7 %collective-permute-start.14 = (bf16[2,3,3,32,128]{4,3,2,1,0:T(8,128)(2,1)S(1)}, bf16[2,3,3,32,128]{4,3,2,1,0:T(8,128)(2,1)S(1)}, u32[]{:S(2)}, u32[]{:S(2)}) collective-permute-start(bf16[2,3,3,32,128]{4,3,2,1,0:T(8,128)(2,1)S(1)} %add_convert_fusion.1), channel_id=1, source_target_pairs={{0,0},{1,9},{2,2},{3,11},{4,4},{5,13},{6,6},{7,15},{8,8},{9,1},{10... | collective-permute-start | bytes 442376 | tf_op jit(solution)/shard_map/ppermute | solution.py:320
  31.4 0.7 %collective-permute-start.17 = (bf16[2,3,3,32,128]{4,3,2,1,0:T(8,128)(2,1)S(1)}, bf16[2,3,3,32,128]{4,3,2,1,0:T(8,128)(2,1)S(1)}, u32[]{:S(2)}, u32[]{:S(2)}) collective-permute-start(bf16[2,3,3,32,128]{4,3,2,1,0:T(8,128)(2,1)S(1)} %add_convert_fusion.mine), channel_id=1, source_target_pairs={{0,0},{1,5},{2,2},{3,7},{4,4},{5,1},{6,6},{7,3},{8,8},{9,13},{10,1... | collective-permute-start | bytes 442376 | tf_op jit(solution)/shard_map/ppermute | solution.py:320
  32.1 0.7 %collective-permute-start.16 = (bf16[2,3,3,32,128]{4,3,2,1,0:T(8,128)(2,1)S(1)}, bf16[2,3,3,32,128]{4,3,2,1,0:T(8,128)(2,1)S(1)}, u32[]{:S(2)}, u32[]{:S(2)}) collective-permute-start(bf16[2,3,3,32,128]{4,3,2,1,0:T(8,128)(2,1)S(1)} %add_convert_fusion.mine), channel_id=1, source_target_pairs={{0,0},{1,3},{2,2},{3,1},{4,4},{5,7},{6,6},{7,5},{8,8},{9,11},{10,1... | collective-permute-start | bytes 442376 | tf_op jit(solution)/shard_map/ppermute | solution.py:320
  32.8 0.7 %collective-permute-start.15 = (bf16[2,3,3,32,128]{4,3,2,1,0:T(8,128)(2,1)S(1)}, bf16[2,3,3,32,128]{4,3,2,1,0:T(8,128)(2,1)S(1)}, u32[]{:S(2)}, u32[]{:S(2)}) collective-permute-start(bf16[2,3,3,32,128]{4,3,2,1,0:T(8,128)(2,1)S(1)} %add_convert_fusion.mine), channel_id=1, source_target_pairs={{0,0},{1,7},{2,2},{3,5},{4,4},{5,3},{6,6},{7,1},{8,8},{9,15},{10,1... | collective-permute-start | bytes 442376 | tf_op jit(solution)/shard_map/ppermute | solution.py:320
  33.5 28.4 %collective-permute-start.18 = (bf16[2,3,3,128,128]{4,3,2,1,0:T(8,128)(2,1)S(1)}, bf16[2,3,3,128,128]{4,3,2,1,0:T(8,128)(2,1)S(1)}, u32[]{:S(2)}, u32[]{:S(2)}) collective-permute-start(bf16[2,3,3,128,128]{4,3,2,1,0:T(8,128)(2,1)S(1)} %shard_map.83.mine), channel_id=1, source_target_pairs={{0,1},{1,0},{2,3},{3,2},{4,5},{5,4},{6,7},{7,6},{8,9},{9,8},{10,11... | collective-permute-start | bytes 1769480 | tf_op jit(solution)/shard_map/ppermute | solution.py:320
  62.0 1.1 %shard_map.81 = (bf16[4,128,128]{2,1,0:T(8,128)(2,1)}, bf16[4,128,128]{2,1,0:T(8,128)(2,1)}) custom-call(bf16[6,128,384]{2,1,0:T(8,128)(2,1)S(1)} %get-tuple-element.58.hw, bf16[3,3,128,128]{3,2,1,0:T(8,128)(2,1)S(1)} %bitcast.14, bf16[4,128,128]{2,1,0:T(8,128)(2,1)S(1)} %get-tuple-element.59.out), custom_call_target="tpu_custom_call" | custom-call | flops 150994944 | bytes 1277952 | tf_op jit(solution)/shard_map/pallas_call | solution.py:283
  63.1 0.5 collective-permute-done.18.theirs
  63.6 1.1 %shard_map.84 = (f32[3,3,128,128]{3,2,1,0:T(8,128)}, f32[3,3,128,128]{3,2,1,0:T(8,128)}) custom-call(bf16[2,3,3,128,128]{4,3,2,1,0:T(8,128)(2,1)S(1)} %shard_map.83.mine, bf16[2,3,3,128,128]{4,3,2,1,0:T(8,128)(2,1)S(1)} %collective-permute-done.18.theirs), custom_call_target="tpu_custom_call" | custom-call | flops 147456 | bytes 2359296 | tf_op jit(solution)/shard_map/pallas_call | solution.py:283
  (27 shorter events, 0.4 us)
Async XLA Ops:
  0.6 1.7 %collective-permute-start = (bf16[4,128,128]{2,1,0:T(8,128)(2,1)}, bf16[4,128,128]{2,1,0:T(8,128)(2,1)S(1)}, u32[]{:S(2)}, u32[]{:S(2)}) collective-permute-start(bf16[4,128,128]{2,1,0:T(8,128)(2,1)} %bitcast.18), channel_id=1, source_target_pairs={{0,1},{1,0},{2,3},{3,2},{4,5},{5,4},{6,7},{7,6},{8,9},{9,8},{10,11... | collective-permute-start | bytes 393224 | tf_op jit(solution)/shard_map/ppermute | solution.py:320
  1.1 4.1 %copy-start = (bf16[1,3,3,128,128]{4,3,2,1,0:T(8,128)(2,1)S(1)}, bf16[1,3,3,128,128]{4,3,2,1,0:T(8,128)(2,1)}, u32[]{:S(2)}) copy-start(bf16[1,3,3,128,128]{4,3,2,1,0:T(8,128)(2,1)} %param.7) | copy-start | bytes 884740
  1.2 4.1 %copy-start.1 = (bf16[1,3,3,128,128]{4,3,2,1,0:T(8,128)(2,1)S(1)}, bf16[1,3,3,128,128]{4,3,2,1,0:T(8,128)(2,1)}, u32[]{:S(2)}) copy-start(bf16[1,3,3,128,128]{4,3,2,1,0:T(8,128)(2,1)} %param.6) | copy-start | bytes 884740
  1.2 4.0 %collective-permute-start.2 = (bf16[4,128,128]{2,1,0:T(8,128)(2,1)}, bf16[4,128,128]{2,1,0:T(8,128)(2,1)S(1)}, u32[]{:S(2)}, u32[]{:S(2)}) collective-permute-start(bf16[4,128,128]{2,1,0:T(8,128)(2,1)} %bitcast.15), channel_id=1, source_target_pairs={{0,1},{1,0},{2,3},{3,2},{4,5},{5,4},{6,7},{7,6},{8,9},{9,8},{10,11... | collective-permute-start | bytes 393224 | tf_op jit(solution)/shard_map/ppermute | solution.py:320
  1.3 4.0 %copy-start.3 = (bf16[1,4,128,128]{3,2,1,0:T(8,128)(2,1)S(1)}, bf16[1,4,128,128]{3,2,1,0:T(8,128)(2,1)}, u32[]{:S(2)}) copy-start(bf16[1,4,128,128]{3,2,1,0:T(8,128)(2,1)} %param.4) | copy-start | bytes 393220
  2.3 7.4 %collective-permute-start.1 = (bf16[4,128,128]{2,1,0:T(8,128)(2,1)S(1)}, bf16[4,128,128]{2,1,0:T(8,128)(2,1)S(1)}, u32[]{:S(2)}, u32[]{:S(2)}) collective-permute-start(bf16[4,128,128]{2,1,0:T(8,128)(2,1)S(1)} %collective-permute-done.x_core), channel_id=1, source_target_pairs={{0,2},{1,0},{2,4},{3,1},{4,6},{5,3},{6,8},{7,5},{8,10},{9,7},{10,1... | collective-permute-start | bytes 393224 | tf_op jit(solution)/shard_map/ppermute | solution.py:320
  6.5 4.5 %collective-permute-start.3 = (bf16[2,128,128]{2,1,0:T(8,128)(2,1)S(1)}, bf16[2,128,128]{2,1,0:T(8,128)(2,1)S(1)}, u32[]{:S(2)}, u32[]{:S(2)}) collective-permute-start(bf16[2,128,128]{2,1,0:T(8,128)(2,1)S(1)} %slice_select_fusion), channel_id=1, source_target_pairs={{0,2},{1,0},{2,4},{3,1},{4,6},{5,3},{6,8},{7,5},{8,10},{9,7},{10,1... | collective-permute-start | bytes 196616 | tf_op jit(solution)/shard_map/ppermute | solution.py:320
  8.1 6.3 %collective-permute-start.4 = (bf16[4,128,128]{2,1,0:T(8,128)(2,1)S(1)}, bf16[4,128,128]{2,1,0:T(8,128)(2,1)S(1)}, u32[]{:S(2)}, u32[]{:S(2)}) collective-permute-start(bf16[4,128,128]{2,1,0:T(8,128)(2,1)S(1)} %get-tuple-element.48.near_here), channel_id=1, source_target_pairs={{0,16},{1,17},{2,18},{3,19},{4,20},{5,21},{6,22},{7,23},{8,24},{9,... | collective-permute-start | bytes 393224 | tf_op jit(solution)/shard_map/ppermute | solution.py:320
  9.8 6.3 %copy-start.2 = (bf16[1,4,128,128]{3,2,1,0:T(8,128)(2,1)S(1)}, bf16[1,4,128,128]{3,2,1,0:T(8,128)(2,1)}, u32[]{:S(2)}) copy-start(bf16[1,4,128,128]{3,2,1,0:T(8,128)(2,1)} %param.5) | copy-start | bytes 393220
  11.1 5.0 %collective-permute-start.5 = (bf16[4,128,128]{2,1,0:T(8,128)(2,1)S(1)}, bf16[4,128,128]{2,1,0:T(8,128)(2,1)S(1)}, u32[]{:S(2)}, u32[]{:S(2)}) collective-permute-start(bf16[4,128,128]{2,1,0:T(8,128)(2,1)S(1)} %get-tuple-element.49.far_here), channel_id=1, source_target_pairs={{0,16},{1,17},{2,18},{3,19},{4,20},{5,21},{6,22},{7,23},{8,24},{9,... | collective-permute-start | bytes 393224 | tf_op jit(solution)/shard_map/ppermute | solution.py:320
  16.1 8.3 %collective-permute-start.6 = (bf16[4,128,128]{2,1,0:T(8,128)(2,1)S(1)}, bf16[4,128,128]{2,1,0:T(8,128)(2,1)S(1)}, u32[]{:S(2)}, u32[]{:S(2)}) collective-permute-start(bf16[4,128,128]{2,1,0:T(8,128)(2,1)S(1)} %get-tuple-element.50), channel_id=1, source_target_pairs={{0,16},{1,17},{2,18},{3,19},{4,20},{5,21},{6,22},{7,23},{8,24},{9,... | collective-permute-start | bytes 393224 | tf_op jit(solution)/shard_map/ppermute | solution.py:320
  18.7 5.2 %collective-permute-start.7 = (bf16[2,128,128]{2,1,0:T(8,128)(2,1)S(1)}, bf16[2,128,128]{2,1,0:T(8,128)(2,1)S(1)}, u32[]{:S(2)}, u32[]{:S(2)}) collective-permute-start(bf16[2,128,128]{2,1,0:T(8,128)(2,1)S(1)} %get-tuple-element.51), channel_id=1, source_target_pairs={{0,17},{1,16},{2,19},{3,18},{4,21},{5,20},{6,23},{7,22},{8,25},{9,... | collective-permute-start | bytes 196616 | tf_op jit(solution)/shard_map/ppermute | solution.py:320
  18.7 5.8 %collective-permute-start.8 = (bf16[2,128,128]{2,1,0:T(8,128)(2,1)S(1)}, bf16[2,128,128]{2,1,0:T(8,128)(2,1)S(1)}, u32[]{:S(2)}, u32[]{:S(2)}) collective-permute-start(bf16[2,128,128]{2,1,0:T(8,128)(2,1)S(1)} %get-tuple-element.52), channel_id=1, source_target_pairs={{0,16},{1,18},{2,17},{3,20},{4,19},{5,22},{6,21},{7,24},{8,23},{9,... | collective-permute-start | bytes 196616 | tf_op jit(solution)/shard_map/ppermute | solution.py:320
  26.3 1.6 %collective-permute-start.9 = (bf16[3,3,128,128]{3,2,1,0:T(8,128)(2,1)S(1)}, bf16[3,3,128,128]{3,2,1,0:T(8,128)(2,1)S(1)}, u32[]{:S(2)}, u32[]{:S(2)}) collective-permute-start(bf16[3,3,128,128]{3,2,1,0:T(8,128)(2,1)S(1)} %get-tuple-element.63), channel_id=1, source_target_pairs={{0,1},{1,0},{2,3},{3,2},{4,5},{5,4},{6,7},{7,6},{8,9},{9,8},{10,11... | collective-permute-start | bytes 884744 | tf_op jit(solution)/shard_map/ppermute | solution.py:320
  26.4 2.0 %collective-permute-start.10 = (bf16[3,3,128,128]{3,2,1,0:T(8,128)(2,1)S(1)}, bf16[3,3,128,128]{3,2,1,0:T(8,128)(2,1)S(1)}, u32[]{:S(2)}, u32[]{:S(2)}) collective-permute-start(bf16[3,3,128,128]{3,2,1,0:T(8,128)(2,1)S(1)} %get-tuple-element.65), channel_id=1, source_target_pairs={{0,1},{1,0},{2,3},{3,2},{4,5},{5,4},{6,7},{7,6},{8,9},{9,8},{10,11... | collective-permute-start | bytes 884744 | tf_op jit(solution)/shard_map/ppermute | solution.py:320
  28.5 2.0 %collective-permute-start.11 = (bf16[2,3,3,32,128]{4,3,2,1,0:T(8,128)(2,1)S(1)}, bf16[2,3,3,32,128]{4,3,2,1,0:T(8,128)(2,1)S(1)}, u32[]{:S(2)}, u32[]{:S(2)}) collective-permute-start(bf16[2,3,3,32,128]{4,3,2,1,0:T(8,128)(2,1)S(1)} %get-tuple-element.67), channel_id=1, source_target_pairs={{0,0},{1,7},{2,2},{3,5},{4,4},{5,3},{6,6},{7,1},{8,8},{9,15},{10,1... | collective-permute-start | bytes 442376 | tf_op jit(solution)/shard_map/ppermute | solution.py:320
  29.2 1.4 %collective-permute-start.12 = (bf16[2,3,3,32,128]{4,3,2,1,0:T(8,128)(2,1)S(1)}, bf16[2,3,3,32,128]{4,3,2,1,0:T(8,128)(2,1)S(1)}, u32[]{:S(2)}, u32[]{:S(2)}) collective-permute-start(bf16[2,3,3,32,128]{4,3,2,1,0:T(8,128)(2,1)S(1)} %get-tuple-element.68), channel_id=1, source_target_pairs={{0,0},{1,3},{2,2},{3,1},{4,4},{5,7},{6,6},{7,5},{8,8},{9,11},{10,1... | collective-permute-start | bytes 442376 | tf_op jit(solution)/shard_map/ppermute | solution.py:320
  29.9 0.7 %collective-permute-start.13 = (bf16[2,3,3,32,128]{4,3,2,1,0:T(8,128)(2,1)S(1)}, bf16[2,3,3,32,128]{4,3,2,1,0:T(8,128)(2,1)S(1)}, u32[]{:S(2)}, u32[]{:S(2)}) collective-permute-start(bf16[2,3,3,32,128]{4,3,2,1,0:T(8,128)(2,1)S(1)} %get-tuple-element.69), channel_id=1, source_target_pairs={{0,0},{1,5},{2,2},{3,7},{4,4},{5,1},{6,6},{7,3},{8,8},{9,13},{10,1... | collective-permute-start | bytes 442376 | tf_op jit(solution)/shard_map/ppermute | solution.py:320
  30.7 0.7 %collective-permute-start.14 = (bf16[2,3,3,32,128]{4,3,2,1,0:T(8,128)(2,1)S(1)}, bf16[2,3,3,32,128]{4,3,2,1,0:T(8,128)(2,1)S(1)}, u32[]{:S(2)}, u32[]{:S(2)}) collective-permute-start(bf16[2,3,3,32,128]{4,3,2,1,0:T(8,128)(2,1)S(1)} %add_convert_fusion.1), channel_id=1, source_target_pairs={{0,0},{1,9},{2,2},{3,11},{4,4},{5,13},{6,6},{7,15},{8,8},{9,1},{10... | collective-permute-start | bytes 442376 | tf_op jit(solution)/shard_map/ppermute | solution.py:320
  31.4 2.0 %collective-permute-start.17 = (bf16[2,3,3,32,128]{4,3,2,1,0:T(8,128)(2,1)S(1)}, bf16[2,3,3,32,128]{4,3,2,1,0:T(8,128)(2,1)S(1)}, u32[]{:S(2)}, u32[]{:S(2)}) collective-permute-start(bf16[2,3,3,32,128]{4,3,2,1,0:T(8,128)(2,1)S(1)} %add_convert_fusion.mine), channel_id=1, source_target_pairs={{0,0},{1,5},{2,2},{3,7},{4,4},{5,1},{6,6},{7,3},{8,8},{9,13},{10,1... | collective-permute-start | bytes 442376 | tf_op jit(solution)/shard_map/ppermute | solution.py:320
  32.1 1.4 %collective-permute-start.16 = (bf16[2,3,3,32,128]{4,3,2,1,0:T(8,128)(2,1)S(1)}, bf16[2,3,3,32,128]{4,3,2,1,0:T(8,128)(2,1)S(1)}, u32[]{:S(2)}, u32[]{:S(2)}) collective-permute-start(bf16[2,3,3,32,128]{4,3,2,1,0:T(8,128)(2,1)S(1)} %add_convert_fusion.mine), channel_id=1, source_target_pairs={{0,0},{1,3},{2,2},{3,1},{4,4},{5,7},{6,6},{7,5},{8,8},{9,11},{10,1... | collective-permute-start | bytes 442376 | tf_op jit(solution)/shard_map/ppermute | solution.py:320
  32.8 0.7 %collective-permute-start.15 = (bf16[2,3,3,32,128]{4,3,2,1,0:T(8,128)(2,1)S(1)}, bf16[2,3,3,32,128]{4,3,2,1,0:T(8,128)(2,1)S(1)}, u32[]{:S(2)}, u32[]{:S(2)}) collective-permute-start(bf16[2,3,3,32,128]{4,3,2,1,0:T(8,128)(2,1)S(1)} %add_convert_fusion.mine), channel_id=1, source_target_pairs={{0,0},{1,7},{2,2},{3,5},{4,4},{5,3},{6,6},{7,1},{8,8},{9,15},{10,1... | collective-permute-start | bytes 442376 | tf_op jit(solution)/shard_map/ppermute | solution.py:320
  33.5 30.1 %collective-permute-start.18 = (bf16[2,3,3,128,128]{4,3,2,1,0:T(8,128)(2,1)S(1)}, bf16[2,3,3,128,128]{4,3,2,1,0:T(8,128)(2,1)S(1)}, u32[]{:S(2)}, u32[]{:S(2)}) collective-permute-start(bf16[2,3,3,128,128]{4,3,2,1,0:T(8,128)(2,1)S(1)} %shard_map.83.mine), channel_id=1, source_target_pairs={{0,1},{1,0},{2,3},{3,2},{4,5},{5,4},{6,7},{7,6},{8,9},{9,8},{10,11... | collective-permute-start | bytes 1769480 | tf_op jit(solution)/shard_map/ppermute | solution.py:320

commit v12 on v9

--- a/solution.py
+++ b/solution.py
@@ -13,7 +13,7 @@
 TAPS = [(ty, tx) for ty in range(3) for tx in range(3)]
 
 
-TURNS = ((1, 2), (2, 1), (3, 3))
+TURNS = ((3, 3), (1, 2), (2, 1))
 
 
 def silu(values):
@@ -153,7 +153,7 @@
 
 
 def middle_kernel(
-    segments, strips, near_here, far_here, near, far, near_first, far_first, g, g_core, g_other, second, out, gw, back, edge_core, edge_other, yw
+    segments, strips, near_here, far_here, near, far, near_first, far_first, g, g_core, g_other, second, out, gw, back, edge_other, yw
 ):
     encoder, row, even = here(segments)
     own = g.shape[0]
@@ -182,7 +182,6 @@
             value = masked(upstream * slope(pre), inside(row, strips, own, i - 1))
             place(gw, i, value)
         back[...] = conv_back(gw, 0, own, second).astype(BF16)
-        edge_core[...] = jnp.where(even, back[own - 2 : own], back[0:2])
         edge_other[...] = jnp.where(even, back[0:2], back[own - 2 : own])
 
 
@@ -195,27 +194,36 @@
     return put
 
 
+def edge_kernel(segments, strips, g_other, back_other, far_pre, edge_grad):
+    encoder, row, even = here(segments)
+    far_in = jnp.where(even, row > 0, row < strips - 1)
+
+    @pl.when(encoder)
+    def _():
+        for i in range(2):
+            value = g_other[i].astype(F32) + back_other[i].astype(F32)
+            value = value * slope(jnp.where(even, far_pre[i], far_pre[2 + i]))
+            edge_grad[i] = masked(value, far_in).astype(BF16)
+
+
 def second_kernel(
-    segments, strips, g, g_core, g_other, back, back_core, back_other, near_pre, far_pre, hid, near, far, gw, kept, sent, ew
+    segments, g, g_core, edge_grad, back, back_core, near_pre, far_pre, hid, near, far, gw, kept, sent, ew
 ):
     encoder, row, even = here(segments)
     own = g.shape[0]
 
     @pl.when(encoder)
     def _():
-        for i in range(own + 4):
-            if i < 2:
-                upstream = jnp.where(even, g_other[i].astype(F32), g_core[own - 2 + i].astype(F32))
-                returned = jnp.where(even, back_other[i].astype(F32), back_core[i].astype(F32))
-            elif i >= own + 2:
-                k = i - own - 2
-                upstream = jnp.where(even, g_core[k].astype(F32), g_other[k].astype(F32))
-                returned = jnp.where(even, back_core[k].astype(F32), back_other[k].astype(F32))
-            else:
-                upstream = g[i - 2].astype(F32)
-                returned = back[i - 2].astype(F32)
-            value = (upstream + returned) * slope(joined(even, near_pre, far_pre, i))
-            place(ew, i, masked(value, inside(row, strips, own, i - 2)))
+        for i in range(2):
+            place(ew, jnp.where(even, 0, own + 2) + i, edge_grad[i].astype(F32))
+        for i in range(own):
+            value = g[i].astype(F32) + back[i].astype(F32)
+            place(ew, 2 + i, value * slope(joined(even, near_pre, far_pre, i + 2)))
+        for i in range(2):
+            upstream = jnp.where(even, g_core[i].astype(F32), g_core[own - 2 + i].astype(F32))
+            returned = jnp.where(even, back_core[i].astype(F32), back_core[own - 2 + i].astype(F32))
+            value = (upstream + returned) * slope(jnp.where(even, near_pre[2 + i], near_pre[i]))
+            place(ew, jnp.where(even, own + 2, 0) + i, value)
         conv_weight(hid[...], ew, 1, store(even, kept, sent))
 
     @pl.when(jnp.logical_not(encoder))
@@ -354,24 +362,27 @@
         work * 2 * own,
     )
     far_there = swap(far_here, True, same)
-    out, gw, back, edge_core, edge_other = call(
+    out, gw, back, edge_other = call(
         functools.partial(middle_kernel, segments, strips),
-        [like(own, BF16), wide_out(own + 2), like(own, BF16), like(2, BF16), like(2, BF16)],
+        [like(own, BF16), wide_out(own + 2), like(own, BF16), like(2, BF16)],
         [wide(own + 4)],
         (near_here, far_here, near_there, far_there, near_first, far_first, g, g_core, g_other, second),
         work * (2 * own + 2),
     )
     back_own = swap(back, True, same)
     back_other = swap(edge_other, True, other)
-    back_core = swap(edge_core, True, core)
+    back_core = swap(back_own, False, core)
+    (edge_grad,) = call(
+        functools.partial(edge_kernel, segments, strips), [like(2, BF16)], [], (g_other, back_other, far_pre), 2 * 10**9
+    )
     taps = (3, 3, channels, channels)
     halves = (3, 3, channels // 2, channels)
     terms = [jax.ShapeDtypeStruct(halves, F32), jax.ShapeDtypeStruct(halves, BF16)]
     kept2, sent2, ew = call(
-        functools.partial(second_kernel, segments, strips),
+        functools.partial(second_kernel, segments),
         terms + [wide_out(own + 4)],
         [],
-        (g, g_core, g_other, back_own, back_core, back_other, near_pre, far_pre, hid, near_there, far_there, gw),
+        (g, g_core, edge_grad, back_own, back_core, near_pre, far_pre, hid, near_there, far_there, gw),
         work * own,
     )
     kept1, sent1, hw = call(

time: 53 us -> 52.4 us (0.989)
  waiting for transfers between devices: 23.5 us -> 21.8 us
  starting transfers between devices: 21.8 us -> 22.7 us
    ppermute x19, waiting for transfers between devices: 23.5 us -> 21.8 us  [swap(): return lax.ppermute(array, ('segment', 'rows'), pairs)]
    ppermute x19, starting transfers between devices: 21.8 us -> 22.7 us  [swap(): return lax.ppermute(array, ('segment', 'rows'), pairs)]
    pallas_call x10 -> x11, Pallas kernels: 6.77 us -> 6.9 us  [call(): pl.pallas_call(kernel, out_shape=outs, in_specs=[pl.BlockSpec(memory_spac...]
  transfers between devices with their start and end apart: 19 -> 19, of which waited for: 15 -> 14; matrix products, arithmetic and copies ran while one was open for 0% -> 0% of each run, Pallas kernels for 7% -> 7%
where the time goes in v12:
time: 52.4 us; the launch traced here: 52.3 us
  starting transfers between devices  22.7 us (43%)
  waiting for transfers between devices  21.8 us (42%)
  Pallas kernels  6.9 us (13%)
  between operations  0.76 us (1%)
    ppermute x19, starting transfers between devices, swap(): return lax.ppermute(array, ('segment', 'rows'), pairs)  22.7 us
    ppermute x19, waiting for transfers between devices, swap(): return lax.ppermute(array, ('segment', 'rows'), pairs)  21.8 us
    pallas_call x11, Pallas kernels, call(): pl.pallas_call(kernel, out_shape=outs, in_specs=[pl.BlockSpec(memory_spac...  6.9 us
  transfers between devices with their start and end apart: 19, of which 14 were waited for; matrix products, arithmetic and copies ran while one was open for 0% of the time, Pallas kernels for 7%

profile of v12, /device:TPU:0, one launch (start us, length us, event | category | flops | bytes accessed | tf_op | source)
XLA Modules:
  0.0 52.3 jit_solution(4083621538140174139)
XLA Ops:
  0.6 0.5 collective-permute-start
  1.3 1.1 %collective-permute-done.x_core = bf16[4,128,128]{2,1,0:T(8,128)(2,1)S(1)} collective-permute-done((bf16[4,128,128]{2,1,0:T(8,128)(2,1)}, bf16[4,128,128]{2,1,0:T(8,128)(2,1)S(1)}, u32[]{:S(2)}, u32[]{:S(2)}) %collective-permute-start) | collective-permute-done | bytes 131104 | tf_op jit(solution)/shard_map/ppermute | solution.py:330
  2.3 2.8 %collective-permute-start.1 = (bf16[4,128,128]{2,1,0:T(8,128)(2,1)S(1)}, bf16[4,128,128]{2,1,0:T(8,128)(2,1)S(1)}, u32[]{:S(2)}, u32[]{:S(2)}) collective-permute-start(bf16[4,128,128]{2,1,0:T(8,128)(2,1)S(1)} %collective-permute-done.x_core), channel_id=1, source_target_pairs={{0,2},{1,0},{2,4},{3,1},{4,6},{5,3},{6,8},{7,5},{8,10},{9,7},{10,1... | collective-permute-start | bytes 393224 | tf_op jit(solution)/shard_map/ppermute | solution.py:330
  5.2 1.3 %shard_map.76 = (bf16[8,128,384]{2,1,0:T(8,128)(2,1)S(1)}, f32[6,128,128]{2,1,0:T(8,128)S(1)}, bf16[6,128,384]{2,1,0:T(8,128)(2,1)S(1)}, f32[4,128,128]{2,1,0:T(8,128)S(1)}, bf16[4,128,128]{2,1,0:T(8,128)(2,1)S(1)}) custom-call(f32[8,128]{1,0:T(8,128)S(1)} %shard_map.75.token, bf16[4,128,128]{2,1,0:T(8,128)(2,1)S(1)} %bitcast.19, ...), custom_call_target="tpu_custom_call" | custom-call | flops 377487360 | bytes 3018752 | tf_op jit(solution)/shard_map/pallas_call | solution.py:293
  6.5 1.1 %collective-permute-start.4 = (bf16[4,128,128]{2,1,0:T(8,128)(2,1)S(1)}, bf16[4,128,128]{2,1,0:T(8,128)(2,1)S(1)}, u32[]{:S(2)}, u32[]{:S(2)}) collective-permute-start(bf16[4,128,128]{2,1,0:T(8,128)(2,1)S(1)} %get-tuple-element.43.near_here), channel_id=1, source_target_pairs={{0,16},{1,17},{2,18},{3,19},{4,20},{5,21},{6,22},{7,23},{8,24},{9,... | collective-permute-start | bytes 393224 | tf_op jit(solution)/shard_map/ppermute | solution.py:330
  7.6 1.5 %collective-permute-done.1.x_far = bf16[4,128,128]{2,1,0:T(8,128)(2,1)S(1)} collective-permute-done((bf16[4,128,128]{2,1,0:T(8,128)(2,1)S(1)}, bf16[4,128,128]{2,1,0:T(8,128)(2,1)S(1)}, u32[]{:S(2)}, u32[]{:S(2)}) %collective-permute-start.1) | collective-permute-done | bytes 131104 | tf_op jit(solution)/shard_map/ppermute | solution.py:330
  9.1 1.3 %shard_map.77 = (f32[4,128,128]{2,1,0:T(8,128)S(1)}, f32[4,128,128]{2,1,0:T(8,128)S(1)}, bf16[4,128,128]{2,1,0:T(8,128)(2,1)S(1)}, bf16[4,128,128]{2,1,0:T(8,128)(2,1)S(1)}) custom-call(bf16[8,128,384]{2,1,0:T(8,128)(2,1)S(1)} %get-tuple-element.38.xa, bf16[6,128,384]{2,1,0:T(8,128)(2,1)S(1)} %get-tuple-element.39.ha, ...), custom_call_target="tpu_custom_call" | custom-call | flops 301989888 | bytes 2883584 | tf_op jit(solution)/shard_map/pallas_call | solution.py:293
  10.4 0.9 %collective-permute-start.5 = (bf16[4,128,128]{2,1,0:T(8,128)(2,1)S(1)}, bf16[4,128,128]{2,1,0:T(8,128)(2,1)S(1)}, u32[]{:S(2)}, u32[]{:S(2)}) collective-permute-start(bf16[4,128,128]{2,1,0:T(8,128)(2,1)S(1)} %get-tuple-element.44.far_here), channel_id=1, source_target_pairs={{0,16},{1,17},{2,18},{3,19},{4,20},{5,21},{6,22},{7,23},{8,24},{9,... | collective-permute-start | bytes 393224 | tf_op jit(solution)/shard_map/ppermute | solution.py:330
  11.3 2.5 %collective-permute-start.3 = (bf16[2,128,128]{2,1,0:T(8,128)(2,1)S(1)}, bf16[2,128,128]{2,1,0:T(8,128)(2,1)S(1)}, u32[]{:S(2)}, u32[]{:S(2)}) collective-permute-start(bf16[2,128,128]{2,1,0:T(8,128)(2,1)S(1)} %slice_select_fusion), channel_id=1, source_target_pairs={{0,2},{1,0},{2,4},{3,1},{4,6},{5,3},{6,8},{7,5},{8,10},{9,7},{10,1... | collective-permute-start | bytes 196616 | tf_op jit(solution)/shard_map/ppermute | solution.py:330
  13.7 1.9 %collective-permute-done.3.g_other = bf16[2,128,128]{2,1,0:T(8,128)(2,1)S(1)} collective-permute-done((bf16[2,128,128]{2,1,0:T(8,128)(2,1)S(1)}, bf16[2,128,128]{2,1,0:T(8,128)(2,1)S(1)}, u32[]{:S(2)}, u32[]{:S(2)}) %collective-permute-start.3) | collective-permute-done | bytes 65568 | tf_op jit(solution)/shard_map/ppermute | solution.py:330
  15.7 2.8 %collective-permute-start.7 = (bf16[4,128,128]{2,1,0:T(8,128)(2,1)S(1)}, bf16[4,128,128]{2,1,0:T(8,128)(2,1)S(1)}, u32[]{:S(2)}, u32[]{:S(2)}) collective-permute-start(bf16[4,128,128]{2,1,0:T(8,128)(2,1)S(1)} %get-tuple-element.47), channel_id=1, source_target_pairs={{0,16},{1,17},{2,18},{3,19},{4,20},{5,21},{6,22},{7,23},{8,24},{9,... | collective-permute-start | bytes 393224 | tf_op jit(solution)/shard_map/ppermute | solution.py:330
  18.7 2.9 %collective-permute-done.7.back = bf16[4,128,128]{2,1,0:T(8,128)(2,1)S(1)} collective-permute-done((bf16[4,128,128]{2,1,0:T(8,128)(2,1)S(1)}, bf16[4,128,128]{2,1,0:T(8,128)(2,1)S(1)}, u32[]{:S(2)}, u32[]{:S(2)}) %collective-permute-start.7) | collective-permute-done | bytes 131104 | tf_op jit(solution)/shard_map/ppermute | solution.py:330
  21.5 1.9 %collective-permute-done.6.back_other = bf16[2,128,128]{2,1,0:T(8,128)(2,1)S(1)} collective-permute-done((bf16[2,128,128]{2,1,0:T(8,128)(2,1)S(1)}, bf16[2,128,128]{2,1,0:T(8,128)(2,1)S(1)}, u32[]{:S(2)}, u32[]{:S(2)}) %collective-permute-start.6) | collective-permute-done | bytes 65568 | tf_op jit(solution)/shard_map/ppermute | solution.py:330
  23.5 0.8 %shard_map.80 = (f32[3,3,64,128]{3,2,1,0:T(8,128)S(1)}, bf16[3,3,64,128]{3,2,1,0:T(8,128)(2,1)S(1)}, bf16[8,128,384]{2,1,0:T(8,128)(2,1)S(1)}) custom-call(bf16[4,128,128]{2,1,0:T(8,128)(2,1)S(1)} %bitcast.17, bf16[4,128,128]{2,1,0:T(8,128)(2,1)S(1)} %collective-permute-done.2.g_core, bf16[2,128,128]{2,1,0:T(8,128)(2,1)S(1)} %shard_map.79.edge_grad, ...), custom_call_target="tpu_custom_call" | custom-call | flops 150994944 | bytes 3325952 | tf_op jit(solution)/shard_map/pallas_call | solution.py:293
  24.3 1.1 %shard_map.81 = (f32[3,3,64,128]{3,2,1,0:T(8,128)S(1)}, bf16[3,3,64,128]{3,2,1,0:T(8,128)(2,1)S(1)}, bf16[6,128,384]{2,1,0:T(8,128)(2,1)S(1)}) custom-call(bf16[4,128,128]{2,1,0:T(8,128)(2,1)S(1)} %bitcast.20, f32[6,128,128]{2,1,0:T(8,128)S(1)} %get-tuple-element.37.near_first, f32[4,128,128]{2,1,0:T(8,128)S(1)} %get-tuple-element.40.far_first, ...), custom_call_target="tpu_custom_call" | custom-call | flops 377487360 | bytes 3489792 | tf_op jit(solution)/shard_map/pallas_call | solution.py:293
  25.5 0.5 collective-permute-start.10
  26.0 0.9 %collective-permute-done.9.got1 = bf16[3,3,64,128]{3,2,1,0:T(8,128)(2,1)S(1)} collective-permute-done((bf16[3,3,64,128]{3,2,1,0:T(8,128)(2,1)S(1)}, bf16[3,3,64,128]{3,2,1,0:T(8,128)(2,1)S(1)}, u32[]{:S(2)}, u32[]{:S(2)}) %collective-permute-start.9) | collective-permute-done | bytes 147488 | tf_op jit(solution)/shard_map/ppermute | solution.py:330
  27.1 3.8 %collective-permute-start.11 = (bf16[2,3,3,16,128]{4,3,2,1,0:T(8,128)(2,1)S(1)}, bf16[2,3,3,16,128]{4,3,2,1,0:T(8,128)(2,1)S(1)}, u32[]{:S(2)}, u32[]{:S(2)}) collective-permute-start(bf16[2,3,3,16,128]{4,3,2,1,0:T(8,128)(2,1)S(1)} %get-tuple-element.61), channel_id=1, source_target_pairs={{0,6},{1,7},{2,4},{3,5},{4,2},{5,3},{6,0},{7,1},{8,14},{9,15},{10,... | collective-permute-start | bytes 221192 | tf_op jit(solution)/shard_map/ppermute | solution.py:330
  30.9 1.3 %collective-permute-start.12 = (bf16[2,3,3,16,128]{4,3,2,1,0:T(8,128)(2,1)S(1)}, bf16[2,3,3,16,128]{4,3,2,1,0:T(8,128)(2,1)S(1)}, u32[]{:S(2)}, u32[]{:S(2)}) collective-permute-start(bf16[2,3,3,16,128]{4,3,2,1,0:T(8,128)(2,1)S(1)} %get-tuple-element.62), channel_id=1, source_target_pairs={{0,2},{1,5},{2,0},{3,7},{4,6},{5,1},{6,4},{7,3},{8,10},{9,13},{10,... | collective-permute-start | bytes 221192 | tf_op jit(solution)/shard_map/ppermute | solution.py:330
  32.2 1.5 %collective-permute-done.11 = bf16[2,3,3,16,128]{4,3,2,1,0:T(8,128)(2,1)S(1)} collective-permute-done((bf16[2,3,3,16,128]{4,3,2,1,0:T(8,128)(2,1)S(1)}, bf16[2,3,3,16,128]{4,3,2,1,0:T(8,128)(2,1)S(1)}, u32[]{:S(2)}, u32[]{:S(2)}) %collective-permute-start.11) | collective-permute-done | bytes 73760 | tf_op jit(solution)/shard_map/ppermute | solution.py:330
  33.6 1.6 %collective-permute-done.12 = bf16[2,3,3,16,128]{4,3,2,1,0:T(8,128)(2,1)S(1)} collective-permute-done((bf16[2,3,3,16,128]{4,3,2,1,0:T(8,128)(2,1)S(1)}, bf16[2,3,3,16,128]{4,3,2,1,0:T(8,128)(2,1)S(1)}, u32[]{:S(2)}, u32[]{:S(2)}) %collective-permute-start.12) | collective-permute-done | bytes 73760 | tf_op jit(solution)/shard_map/ppermute | solution.py:330
  35.3 1.3 %collective-permute-done.13 = bf16[2,3,3,16,128]{4,3,2,1,0:T(8,128)(2,1)S(1)} collective-permute-done((bf16[2,3,3,16,128]{4,3,2,1,0:T(8,128)(2,1)S(1)}, bf16[2,3,3,16,128]{4,3,2,1,0:T(8,128)(2,1)S(1)}, u32[]{:S(2)}, u32[]{:S(2)}) %collective-permute-start.13) | collective-permute-done | bytes 73760 | tf_op jit(solution)/shard_map/ppermute | solution.py:330
  36.6 2.7 %collective-permute-start.14 = (bf16[2,3,3,16,128]{4,3,2,1,0:T(8,128)(2,1)S(1)}, bf16[2,3,3,16,128]{4,3,2,1,0:T(8,128)(2,1)S(1)}, u32[]{:S(2)}, u32[]{:S(2)}) collective-permute-start(bf16[2,3,3,16,128]{4,3,2,1,0:T(8,128)(2,1)S(1)} %add_convert_fusion.1), channel_id=1, source_target_pairs={{0,8},{1,9},{2,10},{3,11},{4,12},{5,13},{6,14},{7,15},{8,0},{9,1},... | collective-permute-start | bytes 221192 | tf_op jit(solution)/shard_map/ppermute | solution.py:330
  39.2 3.9 %collective-permute-done.14 = bf16[2,3,3,16,128]{4,3,2,1,0:T(8,128)(2,1)S(1)} collective-permute-done((bf16[2,3,3,16,128]{4,3,2,1,0:T(8,128)(2,1)S(1)}, bf16[2,3,3,16,128]{4,3,2,1,0:T(8,128)(2,1)S(1)}, u32[]{:S(2)}, u32[]{:S(2)}) %collective-permute-start.14) | collective-permute-done | bytes 73760 | tf_op jit(solution)/shard_map/ppermute | solution.py:330
  43.2 0.5 %collective-permute-start.17 = (bf16[2,3,3,16,128]{4,3,2,1,0:T(8,128)(2,1)S(1)}, bf16[2,3,3,16,128]{4,3,2,1,0:T(8,128)(2,1)S(1)}, u32[]{:S(2)}, u32[]{:S(2)}) collective-permute-start(bf16[2,3,3,16,128]{4,3,2,1,0:T(8,128)(2,1)S(1)} %add_convert_fusion.mine), channel_id=1, source_target_pairs={{0,4},{1,3},{2,6},{3,1},{4,0},{5,7},{6,2},{7,5},{8,12},{9,11},{10,... | collective-permute-start | bytes 221192 | tf_op jit(solution)/shard_map/ppermute | solution.py:330
  43.7 0.2 collective-permute-start.16
  43.9 2.8 %collective-permute-start.15 = (bf16[2,3,3,16,128]{4,3,2,1,0:T(8,128)(2,1)S(1)}, bf16[2,3,3,16,128]{4,3,2,1,0:T(8,128)(2,1)S(1)}, u32[]{:S(2)}, u32[]{:S(2)}) collective-permute-start(bf16[2,3,3,16,128]{4,3,2,1,0:T(8,128)(2,1)S(1)} %add_convert_fusion.mine), channel_id=1, source_target_pairs={{0,6},{1,7},{2,4},{3,5},{4,2},{5,3},{6,0},{7,1},{8,14},{9,15},{10,... | collective-permute-start | bytes 221192 | tf_op jit(solution)/shard_map/ppermute | solution.py:330
  46.7 1.3 %collective-permute-done.17.rest_2_ = bf16[2,3,3,16,128]{4,3,2,1,0:T(8,128)(2,1)S(1)} collective-permute-done((bf16[2,3,3,16,128]{4,3,2,1,0:T(8,128)(2,1)S(1)}, bf16[2,3,3,16,128]{4,3,2,1,0:T(8,128)(2,1)S(1)}, u32[]{:S(2)}, u32[]{:S(2)}) %collective-permute-start.17) | collective-permute-done | bytes 73760 | tf_op jit(solution)/shard_map/ppermute | solution.py:330
  48.0 1.4 %collective-permute-done.16.rest_1_ = bf16[2,3,3,16,128]{4,3,2,1,0:T(8,128)(2,1)S(1)} collective-permute-done((bf16[2,3,3,16,128]{4,3,2,1,0:T(8,128)(2,1)S(1)}, bf16[2,3,3,16,128]{4,3,2,1,0:T(8,128)(2,1)S(1)}, u32[]{:S(2)}, u32[]{:S(2)}) %collective-permute-start.16) | collective-permute-done | bytes 73760 | tf_op jit(solution)/shard_map/ppermute | solution.py:330
  49.6 1.1 %shard_map.82 = (bf16[4,128,128]{2,1,0:T(8,128)(2,1)}, bf16[4,128,128]{2,1,0:T(8,128)(2,1)}) custom-call(bf16[6,128,384]{2,1,0:T(8,128)(2,1)S(1)} %get-tuple-element.52.hw, bf16[3,3,128,128]{3,2,1,0:T(8,128)(2,1)S(1)} %bitcast.14, bf16[4,128,128]{2,1,0:T(8,128)(2,1)S(1)} %get-tuple-element.53.out), custom_call_target="tpu_custom_call" | custom-call | flops 150994944 | bytes 1277952 | tf_op jit(solution)/shard_map/pallas_call | solution.py:293
  50.7 0.4 collective-permute-done.18.theirs
  51.2 1.1 %shard_map.85 = (f32[3,3,128,128]{3,2,1,0:T(8,128)}, f32[3,3,128,128]{3,2,1,0:T(8,128)}) custom-call(bf16[2,3,3,64,128]{4,3,2,1,0:T(8,128)(2,1)S(1)} %shard_map.84.mine, bf16[2,3,3,64,128]{4,3,2,1,0:T(8,128)(2,1)S(1)} %collective-permute-done.18.theirs), custom_call_target="tpu_custom_call" | custom-call | flops 73728 | bytes 1769472 | tf_op jit(solution)/shard_map/pallas_call | solution.py:293
  (28 shorter events, 0.9 us)
Async XLA Ops:
  0.6 1.7 %collective-permute-start = (bf16[4,128,128]{2,1,0:T(8,128)(2,1)}, bf16[4,128,128]{2,1,0:T(8,128)(2,1)S(1)}, u32[]{:S(2)}, u32[]{:S(2)}) collective-permute-start(bf16[4,128,128]{2,1,0:T(8,128)(2,1)} %bitcast.18), channel_id=1, source_target_pairs={{0,1},{1,0},{2,3},{3,2},{4,5},{5,4},{6,7},{7,6},{8,9},{9,8},{10,11... | collective-permute-start | bytes 393224 | tf_op jit(solution)/shard_map/ppermute | solution.py:330
  1.1 4.1 %copy-start = (bf16[1,3,3,128,128]{4,3,2,1,0:T(8,128)(2,1)S(1)}, bf16[1,3,3,128,128]{4,3,2,1,0:T(8,128)(2,1)}, u32[]{:S(2)}) copy-start(bf16[1,3,3,128,128]{4,3,2,1,0:T(8,128)(2,1)} %param.7) | copy-start | bytes 884740
  1.2 4.1 %copy-start.1 = (bf16[1,3,3,128,128]{4,3,2,1,0:T(8,128)(2,1)S(1)}, bf16[1,3,3,128,128]{4,3,2,1,0:T(8,128)(2,1)}, u32[]{:S(2)}) copy-start(bf16[1,3,3,128,128]{4,3,2,1,0:T(8,128)(2,1)} %param.6) | copy-start | bytes 884740
  1.2 4.0 %collective-permute-start.2 = (bf16[4,128,128]{2,1,0:T(8,128)(2,1)}, bf16[4,128,128]{2,1,0:T(8,128)(2,1)S(1)}, u32[]{:S(2)}, u32[]{:S(2)}) collective-permute-start(bf16[4,128,128]{2,1,0:T(8,128)(2,1)} %bitcast.15), channel_id=1, source_target_pairs={{0,1},{1,0},{2,3},{3,2},{4,5},{5,4},{6,7},{7,6},{8,9},{9,8},{10,11... | collective-permute-start | bytes 393224 | tf_op jit(solution)/shard_map/ppermute | solution.py:330
  1.3 4.0 %copy-start.3 = (bf16[1,4,128,128]{3,2,1,0:T(8,128)(2,1)S(1)}, bf16[1,4,128,128]{3,2,1,0:T(8,128)(2,1)}, u32[]{:S(2)}) copy-start(bf16[1,4,128,128]{3,2,1,0:T(8,128)(2,1)} %param.4) | copy-start | bytes 393220
  2.3 6.7 %collective-permute-start.1 = (bf16[4,128,128]{2,1,0:T(8,128)(2,1)S(1)}, bf16[4,128,128]{2,1,0:T(8,128)(2,1)S(1)}, u32[]{:S(2)}, u32[]{:S(2)}) collective-permute-start(bf16[4,128,128]{2,1,0:T(8,128)(2,1)S(1)} %collective-permute-done.x_core), channel_id=1, source_target_pairs={{0,2},{1,0},{2,4},{3,1},{4,6},{5,3},{6,8},{7,5},{8,10},{9,7},{10,1... | collective-permute-start | bytes 393224 | tf_op jit(solution)/shard_map/ppermute | solution.py:330
  6.5 9.1 %collective-permute-start.4 = (bf16[4,128,128]{2,1,0:T(8,128)(2,1)S(1)}, bf16[4,128,128]{2,1,0:T(8,128)(2,1)S(1)}, u32[]{:S(2)}, u32[]{:S(2)}) collective-permute-start(bf16[4,128,128]{2,1,0:T(8,128)(2,1)S(1)} %get-tuple-element.43.near_here), channel_id=1, source_target_pairs={{0,16},{1,17},{2,18},{3,19},{4,20},{5,21},{6,22},{7,23},{8,24},{9,... | collective-permute-start | bytes 393224 | tf_op jit(solution)/shard_map/ppermute | solution.py:330
  9.1 6.6 %copy-start.2 = (bf16[1,4,128,128]{3,2,1,0:T(8,128)(2,1)S(1)}, bf16[1,4,128,128]{3,2,1,0:T(8,128)(2,1)}, u32[]{:S(2)}) copy-start(bf16[1,4,128,128]{3,2,1,0:T(8,128)(2,1)} %param.5) | copy-start | bytes 393220
  10.4 5.3 %collective-permute-start.5 = (bf16[4,128,128]{2,1,0:T(8,128)(2,1)S(1)}, bf16[4,128,128]{2,1,0:T(8,128)(2,1)S(1)}, u32[]{:S(2)}, u32[]{:S(2)}) collective-permute-start(bf16[4,128,128]{2,1,0:T(8,128)(2,1)S(1)} %get-tuple-element.44.far_here), channel_id=1, source_target_pairs={{0,16},{1,17},{2,18},{3,19},{4,20},{5,21},{6,22},{7,23},{8,24},{9,... | collective-permute-start | bytes 393224 | tf_op jit(solution)/shard_map/ppermute | solution.py:330
  11.3 4.4 %collective-permute-start.3 = (bf16[2,128,128]{2,1,0:T(8,128)(2,1)S(1)}, bf16[2,128,128]{2,1,0:T(8,128)(2,1)S(1)}, u32[]{:S(2)}, u32[]{:S(2)}) collective-permute-start(bf16[2,128,128]{2,1,0:T(8,128)(2,1)S(1)} %slice_select_fusion), channel_id=1, source_target_pairs={{0,2},{1,0},{2,4},{3,1},{4,6},{5,3},{6,8},{7,5},{8,10},{9,7},{10,1... | collective-permute-start | bytes 196616 | tf_op jit(solution)/shard_map/ppermute | solution.py:330
  15.7 5.8 %collective-permute-start.7 = (bf16[4,128,128]{2,1,0:T(8,128)(2,1)S(1)}, bf16[4,128,128]{2,1,0:T(8,128)(2,1)S(1)}, u32[]{:S(2)}, u32[]{:S(2)}) collective-permute-start(bf16[4,128,128]{2,1,0:T(8,128)(2,1)S(1)} %get-tuple-element.47), channel_id=1, source_target_pairs={{0,16},{1,17},{2,18},{3,19},{4,20},{5,21},{6,22},{7,23},{8,24},{9,... | collective-permute-start | bytes 393224 | tf_op jit(solution)/shard_map/ppermute | solution.py:330
  18.6 4.8 %collective-permute-start.6 = (bf16[2,128,128]{2,1,0:T(8,128)(2,1)S(1)}, bf16[2,128,128]{2,1,0:T(8,128)(2,1)S(1)}, u32[]{:S(2)}, u32[]{:S(2)}) collective-permute-start(bf16[2,128,128]{2,1,0:T(8,128)(2,1)S(1)} %get-tuple-element.45), channel_id=1, source_target_pairs={{0,16},{1,18},{2,17},{3,20},{4,19},{5,22},{6,21},{7,24},{8,23},{9,... | collective-permute-start | bytes 196616 | tf_op jit(solution)/shard_map/ppermute | solution.py:330
  21.5 1.9 %collective-permute-start.8 = (bf16[4,128,128]{2,1,0:T(8,128)(2,1)S(1)}, bf16[4,128,128]{2,1,0:T(8,128)(2,1)S(1)}, u32[]{:S(2)}, u32[]{:S(2)}) collective-permute-start(bf16[4,128,128]{2,1,0:T(8,128)(2,1)S(1)} %collective-permute-done.7.back), channel_id=1, source_target_pairs={{0,1},{1,0},{2,3},{3,2},{4,5},{5,4},{6,7},{7,6},{8,9},{9,8},{10,11... | collective-permute-start | bytes 393224 | tf_op jit(solution)/shard_map/ppermute | solution.py:330
  25.4 1.4 %collective-permute-start.9 = (bf16[3,3,64,128]{3,2,1,0:T(8,128)(2,1)S(1)}, bf16[3,3,64,128]{3,2,1,0:T(8,128)(2,1)S(1)}, u32[]{:S(2)}, u32[]{:S(2)}) collective-permute-start(bf16[3,3,64,128]{3,2,1,0:T(8,128)(2,1)S(1)} %get-tuple-element.57), channel_id=1, source_target_pairs={{0,1},{1,0},{2,3},{3,2},{4,5},{5,4},{6,7},{7,6},{8,9},{9,8},{10,11... | collective-permute-start | bytes 442376 | tf_op jit(solution)/shard_map/ppermute | solution.py:330
  25.5 1.6 %collective-permute-start.10 = (bf16[3,3,64,128]{3,2,1,0:T(8,128)(2,1)S(1)}, bf16[3,3,64,128]{3,2,1,0:T(8,128)(2,1)S(1)}, u32[]{:S(2)}, u32[]{:S(2)}) collective-permute-start(bf16[3,3,64,128]{3,2,1,0:T(8,128)(2,1)S(1)} %get-tuple-element.59), channel_id=1, source_target_pairs={{0,1},{1,0},{2,3},{3,2},{4,5},{5,4},{6,7},{7,6},{8,9},{9,8},{10,11... | collective-permute-start | bytes 442376 | tf_op jit(solution)/shard_map/ppermute | solution.py:330
  27.1 6.5 %collective-permute-start.11 = (bf16[2,3,3,16,128]{4,3,2,1,0:T(8,128)(2,1)S(1)}, bf16[2,3,3,16,128]{4,3,2,1,0:T(8,128)(2,1)S(1)}, u32[]{:S(2)}, u32[]{:S(2)}) collective-permute-start(bf16[2,3,3,16,128]{4,3,2,1,0:T(8,128)(2,1)S(1)} %get-tuple-element.61), channel_id=1, source_target_pairs={{0,6},{1,7},{2,4},{3,5},{4,2},{5,3},{6,0},{7,1},{8,14},{9,15},{10,... | collective-permute-start | bytes 221192 | tf_op jit(solution)/shard_map/ppermute | solution.py:330
  30.9 4.4 %collective-permute-start.12 = (bf16[2,3,3,16,128]{4,3,2,1,0:T(8,128)(2,1)S(1)}, bf16[2,3,3,16,128]{4,3,2,1,0:T(8,128)(2,1)S(1)}, u32[]{:S(2)}, u32[]{:S(2)}) collective-permute-start(bf16[2,3,3,16,128]{4,3,2,1,0:T(8,128)(2,1)S(1)} %get-tuple-element.62), channel_id=1, source_target_pairs={{0,2},{1,5},{2,0},{3,7},{4,6},{5,1},{6,4},{7,3},{8,10},{9,13},{10,... | collective-permute-start | bytes 221192 | tf_op jit(solution)/shard_map/ppermute | solution.py:330
  32.2 4.4 %collective-permute-start.13 = (bf16[2,3,3,16,128]{4,3,2,1,0:T(8,128)(2,1)S(1)}, bf16[2,3,3,16,128]{4,3,2,1,0:T(8,128)(2,1)S(1)}, u32[]{:S(2)}, u32[]{:S(2)}) collective-permute-start(bf16[2,3,3,16,128]{4,3,2,1,0:T(8,128)(2,1)S(1)} %get-tuple-element.63), channel_id=1, source_target_pairs={{0,4},{1,3},{2,6},{3,1},{4,0},{5,7},{6,2},{7,5},{8,12},{9,11},{10,... | collective-permute-start | bytes 221192 | tf_op jit(solution)/shard_map/ppermute | solution.py:330
  36.6 6.6 %collective-permute-start.14 = (bf16[2,3,3,16,128]{4,3,2,1,0:T(8,128)(2,1)S(1)}, bf16[2,3,3,16,128]{4,3,2,1,0:T(8,128)(2,1)S(1)}, u32[]{:S(2)}, u32[]{:S(2)}) collective-permute-start(bf16[2,3,3,16,128]{4,3,2,1,0:T(8,128)(2,1)S(1)} %add_convert_fusion.1), channel_id=1, source_target_pairs={{0,8},{1,9},{2,10},{3,11},{4,12},{5,13},{6,14},{7,15},{8,0},{9,1},... | collective-permute-start | bytes 221192 | tf_op jit(solution)/shard_map/ppermute | solution.py:330
  43.2 4.9 %collective-permute-start.17 = (bf16[2,3,3,16,128]{4,3,2,1,0:T(8,128)(2,1)S(1)}, bf16[2,3,3,16,128]{4,3,2,1,0:T(8,128)(2,1)S(1)}, u32[]{:S(2)}, u32[]{:S(2)}) collective-permute-start(bf16[2,3,3,16,128]{4,3,2,1,0:T(8,128)(2,1)S(1)} %add_convert_fusion.mine), channel_id=1, source_target_pairs={{0,4},{1,3},{2,6},{3,1},{4,0},{5,7},{6,2},{7,5},{8,12},{9,11},{10,... | collective-permute-start | bytes 221192 | tf_op jit(solution)/shard_map/ppermute | solution.py:330
  43.7 5.8 %collective-permute-start.16 = (bf16[2,3,3,16,128]{4,3,2,1,0:T(8,128)(2,1)S(1)}, bf16[2,3,3,16,128]{4,3,2,1,0:T(8,128)(2,1)S(1)}, u32[]{:S(2)}, u32[]{:S(2)}) collective-permute-start(bf16[2,3,3,16,128]{4,3,2,1,0:T(8,128)(2,1)S(1)} %add_convert_fusion.mine), channel_id=1, source_target_pairs={{0,2},{1,5},{2,0},{3,7},{4,6},{5,1},{6,4},{7,3},{8,10},{9,13},{10,... | collective-permute-start | bytes 221192 | tf_op jit(solution)/shard_map/ppermute | solution.py:330
  43.9 5.5 %collective-permute-start.15 = (bf16[2,3,3,16,128]{4,3,2,1,0:T(8,128)(2,1)S(1)}, bf16[2,3,3,16,128]{4,3,2,1,0:T(8,128)(2,1)S(1)}, u32[]{:S(2)}, u32[]{:S(2)}) collective-permute-start(bf16[2,3,3,16,128]{4,3,2,1,0:T(8,128)(2,1)S(1)} %add_convert_fusion.mine), channel_id=1, source_target_pairs={{0,6},{1,7},{2,4},{3,5},{4,2},{5,3},{6,0},{7,1},{8,14},{9,15},{10,... | collective-permute-start | bytes 221192 | tf_op jit(solution)/shard_map/ppermute | solution.py:330
  49.5 1.6 %collective-permute-start.18 = (bf16[2,3,3,64,128]{4,3,2,1,0:T(8,128)(2,1)S(1)}, bf16[2,3,3,64,128]{4,3,2,1,0:T(8,128)(2,1)S(1)}, u32[]{:S(2)}, u32[]{:S(2)}) collective-permute-start(bf16[2,3,3,64,128]{4,3,2,1,0:T(8,128)(2,1)S(1)} %shard_map.84.mine), channel_id=1, source_target_pairs={{0,1},{1,0},{2,3},{3,2},{4,5},{5,4},{6,7},{7,6},{8,9},{9,8},{10,11... | collective-permute-start | bytes 884744 | tf_op jit(solution)/shard_map/ppermute | solution.py:330

commit v13 on v12

--- a/solution.py
+++ b/solution.py
@@ -137,6 +137,14 @@
             hid[i] = jnp.where(even, at_even, at_odd)
 
 
+def rows_kernel(g, g_core, g_other, out):
+    even = lax.rem(lax.axis_index("rows"), 2) == 0
+    own = g.shape[0]
+    out[2 : own + 2] = g[...]
+    out[0:2] = jnp.where(even, g_other[...], g_core[own - 2 :])
+    out[own + 2 : own + 4] = jnp.where(even, g_core[:2], g_other[...])
+
+
 def joined(even, near, far, i):
     half = near.shape[0]
     if i < half:
@@ -153,10 +161,10 @@
 
 
 def middle_kernel(
-    segments, strips, near_here, far_here, near, far, near_first, far_first, g, g_core, g_other, second, out, gw, back, edge_other, yw
+    segments, strips, near_here, far_here, near, far, near_first, far_first, g, second, out, gw, back, edge_other, yw
 ):
     encoder, row, even = here(segments)
-    own = g.shape[0]
+    own = out.shape[0]
 
     @pl.when(encoder)
     def _():
@@ -172,14 +180,9 @@
         skip_pre = conv(yw, 0, own + 2, second)
         for i in range(own + 2):
             pre = skip_pre[i] + joined_first(even, near_first, far_first, i)
-            if i == 0:
-                upstream = jnp.where(even, g_other[1].astype(F32), g_core[own - 1].astype(F32))
-            elif i == own + 1:
-                upstream = jnp.where(even, g_core[0].astype(F32), g_other[0].astype(F32))
-            else:
-                upstream = g[i - 1].astype(F32)
+            if 1 <= i <= own:
                 out[i - 1] = silu(pre).astype(BF16)
-            value = masked(upstream * slope(pre), inside(row, strips, own, i - 1))
+            value = masked(g[i + 1].astype(F32) * slope(pre), inside(row, strips, own, i - 1))
             place(gw, i, value)
         back[...] = conv_back(gw, 0, own, second).astype(BF16)
         edge_other[...] = jnp.where(even, back[0:2], back[own - 2 : own])
@@ -194,33 +197,33 @@
     return put
 
 
-def edge_kernel(segments, strips, g_other, back_other, far_pre, edge_grad):
+def edge_kernel(segments, strips, g, back_other, far_pre, edge_grad):
     encoder, row, even = here(segments)
     far_in = jnp.where(even, row > 0, row < strips - 1)
 
     @pl.when(encoder)
     def _():
         for i in range(2):
-            value = g_other[i].astype(F32) + back_other[i].astype(F32)
+            value = g[jnp.where(even, 0, g.shape[0] - 2) + i].astype(F32) + back_other[i].astype(F32)
             value = value * slope(jnp.where(even, far_pre[i], far_pre[2 + i]))
             edge_grad[i] = masked(value, far_in).astype(BF16)
 
 
 def second_kernel(
-    segments, g, g_core, edge_grad, back, back_core, near_pre, far_pre, hid, near, far, gw, kept, sent, ew
+    segments, g, edge_grad, back, back_core, near_pre, far_pre, hid, near, far, gw, kept, sent, ew
 ):
     encoder, row, even = here(segments)
-    own = g.shape[0]
+    own = back.shape[0]
 
     @pl.when(encoder)
     def _():
         for i in range(2):
             place(ew, jnp.where(even, 0, own + 2) + i, edge_grad[i].astype(F32))
         for i in range(own):
-            value = g[i].astype(F32) + back[i].astype(F32)
+            value = g[i + 2].astype(F32) + back[i].astype(F32)
             place(ew, 2 + i, value * slope(joined(even, near_pre, far_pre, i + 2)))
         for i in range(2):
-            upstream = jnp.where(even, g_core[i].astype(F32), g_core[own - 2 + i].astype(F32))
+            upstream = g[jnp.where(even, own + 2, 0) + i].astype(F32)
             returned = jnp.where(even, back_core[i].astype(F32), back_core[own - 2 + i].astype(F32))
             value = (upstream + returned) * slope(jnp.where(even, near_pre[2 + i], near_pre[i]))
             place(ew, jnp.where(even, own + 2, 0) + i, value)
@@ -262,10 +265,14 @@
     return [pl.ds(pl.multiple_of(partner * rows, rows), rows) for partner in [quad] + partners]
 
 
-def pack_kernel(kept1, got1, kept2, got2, mine, *sends):
+def sum_kernel(kept, got, out):
+    out[...] = kept[...] + got[...].astype(F32)
+
+
+def pack_kernel(kept1, got1, total2, mine, *sends):
     for k, rows in enumerate(quarters(mine.shape[3])):
-        for t, (kept, got) in enumerate(((kept1, got1), (kept2, got2))):
-            value = kept[:, :, rows, :] + got[:, :, rows, :].astype(F32)
+        values = (kept1[:, :, rows, :] + got1[:, :, rows, :].astype(F32), total2[:, :, rows, :])
+        for t, value in enumerate(values):
             if k == 0:
                 mine[t] = value
             else:
@@ -354,6 +361,7 @@
     near_here, edge = lax.optimization_barrier((near_here, jnp.where(even, g_core[own - 2 :], g_core[:2])))
     near_there = swap(near_here, True, same)
     g_other = swap(edge, False, far)
+    (g_rows,) = call(rows_kernel, [like(own + 4, BF16)], [], (g, g_core, g_other), 2 * 10**9)
     far_first, far_pre, hid, far_here = call(
         functools.partial(far_kernel, segments, strips),
         [like(own, F32), like(own, F32), like(own, BF16), like(own, BF16)],
@@ -366,14 +374,14 @@
         functools.partial(middle_kernel, segments, strips),
         [like(own, BF16), wide_out(own + 2), like(own, BF16), like(2, BF16)],
         [wide(own + 4)],
-        (near_here, far_here, near_there, far_there, near_first, far_first, g, g_core, g_other, second),
+        (near_here, far_here, near_there, far_there, near_first, far_first, g_rows, second),
         work * (2 * own + 2),
     )
     back_own = swap(back, True, same)
     back_other = swap(edge_other, True, other)
     back_core = swap(back_own, False, core)
     (edge_grad,) = call(
-        functools.partial(edge_kernel, segments, strips), [like(2, BF16)], [], (g_other, back_other, far_pre), 2 * 10**9
+        functools.partial(edge_kernel, segments, strips), [like(2, BF16)], [], (g_rows, back_other, far_pre), 2 * 10**9
     )
     taps = (3, 3, channels, channels)
     halves = (3, 3, channels // 2, channels)
@@ -382,7 +390,7 @@
         functools.partial(second_kernel, segments),
         terms + [wide_out(own + 4)],
         [],
-        (g, g_core, edge_grad, back_own, back_core, near_pre, far_pre, hid, near_there, far_there, gw),
+        (g_rows, edge_grad, back_own, back_core, near_pre, far_pre, hid, near_there, far_there, gw),
         work * own,
     )
     kept1, sent1, hw = call(
@@ -403,12 +411,13 @@
 
     bits = strips.bit_length() - 1
     quarter = (2, 3, 3, channels // 8, channels)
-    got2, got1 = jump(sent2, 0), jump(sent1, 0)
+    (total2,) = call(sum_kernel, [jax.ShapeDtypeStruct(halves, F32)], [], (kept2, jump(sent2, 0)), 3 * 10**9)
+    got1 = jump(sent1, 0)
     mine, *sends = call(
         pack_kernel,
         [jax.ShapeDtypeStruct(quarter, F32)] + [jax.ShapeDtypeStruct(quarter, BF16)] * 3,
         [],
-        (kept1, got1, kept2, got2),
+        (kept1, got1, total2),
         kept1.size,
     )
     for turn, send in zip(TURNS, sends):

time: 52.4 us -> 52.3 us (level)
  starting transfers between devices: 22.7 us -> 20.7 us
  waiting for transfers between devices: 21.8 us -> 23.6 us
    ppermute x19, starting transfers between devices: 22.7 us -> 20.7 us  [swap(): return lax.ppermute(array, ('segment', 'rows'), pairs)]
    ppermute x19, waiting for transfers between devices: 21.8 us -> 23.6 us  [swap(): return lax.ppermute(array, ('segment', 'rows'), pairs)]
    pallas_call x11 -> x13, Pallas kernels: 6.9 us -> 6.93 us  [call(): pl.pallas_call(kernel, out_shape=outs, in_specs=[pl.BlockSpec(memory_spac...]
  transfers between devices with their start and end apart: 19 -> 19, of which waited for: 14 -> 13; matrix products, arithmetic and copies ran while one was open for 0% -> 0% of each run, Pallas kernels for 7% -> 10%
where the time goes in v13:
time: 52.3 us; the launch traced here: 52.1 us
  waiting for transfers between devices  23.6 us (45%)
  starting transfers between devices  20.7 us (40%)
  Pallas kernels  6.93 us (13%)
  between operations  0.77 us (1%)
    ppermute x19, waiting for transfers between devices, swap(): return lax.ppermute(array, ('segment', 'rows'), pairs)  23.6 us
    ppermute x19, starting transfers between devices, swap(): return lax.ppermute(array, ('segment', 'rows'), pairs)  20.7 us
    pallas_call x13, Pallas kernels, call(): pl.pallas_call(kernel, out_shape=outs, in_specs=[pl.BlockSpec(memory_spac...  6.93 us
  transfers between devices with their start and end apart: 19, of which 13 were waited for; matrix products, arithmetic and copies ran while one was open for 0% of the time, Pallas kernels for 10%

profile of v13, /device:TPU:0, one launch (start us, length us, event | category | flops | bytes accessed | tf_op | source)
XLA Modules:
  0.0 52.1 jit_solution(110290024061279944)
XLA Ops:
  0.6 0.5 collective-permute-start
  1.3 1.1 %collective-permute-done.x_core = bf16[4,128,128]{2,1,0:T(8,128)(2,1)S(1)} collective-permute-done((bf16[4,128,128]{2,1,0:T(8,128)(2,1)}, bf16[4,128,128]{2,1,0:T(8,128)(2,1)S(1)}, u32[]{:S(2)}, u32[]{:S(2)}) %collective-permute-start) | collective-permute-done | bytes 131104 | tf_op jit(solution)/shard_map/ppermute | solution.py:337
  2.3 2.8 %collective-permute-start.1 = (bf16[4,128,128]{2,1,0:T(8,128)(2,1)S(1)}, bf16[4,128,128]{2,1,0:T(8,128)(2,1)S(1)}, u32[]{:S(2)}, u32[]{:S(2)}) collective-permute-start(bf16[4,128,128]{2,1,0:T(8,128)(2,1)S(1)} %collective-permute-done.x_core), channel_id=1, source_target_pairs={{0,2},{1,0},{2,4},{3,1},{4,6},{5,3},{6,8},{7,5},{8,10},{9,7},{10,1... | collective-permute-start | bytes 393224 | tf_op jit(solution)/shard_map/ppermute | solution.py:337
  5.2 1.3 %shard_map.76 = (bf16[8,128,384]{2,1,0:T(8,128)(2,1)S(1)}, f32[6,128,128]{2,1,0:T(8,128)S(1)}, bf16[6,128,384]{2,1,0:T(8,128)(2,1)S(1)}, f32[4,128,128]{2,1,0:T(8,128)S(1)}, bf16[4,128,128]{2,1,0:T(8,128)(2,1)S(1)}) custom-call(f32[8,128]{1,0:T(8,128)S(1)} %shard_map.75.token, bf16[4,128,128]{2,1,0:T(8,128)(2,1)S(1)} %bitcast.16, ...), custom_call_target="tpu_custom_call" | custom-call | flops 377487360 | bytes 3018752 | tf_op jit(solution)/shard_map/pallas_call | solution.py:300
  6.5 1.6 %collective-permute-start.3 = (bf16[2,128,128]{2,1,0:T(8,128)(2,1)S(1)}, bf16[2,128,128]{2,1,0:T(8,128)(2,1)S(1)}, u32[]{:S(2)}, u32[]{:S(2)}) collective-permute-start(bf16[2,128,128]{2,1,0:T(8,128)(2,1)S(1)} %slice_select_fusion), channel_id=1, source_target_pairs={{0,2},{1,0},{2,4},{3,1},{4,6},{5,3},{6,8},{7,5},{8,10},{9,7},{10,1... | collective-permute-start | bytes 196616 | tf_op jit(solution)/shard_map/ppermute | solution.py:337
  8.1 1.0 %collective-permute-start.4 = (bf16[4,128,128]{2,1,0:T(8,128)(2,1)S(1)}, bf16[4,128,128]{2,1,0:T(8,128)(2,1)S(1)}, u32[]{:S(2)}, u32[]{:S(2)}) collective-permute-start(bf16[4,128,128]{2,1,0:T(8,128)(2,1)S(1)} %get-tuple-element.43.near_here), channel_id=1, source_target_pairs={{0,16},{1,17},{2,18},{3,19},{4,20},{5,21},{6,22},{7,23},{8,24},{9,... | collective-permute-start | bytes 393224 | tf_op jit(solution)/shard_map/ppermute | solution.py:337
  9.1 0.6 %collective-permute-done.1.x_far = bf16[4,128,128]{2,1,0:T(8,128)(2,1)S(1)} collective-permute-done((bf16[4,128,128]{2,1,0:T(8,128)(2,1)S(1)}, bf16[4,128,128]{2,1,0:T(8,128)(2,1)S(1)}, u32[]{:S(2)}, u32[]{:S(2)}) %collective-permute-start.1) | collective-permute-done | bytes 131104 | tf_op jit(solution)/shard_map/ppermute | solution.py:337
  9.8 1.3 %shard_map.77 = (f32[4,128,128]{2,1,0:T(8,128)S(1)}, f32[4,128,128]{2,1,0:T(8,128)S(1)}, bf16[4,128,128]{2,1,0:T(8,128)(2,1)S(1)}, bf16[4,128,128]{2,1,0:T(8,128)(2,1)S(1)}) custom-call(bf16[8,128,384]{2,1,0:T(8,128)(2,1)S(1)} %get-tuple-element.38.xa, bf16[6,128,384]{2,1,0:T(8,128)(2,1)S(1)} %get-tuple-element.39.ha, ...), custom_call_target="tpu_custom_call" | custom-call | flops 301989888 | bytes 2883584 | tf_op jit(solution)/shard_map/pallas_call | solution.py:300
  11.1 0.9 %collective-permute-start.5 = (bf16[4,128,128]{2,1,0:T(8,128)(2,1)S(1)}, bf16[4,128,128]{2,1,0:T(8,128)(2,1)S(1)}, u32[]{:S(2)}, u32[]{:S(2)}) collective-permute-start(bf16[4,128,128]{2,1,0:T(8,128)(2,1)S(1)} %get-tuple-element.44.far_here), channel_id=1, source_target_pairs={{0,16},{1,17},{2,18},{3,19},{4,20},{5,21},{6,22},{7,23},{8,24},{9,... | collective-permute-start | bytes 393224 | tf_op jit(solution)/shard_map/ppermute | solution.py:337
  12.0 2.4 %collective-permute-done.4.near = bf16[4,128,128]{2,1,0:T(8,128)(2,1)S(1)} collective-permute-done((bf16[4,128,128]{2,1,0:T(8,128)(2,1)S(1)}, bf16[4,128,128]{2,1,0:T(8,128)(2,1)S(1)}, u32[]{:S(2)}, u32[]{:S(2)}) %collective-permute-start.4) | collective-permute-done | bytes 131104 | tf_op jit(solution)/shard_map/ppermute | solution.py:337
  14.4 1.6 %collective-permute-done.5.far = bf16[4,128,128]{2,1,0:T(8,128)(2,1)S(1)} collective-permute-done((bf16[4,128,128]{2,1,0:T(8,128)(2,1)S(1)}, bf16[4,128,128]{2,1,0:T(8,128)(2,1)S(1)}, u32[]{:S(2)}, u32[]{:S(2)}) %collective-permute-start.5) | collective-permute-done | bytes 131104 | tf_op jit(solution)/shard_map/ppermute | solution.py:337
  16.1 2.5 %collective-permute-start.7 = (bf16[4,128,128]{2,1,0:T(8,128)(2,1)S(1)}, bf16[4,128,128]{2,1,0:T(8,128)(2,1)S(1)}, u32[]{:S(2)}, u32[]{:S(2)}) collective-permute-start(bf16[4,128,128]{2,1,0:T(8,128)(2,1)S(1)} %get-tuple-element.47), channel_id=1, source_target_pairs={{0,16},{1,17},{2,18},{3,19},{4,20},{5,21},{6,22},{7,23},{8,24},{9,... | collective-permute-start | bytes 393224 | tf_op jit(solution)/shard_map/ppermute | solution.py:337
  18.7 2.9 %collective-permute-done.7.back = bf16[4,128,128]{2,1,0:T(8,128)(2,1)S(1)} collective-permute-done((bf16[4,128,128]{2,1,0:T(8,128)(2,1)S(1)}, bf16[4,128,128]{2,1,0:T(8,128)(2,1)S(1)}, u32[]{:S(2)}, u32[]{:S(2)}) %collective-permute-start.7) | collective-permute-done | bytes 131104 | tf_op jit(solution)/shard_map/ppermute | solution.py:337
  21.6 2.0 %collective-permute-done.6.back_other = bf16[2,128,128]{2,1,0:T(8,128)(2,1)S(1)} collective-permute-done((bf16[2,128,128]{2,1,0:T(8,128)(2,1)S(1)}, bf16[2,128,128]{2,1,0:T(8,128)(2,1)S(1)}, u32[]{:S(2)}, u32[]{:S(2)}) %collective-permute-start.6) | collective-permute-done | bytes 65568 | tf_op jit(solution)/shard_map/ppermute | solution.py:337
  23.7 0.8 %shard_map.81 = (f32[3,3,64,128]{3,2,1,0:T(8,128)S(1)}, bf16[3,3,64,128]{3,2,1,0:T(8,128)(2,1)S(1)}, bf16[8,128,384]{2,1,0:T(8,128)(2,1)S(1)}) custom-call(bf16[8,128,128]{2,1,0:T(8,128)(2,1)S(1)} %shard_map.78.g, bf16[2,128,128]{2,1,0:T(8,128)(2,1)S(1)} %shard_map.80.edge_grad, bf16[4,128,128]{2,1,0:T(8,128)(2,1)S(1)} %collective-permute-done.7.back, ...), custom_call_target="tpu_custom_call" | custom-call | flops 150994944 | bytes 3325952 | tf_op jit(solution)/shard_map/pallas_call | solution.py:300
  24.5 1.1 %shard_map.82 = (f32[3,3,64,128]{3,2,1,0:T(8,128)S(1)}, bf16[3,3,64,128]{3,2,1,0:T(8,128)(2,1)S(1)}, bf16[6,128,384]{2,1,0:T(8,128)(2,1)S(1)}) custom-call(bf16[4,128,128]{2,1,0:T(8,128)(2,1)S(1)} %bitcast.17, f32[6,128,128]{2,1,0:T(8,128)S(1)} %get-tuple-element.37.near_first, f32[4,128,128]{2,1,0:T(8,128)S(1)} %get-tuple-element.40.far_first, ...), custom_call_target="tpu_custom_call" | custom-call | flops 377487360 | bytes 3489792 | tf_op jit(solution)/shard_map/pallas_call | solution.py:300
  25.7 0.5 %collective-permute-start.9 = (bf16[3,3,64,128]{3,2,1,0:T(8,128)(2,1)S(1)}, bf16[3,3,64,128]{3,2,1,0:T(8,128)(2,1)S(1)}, u32[]{:S(2)}, u32[]{:S(2)}) collective-permute-start(bf16[3,3,64,128]{3,2,1,0:T(8,128)(2,1)S(1)} %get-tuple-element.57), channel_id=1, source_target_pairs={{0,1},{1,0},{2,3},{3,2},{4,5},{5,4},{6,7},{7,6},{8,9},{9,8},{10,11... | collective-permute-start | bytes 442376 | tf_op jit(solution)/shard_map/ppermute | solution.py:337
  26.3 1.0 %collective-permute-done.9.got1 = bf16[3,3,64,128]{3,2,1,0:T(8,128)(2,1)S(1)} collective-permute-done((bf16[3,3,64,128]{3,2,1,0:T(8,128)(2,1)S(1)}, bf16[3,3,64,128]{3,2,1,0:T(8,128)(2,1)S(1)}, u32[]{:S(2)}, u32[]{:S(2)}) %collective-permute-start.9) | collective-permute-done | bytes 147488 | tf_op jit(solution)/shard_map/ppermute | solution.py:337
  27.3 3.8 %collective-permute-start.11 = (bf16[2,3,3,16,128]{4,3,2,1,0:T(8,128)(2,1)S(1)}, bf16[2,3,3,16,128]{4,3,2,1,0:T(8,128)(2,1)S(1)}, u32[]{:S(2)}, u32[]{:S(2)}) collective-permute-start(bf16[2,3,3,16,128]{4,3,2,1,0:T(8,128)(2,1)S(1)} %get-tuple-element.61), channel_id=1, source_target_pairs={{0,6},{1,7},{2,4},{3,5},{4,2},{5,3},{6,0},{7,1},{8,14},{9,15},{10,... | collective-permute-start | bytes 221192 | tf_op jit(solution)/shard_map/ppermute | solution.py:337
  31.1 0.6 %collective-permute-start.13 = (bf16[2,3,3,16,128]{4,3,2,1,0:T(8,128)(2,1)S(1)}, bf16[2,3,3,16,128]{4,3,2,1,0:T(8,128)(2,1)S(1)}, u32[]{:S(2)}, u32[]{:S(2)}) collective-permute-start(bf16[2,3,3,16,128]{4,3,2,1,0:T(8,128)(2,1)S(1)} %get-tuple-element.63), channel_id=1, source_target_pairs={{0,4},{1,3},{2,6},{3,1},{4,0},{5,7},{6,2},{7,5},{8,12},{9,11},{10,... | collective-permute-start | bytes 221192 | tf_op jit(solution)/shard_map/ppermute | solution.py:337
  31.7 2.5 %collective-permute-done.11 = bf16[2,3,3,16,128]{4,3,2,1,0:T(8,128)(2,1)S(1)} collective-permute-done((bf16[2,3,3,16,128]{4,3,2,1,0:T(8,128)(2,1)S(1)}, bf16[2,3,3,16,128]{4,3,2,1,0:T(8,128)(2,1)S(1)}, u32[]{:S(2)}, u32[]{:S(2)}) %collective-permute-start.11) | collective-permute-done | bytes 73760 | tf_op jit(solution)/shard_map/ppermute | solution.py:337
  34.2 1.4 %collective-permute-done.12 = bf16[2,3,3,16,128]{4,3,2,1,0:T(8,128)(2,1)S(1)} collective-permute-done((bf16[2,3,3,16,128]{4,3,2,1,0:T(8,128)(2,1)S(1)}, bf16[2,3,3,16,128]{4,3,2,1,0:T(8,128)(2,1)S(1)}, u32[]{:S(2)}, u32[]{:S(2)}) %collective-permute-start.12) | collective-permute-done | bytes 73760 | tf_op jit(solution)/shard_map/ppermute | solution.py:337
  35.7 2.5 %collective-permute-start.14 = (bf16[2,3,3,16,128]{4,3,2,1,0:T(8,128)(2,1)S(1)}, bf16[2,3,3,16,128]{4,3,2,1,0:T(8,128)(2,1)S(1)}, u32[]{:S(2)}, u32[]{:S(2)}) collective-permute-start(bf16[2,3,3,16,128]{4,3,2,1,0:T(8,128)(2,1)S(1)} %add_convert_fusion.1), channel_id=1, source_target_pairs={{0,8},{1,9},{2,10},{3,11},{4,12},{5,13},{6,14},{7,15},{8,0},{9,1},... | collective-permute-start | bytes 221192 | tf_op jit(solution)/shard_map/ppermute | solution.py:337
  38.2 4.2 %collective-permute-done.14 = bf16[2,3,3,16,128]{4,3,2,1,0:T(8,128)(2,1)S(1)} collective-permute-done((bf16[2,3,3,16,128]{4,3,2,1,0:T(8,128)(2,1)S(1)}, bf16[2,3,3,16,128]{4,3,2,1,0:T(8,128)(2,1)S(1)}, u32[]{:S(2)}, u32[]{:S(2)}) %collective-permute-start.14) | collective-permute-done | bytes 73760 | tf_op jit(solution)/shard_map/ppermute | solution.py:337
  42.4 0.3 collective-permute-start.17
  42.7 1.4 %collective-permute-start.16 = (bf16[2,3,3,16,128]{4,3,2,1,0:T(8,128)(2,1)S(1)}, bf16[2,3,3,16,128]{4,3,2,1,0:T(8,128)(2,1)S(1)}, u32[]{:S(2)}, u32[]{:S(2)}) collective-permute-start(bf16[2,3,3,16,128]{4,3,2,1,0:T(8,128)(2,1)S(1)} %add_convert_fusion.mine), channel_id=1, source_target_pairs={{0,2},{1,5},{2,0},{3,7},{4,6},{5,1},{6,4},{7,3},{8,10},{9,13},{10,... | collective-permute-start | bytes 221192 | tf_op jit(solution)/shard_map/ppermute | solution.py:337
  44.1 1.9 %collective-permute-start.15 = (bf16[2,3,3,16,128]{4,3,2,1,0:T(8,128)(2,1)S(1)}, bf16[2,3,3,16,128]{4,3,2,1,0:T(8,128)(2,1)S(1)}, u32[]{:S(2)}, u32[]{:S(2)}) collective-permute-start(bf16[2,3,3,16,128]{4,3,2,1,0:T(8,128)(2,1)S(1)} %add_convert_fusion.mine), channel_id=1, source_target_pairs={{0,6},{1,7},{2,4},{3,5},{4,2},{5,3},{6,0},{7,1},{8,14},{9,15},{10,... | collective-permute-start | bytes 221192 | tf_op jit(solution)/shard_map/ppermute | solution.py:337
  46.0 1.6 %collective-permute-done.17.rest_2_ = bf16[2,3,3,16,128]{4,3,2,1,0:T(8,128)(2,1)S(1)} collective-permute-done((bf16[2,3,3,16,128]{4,3,2,1,0:T(8,128)(2,1)S(1)}, bf16[2,3,3,16,128]{4,3,2,1,0:T(8,128)(2,1)S(1)}, u32[]{:S(2)}, u32[]{:S(2)}) %collective-permute-start.17) | collective-permute-done | bytes 73760 | tf_op jit(solution)/shard_map/ppermute | solution.py:337
  47.7 1.7 %collective-permute-done.15.rest_0_ = bf16[2,3,3,16,128]{4,3,2,1,0:T(8,128)(2,1)S(1)} collective-permute-done((bf16[2,3,3,16,128]{4,3,2,1,0:T(8,128)(2,1)S(1)}, bf16[2,3,3,16,128]{4,3,2,1,0:T(8,128)(2,1)S(1)}, u32[]{:S(2)}, u32[]{:S(2)}) %collective-permute-start.15) | collective-permute-done | bytes 73760 | tf_op jit(solution)/shard_map/ppermute | solution.py:337
  49.5 1.1 %shard_map.83 = (bf16[4,128,128]{2,1,0:T(8,128)(2,1)}, bf16[4,128,128]{2,1,0:T(8,128)(2,1)}) custom-call(bf16[6,128,384]{2,1,0:T(8,128)(2,1)S(1)} %get-tuple-element.52.hw, bf16[3,3,128,128]{3,2,1,0:T(8,128)(2,1)S(1)} %bitcast.14, bf16[4,128,128]{2,1,0:T(8,128)(2,1)S(1)} %get-tuple-element.53.out), custom_call_target="tpu_custom_call" | custom-call | flops 150994944 | bytes 1277952 | tf_op jit(solution)/shard_map/pallas_call | solution.py:300
  50.6 0.4 collective-permute-done.18.theirs
  51.0 1.1 %shard_map.87 = (f32[3,3,128,128]{3,2,1,0:T(8,128)}, f32[3,3,128,128]{3,2,1,0:T(8,128)}) custom-call(bf16[2,3,3,64,128]{4,3,2,1,0:T(8,128)(2,1)S(1)} %shard_map.86.mine, bf16[2,3,3,64,128]{4,3,2,1,0:T(8,128)(2,1)S(1)} %collective-permute-done.18.theirs), custom_call_target="tpu_custom_call" | custom-call | flops 73728 | bytes 1769472 | tf_op jit(solution)/shard_map/pallas_call | solution.py:300
  (30 shorter events, 0.7 us)
Async XLA Ops:
  0.6 1.7 %collective-permute-start = (bf16[4,128,128]{2,1,0:T(8,128)(2,1)}, bf16[4,128,128]{2,1,0:T(8,128)(2,1)S(1)}, u32[]{:S(2)}, u32[]{:S(2)}) collective-permute-start(bf16[4,128,128]{2,1,0:T(8,128)(2,1)} %bitcast.15), channel_id=1, source_target_pairs={{0,1},{1,0},{2,3},{3,2},{4,5},{5,4},{6,7},{7,6},{8,9},{9,8},{10,11... | collective-permute-start | bytes 393224 | tf_op jit(solution)/shard_map/ppermute | solution.py:337
  1.1 4.1 %copy-start = (bf16[1,3,3,128,128]{4,3,2,1,0:T(8,128)(2,1)S(1)}, bf16[1,3,3,128,128]{4,3,2,1,0:T(8,128)(2,1)}, u32[]{:S(2)}) copy-start(bf16[1,3,3,128,128]{4,3,2,1,0:T(8,128)(2,1)} %param.7) | copy-start | bytes 884740
  1.2 4.1 %copy-start.1 = (bf16[1,3,3,128,128]{4,3,2,1,0:T(8,128)(2,1)S(1)}, bf16[1,3,3,128,128]{4,3,2,1,0:T(8,128)(2,1)}, u32[]{:S(2)}) copy-start(bf16[1,3,3,128,128]{4,3,2,1,0:T(8,128)(2,1)} %param.6) | copy-start | bytes 884740
  1.2 4.0 %collective-permute-start.2 = (bf16[4,128,128]{2,1,0:T(8,128)(2,1)}, bf16[4,128,128]{2,1,0:T(8,128)(2,1)S(1)}, u32[]{:S(2)}, u32[]{:S(2)}) collective-permute-start(bf16[4,128,128]{2,1,0:T(8,128)(2,1)} %bitcast.18), channel_id=1, source_target_pairs={{0,1},{1,0},{2,3},{3,2},{4,5},{5,4},{6,7},{7,6},{8,9},{9,8},{10,11... | collective-permute-start | bytes 393224 | tf_op jit(solution)/shard_map/ppermute | solution.py:337
  1.3 4.0 %copy-start.2 = (bf16[1,4,128,128]{3,2,1,0:T(8,128)(2,1)S(1)}, bf16[1,4,128,128]{3,2,1,0:T(8,128)(2,1)}, u32[]{:S(2)}) copy-start(bf16[1,4,128,128]{3,2,1,0:T(8,128)(2,1)} %param.4) | copy-start | bytes 393220
  2.3 7.4 %collective-permute-start.1 = (bf16[4,128,128]{2,1,0:T(8,128)(2,1)S(1)}, bf16[4,128,128]{2,1,0:T(8,128)(2,1)S(1)}, u32[]{:S(2)}, u32[]{:S(2)}) collective-permute-start(bf16[4,128,128]{2,1,0:T(8,128)(2,1)S(1)} %collective-permute-done.x_core), channel_id=1, source_target_pairs={{0,2},{1,0},{2,4},{3,1},{4,6},{5,3},{6,8},{7,5},{8,10},{9,7},{10,1... | collective-permute-start | bytes 393224 | tf_op jit(solution)/shard_map/ppermute | solution.py:337
  6.5 5.4 %collective-permute-start.3 = (bf16[2,128,128]{2,1,0:T(8,128)(2,1)S(1)}, bf16[2,128,128]{2,1,0:T(8,128)(2,1)S(1)}, u32[]{:S(2)}, u32[]{:S(2)}) collective-permute-start(bf16[2,128,128]{2,1,0:T(8,128)(2,1)S(1)} %slice_select_fusion), channel_id=1, source_target_pairs={{0,2},{1,0},{2,4},{3,1},{4,6},{5,3},{6,8},{7,5},{8,10},{9,7},{10,1... | collective-permute-start | bytes 196616 | tf_op jit(solution)/shard_map/ppermute | solution.py:337
  8.1 6.3 %collective-permute-start.4 = (bf16[4,128,128]{2,1,0:T(8,128)(2,1)S(1)}, bf16[4,128,128]{2,1,0:T(8,128)(2,1)S(1)}, u32[]{:S(2)}, u32[]{:S(2)}) collective-permute-start(bf16[4,128,128]{2,1,0:T(8,128)(2,1)S(1)} %get-tuple-element.43.near_here), channel_id=1, source_target_pairs={{0,16},{1,17},{2,18},{3,19},{4,20},{5,21},{6,22},{7,23},{8,24},{9,... | collective-permute-start | bytes 393224 | tf_op jit(solution)/shard_map/ppermute | solution.py:337
  9.8 2.2 %copy-start.3 = (bf16[1,4,128,128]{3,2,1,0:T(8,128)(2,1)S(1)}, bf16[1,4,128,128]{3,2,1,0:T(8,128)(2,1)}, u32[]{:S(2)}) copy-start(bf16[1,4,128,128]{3,2,1,0:T(8,128)(2,1)} %param.5) | copy-start | bytes 393220
  11.1 5.0 %collective-permute-start.5 = (bf16[4,128,128]{2,1,0:T(8,128)(2,1)S(1)}, bf16[4,128,128]{2,1,0:T(8,128)(2,1)S(1)}, u32[]{:S(2)}, u32[]{:S(2)}) collective-permute-start(bf16[4,128,128]{2,1,0:T(8,128)(2,1)S(1)} %get-tuple-element.44.far_here), channel_id=1, source_target_pairs={{0,16},{1,17},{2,18},{3,19},{4,20},{5,21},{6,22},{7,23},{8,24},{9,... | collective-permute-start | bytes 393224 | tf_op jit(solution)/shard_map/ppermute | solution.py:337
  16.1 5.5 %collective-permute-start.7 = (bf16[4,128,128]{2,1,0:T(8,128)(2,1)S(1)}, bf16[4,128,128]{2,1,0:T(8,128)(2,1)S(1)}, u32[]{:S(2)}, u32[]{:S(2)}) collective-permute-start(bf16[4,128,128]{2,1,0:T(8,128)(2,1)S(1)} %get-tuple-element.47), channel_id=1, source_target_pairs={{0,16},{1,17},{2,18},{3,19},{4,20},{5,21},{6,22},{7,23},{8,24},{9,... | collective-permute-start | bytes 393224 | tf_op jit(solution)/shard_map/ppermute | solution.py:337
  18.7 4.9 %collective-permute-start.6 = (bf16[2,128,128]{2,1,0:T(8,128)(2,1)S(1)}, bf16[2,128,128]{2,1,0:T(8,128)(2,1)S(1)}, u32[]{:S(2)}, u32[]{:S(2)}) collective-permute-start(bf16[2,128,128]{2,1,0:T(8,128)(2,1)S(1)} %get-tuple-element.45), channel_id=1, source_target_pairs={{0,16},{1,18},{2,17},{3,20},{4,19},{5,22},{6,21},{7,24},{8,23},{9,... | collective-permute-start | bytes 196616 | tf_op jit(solution)/shard_map/ppermute | solution.py:337
  21.6 2.1 %collective-permute-start.8 = (bf16[4,128,128]{2,1,0:T(8,128)(2,1)S(1)}, bf16[4,128,128]{2,1,0:T(8,128)(2,1)S(1)}, u32[]{:S(2)}, u32[]{:S(2)}) collective-permute-start(bf16[4,128,128]{2,1,0:T(8,128)(2,1)S(1)} %collective-permute-done.7.back), channel_id=1, source_target_pairs={{0,1},{1,0},{2,3},{3,2},{4,5},{5,4},{6,7},{7,6},{8,9},{9,8},{10,11... | collective-permute-start | bytes 393224 | tf_op jit(solution)/shard_map/ppermute | solution.py:337
  24.4 1.8 %collective-permute-start.10 = (bf16[3,3,64,128]{3,2,1,0:T(8,128)(2,1)S(1)}, bf16[3,3,64,128]{3,2,1,0:T(8,128)(2,1)S(1)}, u32[]{:S(2)}, u32[]{:S(2)}) collective-permute-start(bf16[3,3,64,128]{3,2,1,0:T(8,128)(2,1)S(1)} %get-tuple-element.59), channel_id=1, source_target_pairs={{0,1},{1,0},{2,3},{3,2},{4,5},{5,4},{6,7},{7,6},{8,9},{9,8},{10,11... | collective-permute-start | bytes 442376 | tf_op jit(solution)/shard_map/ppermute | solution.py:337
  25.7 1.6 %collective-permute-start.9 = (bf16[3,3,64,128]{3,2,1,0:T(8,128)(2,1)S(1)}, bf16[3,3,64,128]{3,2,1,0:T(8,128)(2,1)S(1)}, u32[]{:S(2)}, u32[]{:S(2)}) collective-permute-start(bf16[3,3,64,128]{3,2,1,0:T(8,128)(2,1)S(1)} %get-tuple-element.57), channel_id=1, source_target_pairs={{0,1},{1,0},{2,3},{3,2},{4,5},{5,4},{6,7},{7,6},{8,9},{9,8},{10,11... | collective-permute-start | bytes 442376 | tf_op jit(solution)/shard_map/ppermute | solution.py:337
  27.3 6.9 %collective-permute-start.11 = (bf16[2,3,3,16,128]{4,3,2,1,0:T(8,128)(2,1)S(1)}, bf16[2,3,3,16,128]{4,3,2,1,0:T(8,128)(2,1)S(1)}, u32[]{:S(2)}, u32[]{:S(2)}) collective-permute-start(bf16[2,3,3,16,128]{4,3,2,1,0:T(8,128)(2,1)S(1)} %get-tuple-element.61), channel_id=1, source_target_pairs={{0,6},{1,7},{2,4},{3,5},{4,2},{5,3},{6,0},{7,1},{8,14},{9,15},{10,... | collective-permute-start | bytes 221192 | tf_op jit(solution)/shard_map/ppermute | solution.py:337
  31.1 4.6 %collective-permute-start.12 = (bf16[2,3,3,16,128]{4,3,2,1,0:T(8,128)(2,1)S(1)}, bf16[2,3,3,16,128]{4,3,2,1,0:T(8,128)(2,1)S(1)}, u32[]{:S(2)}, u32[]{:S(2)}) collective-permute-start(bf16[2,3,3,16,128]{4,3,2,1,0:T(8,128)(2,1)S(1)} %get-tuple-element.62), channel_id=1, source_target_pairs={{0,2},{1,5},{2,0},{3,7},{4,6},{5,1},{6,4},{7,3},{8,10},{9,13},{10,... | collective-permute-start | bytes 221192 | tf_op jit(solution)/shard_map/ppermute | solution.py:337
  31.1 4.6 %collective-permute-start.13 = (bf16[2,3,3,16,128]{4,3,2,1,0:T(8,128)(2,1)S(1)}, bf16[2,3,3,16,128]{4,3,2,1,0:T(8,128)(2,1)S(1)}, u32[]{:S(2)}, u32[]{:S(2)}) collective-permute-start(bf16[2,3,3,16,128]{4,3,2,1,0:T(8,128)(2,1)S(1)} %get-tuple-element.63), channel_id=1, source_target_pairs={{0,4},{1,3},{2,6},{3,1},{4,0},{5,7},{6,2},{7,5},{8,12},{9,11},{10,... | collective-permute-start | bytes 221192 | tf_op jit(solution)/shard_map/ppermute | solution.py:337
  35.7 6.7 %collective-permute-start.14 = (bf16[2,3,3,16,128]{4,3,2,1,0:T(8,128)(2,1)S(1)}, bf16[2,3,3,16,128]{4,3,2,1,0:T(8,128)(2,1)S(1)}, u32[]{:S(2)}, u32[]{:S(2)}) collective-permute-start(bf16[2,3,3,16,128]{4,3,2,1,0:T(8,128)(2,1)S(1)} %add_convert_fusion.1), channel_id=1, source_target_pairs={{0,8},{1,9},{2,10},{3,11},{4,12},{5,13},{6,14},{7,15},{8,0},{9,1},... | collective-permute-start | bytes 221192 | tf_op jit(solution)/shard_map/ppermute | solution.py:337
  42.4 5.2 %collective-permute-start.17 = (bf16[2,3,3,16,128]{4,3,2,1,0:T(8,128)(2,1)S(1)}, bf16[2,3,3,16,128]{4,3,2,1,0:T(8,128)(2,1)S(1)}, u32[]{:S(2)}, u32[]{:S(2)}) collective-permute-start(bf16[2,3,3,16,128]{4,3,2,1,0:T(8,128)(2,1)S(1)} %add_convert_fusion.mine), channel_id=1, source_target_pairs={{0,4},{1,3},{2,6},{3,1},{4,0},{5,7},{6,2},{7,5},{8,12},{9,11},{10,... | collective-permute-start | bytes 221192 | tf_op jit(solution)/shard_map/ppermute | solution.py:337
  42.7 5.0 %collective-permute-start.16 = (bf16[2,3,3,16,128]{4,3,2,1,0:T(8,128)(2,1)S(1)}, bf16[2,3,3,16,128]{4,3,2,1,0:T(8,128)(2,1)S(1)}, u32[]{:S(2)}, u32[]{:S(2)}) collective-permute-start(bf16[2,3,3,16,128]{4,3,2,1,0:T(8,128)(2,1)S(1)} %add_convert_fusion.mine), channel_id=1, source_target_pairs={{0,2},{1,5},{2,0},{3,7},{4,6},{5,1},{6,4},{7,3},{8,10},{9,13},{10,... | collective-permute-start | bytes 221192 | tf_op jit(solution)/shard_map/ppermute | solution.py:337
  44.1 5.3 %collective-permute-start.15 = (bf16[2,3,3,16,128]{4,3,2,1,0:T(8,128)(2,1)S(1)}, bf16[2,3,3,16,128]{4,3,2,1,0:T(8,128)(2,1)S(1)}, u32[]{:S(2)}, u32[]{:S(2)}) collective-permute-start(bf16[2,3,3,16,128]{4,3,2,1,0:T(8,128)(2,1)S(1)} %add_convert_fusion.mine), channel_id=1, source_target_pairs={{0,6},{1,7},{2,4},{3,5},{4,2},{5,3},{6,0},{7,1},{8,14},{9,15},{10,... | collective-permute-start | bytes 221192 | tf_op jit(solution)/shard_map/ppermute | solution.py:337
  49.4 1.6 %collective-permute-start.18 = (bf16[2,3,3,64,128]{4,3,2,1,0:T(8,128)(2,1)S(1)}, bf16[2,3,3,64,128]{4,3,2,1,0:T(8,128)(2,1)S(1)}, u32[]{:S(2)}, u32[]{:S(2)}) collective-permute-start(bf16[2,3,3,64,128]{4,3,2,1,0:T(8,128)(2,1)S(1)} %shard_map.86.mine), channel_id=1, source_target_pairs={{0,1},{1,0},{2,3},{3,2},{4,5},{5,4},{6,7},{7,6},{8,9},{9,8},{10,11... | collective-permute-start | bytes 884744 | tf_op jit(solution)/shard_map/ppermute | solution.py:337

commit v14 on v13

--- a/solution.py
+++ b/solution.py
@@ -86,7 +86,7 @@
     token[...] = jnp.zeros_like(token)
 
 
-def near_kernel(segments, token, x, x_core, main, second, xa, first, ha, pre, skip):
+def near_kernel(segments, token, x, x_core, main, second, xa, first, ha, pre, skip, skip_own):
     encoder, _, even = here(segments)
     own = x.shape[0]
     for i in range(own):
@@ -101,6 +101,7 @@
         pre[...] = conv(ha, 0, 2 * own - 4, second)
         for i in range(2 * own - 4):
             skip[i] = silu(pre[i]).astype(BF16)
+        skip_own[...] = jnp.where(even, skip[0:2], skip[own - 2 : own])
 
 
 def far_kernel(segments, strips, xa, ha, x_far, main, second, first, pre, hid, skip, xb, hb):
@@ -161,7 +162,7 @@
 
 
 def middle_kernel(
-    segments, strips, near_here, far_here, near, far, near_first, far_first, g, second, out, gw, back, edge_other, yw
+    segments, strips, near_here, far_here, near_own, near_core, far, near_first, far_first, g, second, out, gw, back, edge_other, yw
 ):
     encoder, row, even = here(segments)
     own = out.shape[0]
@@ -173,10 +174,11 @@
 
     @pl.when(jnp.logical_not(encoder))
     def _():
-        half = near.shape[0]
-        for i in range(half):
-            place(yw, jnp.where(even, half, 0) + i, near[i].astype(F32))
-            place(yw, jnp.where(even, 0, half) + i, far[i].astype(F32))
+        for i in range(2):
+            place(yw, jnp.where(even, own, own - 2) + i, near_own[i].astype(F32))
+            place(yw, jnp.where(even, own + 2, 0) + i, near_core[i].astype(F32))
+        for i in range(own):
+            place(yw, jnp.where(even, 0, own) + i, far[i].astype(F32))
         skip_pre = conv(yw, 0, own + 2, second)
         for i in range(own + 2):
             pre = skip_pre[i] + joined_first(even, near_first, far_first, i)
@@ -210,7 +212,7 @@
 
 
 def second_kernel(
-    segments, g, edge_grad, back, back_core, near_pre, far_pre, hid, near, far, gw, kept, sent, ew
+    segments, g, edge_grad, back, back_core, near_pre, far_pre, hid, near_own, far, gw, kept, sent, ew
 ):
     encoder, row, even = here(segments)
     own = back.shape[0]
@@ -231,7 +233,10 @@
 
     @pl.when(jnp.logical_not(encoder))
     def _():
-        skip = jnp.stack([joined(even, near, far, i + 2) for i in range(own)])
+        half = own // 2
+        rows = [jnp.where(even, far[own - half + i], near_own[i]) for i in range(half)]
+        rows += [jnp.where(even, near_own[i], far[i]) for i in range(half)]
+        skip = jnp.stack(rows)
         conv_weight(skip, gw, 0, store(even, kept, sent))
 
 
@@ -351,15 +356,15 @@
     g_core = swap(g, False, core)
     x_core, token = lax.optimization_barrier((x_core, token))
     x_far = swap(x_core, False, far)
-    xa, near_first, ha, near_pre, near_here = call(
+    xa, near_first, ha, near_pre, near_here, near_sent = call(
         functools.partial(near_kernel, segments),
-        [wide_out(2 * own), like(2 * own - 2, F32), wide_out(2 * own - 2), like(2 * own - 4, F32), like(2 * own - 4, BF16)],
+        [wide_out(2 * own), like(2 * own - 2, F32), wide_out(2 * own - 2), like(2 * own - 4, F32), like(2 * own - 4, BF16), like(2, BF16)],
         [],
         (token, x, x_core, main, second),
         work * (4 * own - 6),
     )
-    near_here, edge = lax.optimization_barrier((near_here, jnp.where(even, g_core[own - 2 :], g_core[:2])))
-    near_there = swap(near_here, True, same)
+    near_sent, edge = lax.optimization_barrier((near_sent, jnp.where(even, g_core[own - 2 :], g_core[:2])))
+    near_own = swap(near_sent, True, same)
     g_other = swap(edge, False, far)
     (g_rows,) = call(rows_kernel, [like(own + 4, BF16)], [], (g, g_core, g_other), 2 * 10**9)
     far_first, far_pre, hid, far_here = call(
@@ -370,11 +375,13 @@
         work * 2 * own,
     )
     far_there = swap(far_here, True, same)
+    near_own, hid = lax.optimization_barrier((near_own, hid))
+    near_core = swap(near_own, False, core)
     out, gw, back, edge_other = call(
         functools.partial(middle_kernel, segments, strips),
         [like(own, BF16), wide_out(own + 2), like(own, BF16), like(2, BF16)],
         [wide(own + 4)],
-        (near_here, far_here, near_there, far_there, near_first, far_first, g_rows, second),
+        (near_here, far_here, near_own, near_core, far_there, near_first, far_first, g_rows, second),
         work * (2 * own + 2),
     )
     back_own = swap(back, True, same)
@@ -390,7 +397,7 @@
         functools.partial(second_kernel, segments),
         terms + [wide_out(own + 4)],
         [],
-        (g_rows, edge_grad, back_own, back_core, near_pre, far_pre, hid, near_there, far_there, gw),
+        (g_rows, edge_grad, back_own, back_core, near_pre, far_pre, hid, near_own, far_there, gw),
         work * own,
     )
     kept1, sent1, hw = call(

time: 52.3 us -> 53.4 us (1.021)
  starting transfers between devices: 20.7 us -> 21.5 us
    ppermute x19 -> x20, starting transfers between devices: 20.7 us -> 21.5 us  [swap(): return lax.ppermute(array, ('segment', 'rows'), pairs)]
    ppermute x19 -> x20, waiting for transfers between devices: 23.6 us -> 23.9 us  [swap(): return lax.ppermute(array, ('segment', 'rows'), pairs)]
  transfers between devices with their start and end apart: 19 -> 20, of which waited for: 13 -> 13; matrix products, arithmetic and copies ran while one was open for 0% -> 0% of each run, Pallas kernels for 10% -> 9%
where the time goes in v14:
time: 53.4 us; the launch traced here: 53.2 us
  waiting for transfers between devices  23.9 us (45%)
  starting transfers between devices  21.5 us (40%)
  Pallas kernels  6.95 us (13%)
  between operations  0.76 us (1%)
    ppermute x20, waiting for transfers between devices, swap(): return lax.ppermute(array, ('segment', 'rows'), pairs)  23.9 us
    ppermute x20, starting transfers between devices, swap(): return lax.ppermute(array, ('segment', 'rows'), pairs)  21.5 us
    pallas_call x13, Pallas kernels, call(): pl.pallas_call(kernel, out_shape=outs, in_specs=[pl.BlockSpec(memory_spac...  6.95 us
  transfers between devices with their start and end apart: 20, of which 13 were waited for; matrix products, arithmetic and copies ran while one was open for 0% of the time, Pallas kernels for 9%

profile of v14, /device:TPU:0, one launch (start us, length us, event | category | flops | bytes accessed | tf_op | source)
XLA Modules:
  0.0 53.2 jit_solution(12201444956296374359)
XLA Ops:
  0.6 0.5 collective-permute-start
  1.3 1.1 %collective-permute-done.x_core = bf16[4,128,128]{2,1,0:T(8,128)(2,1)S(1)} collective-permute-done((bf16[4,128,128]{2,1,0:T(8,128)(2,1)}, bf16[4,128,128]{2,1,0:T(8,128)(2,1)S(1)}, u32[]{:S(2)}, u32[]{:S(2)}) %collective-permute-start) | collective-permute-done | bytes 131104 | tf_op jit(solution)/shard_map/ppermute | solution.py:342
  2.3 2.8 %collective-permute-start.1 = (bf16[4,128,128]{2,1,0:T(8,128)(2,1)S(1)}, bf16[4,128,128]{2,1,0:T(8,128)(2,1)S(1)}, u32[]{:S(2)}, u32[]{:S(2)}) collective-permute-start(bf16[4,128,128]{2,1,0:T(8,128)(2,1)S(1)} %collective-permute-done.x_core), channel_id=1, source_target_pairs={{0,2},{1,0},{2,4},{3,1},{4,6},{5,3},{6,8},{7,5},{8,10},{9,7},{10,1... | collective-permute-start | bytes 393224 | tf_op jit(solution)/shard_map/ppermute | solution.py:342
  5.2 1.3 %shard_map.76 = (bf16[8,128,384]{2,1,0:T(8,128)(2,1)S(1)}, f32[6,128,128]{2,1,0:T(8,128)S(1)}, bf16[6,128,384]{2,1,0:T(8,128)(2,1)S(1)}, f32[4,128,128]{2,1,0:T(...) custom-call(f32[8,128]{1,0:T(8,128)S(1)} %shard_map.75.token, ...), custom_call_target="tpu_custom_call" | custom-call | flops 377487360 | bytes 3084288 | tf_op jit(solution)/shard_map/pallas_call | solution.py:305
  6.5 1.1 %collective-permute-start.4 = (bf16[2,128,128]{2,1,0:T(8,128)(2,1)S(1)}, bf16[2,128,128]{2,1,0:T(8,128)(2,1)S(1)}, u32[]{:S(2)}, u32[]{:S(2)}) collective-permute-start(bf16[2,128,128]{2,1,0:T(8,128)(2,1)S(1)} %get-tuple-element.48), channel_id=1, source_target_pairs={{0,16},{1,17},{2,18},{3,19},{4,20},{5,21},{6,22},{7,23},{8,24},{9,... | collective-permute-start | bytes 196616 | tf_op jit(solution)/shard_map/ppermute | solution.py:342
  7.6 1.5 %collective-permute-start.3 = (bf16[2,128,128]{2,1,0:T(8,128)(2,1)S(1)}, bf16[2,128,128]{2,1,0:T(8,128)(2,1)S(1)}, u32[]{:S(2)}, u32[]{:S(2)}) collective-permute-start(bf16[2,128,128]{2,1,0:T(8,128)(2,1)S(1)} %slice_select_fusion), channel_id=1, source_target_pairs={{0,2},{1,0},{2,4},{3,1},{4,6},{5,3},{6,8},{7,5},{8,10},{9,7},{10,1... | collective-permute-start | bytes 196616 | tf_op jit(solution)/shard_map/ppermute | solution.py:342
  9.2 1.3 %shard_map.77 = (f32[4,128,128]{2,1,0:T(8,128)S(1)}, f32[4,128,128]{2,1,0:T(8,128)S(1)}, bf16[4,128,128]{2,1,0:T(8,128)(2,1)S(1)}, bf16[4,128,128]{2,1,0:T(8,128)(2,1)S(1)}) custom-call(bf16[8,128,384]{2,1,0:T(8,128)(2,1)S(1)} %get-tuple-element.41.xa, bf16[6,128,384]{2,1,0:T(8,128)(2,1)S(1)} %get-tuple-element.42.ha, ...), custom_call_target="tpu_custom_call" | custom-call | flops 301989888 | bytes 2883584 | tf_op jit(solution)/shard_map/pallas_call | solution.py:305
  10.4 0.5 collective-permute-done.4.near_own
  10.9 1.2 %collective-permute-start.6 = (bf16[4,128,128]{2,1,0:T(8,128)(2,1)S(1)}, bf16[4,128,128]{2,1,0:T(8,128)(2,1)S(1)}, u32[]{:S(2)}, u32[]{:S(2)}) collective-permute-start(bf16[4,128,128]{2,1,0:T(8,128)(2,1)S(1)} %get-tuple-element.47.far_here), channel_id=1, source_target_pairs={{0,16},{1,17},{2,18},{3,19},{4,20},{5,21},{6,22},{7,23},{8,24},{9,... | collective-permute-start | bytes 393224 | tf_op jit(solution)/shard_map/ppermute | solution.py:342
  12.1 4.7 %collective-permute-done.6.far = bf16[4,128,128]{2,1,0:T(8,128)(2,1)S(1)} collective-permute-done((bf16[4,128,128]{2,1,0:T(8,128)(2,1)S(1)}, bf16[4,128,128]{2,1,0:T(8,128)(2,1)S(1)}, u32[]{:S(2)}, u32[]{:S(2)}) %collective-permute-start.6) | collective-permute-done | bytes 131104 | tf_op jit(solution)/shard_map/ppermute | solution.py:342
  16.8 2.8 %collective-permute-start.8 = (bf16[4,128,128]{2,1,0:T(8,128)(2,1)S(1)}, bf16[4,128,128]{2,1,0:T(8,128)(2,1)S(1)}, u32[]{:S(2)}, u32[]{:S(2)}) collective-permute-start(bf16[4,128,128]{2,1,0:T(8,128)(2,1)S(1)} %get-tuple-element.53), channel_id=1, source_target_pairs={{0,16},{1,17},{2,18},{3,19},{4,20},{5,21},{6,22},{7,23},{8,24},{9,... | collective-permute-start | bytes 393224 | tf_op jit(solution)/shard_map/ppermute | solution.py:342
  19.7 3.2 %collective-permute-done.8.back = bf16[4,128,128]{2,1,0:T(8,128)(2,1)S(1)} collective-permute-done((bf16[4,128,128]{2,1,0:T(8,128)(2,1)S(1)}, bf16[4,128,128]{2,1,0:T(8,128)(2,1)S(1)}, u32[]{:S(2)}, u32[]{:S(2)}) %collective-permute-start.8) | collective-permute-done | bytes 131104 | tf_op jit(solution)/shard_map/ppermute | solution.py:342
  22.9 1.6 %collective-permute-done.7.back_other = bf16[2,128,128]{2,1,0:T(8,128)(2,1)S(1)} collective-permute-done((bf16[2,128,128]{2,1,0:T(8,128)(2,1)S(1)}, bf16[2,128,128]{2,1,0:T(8,128)(2,1)S(1)}, u32[]{:S(2)}, u32[]{:S(2)}) %collective-permute-start.7) | collective-permute-done | bytes 65568 | tf_op jit(solution)/shard_map/ppermute | solution.py:342
  24.6 0.8 %shard_map.81 = (f32[3,3,64,128]{3,2,1,0:T(8,128)S(1)}, bf16[3,3,64,128]{3,2,1,0:T(8,128)(2,1)S(1)}, bf16[8,128,384]{2,1,0:T(8,128)(2,1)S(1)}) custom-call(bf16[8,128,128]{2,1,0:T(8,128)(2,1)S(1)} %shard_map.78.g, bf16[2,128,128]{2,1,0:T(8,128)(2,1)S(1)} %shard_map.80.edge_grad, bf16[4,128,128]{2,1,0:T(8,128)(2,1)S(1)} %collective-permute-done.8.back, ...), custom_call_target="tpu_custom_call" | custom-call | flops 150994944 | bytes 3260416 | tf_op jit(solution)/shard_map/pallas_call | solution.py:305
  25.5 1.1 %shard_map.82 = (f32[3,3,64,128]{3,2,1,0:T(8,128)S(1)}, bf16[3,3,64,128]{3,2,1,0:T(8,128)(2,1)S(1)}, bf16[6,128,384]{2,1,0:T(8,128)(2,1)S(1)}) custom-call(bf16[4,128,128]{2,1,0:T(8,128)(2,1)S(1)} %bitcast.17, f32[6,128,128]{2,1,0:T(8,128)S(1)} %get-tuple-element.40.near_first, f32[4,128,128]{2,1,0:T(8,128)S(1)} %get-tuple-element.43.far_first, ...), custom_call_target="tpu_custom_call" | custom-call | flops 377487360 | bytes 3489792 | tf_op jit(solution)/shard_map/pallas_call | solution.py:305
  26.6 0.5 %collective-permute-start.10 = (bf16[3,3,64,128]{3,2,1,0:T(8,128)(2,1)S(1)}, bf16[3,3,64,128]{3,2,1,0:T(8,128)(2,1)S(1)}, u32[]{:S(2)}, u32[]{:S(2)}) collective-permute-start(bf16[3,3,64,128]{3,2,1,0:T(8,128)(2,1)S(1)} %get-tuple-element.63), channel_id=1, source_target_pairs={{0,1},{1,0},{2,3},{3,2},{4,5},{5,4},{6,7},{7,6},{8,9},{9,8},{10,11... | collective-permute-start | bytes 442376 | tf_op jit(solution)/shard_map/ppermute | solution.py:342
  27.2 1.0 %collective-permute-done.10.got1 = bf16[3,3,64,128]{3,2,1,0:T(8,128)(2,1)S(1)} collective-permute-done((bf16[3,3,64,128]{3,2,1,0:T(8,128)(2,1)S(1)}, bf16[3,3,64,128]{3,2,1,0:T(8,128)(2,1)S(1)}, u32[]{:S(2)}, u32[]{:S(2)}) %collective-permute-start.10) | collective-permute-done | bytes 147488 | tf_op jit(solution)/shard_map/ppermute | solution.py:342
  28.2 3.9 %collective-permute-start.12 = (bf16[2,3,3,16,128]{4,3,2,1,0:T(8,128)(2,1)S(1)}, bf16[2,3,3,16,128]{4,3,2,1,0:T(8,128)(2,1)S(1)}, u32[]{:S(2)}, u32[]{:S(2)}) collective-permute-start(bf16[2,3,3,16,128]{4,3,2,1,0:T(8,128)(2,1)S(1)} %get-tuple-element.67), channel_id=1, source_target_pairs={{0,6},{1,7},{2,4},{3,5},{4,2},{5,3},{6,0},{7,1},{8,14},{9,15},{10,... | collective-permute-start | bytes 221192 | tf_op jit(solution)/shard_map/ppermute | solution.py:342
  32.2 0.6 %collective-permute-start.14 = (bf16[2,3,3,16,128]{4,3,2,1,0:T(8,128)(2,1)S(1)}, bf16[2,3,3,16,128]{4,3,2,1,0:T(8,128)(2,1)S(1)}, u32[]{:S(2)}, u32[]{:S(2)}) collective-permute-start(bf16[2,3,3,16,128]{4,3,2,1,0:T(8,128)(2,1)S(1)} %get-tuple-element.69), channel_id=1, source_target_pairs={{0,4},{1,3},{2,6},{3,1},{4,0},{5,7},{6,2},{7,5},{8,12},{9,11},{10,... | collective-permute-start | bytes 221192 | tf_op jit(solution)/shard_map/ppermute | solution.py:342
  32.8 2.5 %collective-permute-done.12 = bf16[2,3,3,16,128]{4,3,2,1,0:T(8,128)(2,1)S(1)} collective-permute-done((bf16[2,3,3,16,128]{4,3,2,1,0:T(8,128)(2,1)S(1)}, bf16[2,3,3,16,128]{4,3,2,1,0:T(8,128)(2,1)S(1)}, u32[]{:S(2)}, u32[]{:S(2)}) %collective-permute-start.12) | collective-permute-done | bytes 73760 | tf_op jit(solution)/shard_map/ppermute | solution.py:342
  35.3 1.4 %collective-permute-done.13 = bf16[2,3,3,16,128]{4,3,2,1,0:T(8,128)(2,1)S(1)} collective-permute-done((bf16[2,3,3,16,128]{4,3,2,1,0:T(8,128)(2,1)S(1)}, bf16[2,3,3,16,128]{4,3,2,1,0:T(8,128)(2,1)S(1)}, u32[]{:S(2)}, u32[]{:S(2)}) %collective-permute-start.13) | collective-permute-done | bytes 73760 | tf_op jit(solution)/shard_map/ppermute | solution.py:342
  36.8 2.6 %collective-permute-start.15 = (bf16[2,3,3,16,128]{4,3,2,1,0:T(8,128)(2,1)S(1)}, bf16[2,3,3,16,128]{4,3,2,1,0:T(8,128)(2,1)S(1)}, u32[]{:S(2)}, u32[]{:S(2)}) collective-permute-start(bf16[2,3,3,16,128]{4,3,2,1,0:T(8,128)(2,1)S(1)} %add_convert_fusion.1), channel_id=1, source_target_pairs={{0,8},{1,9},{2,10},{3,11},{4,12},{5,13},{6,14},{7,15},{8,0},{9,1},... | collective-permute-start | bytes 221192 | tf_op jit(solution)/shard_map/ppermute | solution.py:342
  39.4 4.0 %collective-permute-done.15 = bf16[2,3,3,16,128]{4,3,2,1,0:T(8,128)(2,1)S(1)} collective-permute-done((bf16[2,3,3,16,128]{4,3,2,1,0:T(8,128)(2,1)S(1)}, bf16[2,3,3,16,128]{4,3,2,1,0:T(8,128)(2,1)S(1)}, u32[]{:S(2)}, u32[]{:S(2)}) %collective-permute-start.15) | collective-permute-done | bytes 73760 | tf_op jit(solution)/shard_map/ppermute | solution.py:342
  43.4 0.3 collective-permute-start.18
  43.8 1.4 %collective-permute-start.17 = (bf16[2,3,3,16,128]{4,3,2,1,0:T(8,128)(2,1)S(1)}, bf16[2,3,3,16,128]{4,3,2,1,0:T(8,128)(2,1)S(1)}, u32[]{:S(2)}, u32[]{:S(2)}) collective-permute-start(bf16[2,3,3,16,128]{4,3,2,1,0:T(8,128)(2,1)S(1)} %add_convert_fusion.mine), channel_id=1, source_target_pairs={{0,2},{1,5},{2,0},{3,7},{4,6},{5,1},{6,4},{7,3},{8,10},{9,13},{10,... | collective-permute-start | bytes 221192 | tf_op jit(solution)/shard_map/ppermute | solution.py:342
  45.2 1.8 %collective-permute-start.16 = (bf16[2,3,3,16,128]{4,3,2,1,0:T(8,128)(2,1)S(1)}, bf16[2,3,3,16,128]{4,3,2,1,0:T(8,128)(2,1)S(1)}, u32[]{:S(2)}, u32[]{:S(2)}) collective-permute-start(bf16[2,3,3,16,128]{4,3,2,1,0:T(8,128)(2,1)S(1)} %add_convert_fusion.mine), channel_id=1, source_target_pairs={{0,6},{1,7},{2,4},{3,5},{4,2},{5,3},{6,0},{7,1},{8,14},{9,15},{10,... | collective-permute-start | bytes 221192 | tf_op jit(solution)/shard_map/ppermute | solution.py:342
  47.0 1.7 %collective-permute-done.18.rest_2_ = bf16[2,3,3,16,128]{4,3,2,1,0:T(8,128)(2,1)S(1)} collective-permute-done((bf16[2,3,3,16,128]{4,3,2,1,0:T(8,128)(2,1)S(1)}, bf16[2,3,3,16,128]{4,3,2,1,0:T(8,128)(2,1)S(1)}, u32[]{:S(2)}, u32[]{:S(2)}) %collective-permute-start.18) | collective-permute-done | bytes 73760 | tf_op jit(solution)/shard_map/ppermute | solution.py:342
  48.6 0.2 collective-permute-done.17.rest_1_
  48.8 1.6 %collective-permute-done.16.rest_0_ = bf16[2,3,3,16,128]{4,3,2,1,0:T(8,128)(2,1)S(1)} collective-permute-done((bf16[2,3,3,16,128]{4,3,2,1,0:T(8,128)(2,1)S(1)}, bf16[2,3,3,16,128]{4,3,2,1,0:T(8,128)(2,1)S(1)}, u32[]{:S(2)}, u32[]{:S(2)}) %collective-permute-start.16) | collective-permute-done | bytes 73760 | tf_op jit(solution)/shard_map/ppermute | solution.py:342
  50.6 1.1 %shard_map.83 = (bf16[4,128,128]{2,1,0:T(8,128)(2,1)}, bf16[4,128,128]{2,1,0:T(8,128)(2,1)}) custom-call(bf16[6,128,384]{2,1,0:T(8,128)(2,1)S(1)} %get-tuple-element.58.hw, bf16[3,3,128,128]{3,2,1,0:T(8,128)(2,1)S(1)} %bitcast.14, bf16[4,128,128]{2,1,0:T(8,128)(2,1)S(1)} %get-tuple-element.59.out), custom_call_target="tpu_custom_call" | custom-call | flops 150994944 | bytes 1277952 | tf_op jit(solution)/shard_map/pallas_call | solution.py:305
  51.7 0.4 collective-permute-done.19.theirs
  52.1 1.1 %shard_map.87 = (f32[3,3,128,128]{3,2,1,0:T(8,128)}, f32[3,3,128,128]{3,2,1,0:T(8,128)}) custom-call(bf16[2,3,3,64,128]{4,3,2,1,0:T(8,128)(2,1)S(1)} %shard_map.86.mine, bf16[2,3,3,64,128]{4,3,2,1,0:T(8,128)(2,1)S(1)} %collective-permute-done.19.theirs), custom_call_target="tpu_custom_call" | custom-call | flops 73728 | bytes 1769472 | tf_op jit(solution)/shard_map/pallas_call | solution.py:305
  (32 shorter events, 0.7 us)
Async XLA Ops:
  0.6 1.7 %collective-permute-start = (bf16[4,128,128]{2,1,0:T(8,128)(2,1)}, bf16[4,128,128]{2,1,0:T(8,128)(2,1)S(1)}, u32[]{:S(2)}, u32[]{:S(2)}) collective-permute-start(bf16[4,128,128]{2,1,0:T(8,128)(2,1)} %bitcast.15), channel_id=1, source_target_pairs={{0,1},{1,0},{2,3},{3,2},{4,5},{5,4},{6,7},{7,6},{8,9},{9,8},{10,11... | collective-permute-start | bytes 393224 | tf_op jit(solution)/shard_map/ppermute | solution.py:342
  1.1 4.1 %copy-start = (bf16[1,3,3,128,128]{4,3,2,1,0:T(8,128)(2,1)S(1)}, bf16[1,3,3,128,128]{4,3,2,1,0:T(8,128)(2,1)}, u32[]{:S(2)}) copy-start(bf16[1,3,3,128,128]{4,3,2,1,0:T(8,128)(2,1)} %param.7) | copy-start | bytes 884740
  1.2 4.1 %copy-start.1 = (bf16[1,3,3,128,128]{4,3,2,1,0:T(8,128)(2,1)S(1)}, bf16[1,3,3,128,128]{4,3,2,1,0:T(8,128)(2,1)}, u32[]{:S(2)}) copy-start(bf16[1,3,3,128,128]{4,3,2,1,0:T(8,128)(2,1)} %param.6) | copy-start | bytes 884740
  1.2 4.0 %collective-permute-start.2 = (bf16[4,128,128]{2,1,0:T(8,128)(2,1)}, bf16[4,128,128]{2,1,0:T(8,128)(2,1)S(1)}, u32[]{:S(2)}, u32[]{:S(2)}) collective-permute-start(bf16[4,128,128]{2,1,0:T(8,128)(2,1)} %bitcast.18), channel_id=1, source_target_pairs={{0,1},{1,0},{2,3},{3,2},{4,5},{5,4},{6,7},{7,6},{8,9},{9,8},{10,11... | collective-permute-start | bytes 393224 | tf_op jit(solution)/shard_map/ppermute | solution.py:342
  1.3 4.0 %copy-start.2 = (bf16[1,4,128,128]{3,2,1,0:T(8,128)(2,1)S(1)}, bf16[1,4,128,128]{3,2,1,0:T(8,128)(2,1)}, u32[]{:S(2)}) copy-start(bf16[1,4,128,128]{3,2,1,0:T(8,128)(2,1)} %param.4) | copy-start | bytes 393220
  2.3 6.8 %collective-permute-start.1 = (bf16[4,128,128]{2,1,0:T(8,128)(2,1)S(1)}, bf16[4,128,128]{2,1,0:T(8,128)(2,1)S(1)}, u32[]{:S(2)}, u32[]{:S(2)}) collective-permute-start(bf16[4,128,128]{2,1,0:T(8,128)(2,1)S(1)} %collective-permute-done.x_core), channel_id=1, source_target_pairs={{0,2},{1,0},{2,4},{3,1},{4,6},{5,3},{6,8},{7,5},{8,10},{9,7},{10,1... | collective-permute-start | bytes 393224 | tf_op jit(solution)/shard_map/ppermute | solution.py:342
  6.5 4.3 %collective-permute-start.4 = (bf16[2,128,128]{2,1,0:T(8,128)(2,1)S(1)}, bf16[2,128,128]{2,1,0:T(8,128)(2,1)S(1)}, u32[]{:S(2)}, u32[]{:S(2)}) collective-permute-start(bf16[2,128,128]{2,1,0:T(8,128)(2,1)S(1)} %get-tuple-element.48), channel_id=1, source_target_pairs={{0,16},{1,17},{2,18},{3,19},{4,20},{5,21},{6,22},{7,23},{8,24},{9,... | collective-permute-start | bytes 196616 | tf_op jit(solution)/shard_map/ppermute | solution.py:342
  7.6 4.5 %collective-permute-start.3 = (bf16[2,128,128]{2,1,0:T(8,128)(2,1)S(1)}, bf16[2,128,128]{2,1,0:T(8,128)(2,1)S(1)}, u32[]{:S(2)}, u32[]{:S(2)}) collective-permute-start(bf16[2,128,128]{2,1,0:T(8,128)(2,1)S(1)} %slice_select_fusion), channel_id=1, source_target_pairs={{0,2},{1,0},{2,4},{3,1},{4,6},{5,3},{6,8},{7,5},{8,10},{9,7},{10,1... | collective-permute-start | bytes 196616 | tf_op jit(solution)/shard_map/ppermute | solution.py:342
  9.2 2.9 %copy-start.3 = (bf16[1,4,128,128]{3,2,1,0:T(8,128)(2,1)S(1)}, bf16[1,4,128,128]{3,2,1,0:T(8,128)(2,1)}, u32[]{:S(2)}) copy-start(bf16[1,4,128,128]{3,2,1,0:T(8,128)(2,1)} %param.5) | copy-start | bytes 393220
  10.9 1.3 %collective-permute-start.5 = (bf16[2,128,128]{2,1,0:T(8,128)(2,1)S(1)}, bf16[2,128,128]{2,1,0:T(8,128)(2,1)S(1)}, u32[]{:S(2)}, u32[]{:S(2)}) collective-permute-start(bf16[2,128,128]{2,1,0:T(8,128)(2,1)S(1)} %collective-permute-done.4.near_own), channel_id=1, source_target_pairs={{0,1},{1,0},{2,3},{3,2},{4,5},{5,4},{6,7},{7,6},{8,9},{9,8},{10,11... | collective-permute-start | bytes 196616 | tf_op jit(solution)/shard_map/ppermute | solution.py:342
  10.9 5.9 %collective-permute-start.6 = (bf16[4,128,128]{2,1,0:T(8,128)(2,1)S(1)}, bf16[4,128,128]{2,1,0:T(8,128)(2,1)S(1)}, u32[]{:S(2)}, u32[]{:S(2)}) collective-permute-start(bf16[4,128,128]{2,1,0:T(8,128)(2,1)S(1)} %get-tuple-element.47.far_here), channel_id=1, source_target_pairs={{0,16},{1,17},{2,18},{3,19},{4,20},{5,21},{6,22},{7,23},{8,24},{9,... | collective-permute-start | bytes 393224 | tf_op jit(solution)/shard_map/ppermute | solution.py:342
  16.8 6.1 %collective-permute-start.8 = (bf16[4,128,128]{2,1,0:T(8,128)(2,1)S(1)}, bf16[4,128,128]{2,1,0:T(8,128)(2,1)S(1)}, u32[]{:S(2)}, u32[]{:S(2)}) collective-permute-start(bf16[4,128,128]{2,1,0:T(8,128)(2,1)S(1)} %get-tuple-element.53), channel_id=1, source_target_pairs={{0,16},{1,17},{2,18},{3,19},{4,20},{5,21},{6,22},{7,23},{8,24},{9,... | collective-permute-start | bytes 393224 | tf_op jit(solution)/shard_map/ppermute | solution.py:342
  19.6 4.9 %collective-permute-start.7 = (bf16[2,128,128]{2,1,0:T(8,128)(2,1)S(1)}, bf16[2,128,128]{2,1,0:T(8,128)(2,1)S(1)}, u32[]{:S(2)}, u32[]{:S(2)}) collective-permute-start(bf16[2,128,128]{2,1,0:T(8,128)(2,1)S(1)} %get-tuple-element.51), channel_id=1, source_target_pairs={{0,16},{1,18},{2,17},{3,20},{4,19},{5,22},{6,21},{7,24},{8,23},{9,... | collective-permute-start | bytes 196616 | tf_op jit(solution)/shard_map/ppermute | solution.py:342
  22.9 1.7 %collective-permute-start.9 = (bf16[4,128,128]{2,1,0:T(8,128)(2,1)S(1)}, bf16[4,128,128]{2,1,0:T(8,128)(2,1)S(1)}, u32[]{:S(2)}, u32[]{:S(2)}) collective-permute-start(bf16[4,128,128]{2,1,0:T(8,128)(2,1)S(1)} %collective-permute-done.8.back), channel_id=1, source_target_pairs={{0,1},{1,0},{2,3},{3,2},{4,5},{5,4},{6,7},{7,6},{8,9},{9,8},{10,11... | collective-permute-start | bytes 393224 | tf_op jit(solution)/shard_map/ppermute | solution.py:342
  25.4 1.8 %collective-permute-start.11 = (bf16[3,3,64,128]{3,2,1,0:T(8,128)(2,1)S(1)}, bf16[3,3,64,128]{3,2,1,0:T(8,128)(2,1)S(1)}, u32[]{:S(2)}, u32[]{:S(2)}) collective-permute-start(bf16[3,3,64,128]{3,2,1,0:T(8,128)(2,1)S(1)} %get-tuple-element.65), channel_id=1, source_target_pairs={{0,1},{1,0},{2,3},{3,2},{4,5},{5,4},{6,7},{7,6},{8,9},{9,8},{10,11... | collective-permute-start | bytes 442376 | tf_op jit(solution)/shard_map/ppermute | solution.py:342
  26.6 1.5 %collective-permute-start.10 = (bf16[3,3,64,128]{3,2,1,0:T(8,128)(2,1)S(1)}, bf16[3,3,64,128]{3,2,1,0:T(8,128)(2,1)S(1)}, u32[]{:S(2)}, u32[]{:S(2)}) collective-permute-start(bf16[3,3,64,128]{3,2,1,0:T(8,128)(2,1)S(1)} %get-tuple-element.63), channel_id=1, source_target_pairs={{0,1},{1,0},{2,3},{3,2},{4,5},{5,4},{6,7},{7,6},{8,9},{9,8},{10,11... | collective-permute-start | bytes 442376 | tf_op jit(solution)/shard_map/ppermute | solution.py:342
  28.2 7.0 %collective-permute-start.12 = (bf16[2,3,3,16,128]{4,3,2,1,0:T(8,128)(2,1)S(1)}, bf16[2,3,3,16,128]{4,3,2,1,0:T(8,128)(2,1)S(1)}, u32[]{:S(2)}, u32[]{:S(2)}) collective-permute-start(bf16[2,3,3,16,128]{4,3,2,1,0:T(8,128)(2,1)S(1)} %get-tuple-element.67), channel_id=1, source_target_pairs={{0,6},{1,7},{2,4},{3,5},{4,2},{5,3},{6,0},{7,1},{8,14},{9,15},{10,... | collective-permute-start | bytes 221192 | tf_op jit(solution)/shard_map/ppermute | solution.py:342
  32.2 4.6 %collective-permute-start.13 = (bf16[2,3,3,16,128]{4,3,2,1,0:T(8,128)(2,1)S(1)}, bf16[2,3,3,16,128]{4,3,2,1,0:T(8,128)(2,1)S(1)}, u32[]{:S(2)}, u32[]{:S(2)}) collective-permute-start(bf16[2,3,3,16,128]{4,3,2,1,0:T(8,128)(2,1)S(1)} %get-tuple-element.68), channel_id=1, source_target_pairs={{0,2},{1,5},{2,0},{3,7},{4,6},{5,1},{6,4},{7,3},{8,10},{9,13},{10,... | collective-permute-start | bytes 221192 | tf_op jit(solution)/shard_map/ppermute | solution.py:342
  32.2 4.6 %collective-permute-start.14 = (bf16[2,3,3,16,128]{4,3,2,1,0:T(8,128)(2,1)S(1)}, bf16[2,3,3,16,128]{4,3,2,1,0:T(8,128)(2,1)S(1)}, u32[]{:S(2)}, u32[]{:S(2)}) collective-permute-start(bf16[2,3,3,16,128]{4,3,2,1,0:T(8,128)(2,1)S(1)} %get-tuple-element.69), channel_id=1, source_target_pairs={{0,4},{1,3},{2,6},{3,1},{4,0},{5,7},{6,2},{7,5},{8,12},{9,11},{10,... | collective-permute-start | bytes 221192 | tf_op jit(solution)/shard_map/ppermute | solution.py:342
  36.8 6.6 %collective-permute-start.15 = (bf16[2,3,3,16,128]{4,3,2,1,0:T(8,128)(2,1)S(1)}, bf16[2,3,3,16,128]{4,3,2,1,0:T(8,128)(2,1)S(1)}, u32[]{:S(2)}, u32[]{:S(2)}) collective-permute-start(bf16[2,3,3,16,128]{4,3,2,1,0:T(8,128)(2,1)S(1)} %add_convert_fusion.1), channel_id=1, source_target_pairs={{0,8},{1,9},{2,10},{3,11},{4,12},{5,13},{6,14},{7,15},{8,0},{9,1},... | collective-permute-start | bytes 221192 | tf_op jit(solution)/shard_map/ppermute | solution.py:342
  43.4 5.2 %collective-permute-start.18 = (bf16[2,3,3,16,128]{4,3,2,1,0:T(8,128)(2,1)S(1)}, bf16[2,3,3,16,128]{4,3,2,1,0:T(8,128)(2,1)S(1)}, u32[]{:S(2)}, u32[]{:S(2)}) collective-permute-start(bf16[2,3,3,16,128]{4,3,2,1,0:T(8,128)(2,1)S(1)} %add_convert_fusion.mine), channel_id=1, source_target_pairs={{0,4},{1,3},{2,6},{3,1},{4,0},{5,7},{6,2},{7,5},{8,12},{9,11},{10,... | collective-permute-start | bytes 221192 | tf_op jit(solution)/shard_map/ppermute | solution.py:342
  43.8 5.0 %collective-permute-start.17 = (bf16[2,3,3,16,128]{4,3,2,1,0:T(8,128)(2,1)S(1)}, bf16[2,3,3,16,128]{4,3,2,1,0:T(8,128)(2,1)S(1)}, u32[]{:S(2)}, u32[]{:S(2)}) collective-permute-start(bf16[2,3,3,16,128]{4,3,2,1,0:T(8,128)(2,1)S(1)} %add_convert_fusion.mine), channel_id=1, source_target_pairs={{0,2},{1,5},{2,0},{3,7},{4,6},{5,1},{6,4},{7,3},{8,10},{9,13},{10,... | collective-permute-start | bytes 221192 | tf_op jit(solution)/shard_map/ppermute | solution.py:342
  45.2 5.3 %collective-permute-start.16 = (bf16[2,3,3,16,128]{4,3,2,1,0:T(8,128)(2,1)S(1)}, bf16[2,3,3,16,128]{4,3,2,1,0:T(8,128)(2,1)S(1)}, u32[]{:S(2)}, u32[]{:S(2)}) collective-permute-start(bf16[2,3,3,16,128]{4,3,2,1,0:T(8,128)(2,1)S(1)} %add_convert_fusion.mine), channel_id=1, source_target_pairs={{0,6},{1,7},{2,4},{3,5},{4,2},{5,3},{6,0},{7,1},{8,14},{9,15},{10,... | collective-permute-start | bytes 221192 | tf_op jit(solution)/shard_map/ppermute | solution.py:342
  50.5 1.6 %collective-permute-start.19 = (bf16[2,3,3,64,128]{4,3,2,1,0:T(8,128)(2,1)S(1)}, bf16[2,3,3,64,128]{4,3,2,1,0:T(8,128)(2,1)S(1)}, u32[]{:S(2)}, u32[]{:S(2)}) collective-permute-start(bf16[2,3,3,64,128]{4,3,2,1,0:T(8,128)(2,1)S(1)} %shard_map.86.mine), channel_id=1, source_target_pairs={{0,1},{1,0},{2,3},{3,2},{4,5},{5,4},{6,7},{7,6},{8,9},{9,8},{10,11... | collective-permute-start | bytes 884744 | tf_op jit(solution)/shard_map/ppermute | solution.py:342

commit v15 on v14

--- a/solution.py
+++ b/solution.py
@@ -375,7 +375,7 @@
         work * 2 * own,
     )
     far_there = swap(far_here, True, same)
-    near_own, hid = lax.optimization_barrier((near_own, hid))
+    near_own, g_rows = lax.optimization_barrier((near_own, g_rows))
     near_core = swap(near_own, False, core)
     out, gw, back, edge_other = call(
         functools.partial(middle_kernel, segments, strips),

time: 53.4 us -> 52.2 us (0.978)
  starting transfers between devices: 21.5 us -> 20.7 us
    ppermute x20, starting transfers between devices: 21.5 us -> 20.7 us  [swap(): return lax.ppermute(array, ('segment', 'rows'), pairs)]
  transfers between devices with their start and end apart: 20 -> 20, of which waited for: 13 -> 15; matrix products, arithmetic and copies ran while one was open for 0% -> 0% of each run, Pallas kernels for 9% -> 10%
where the time goes in v15:
time: 52.2 us; the launch traced here: 52.1 us
  waiting for transfers between devices  23.6 us (45%)
  starting transfers between devices  20.7 us (40%)
  Pallas kernels  6.93 us (13%)
  between operations  0.76 us (1%)
    ppermute x20, waiting for transfers between devices, swap(): return lax.ppermute(array, ('segment', 'rows'), pairs)  23.6 us
    ppermute x20, starting transfers between devices, swap(): return lax.ppermute(array, ('segment', 'rows'), pairs)  20.7 us
    pallas_call x13, Pallas kernels, call(): pl.pallas_call(kernel, out_shape=outs, in_specs=[pl.BlockSpec(memory_spac...  6.93 us
  transfers between devices with their start and end apart: 20, of which 15 were waited for; matrix products, arithmetic and copies ran while one was open for 0% of the time, Pallas kernels for 10%

profile of v15, /device:TPU:0, one launch (start us, length us, event | category | flops | bytes accessed | tf_op | source)
XLA Modules:
  0.0 52.1 jit_solution(430226910804372417)
XLA Ops:
  0.6 0.5 collective-permute-start
  1.3 1.1 %collective-permute-done.x_core = bf16[4,128,128]{2,1,0:T(8,128)(2,1)S(1)} collective-permute-done((bf16[4,128,128]{2,1,0:T(8,128)(2,1)}, bf16[4,128,128]{2,1,0:T(8,128)(2,1)S(1)}, u32[]{:S(2)}, u32[]{:S(2)}) %collective-permute-start) | collective-permute-done | bytes 131104 | tf_op jit(solution)/shard_map/ppermute | solution.py:342
  2.3 2.8 %collective-permute-start.1 = (bf16[4,128,128]{2,1,0:T(8,128)(2,1)S(1)}, bf16[4,128,128]{2,1,0:T(8,128)(2,1)S(1)}, u32[]{:S(2)}, u32[]{:S(2)}) collective-permute-start(bf16[4,128,128]{2,1,0:T(8,128)(2,1)S(1)} %collective-permute-done.x_core), channel_id=1, source_target_pairs={{0,2},{1,0},{2,4},{3,1},{4,6},{5,3},{6,8},{7,5},{8,10},{9,7},{10,1... | collective-permute-start | bytes 393224 | tf_op jit(solution)/shard_map/ppermute | solution.py:342
  5.2 1.3 %shard_map.76 = (bf16[8,128,384]{2,1,0:T(8,128)(2,1)S(1)}, f32[6,128,128]{2,1,0:T(8,128)S(1)}, bf16[6,128,384]{2,1,0:T(8,128)(2,1)S(1)}, f32[4,128,128]{2,1,0:T(...) custom-call(f32[8,128]{1,0:T(8,128)S(1)} %shard_map.75.token, ...), custom_call_target="tpu_custom_call" | custom-call | flops 377487360 | bytes 3084288 | tf_op jit(solution)/shard_map/pallas_call | solution.py:305
  6.5 1.6 %collective-permute-start.4 = (bf16[2,128,128]{2,1,0:T(8,128)(2,1)S(1)}, bf16[2,128,128]{2,1,0:T(8,128)(2,1)S(1)}, u32[]{:S(2)}, u32[]{:S(2)}) collective-permute-start(bf16[2,128,128]{2,1,0:T(8,128)(2,1)S(1)} %slice_select_fusion), channel_id=1, source_target_pairs={{0,2},{1,0},{2,4},{3,1},{4,6},{5,3},{6,8},{7,5},{8,10},{9,7},{10,1... | collective-permute-start | bytes 196616 | tf_op jit(solution)/shard_map/ppermute | solution.py:342
  8.1 1.0 %collective-permute-start.3 = (bf16[2,128,128]{2,1,0:T(8,128)(2,1)S(1)}, bf16[2,128,128]{2,1,0:T(8,128)(2,1)S(1)}, u32[]{:S(2)}, u32[]{:S(2)}) collective-permute-start(bf16[2,128,128]{2,1,0:T(8,128)(2,1)S(1)} %get-tuple-element.45), channel_id=1, source_target_pairs={{0,16},{1,17},{2,18},{3,19},{4,20},{5,21},{6,22},{7,23},{8,24},{9,... | collective-permute-start | bytes 196616 | tf_op jit(solution)/shard_map/ppermute | solution.py:342
  9.1 0.6 %collective-permute-done.1.x_far = bf16[4,128,128]{2,1,0:T(8,128)(2,1)S(1)} collective-permute-done((bf16[4,128,128]{2,1,0:T(8,128)(2,1)S(1)}, bf16[4,128,128]{2,1,0:T(8,128)(2,1)S(1)}, u32[]{:S(2)}, u32[]{:S(2)}) %collective-permute-start.1) | collective-permute-done | bytes 131104 | tf_op jit(solution)/shard_map/ppermute | solution.py:342
  9.8 1.3 %shard_map.77 = (f32[4,128,128]{2,1,0:T(8,128)S(1)}, f32[4,128,128]{2,1,0:T(8,128)S(1)}, bf16[4,128,128]{2,1,0:T(8,128)(2,1)S(1)}, bf16[4,128,128]{2,1,0:T(8,128)(2,1)S(1)}) custom-call(bf16[8,128,384]{2,1,0:T(8,128)(2,1)S(1)} %get-tuple-element.41.xa, bf16[6,128,384]{2,1,0:T(8,128)(2,1)S(1)} %get-tuple-element.42.ha, ...), custom_call_target="tpu_custom_call" | custom-call | flops 301989888 | bytes 2883584 | tf_op jit(solution)/shard_map/pallas_call | solution.py:305
  11.1 0.9 %collective-permute-start.6 = (bf16[4,128,128]{2,1,0:T(8,128)(2,1)S(1)}, bf16[4,128,128]{2,1,0:T(8,128)(2,1)S(1)}, u32[]{:S(2)}, u32[]{:S(2)}) collective-permute-start(bf16[4,128,128]{2,1,0:T(8,128)(2,1)S(1)} %get-tuple-element.49.far_here), channel_id=1, source_target_pairs={{0,16},{1,17},{2,18},{3,19},{4,20},{5,21},{6,22},{7,23},{8,24},{9,... | collective-permute-start | bytes 393224 | tf_op jit(solution)/shard_map/ppermute | solution.py:342
  12.0 1.1 %collective-permute-done.3.near_own = bf16[2,128,128]{2,1,0:T(8,128)(2,1)S(1)} collective-permute-done((bf16[2,128,128]{2,1,0:T(8,128)(2,1)S(1)}, bf16[2,128,128]{2,1,0:T(8,128)(2,1)S(1)}, u32[]{:S(2)}, u32[]{:S(2)}) %collective-permute-start.3) | collective-permute-done | bytes 65568 | tf_op jit(solution)/shard_map/ppermute | solution.py:342
  13.1 1.3 %collective-permute-done.5.near_core = bf16[2,128,128]{2,1,0:T(8,128)(2,1)S(1)} collective-permute-done((bf16[2,128,128]{2,1,0:T(8,128)(2,1)S(1)}, bf16[2,128,128]{2,1,0:T(8,128)(2,1)S(1)}, u32[]{:S(2)}, u32[]{:S(2)}) %collective-permute-start.5) | collective-permute-done | bytes 65568 | tf_op jit(solution)/shard_map/ppermute | solution.py:342
  14.3 1.8 %collective-permute-done.6.far = bf16[4,128,128]{2,1,0:T(8,128)(2,1)S(1)} collective-permute-done((bf16[4,128,128]{2,1,0:T(8,128)(2,1)S(1)}, bf16[4,128,128]{2,1,0:T(8,128)(2,1)S(1)}, u32[]{:S(2)}, u32[]{:S(2)}) %collective-permute-start.6) | collective-permute-done | bytes 131104 | tf_op jit(solution)/shard_map/ppermute | solution.py:342
  16.1 2.5 %collective-permute-start.8 = (bf16[4,128,128]{2,1,0:T(8,128)(2,1)S(1)}, bf16[4,128,128]{2,1,0:T(8,128)(2,1)S(1)}, u32[]{:S(2)}, u32[]{:S(2)}) collective-permute-start(bf16[4,128,128]{2,1,0:T(8,128)(2,1)S(1)} %get-tuple-element.53), channel_id=1, source_target_pairs={{0,16},{1,17},{2,18},{3,19},{4,20},{5,21},{6,22},{7,23},{8,24},{9,... | collective-permute-start | bytes 393224 | tf_op jit(solution)/shard_map/ppermute | solution.py:342
  18.7 2.9 %collective-permute-done.8.back = bf16[4,128,128]{2,1,0:T(8,128)(2,1)S(1)} collective-permute-done((bf16[4,128,128]{2,1,0:T(8,128)(2,1)S(1)}, bf16[4,128,128]{2,1,0:T(8,128)(2,1)S(1)}, u32[]{:S(2)}, u32[]{:S(2)}) %collective-permute-start.8) | collective-permute-done | bytes 131104 | tf_op jit(solution)/shard_map/ppermute | solution.py:342
  21.6 2.0 %collective-permute-done.7.back_other = bf16[2,128,128]{2,1,0:T(8,128)(2,1)S(1)} collective-permute-done((bf16[2,128,128]{2,1,0:T(8,128)(2,1)S(1)}, bf16[2,128,128]{2,1,0:T(8,128)(2,1)S(1)}, u32[]{:S(2)}, u32[]{:S(2)}) %collective-permute-start.7) | collective-permute-done | bytes 65568 | tf_op jit(solution)/shard_map/ppermute | solution.py:342
  23.6 0.8 %shard_map.81 = (f32[3,3,64,128]{3,2,1,0:T(8,128)S(1)}, bf16[3,3,64,128]{3,2,1,0:T(8,128)(2,1)S(1)}, bf16[8,128,384]{2,1,0:T(8,128)(2,1)S(1)}) custom-call(bf16[8,128,128]{2,1,0:T(8,128)(2,1)S(1)} %shard_map.78.g, bf16[2,128,128]{2,1,0:T(8,128)(2,1)S(1)} %shard_map.80.edge_grad, bf16[4,128,128]{2,1,0:T(8,128)(2,1)S(1)} %collective-permute-done.8.back, ...), custom_call_target="tpu_custom_call" | custom-call | flops 150994944 | bytes 3260416 | tf_op jit(solution)/shard_map/pallas_call | solution.py:305
  24.5 1.1 %shard_map.82 = (f32[3,3,64,128]{3,2,1,0:T(8,128)S(1)}, bf16[3,3,64,128]{3,2,1,0:T(8,128)(2,1)S(1)}, bf16[6,128,384]{2,1,0:T(8,128)(2,1)S(1)}) custom-call(bf16[4,128,128]{2,1,0:T(8,128)(2,1)S(1)} %bitcast.17, f32[6,128,128]{2,1,0:T(8,128)S(1)} %get-tuple-element.40.near_first, f32[4,128,128]{2,1,0:T(8,128)S(1)} %get-tuple-element.43.far_first, ...), custom_call_target="tpu_custom_call" | custom-call | flops 377487360 | bytes 3489792 | tf_op jit(solution)/shard_map/pallas_call | solution.py:305
  25.6 0.6 %collective-permute-start.10 = (bf16[3,3,64,128]{3,2,1,0:T(8,128)(2,1)S(1)}, bf16[3,3,64,128]{3,2,1,0:T(8,128)(2,1)S(1)}, u32[]{:S(2)}, u32[]{:S(2)}) collective-permute-start(bf16[3,3,64,128]{3,2,1,0:T(8,128)(2,1)S(1)} %get-tuple-element.63), channel_id=1, source_target_pairs={{0,1},{1,0},{2,3},{3,2},{4,5},{5,4},{6,7},{7,6},{8,9},{9,8},{10,11... | collective-permute-start | bytes 442376 | tf_op jit(solution)/shard_map/ppermute | solution.py:342
  26.2 1.0 %collective-permute-done.10.got1 = bf16[3,3,64,128]{3,2,1,0:T(8,128)(2,1)S(1)} collective-permute-done((bf16[3,3,64,128]{3,2,1,0:T(8,128)(2,1)S(1)}, bf16[3,3,64,128]{3,2,1,0:T(8,128)(2,1)S(1)}, u32[]{:S(2)}, u32[]{:S(2)}) %collective-permute-start.10) | collective-permute-done | bytes 147488 | tf_op jit(solution)/shard_map/ppermute | solution.py:342
  27.3 3.8 %collective-permute-start.12 = (bf16[2,3,3,16,128]{4,3,2,1,0:T(8,128)(2,1)S(1)}, bf16[2,3,3,16,128]{4,3,2,1,0:T(8,128)(2,1)S(1)}, u32[]{:S(2)}, u32[]{:S(2)}) collective-permute-start(bf16[2,3,3,16,128]{4,3,2,1,0:T(8,128)(2,1)S(1)} %get-tuple-element.67), channel_id=1, source_target_pairs={{0,6},{1,7},{2,4},{3,5},{4,2},{5,3},{6,0},{7,1},{8,14},{9,15},{10,... | collective-permute-start | bytes 221192 | tf_op jit(solution)/shard_map/ppermute | solution.py:342
  31.0 0.6 %collective-permute-start.14 = (bf16[2,3,3,16,128]{4,3,2,1,0:T(8,128)(2,1)S(1)}, bf16[2,3,3,16,128]{4,3,2,1,0:T(8,128)(2,1)S(1)}, u32[]{:S(2)}, u32[]{:S(2)}) collective-permute-start(bf16[2,3,3,16,128]{4,3,2,1,0:T(8,128)(2,1)S(1)} %get-tuple-element.69), channel_id=1, source_target_pairs={{0,4},{1,3},{2,6},{3,1},{4,0},{5,7},{6,2},{7,5},{8,12},{9,11},{10,... | collective-permute-start | bytes 221192 | tf_op jit(solution)/shard_map/ppermute | solution.py:342
  31.7 2.5 %collective-permute-done.12 = bf16[2,3,3,16,128]{4,3,2,1,0:T(8,128)(2,1)S(1)} collective-permute-done((bf16[2,3,3,16,128]{4,3,2,1,0:T(8,128)(2,1)S(1)}, bf16[2,3,3,16,128]{4,3,2,1,0:T(8,128)(2,1)S(1)}, u32[]{:S(2)}, u32[]{:S(2)}) %collective-permute-start.12) | collective-permute-done | bytes 73760 | tf_op jit(solution)/shard_map/ppermute | solution.py:342
  34.2 1.4 %collective-permute-done.13 = bf16[2,3,3,16,128]{4,3,2,1,0:T(8,128)(2,1)S(1)} collective-permute-done((bf16[2,3,3,16,128]{4,3,2,1,0:T(8,128)(2,1)S(1)}, bf16[2,3,3,16,128]{4,3,2,1,0:T(8,128)(2,1)S(1)}, u32[]{:S(2)}, u32[]{:S(2)}) %collective-permute-start.13) | collective-permute-done | bytes 73760 | tf_op jit(solution)/shard_map/ppermute | solution.py:342
  35.6 2.5 %collective-permute-start.15 = (bf16[2,3,3,16,128]{4,3,2,1,0:T(8,128)(2,1)S(1)}, bf16[2,3,3,16,128]{4,3,2,1,0:T(8,128)(2,1)S(1)}, u32[]{:S(2)}, u32[]{:S(2)}) collective-permute-start(bf16[2,3,3,16,128]{4,3,2,1,0:T(8,128)(2,1)S(1)} %add_convert_fusion.1), channel_id=1, source_target_pairs={{0,8},{1,9},{2,10},{3,11},{4,12},{5,13},{6,14},{7,15},{8,0},{9,1},... | collective-permute-start | bytes 221192 | tf_op jit(solution)/shard_map/ppermute | solution.py:342
  38.2 4.2 %collective-permute-done.15 = bf16[2,3,3,16,128]{4,3,2,1,0:T(8,128)(2,1)S(1)} collective-permute-done((bf16[2,3,3,16,128]{4,3,2,1,0:T(8,128)(2,1)S(1)}, bf16[2,3,3,16,128]{4,3,2,1,0:T(8,128)(2,1)S(1)}, u32[]{:S(2)}, u32[]{:S(2)}) %collective-permute-start.15) | collective-permute-done | bytes 73760 | tf_op jit(solution)/shard_map/ppermute | solution.py:342
  42.7 1.4 %collective-permute-start.17 = (bf16[2,3,3,16,128]{4,3,2,1,0:T(8,128)(2,1)S(1)}, bf16[2,3,3,16,128]{4,3,2,1,0:T(8,128)(2,1)S(1)}, u32[]{:S(2)}, u32[]{:S(2)}) collective-permute-start(bf16[2,3,3,16,128]{4,3,2,1,0:T(8,128)(2,1)S(1)} %add_convert_fusion.mine), channel_id=1, source_target_pairs={{0,2},{1,5},{2,0},{3,7},{4,6},{5,1},{6,4},{7,3},{8,10},{9,13},{10,... | collective-permute-start | bytes 221192 | tf_op jit(solution)/shard_map/ppermute | solution.py:342
  44.1 1.9 %collective-permute-start.16 = (bf16[2,3,3,16,128]{4,3,2,1,0:T(8,128)(2,1)S(1)}, bf16[2,3,3,16,128]{4,3,2,1,0:T(8,128)(2,1)S(1)}, u32[]{:S(2)}, u32[]{:S(2)}) collective-permute-start(bf16[2,3,3,16,128]{4,3,2,1,0:T(8,128)(2,1)S(1)} %add_convert_fusion.mine), channel_id=1, source_target_pairs={{0,6},{1,7},{2,4},{3,5},{4,2},{5,3},{6,0},{7,1},{8,14},{9,15},{10,... | collective-permute-start | bytes 221192 | tf_op jit(solution)/shard_map/ppermute | solution.py:342
  45.9 1.7 %collective-permute-done.18.rest_2_ = bf16[2,3,3,16,128]{4,3,2,1,0:T(8,128)(2,1)S(1)} collective-permute-done((bf16[2,3,3,16,128]{4,3,2,1,0:T(8,128)(2,1)S(1)}, bf16[2,3,3,16,128]{4,3,2,1,0:T(8,128)(2,1)S(1)}, u32[]{:S(2)}, u32[]{:S(2)}) %collective-permute-start.18) | collective-permute-done | bytes 73760 | tf_op jit(solution)/shard_map/ppermute | solution.py:342
  47.7 1.6 %collective-permute-done.16.rest_0_ = bf16[2,3,3,16,128]{4,3,2,1,0:T(8,128)(2,1)S(1)} collective-permute-done((bf16[2,3,3,16,128]{4,3,2,1,0:T(8,128)(2,1)S(1)}, bf16[2,3,3,16,128]{4,3,2,1,0:T(8,128)(2,1)S(1)}, u32[]{:S(2)}, u32[]{:S(2)}) %collective-permute-start.16) | collective-permute-done | bytes 73760 | tf_op jit(solution)/shard_map/ppermute | solution.py:342
  49.4 1.1 %shard_map.83 = (bf16[4,128,128]{2,1,0:T(8,128)(2,1)}, bf16[4,128,128]{2,1,0:T(8,128)(2,1)}) custom-call(bf16[6,128,384]{2,1,0:T(8,128)(2,1)S(1)} %get-tuple-element.58.hw, bf16[3,3,128,128]{3,2,1,0:T(8,128)(2,1)S(1)} %bitcast.14, bf16[4,128,128]{2,1,0:T(8,128)(2,1)S(1)} %get-tuple-element.59.out), custom_call_target="tpu_custom_call" | custom-call | flops 150994944 | bytes 1277952 | tf_op jit(solution)/shard_map/pallas_call | solution.py:305
  50.6 0.4 collective-permute-done.19.theirs
  51.0 1.1 %shard_map.87 = (f32[3,3,128,128]{3,2,1,0:T(8,128)}, f32[3,3,128,128]{3,2,1,0:T(8,128)}) custom-call(bf16[2,3,3,64,128]{4,3,2,1,0:T(8,128)(2,1)S(1)} %shard_map.86.mine, bf16[2,3,3,64,128]{4,3,2,1,0:T(8,128)(2,1)S(1)} %collective-permute-done.19.theirs), custom_call_target="tpu_custom_call" | custom-call | flops 73728 | bytes 1769472 | tf_op jit(solution)/shard_map/pallas_call | solution.py:305
  (32 shorter events, 1.0 us)
Async XLA Ops:
  0.6 1.7 %collective-permute-start = (bf16[4,128,128]{2,1,0:T(8,128)(2,1)}, bf16[4,128,128]{2,1,0:T(8,128)(2,1)S(1)}, u32[]{:S(2)}, u32[]{:S(2)}) collective-permute-start(bf16[4,128,128]{2,1,0:T(8,128)(2,1)} %bitcast.15), channel_id=1, source_target_pairs={{0,1},{1,0},{2,3},{3,2},{4,5},{5,4},{6,7},{7,6},{8,9},{9,8},{10,11... | collective-permute-start | bytes 393224 | tf_op jit(solution)/shard_map/ppermute | solution.py:342
  1.1 4.1 %copy-start = (bf16[1,3,3,128,128]{4,3,2,1,0:T(8,128)(2,1)S(1)}, bf16[1,3,3,128,128]{4,3,2,1,0:T(8,128)(2,1)}, u32[]{:S(2)}) copy-start(bf16[1,3,3,128,128]{4,3,2,1,0:T(8,128)(2,1)} %param.7) | copy-start | bytes 884740
  1.2 4.1 %copy-start.1 = (bf16[1,3,3,128,128]{4,3,2,1,0:T(8,128)(2,1)S(1)}, bf16[1,3,3,128,128]{4,3,2,1,0:T(8,128)(2,1)}, u32[]{:S(2)}) copy-start(bf16[1,3,3,128,128]{4,3,2,1,0:T(8,128)(2,1)} %param.6) | copy-start | bytes 884740
  1.2 4.0 %collective-permute-start.2 = (bf16[4,128,128]{2,1,0:T(8,128)(2,1)}, bf16[4,128,128]{2,1,0:T(8,128)(2,1)S(1)}, u32[]{:S(2)}, u32[]{:S(2)}) collective-permute-start(bf16[4,128,128]{2,1,0:T(8,128)(2,1)} %bitcast.18), channel_id=1, source_target_pairs={{0,1},{1,0},{2,3},{3,2},{4,5},{5,4},{6,7},{7,6},{8,9},{9,8},{10,11... | collective-permute-start | bytes 393224 | tf_op jit(solution)/shard_map/ppermute | solution.py:342
  1.3 4.0 %copy-start.2 = (bf16[1,4,128,128]{3,2,1,0:T(8,128)(2,1)S(1)}, bf16[1,4,128,128]{3,2,1,0:T(8,128)(2,1)}, u32[]{:S(2)}) copy-start(bf16[1,4,128,128]{3,2,1,0:T(8,128)(2,1)} %param.4) | copy-start | bytes 393220
  2.3 7.4 %collective-permute-start.1 = (bf16[4,128,128]{2,1,0:T(8,128)(2,1)S(1)}, bf16[4,128,128]{2,1,0:T(8,128)(2,1)S(1)}, u32[]{:S(2)}, u32[]{:S(2)}) collective-permute-start(bf16[4,128,128]{2,1,0:T(8,128)(2,1)S(1)} %collective-permute-done.x_core), channel_id=1, source_target_pairs={{0,2},{1,0},{2,4},{3,1},{4,6},{5,3},{6,8},{7,5},{8,10},{9,7},{10,1... | collective-permute-start | bytes 393224 | tf_op jit(solution)/shard_map/ppermute | solution.py:342
  6.5 5.4 %collective-permute-start.4 = (bf16[2,128,128]{2,1,0:T(8,128)(2,1)S(1)}, bf16[2,128,128]{2,1,0:T(8,128)(2,1)S(1)}, u32[]{:S(2)}, u32[]{:S(2)}) collective-permute-start(bf16[2,128,128]{2,1,0:T(8,128)(2,1)S(1)} %slice_select_fusion), channel_id=1, source_target_pairs={{0,2},{1,0},{2,4},{3,1},{4,6},{5,3},{6,8},{7,5},{8,10},{9,7},{10,1... | collective-permute-start | bytes 196616 | tf_op jit(solution)/shard_map/ppermute | solution.py:342
  8.1 4.9 %collective-permute-start.3 = (bf16[2,128,128]{2,1,0:T(8,128)(2,1)S(1)}, bf16[2,128,128]{2,1,0:T(8,128)(2,1)S(1)}, u32[]{:S(2)}, u32[]{:S(2)}) collective-permute-start(bf16[2,128,128]{2,1,0:T(8,128)(2,1)S(1)} %get-tuple-element.45), channel_id=1, source_target_pairs={{0,16},{1,17},{2,18},{3,19},{4,20},{5,21},{6,22},{7,23},{8,24},{9,... | collective-permute-start | bytes 196616 | tf_op jit(solution)/shard_map/ppermute | solution.py:342
  9.8 2.2 %copy-start.3 = (bf16[1,4,128,128]{3,2,1,0:T(8,128)(2,1)S(1)}, bf16[1,4,128,128]{3,2,1,0:T(8,128)(2,1)}, u32[]{:S(2)}) copy-start(bf16[1,4,128,128]{3,2,1,0:T(8,128)(2,1)} %param.5) | copy-start | bytes 393220
  11.1 5.0 %collective-permute-start.6 = (bf16[4,128,128]{2,1,0:T(8,128)(2,1)S(1)}, bf16[4,128,128]{2,1,0:T(8,128)(2,1)S(1)}, u32[]{:S(2)}, u32[]{:S(2)}) collective-permute-start(bf16[4,128,128]{2,1,0:T(8,128)(2,1)S(1)} %get-tuple-element.49.far_here), channel_id=1, source_target_pairs={{0,16},{1,17},{2,18},{3,19},{4,20},{5,21},{6,22},{7,23},{8,24},{9,... | collective-permute-start | bytes 393224 | tf_op jit(solution)/shard_map/ppermute | solution.py:342
  13.1 1.3 %collective-permute-start.5 = (bf16[2,128,128]{2,1,0:T(8,128)(2,1)S(1)}, bf16[2,128,128]{2,1,0:T(8,128)(2,1)S(1)}, u32[]{:S(2)}, u32[]{:S(2)}) collective-permute-start(bf16[2,128,128]{2,1,0:T(8,128)(2,1)S(1)} %collective-permute-done.3.near_own), channel_id=1, source_target_pairs={{0,1},{1,0},{2,3},{3,2},{4,5},{5,4},{6,7},{7,6},{8,9},{9,8},{10,11... | collective-permute-start | bytes 196616 | tf_op jit(solution)/shard_map/ppermute | solution.py:342
  16.1 5.4 %collective-permute-start.8 = (bf16[4,128,128]{2,1,0:T(8,128)(2,1)S(1)}, bf16[4,128,128]{2,1,0:T(8,128)(2,1)S(1)}, u32[]{:S(2)}, u32[]{:S(2)}) collective-permute-start(bf16[4,128,128]{2,1,0:T(8,128)(2,1)S(1)} %get-tuple-element.53), channel_id=1, source_target_pairs={{0,16},{1,17},{2,18},{3,19},{4,20},{5,21},{6,22},{7,23},{8,24},{9,... | collective-permute-start | bytes 393224 | tf_op jit(solution)/shard_map/ppermute | solution.py:342
  18.6 4.9 %collective-permute-start.7 = (bf16[2,128,128]{2,1,0:T(8,128)(2,1)S(1)}, bf16[2,128,128]{2,1,0:T(8,128)(2,1)S(1)}, u32[]{:S(2)}, u32[]{:S(2)}) collective-permute-start(bf16[2,128,128]{2,1,0:T(8,128)(2,1)S(1)} %get-tuple-element.51), channel_id=1, source_target_pairs={{0,16},{1,18},{2,17},{3,20},{4,19},{5,22},{6,21},{7,24},{8,23},{9,... | collective-permute-start | bytes 196616 | tf_op jit(solution)/shard_map/ppermute | solution.py:342
  21.6 2.1 %collective-permute-start.9 = (bf16[4,128,128]{2,1,0:T(8,128)(2,1)S(1)}, bf16[4,128,128]{2,1,0:T(8,128)(2,1)S(1)}, u32[]{:S(2)}, u32[]{:S(2)}) collective-permute-start(bf16[4,128,128]{2,1,0:T(8,128)(2,1)S(1)} %collective-permute-done.8.back), channel_id=1, source_target_pairs={{0,1},{1,0},{2,3},{3,2},{4,5},{5,4},{6,7},{7,6},{8,9},{9,8},{10,11... | collective-permute-start | bytes 393224 | tf_op jit(solution)/shard_map/ppermute | solution.py:342
  24.4 1.8 %collective-permute-start.11 = (bf16[3,3,64,128]{3,2,1,0:T(8,128)(2,1)S(1)}, bf16[3,3,64,128]{3,2,1,0:T(8,128)(2,1)S(1)}, u32[]{:S(2)}, u32[]{:S(2)}) collective-permute-start(bf16[3,3,64,128]{3,2,1,0:T(8,128)(2,1)S(1)} %get-tuple-element.65), channel_id=1, source_target_pairs={{0,1},{1,0},{2,3},{3,2},{4,5},{5,4},{6,7},{7,6},{8,9},{9,8},{10,11... | collective-permute-start | bytes 442376 | tf_op jit(solution)/shard_map/ppermute | solution.py:342
  25.6 1.6 %collective-permute-start.10 = (bf16[3,3,64,128]{3,2,1,0:T(8,128)(2,1)S(1)}, bf16[3,3,64,128]{3,2,1,0:T(8,128)(2,1)S(1)}, u32[]{:S(2)}, u32[]{:S(2)}) collective-permute-start(bf16[3,3,64,128]{3,2,1,0:T(8,128)(2,1)S(1)} %get-tuple-element.63), channel_id=1, source_target_pairs={{0,1},{1,0},{2,3},{3,2},{4,5},{5,4},{6,7},{7,6},{8,9},{9,8},{10,11... | collective-permute-start | bytes 442376 | tf_op jit(solution)/shard_map/ppermute | solution.py:342
  27.3 6.9 %collective-permute-start.12 = (bf16[2,3,3,16,128]{4,3,2,1,0:T(8,128)(2,1)S(1)}, bf16[2,3,3,16,128]{4,3,2,1,0:T(8,128)(2,1)S(1)}, u32[]{:S(2)}, u32[]{:S(2)}) collective-permute-start(bf16[2,3,3,16,128]{4,3,2,1,0:T(8,128)(2,1)S(1)} %get-tuple-element.67), channel_id=1, source_target_pairs={{0,6},{1,7},{2,4},{3,5},{4,2},{5,3},{6,0},{7,1},{8,14},{9,15},{10,... | collective-permute-start | bytes 221192 | tf_op jit(solution)/shard_map/ppermute | solution.py:342
  31.0 4.6 %collective-permute-start.13 = (bf16[2,3,3,16,128]{4,3,2,1,0:T(8,128)(2,1)S(1)}, bf16[2,3,3,16,128]{4,3,2,1,0:T(8,128)(2,1)S(1)}, u32[]{:S(2)}, u32[]{:S(2)}) collective-permute-start(bf16[2,3,3,16,128]{4,3,2,1,0:T(8,128)(2,1)S(1)} %get-tuple-element.68), channel_id=1, source_target_pairs={{0,2},{1,5},{2,0},{3,7},{4,6},{5,1},{6,4},{7,3},{8,10},{9,13},{10,... | collective-permute-start | bytes 221192 | tf_op jit(solution)/shard_map/ppermute | solution.py:342
  31.0 4.6 %collective-permute-start.14 = (bf16[2,3,3,16,128]{4,3,2,1,0:T(8,128)(2,1)S(1)}, bf16[2,3,3,16,128]{4,3,2,1,0:T(8,128)(2,1)S(1)}, u32[]{:S(2)}, u32[]{:S(2)}) collective-permute-start(bf16[2,3,3,16,128]{4,3,2,1,0:T(8,128)(2,1)S(1)} %get-tuple-element.69), channel_id=1, source_target_pairs={{0,4},{1,3},{2,6},{3,1},{4,0},{5,7},{6,2},{7,5},{8,12},{9,11},{10,... | collective-permute-start | bytes 221192 | tf_op jit(solution)/shard_map/ppermute | solution.py:342
  35.6 6.7 %collective-permute-start.15 = (bf16[2,3,3,16,128]{4,3,2,1,0:T(8,128)(2,1)S(1)}, bf16[2,3,3,16,128]{4,3,2,1,0:T(8,128)(2,1)S(1)}, u32[]{:S(2)}, u32[]{:S(2)}) collective-permute-start(bf16[2,3,3,16,128]{4,3,2,1,0:T(8,128)(2,1)S(1)} %add_convert_fusion.1), channel_id=1, source_target_pairs={{0,8},{1,9},{2,10},{3,11},{4,12},{5,13},{6,14},{7,15},{8,0},{9,1},... | collective-permute-start | bytes 221192 | tf_op jit(solution)/shard_map/ppermute | solution.py:342
  42.4 5.2 %collective-permute-start.18 = (bf16[2,3,3,16,128]{4,3,2,1,0:T(8,128)(2,1)S(1)}, bf16[2,3,3,16,128]{4,3,2,1,0:T(8,128)(2,1)S(1)}, u32[]{:S(2)}, u32[]{:S(2)}) collective-permute-start(bf16[2,3,3,16,128]{4,3,2,1,0:T(8,128)(2,1)S(1)} %add_convert_fusion.mine), channel_id=1, source_target_pairs={{0,4},{1,3},{2,6},{3,1},{4,0},{5,7},{6,2},{7,5},{8,12},{9,11},{10,... | collective-permute-start | bytes 221192 | tf_op jit(solution)/shard_map/ppermute | solution.py:342
  42.7 5.0 %collective-permute-start.17 = (bf16[2,3,3,16,128]{4,3,2,1,0:T(8,128)(2,1)S(1)}, bf16[2,3,3,16,128]{4,3,2,1,0:T(8,128)(2,1)S(1)}, u32[]{:S(2)}, u32[]{:S(2)}) collective-permute-start(bf16[2,3,3,16,128]{4,3,2,1,0:T(8,128)(2,1)S(1)} %add_convert_fusion.mine), channel_id=1, source_target_pairs={{0,2},{1,5},{2,0},{3,7},{4,6},{5,1},{6,4},{7,3},{8,10},{9,13},{10,... | collective-permute-start | bytes 221192 | tf_op jit(solution)/shard_map/ppermute | solution.py:342
  44.1 5.3 %collective-permute-start.16 = (bf16[2,3,3,16,128]{4,3,2,1,0:T(8,128)(2,1)S(1)}, bf16[2,3,3,16,128]{4,3,2,1,0:T(8,128)(2,1)S(1)}, u32[]{:S(2)}, u32[]{:S(2)}) collective-permute-start(bf16[2,3,3,16,128]{4,3,2,1,0:T(8,128)(2,1)S(1)} %add_convert_fusion.mine), channel_id=1, source_target_pairs={{0,6},{1,7},{2,4},{3,5},{4,2},{5,3},{6,0},{7,1},{8,14},{9,15},{10,... | collective-permute-start | bytes 221192 | tf_op jit(solution)/shard_map/ppermute | solution.py:342
  49.4 1.6 %collective-permute-start.19 = (bf16[2,3,3,64,128]{4,3,2,1,0:T(8,128)(2,1)S(1)}, bf16[2,3,3,64,128]{4,3,2,1,0:T(8,128)(2,1)S(1)}, u32[]{:S(2)}, u32[]{:S(2)}) collective-permute-start(bf16[2,3,3,64,128]{4,3,2,1,0:T(8,128)(2,1)S(1)} %shard_map.86.mine), channel_id=1, source_target_pairs={{0,1},{1,0},{2,3},{3,2},{4,5},{5,4},{6,7},{7,6},{8,9},{9,8},{10,11... | collective-permute-start | bytes 884744 | tf_op jit(solution)/shard_map/ppermute | solution.py:342

commit v16 on v13

--- a/solution.py
+++ b/solution.py
@@ -160,8 +160,34 @@
     return jnp.where(even, at_even, at_odd)
 
 
+def part_conv(yw, rows, upper, kernel):
+    own = rows.shape[0]
+    zeros = jnp.zeros(yw.shape[1:], yw.dtype)
+    for i in range(2):
+        yw[jnp.where(upper, 0, own) + i] = zeros
+    for i in range(own):
+        place(yw, jnp.where(upper, 2, 0) + i, rows[i].astype(F32))
+    return conv(yw, 0, own, kernel)
+
+
+def part_row(part, upper, i):
+    own = part.shape[0]
+    zeros = jnp.zeros(part.shape[1:], part.dtype)
+    return jnp.where(upper, part[i - 2] if i >= 2 else zeros, part[i] if i < own else zeros)
+
+
+def base_kernel(segments, near, near_first, far_first, second, base, yw):
+    encoder, _, even = here(segments)
+
+    @pl.when(jnp.logical_not(encoder))
+    def _():
+        part = part_conv(yw, near, even, second)
+        for i in range(base.shape[0]):
+            base[i] = joined_first(even, near_first, far_first, i) + part_row(part, even, i)
+
+
 def middle_kernel(
-    segments, strips, near_here, far_here, near, far, near_first, far_first, g, second, out, gw, back, edge_other, yw
+    segments, strips, near_here, far_here, far, base, g, second, out, gw, back, edge_other, yw
 ):
     encoder, row, even = here(segments)
     own = out.shape[0]
@@ -173,13 +199,9 @@
 
     @pl.when(jnp.logical_not(encoder))
     def _():
-        half = near.shape[0]
-        for i in range(half):
-            place(yw, jnp.where(even, half, 0) + i, near[i].astype(F32))
-            place(yw, jnp.where(even, 0, half) + i, far[i].astype(F32))
-        skip_pre = conv(yw, 0, own + 2, second)
+        part = part_conv(yw, far, jnp.logical_not(even), second)
         for i in range(own + 2):
-            pre = skip_pre[i] + joined_first(even, near_first, far_first, i)
+            pre = base[i] + part_row(part, jnp.logical_not(even), i)
             if 1 <= i <= own:
                 out[i - 1] = silu(pre).astype(BF16)
             value = masked(g[i + 1].astype(F32) * slope(pre), inside(row, strips, own, i - 1))
@@ -281,7 +303,7 @@
 
 def unpack_kernel(mine, *rest):
     out = rest[-1]
-    for got, rows in zip((mine,) + rest[:-1], quarters(mine.shape[3])):
+    for got, rows in zip((mine,) + rest[-2::-1], quarters(mine.shape[3])):
         out[:, :, :, rows, :] = got[...]
 
 
@@ -370,11 +392,18 @@
         work * 2 * own,
     )
     far_there = swap(far_here, True, same)
+    (base,) = call(
+        functools.partial(base_kernel, segments),
+        [like(own + 2, F32)],
+        [wide(own + 2)],
+        (near_there, near_first, far_first, second),
+        work * own,
+    )
     out, gw, back, edge_other = call(
         functools.partial(middle_kernel, segments, strips),
         [like(own, BF16), wide_out(own + 2), like(own, BF16), like(2, BF16)],
-        [wide(own + 4)],
-        (near_here, far_here, near_there, far_there, near_first, far_first, g_rows, second),
+        [wide(own + 2)],
+        (near_here, far_here, far_there, base, g_rows, second),
         work * (2 * own + 2),
     )
     back_own = swap(back, True, same)
@@ -431,7 +460,7 @@
         unpack_kernel,
         [jax.ShapeDtypeStruct((2,) + halves, BF16)],
         [],
-        (mine, *gots),
+        (mine, *reversed(gots)),
         kept1.size,
     )
     theirs = jump(mine, 0)

time: 52.3 us -> 51.7 us (0.989)
    pallas_call x13 -> x14, Pallas kernels: 6.93 us -> 6.91 us  [call(): pl.pallas_call(kernel, out_shape=outs, in_specs=[pl.BlockSpec(memory_spac...]
where the time goes in v16:
time: 51.7 us; the launch traced here: 51.5 us
  waiting for transfers between devices  23.1 us (45%)
  starting transfers between devices  20.7 us (40%)
  Pallas kernels  6.91 us (13%)
  between operations  0.76 us (1%)
    ppermute x19, waiting for transfers between devices, swap(): return lax.ppermute(array, ('segment', 'rows'), pairs)  23.1 us
    ppermute x19, starting transfers between devices, swap(): return lax.ppermute(array, ('segment', 'rows'), pairs)  20.7 us
    pallas_call x14, Pallas kernels, call(): pl.pallas_call(kernel, out_shape=outs, in_specs=[pl.BlockSpec(memory_spac...  6.91 us
  transfers between devices with their start and end apart: 19, of which 13 were waited for; matrix products, arithmetic and copies ran while one was open for 0% of the time, Pallas kernels for 10%

profile of v16, /device:TPU:0, one launch (start us, length us, event | category | flops | bytes accessed | tf_op | source)
XLA Modules:
  0.0 51.5 jit_solution(7539645040482135196)
XLA Ops:
  0.6 0.5 %collective-permute-start = (bf16[4,128,128]{2,1,0:T(8,128)(2,1)}, bf16[4,128,128]{2,1,0:T(8,128)(2,1)S(1)}, u32[]{:S(2)}, u32[]{:S(2)}) collective-permute-start(bf16[4,128,128]{2,1,0:T(8,128)(2,1)} %bitcast.16), channel_id=1, source_target_pairs={{0,1},{1,0},{2,3},{3,2},{4,5},{5,4},{6,7},{7,6},{8,9},{9,8},{10,11... | collective-permute-start | bytes 393224 | tf_op jit(solution)/shard_map/ppermute | solution.py:359
  1.3 1.1 %collective-permute-done.x_core = bf16[4,128,128]{2,1,0:T(8,128)(2,1)S(1)} collective-permute-done((bf16[4,128,128]{2,1,0:T(8,128)(2,1)}, bf16[4,128,128]{2,1,0:T(8,128)(2,1)S(1)}, u32[]{:S(2)}, u32[]{:S(2)}) %collective-permute-start) | collective-permute-done | bytes 131104 | tf_op jit(solution)/shard_map/ppermute | solution.py:359
  2.3 2.8 %collective-permute-start.1 = (bf16[4,128,128]{2,1,0:T(8,128)(2,1)S(1)}, bf16[4,128,128]{2,1,0:T(8,128)(2,1)S(1)}, u32[]{:S(2)}, u32[]{:S(2)}) collective-permute-start(bf16[4,128,128]{2,1,0:T(8,128)(2,1)S(1)} %collective-permute-done.x_core), channel_id=1, source_target_pairs={{0,2},{1,0},{2,4},{3,1},{4,6},{5,3},{6,8},{7,5},{8,10},{9,7},{10,1... | collective-permute-start | bytes 393224 | tf_op jit(solution)/shard_map/ppermute | solution.py:359
  5.2 1.3 %shard_map.76 = (bf16[8,128,384]{2,1,0:T(8,128)(2,1)S(1)}, f32[6,128,128]{2,1,0:T(8,128)S(1)}, bf16[6,128,384]{2,1,0:T(8,128)(2,1)S(1)}, f32[4,128,128]{2,1,0:T(8,128)S(1)}, bf16[4,128,128]{2,1,0:T(8,128)(2,1)S(1)}) custom-call(f32[8,128]{1,0:T(8,128)S(1)} %shard_map.75.token, bf16[4,128,128]{2,1,0:T(8,128)(2,1)S(1)} %bitcast.17, ...), custom_call_target="tpu_custom_call" | custom-call | flops 377487360 | bytes 3018752 | tf_op jit(solution)/shard_map/pallas_call | solution.py:322
  6.5 1.6 %collective-permute-start.3 = (bf16[2,128,128]{2,1,0:T(8,128)(2,1)S(1)}, bf16[2,128,128]{2,1,0:T(8,128)(2,1)S(1)}, u32[]{:S(2)}, u32[]{:S(2)}) collective-permute-start(bf16[2,128,128]{2,1,0:T(8,128)(2,1)S(1)} %slice_select_fusion), channel_id=1, source_target_pairs={{0,2},{1,0},{2,4},{3,1},{4,6},{5,3},{6,8},{7,5},{8,10},{9,7},{10,1... | collective-permute-start | bytes 196616 | tf_op jit(solution)/shard_map/ppermute | solution.py:359
  8.1 1.0 %collective-permute-start.5 = (bf16[4,128,128]{2,1,0:T(8,128)(2,1)S(1)}, bf16[4,128,128]{2,1,0:T(8,128)(2,1)S(1)}, u32[]{:S(2)}, u32[]{:S(2)}) collective-permute-start(bf16[4,128,128]{2,1,0:T(8,128)(2,1)S(1)} %get-tuple-element.43.near_here), channel_id=1, source_target_pairs={{0,16},{1,17},{2,18},{3,19},{4,20},{5,21},{6,22},{7,23},{8,24},{9,... | collective-permute-start | bytes 393224 | tf_op jit(solution)/shard_map/ppermute | solution.py:359
  9.1 0.6 %collective-permute-done.1.x_far = bf16[4,128,128]{2,1,0:T(8,128)(2,1)S(1)} collective-permute-done((bf16[4,128,128]{2,1,0:T(8,128)(2,1)S(1)}, bf16[4,128,128]{2,1,0:T(8,128)(2,1)S(1)}, u32[]{:S(2)}, u32[]{:S(2)}) %collective-permute-start.1) | collective-permute-done | bytes 131104 | tf_op jit(solution)/shard_map/ppermute | solution.py:359
  9.8 1.3 %shard_map.77 = (f32[4,128,128]{2,1,0:T(8,128)S(1)}, f32[4,128,128]{2,1,0:T(8,128)S(1)}, bf16[4,128,128]{2,1,0:T(8,128)(2,1)S(1)}, bf16[4,128,128]{2,1,0:T(8,128)(2,1)S(1)}) custom-call(bf16[8,128,384]{2,1,0:T(8,128)(2,1)S(1)} %get-tuple-element.38.xa, bf16[6,128,384]{2,1,0:T(8,128)(2,1)S(1)} %get-tuple-element.39.ha, ...), custom_call_target="tpu_custom_call" | custom-call | flops 301989888 | bytes 2883584 | tf_op jit(solution)/shard_map/pallas_call | solution.py:322
  11.1 0.9 %collective-permute-start.4 = (bf16[4,128,128]{2,1,0:T(8,128)(2,1)S(1)}, bf16[4,128,128]{2,1,0:T(8,128)(2,1)S(1)}, u32[]{:S(2)}, u32[]{:S(2)}) collective-permute-start(bf16[4,128,128]{2,1,0:T(8,128)(2,1)S(1)} %get-tuple-element.44.far_here), channel_id=1, source_target_pairs={{0,16},{1,17},{2,18},{3,19},{4,20},{5,21},{6,22},{7,23},{8,24},{9,... | collective-permute-start | bytes 393224 | tf_op jit(solution)/shard_map/ppermute | solution.py:359
  12.0 2.4 %collective-permute-done.5.near = bf16[4,128,128]{2,1,0:T(8,128)(2,1)S(1)} collective-permute-done((bf16[4,128,128]{2,1,0:T(8,128)(2,1)S(1)}, bf16[4,128,128]{2,1,0:T(8,128)(2,1)S(1)}, u32[]{:S(2)}, u32[]{:S(2)}) %collective-permute-start.5) | collective-permute-done | bytes 131104 | tf_op jit(solution)/shard_map/ppermute | solution.py:359
  14.4 1.6 %collective-permute-done.4.far = bf16[4,128,128]{2,1,0:T(8,128)(2,1)S(1)} collective-permute-done((bf16[4,128,128]{2,1,0:T(8,128)(2,1)S(1)}, bf16[4,128,128]{2,1,0:T(8,128)(2,1)S(1)}, u32[]{:S(2)}, u32[]{:S(2)}) %collective-permute-start.4) | collective-permute-done | bytes 131104 | tf_op jit(solution)/shard_map/ppermute | solution.py:359
  16.1 2.3 %collective-permute-start.7 = (bf16[4,128,128]{2,1,0:T(8,128)(2,1)S(1)}, bf16[4,128,128]{2,1,0:T(8,128)(2,1)S(1)}, u32[]{:S(2)}, u32[]{:S(2)}) collective-permute-start(bf16[4,128,128]{2,1,0:T(8,128)(2,1)S(1)} %get-tuple-element.47), channel_id=1, source_target_pairs={{0,16},{1,17},{2,18},{3,19},{4,20},{5,21},{6,22},{7,23},{8,24},{9,... | collective-permute-start | bytes 393224 | tf_op jit(solution)/shard_map/ppermute | solution.py:359
  18.5 2.9 %collective-permute-done.7.back = bf16[4,128,128]{2,1,0:T(8,128)(2,1)S(1)} collective-permute-done((bf16[4,128,128]{2,1,0:T(8,128)(2,1)S(1)}, bf16[4,128,128]{2,1,0:T(8,128)(2,1)S(1)}, u32[]{:S(2)}, u32[]{:S(2)}) %collective-permute-start.7) | collective-permute-done | bytes 131104 | tf_op jit(solution)/shard_map/ppermute | solution.py:359
  21.4 2.0 %collective-permute-done.6.back_other = bf16[2,128,128]{2,1,0:T(8,128)(2,1)S(1)} collective-permute-done((bf16[2,128,128]{2,1,0:T(8,128)(2,1)S(1)}, bf16[2,128,128]{2,1,0:T(8,128)(2,1)S(1)}, u32[]{:S(2)}, u32[]{:S(2)}) %collective-permute-start.6) | collective-permute-done | bytes 65568 | tf_op jit(solution)/shard_map/ppermute | solution.py:359
  23.5 0.8 %shard_map.82 = (f32[3,3,64,128]{3,2,1,0:T(8,128)S(1)}, bf16[3,3,64,128]{3,2,1,0:T(8,128)(2,1)S(1)}, bf16[8,128,384]{2,1,0:T(8,128)(2,1)S(1)}) custom-call(bf16[8,128,128]{2,1,0:T(8,128)(2,1)S(1)} %shard_map.78.g, bf16[2,128,128]{2,1,0:T(8,128)(2,1)S(1)} %shard_map.81.edge_grad, bf16[4,128,128]{2,1,0:T(8,128)(2,1)S(1)} %collective-permute-done.7.back, ...), custom_call_target="tpu_custom_call" | custom-call | flops 150994944 | bytes 3325952 | tf_op jit(solution)/shard_map/pallas_call | solution.py:322
  24.3 1.1 %shard_map.83 = (f32[3,3,64,128]{3,2,1,0:T(8,128)S(1)}, bf16[3,3,64,128]{3,2,1,0:T(8,128)(2,1)S(1)}, bf16[6,128,384]{2,1,0:T(8,128)(2,1)S(1)}) custom-call(bf16[4,128,128]{2,1,0:T(8,128)(2,1)S(1)} %bitcast.18, f32[6,128,128]{2,1,0:T(8,128)S(1)} %get-tuple-element.37.near_first, f32[4,128,128]{2,1,0:T(8,128)S(1)} %get-tuple-element.40.far_first, ...), custom_call_target="tpu_custom_call" | custom-call | flops 377487360 | bytes 3489792 | tf_op jit(solution)/shard_map/pallas_call | solution.py:322
  25.5 0.6 %collective-permute-start.9 = (bf16[3,3,64,128]{3,2,1,0:T(8,128)(2,1)S(1)}, bf16[3,3,64,128]{3,2,1,0:T(8,128)(2,1)S(1)}, u32[]{:S(2)}, u32[]{:S(2)}) collective-permute-start(bf16[3,3,64,128]{3,2,1,0:T(8,128)(2,1)S(1)} %get-tuple-element.57), channel_id=1, source_target_pairs={{0,1},{1,0},{2,3},{3,2},{4,5},{5,4},{6,7},{7,6},{8,9},{9,8},{10,11... | collective-permute-start | bytes 442376 | tf_op jit(solution)/shard_map/ppermute | solution.py:359
  26.1 1.0 %collective-permute-done.9.got1 = bf16[3,3,64,128]{3,2,1,0:T(8,128)(2,1)S(1)} collective-permute-done((bf16[3,3,64,128]{3,2,1,0:T(8,128)(2,1)S(1)}, bf16[3,3,64,128]{3,2,1,0:T(8,128)(2,1)S(1)}, u32[]{:S(2)}, u32[]{:S(2)}) %collective-permute-start.9) | collective-permute-done | bytes 147488 | tf_op jit(solution)/shard_map/ppermute | solution.py:359
  27.1 3.8 %collective-permute-start.11 = (bf16[2,3,3,16,128]{4,3,2,1,0:T(8,128)(2,1)S(1)}, bf16[2,3,3,16,128]{4,3,2,1,0:T(8,128)(2,1)S(1)}, u32[]{:S(2)}, u32[]{:S(2)}) collective-permute-start(bf16[2,3,3,16,128]{4,3,2,1,0:T(8,128)(2,1)S(1)} %get-tuple-element.61), channel_id=1, source_target_pairs={{0,6},{1,7},{2,4},{3,5},{4,2},{5,3},{6,0},{7,1},{8,14},{9,15},{10,... | collective-permute-start | bytes 221192 | tf_op jit(solution)/shard_map/ppermute | solution.py:359
  30.9 0.6 %collective-permute-start.13 = (bf16[2,3,3,16,128]{4,3,2,1,0:T(8,128)(2,1)S(1)}, bf16[2,3,3,16,128]{4,3,2,1,0:T(8,128)(2,1)S(1)}, u32[]{:S(2)}, u32[]{:S(2)}) collective-permute-start(bf16[2,3,3,16,128]{4,3,2,1,0:T(8,128)(2,1)S(1)} %get-tuple-element.63), channel_id=1, source_target_pairs={{0,4},{1,3},{2,6},{3,1},{4,0},{5,7},{6,2},{7,5},{8,12},{9,11},{10,... | collective-permute-start | bytes 221192 | tf_op jit(solution)/shard_map/ppermute | solution.py:359
  31.5 2.5 %collective-permute-done.11 = bf16[2,3,3,16,128]{4,3,2,1,0:T(8,128)(2,1)S(1)} collective-permute-done((bf16[2,3,3,16,128]{4,3,2,1,0:T(8,128)(2,1)S(1)}, bf16[2,3,3,16,128]{4,3,2,1,0:T(8,128)(2,1)S(1)}, u32[]{:S(2)}, u32[]{:S(2)}) %collective-permute-start.11) | collective-permute-done | bytes 73760 | tf_op jit(solution)/shard_map/ppermute | solution.py:359
  34.0 1.4 %collective-permute-done.12 = bf16[2,3,3,16,128]{4,3,2,1,0:T(8,128)(2,1)S(1)} collective-permute-done((bf16[2,3,3,16,128]{4,3,2,1,0:T(8,128)(2,1)S(1)}, bf16[2,3,3,16,128]{4,3,2,1,0:T(8,128)(2,1)S(1)}, u32[]{:S(2)}, u32[]{:S(2)}) %collective-permute-start.12) | collective-permute-done | bytes 73760 | tf_op jit(solution)/shard_map/ppermute | solution.py:359
  35.5 2.5 %collective-permute-start.14 = (bf16[2,3,3,16,128]{4,3,2,1,0:T(8,128)(2,1)S(1)}, bf16[2,3,3,16,128]{4,3,2,1,0:T(8,128)(2,1)S(1)}, u32[]{:S(2)}, u32[]{:S(2)}) collective-permute-start(bf16[2,3,3,16,128]{4,3,2,1,0:T(8,128)(2,1)S(1)} %add_convert_fusion.1), channel_id=1, source_target_pairs={{0,8},{1,9},{2,10},{3,11},{4,12},{5,13},{6,14},{7,15},{8,0},{9,1},... | collective-permute-start | bytes 221192 | tf_op jit(solution)/shard_map/ppermute | solution.py:359
  38.0 4.2 %collective-permute-done.14 = bf16[2,3,3,16,128]{4,3,2,1,0:T(8,128)(2,1)S(1)} collective-permute-done((bf16[2,3,3,16,128]{4,3,2,1,0:T(8,128)(2,1)S(1)}, bf16[2,3,3,16,128]{4,3,2,1,0:T(8,128)(2,1)S(1)}, u32[]{:S(2)}, u32[]{:S(2)}) %collective-permute-start.14) | collective-permute-done | bytes 73760 | tf_op jit(solution)/shard_map/ppermute | solution.py:359
  42.2 0.8 %collective-permute-start.17 = (bf16[2,3,3,16,128]{4,3,2,1,0:T(8,128)(2,1)S(1)}, bf16[2,3,3,16,128]{4,3,2,1,0:T(8,128)(2,1)S(1)}, u32[]{:S(2)}, u32[]{:S(2)}) collective-permute-start(bf16[2,3,3,16,128]{4,3,2,1,0:T(8,128)(2,1)S(1)} %add_convert_fusion.mine), channel_id=1, source_target_pairs={{0,6},{1,7},{2,4},{3,5},{4,2},{5,3},{6,0},{7,1},{8,14},{9,15},{10,... | collective-permute-start | bytes 221192 | tf_op jit(solution)/shard_map/ppermute | solution.py:359
  43.0 0.9 %collective-permute-start.16 = (bf16[2,3,3,16,128]{4,3,2,1,0:T(8,128)(2,1)S(1)}, bf16[2,3,3,16,128]{4,3,2,1,0:T(8,128)(2,1)S(1)}, u32[]{:S(2)}, u32[]{:S(2)}) collective-permute-start(bf16[2,3,3,16,128]{4,3,2,1,0:T(8,128)(2,1)S(1)} %add_convert_fusion.mine), channel_id=1, source_target_pairs={{0,2},{1,5},{2,0},{3,7},{4,6},{5,1},{6,4},{7,3},{8,10},{9,13},{10,... | collective-permute-start | bytes 221192 | tf_op jit(solution)/shard_map/ppermute | solution.py:359
  43.9 1.8 %collective-permute-start.15 = (bf16[2,3,3,16,128]{4,3,2,1,0:T(8,128)(2,1)S(1)}, bf16[2,3,3,16,128]{4,3,2,1,0:T(8,128)(2,1)S(1)}, u32[]{:S(2)}, u32[]{:S(2)}) collective-permute-start(bf16[2,3,3,16,128]{4,3,2,1,0:T(8,128)(2,1)S(1)} %add_convert_fusion.mine), channel_id=1, source_target_pairs={{0,4},{1,3},{2,6},{3,1},{4,0},{5,7},{6,2},{7,5},{8,12},{9,11},{10,... | collective-permute-start | bytes 221192 | tf_op jit(solution)/shard_map/ppermute | solution.py:359
  45.8 1.9 %collective-permute-done.17.rest_2_ = bf16[2,3,3,16,128]{4,3,2,1,0:T(8,128)(2,1)S(1)} collective-permute-done((bf16[2,3,3,16,128]{4,3,2,1,0:T(8,128)(2,1)S(1)}, bf16[2,3,3,16,128]{4,3,2,1,0:T(8,128)(2,1)S(1)}, u32[]{:S(2)}, u32[]{:S(2)}) %collective-permute-start.17) | collective-permute-done | bytes 73760 | tf_op jit(solution)/shard_map/ppermute | solution.py:359
  47.6 1.1 %collective-permute-done.16.rest_1_ = bf16[2,3,3,16,128]{4,3,2,1,0:T(8,128)(2,1)S(1)} collective-permute-done((bf16[2,3,3,16,128]{4,3,2,1,0:T(8,128)(2,1)S(1)}, bf16[2,3,3,16,128]{4,3,2,1,0:T(8,128)(2,1)S(1)}, u32[]{:S(2)}, u32[]{:S(2)}) %collective-permute-start.16) | collective-permute-done | bytes 73760 | tf_op jit(solution)/shard_map/ppermute | solution.py:359
  49.0 1.1 %shard_map.84 = (bf16[4,128,128]{2,1,0:T(8,128)(2,1)}, bf16[4,128,128]{2,1,0:T(8,128)(2,1)}) custom-call(bf16[6,128,384]{2,1,0:T(8,128)(2,1)S(1)} %get-tuple-element.52.hw, bf16[3,3,128,128]{3,2,1,0:T(8,128)(2,1)S(1)} %bitcast.15, bf16[4,128,128]{2,1,0:T(8,128)(2,1)S(1)} %get-tuple-element.53.out), custom_call_target="tpu_custom_call" | custom-call | flops 150994944 | bytes 1277952 | tf_op jit(solution)/shard_map/pallas_call | solution.py:322
  50.1 0.3 collective-permute-done.18.theirs
  50.4 1.1 %shard_map.88 = (f32[3,3,128,128]{3,2,1,0:T(8,128)}, f32[3,3,128,128]{3,2,1,0:T(8,128)}) custom-call(bf16[2,3,3,64,128]{4,3,2,1,0:T(8,128)(2,1)S(1)} %shard_map.87.mine, bf16[2,3,3,64,128]{4,3,2,1,0:T(8,128)(2,1)S(1)} %collective-permute-done.18.theirs), custom_call_target="tpu_custom_call" | custom-call | flops 73728 | bytes 1769472 | tf_op jit(solution)/shard_map/pallas_call | solution.py:322
  (31 shorter events, 0.8 us)
Async XLA Ops:
  0.6 1.7 %collective-permute-start = (bf16[4,128,128]{2,1,0:T(8,128)(2,1)}, bf16[4,128,128]{2,1,0:T(8,128)(2,1)S(1)}, u32[]{:S(2)}, u32[]{:S(2)}) collective-permute-start(bf16[4,128,128]{2,1,0:T(8,128)(2,1)} %bitcast.16), channel_id=1, source_target_pairs={{0,1},{1,0},{2,3},{3,2},{4,5},{5,4},{6,7},{7,6},{8,9},{9,8},{10,11... | collective-permute-start | bytes 393224 | tf_op jit(solution)/shard_map/ppermute | solution.py:359
  1.1 4.1 %copy-start = (bf16[1,3,3,128,128]{4,3,2,1,0:T(8,128)(2,1)S(1)}, bf16[1,3,3,128,128]{4,3,2,1,0:T(8,128)(2,1)}, u32[]{:S(2)}) copy-start(bf16[1,3,3,128,128]{4,3,2,1,0:T(8,128)(2,1)} %param.7) | copy-start | bytes 884740
  1.2 4.1 %copy-start.1 = (bf16[1,3,3,128,128]{4,3,2,1,0:T(8,128)(2,1)S(1)}, bf16[1,3,3,128,128]{4,3,2,1,0:T(8,128)(2,1)}, u32[]{:S(2)}) copy-start(bf16[1,3,3,128,128]{4,3,2,1,0:T(8,128)(2,1)} %param.6) | copy-start | bytes 884740
  1.2 4.0 %collective-permute-start.2 = (bf16[4,128,128]{2,1,0:T(8,128)(2,1)}, bf16[4,128,128]{2,1,0:T(8,128)(2,1)S(1)}, u32[]{:S(2)}, u32[]{:S(2)}) collective-permute-start(bf16[4,128,128]{2,1,0:T(8,128)(2,1)} %bitcast.19), channel_id=1, source_target_pairs={{0,1},{1,0},{2,3},{3,2},{4,5},{5,4},{6,7},{7,6},{8,9},{9,8},{10,11... | collective-permute-start | bytes 393224 | tf_op jit(solution)/shard_map/ppermute | solution.py:359
  1.3 4.0 %copy-start.2 = (bf16[1,4,128,128]{3,2,1,0:T(8,128)(2,1)S(1)}, bf16[1,4,128,128]{3,2,1,0:T(8,128)(2,1)}, u32[]{:S(2)}) copy-start(bf16[1,4,128,128]{3,2,1,0:T(8,128)(2,1)} %param.4) | copy-start | bytes 393220
  2.3 7.4 %collective-permute-start.1 = (bf16[4,128,128]{2,1,0:T(8,128)(2,1)S(1)}, bf16[4,128,128]{2,1,0:T(8,128)(2,1)S(1)}, u32[]{:S(2)}, u32[]{:S(2)}) collective-permute-start(bf16[4,128,128]{2,1,0:T(8,128)(2,1)S(1)} %collective-permute-done.x_core), channel_id=1, source_target_pairs={{0,2},{1,0},{2,4},{3,1},{4,6},{5,3},{6,8},{7,5},{8,10},{9,7},{10,1... | collective-permute-start | bytes 393224 | tf_op jit(solution)/shard_map/ppermute | solution.py:359
  6.5 5.4 %collective-permute-start.3 = (bf16[2,128,128]{2,1,0:T(8,128)(2,1)S(1)}, bf16[2,128,128]{2,1,0:T(8,128)(2,1)S(1)}, u32[]{:S(2)}, u32[]{:S(2)}) collective-permute-start(bf16[2,128,128]{2,1,0:T(8,128)(2,1)S(1)} %slice_select_fusion), channel_id=1, source_target_pairs={{0,2},{1,0},{2,4},{3,1},{4,6},{5,3},{6,8},{7,5},{8,10},{9,7},{10,1... | collective-permute-start | bytes 196616 | tf_op jit(solution)/shard_map/ppermute | solution.py:359
  8.1 6.3 %collective-permute-start.5 = (bf16[4,128,128]{2,1,0:T(8,128)(2,1)S(1)}, bf16[4,128,128]{2,1,0:T(8,128)(2,1)S(1)}, u32[]{:S(2)}, u32[]{:S(2)}) collective-permute-start(bf16[4,128,128]{2,1,0:T(8,128)(2,1)S(1)} %get-tuple-element.43.near_here), channel_id=1, source_target_pairs={{0,16},{1,17},{2,18},{3,19},{4,20},{5,21},{6,22},{7,23},{8,24},{9,... | collective-permute-start | bytes 393224 | tf_op jit(solution)/shard_map/ppermute | solution.py:359
  9.8 2.2 %copy-start.3 = (bf16[1,4,128,128]{3,2,1,0:T(8,128)(2,1)S(1)}, bf16[1,4,128,128]{3,2,1,0:T(8,128)(2,1)}, u32[]{:S(2)}) copy-start(bf16[1,4,128,128]{3,2,1,0:T(8,128)(2,1)} %param.5) | copy-start | bytes 393220
  11.1 5.0 %collective-permute-start.4 = (bf16[4,128,128]{2,1,0:T(8,128)(2,1)S(1)}, bf16[4,128,128]{2,1,0:T(8,128)(2,1)S(1)}, u32[]{:S(2)}, u32[]{:S(2)}) collective-permute-start(bf16[4,128,128]{2,1,0:T(8,128)(2,1)S(1)} %get-tuple-element.44.far_here), channel_id=1, source_target_pairs={{0,16},{1,17},{2,18},{3,19},{4,20},{5,21},{6,22},{7,23},{8,24},{9,... | collective-permute-start | bytes 393224 | tf_op jit(solution)/shard_map/ppermute | solution.py:359
  16.1 5.3 %collective-permute-start.7 = (bf16[4,128,128]{2,1,0:T(8,128)(2,1)S(1)}, bf16[4,128,128]{2,1,0:T(8,128)(2,1)S(1)}, u32[]{:S(2)}, u32[]{:S(2)}) collective-permute-start(bf16[4,128,128]{2,1,0:T(8,128)(2,1)S(1)} %get-tuple-element.47), channel_id=1, source_target_pairs={{0,16},{1,17},{2,18},{3,19},{4,20},{5,21},{6,22},{7,23},{8,24},{9,... | collective-permute-start | bytes 393224 | tf_op jit(solution)/shard_map/ppermute | solution.py:359
  18.5 4.9 %collective-permute-start.6 = (bf16[2,128,128]{2,1,0:T(8,128)(2,1)S(1)}, bf16[2,128,128]{2,1,0:T(8,128)(2,1)S(1)}, u32[]{:S(2)}, u32[]{:S(2)}) collective-permute-start(bf16[2,128,128]{2,1,0:T(8,128)(2,1)S(1)} %get-tuple-element.45), channel_id=1, source_target_pairs={{0,16},{1,18},{2,17},{3,20},{4,19},{5,22},{6,21},{7,24},{8,23},{9,... | collective-permute-start | bytes 196616 | tf_op jit(solution)/shard_map/ppermute | solution.py:359
  21.4 2.1 %collective-permute-start.8 = (bf16[4,128,128]{2,1,0:T(8,128)(2,1)S(1)}, bf16[4,128,128]{2,1,0:T(8,128)(2,1)S(1)}, u32[]{:S(2)}, u32[]{:S(2)}) collective-permute-start(bf16[4,128,128]{2,1,0:T(8,128)(2,1)S(1)} %collective-permute-done.7.back), channel_id=1, source_target_pairs={{0,1},{1,0},{2,3},{3,2},{4,5},{5,4},{6,7},{7,6},{8,9},{9,8},{10,11... | collective-permute-start | bytes 393224 | tf_op jit(solution)/shard_map/ppermute | solution.py:359
  24.3 1.8 %collective-permute-start.10 = (bf16[3,3,64,128]{3,2,1,0:T(8,128)(2,1)S(1)}, bf16[3,3,64,128]{3,2,1,0:T(8,128)(2,1)S(1)}, u32[]{:S(2)}, u32[]{:S(2)}) collective-permute-start(bf16[3,3,64,128]{3,2,1,0:T(8,128)(2,1)S(1)} %get-tuple-element.59), channel_id=1, source_target_pairs={{0,1},{1,0},{2,3},{3,2},{4,5},{5,4},{6,7},{7,6},{8,9},{9,8},{10,11... | collective-permute-start | bytes 442376 | tf_op jit(solution)/shard_map/ppermute | solution.py:359
  25.5 1.6 %collective-permute-start.9 = (bf16[3,3,64,128]{3,2,1,0:T(8,128)(2,1)S(1)}, bf16[3,3,64,128]{3,2,1,0:T(8,128)(2,1)S(1)}, u32[]{:S(2)}, u32[]{:S(2)}) collective-permute-start(bf16[3,3,64,128]{3,2,1,0:T(8,128)(2,1)S(1)} %get-tuple-element.57), channel_id=1, source_target_pairs={{0,1},{1,0},{2,3},{3,2},{4,5},{5,4},{6,7},{7,6},{8,9},{9,8},{10,11... | collective-permute-start | bytes 442376 | tf_op jit(solution)/shard_map/ppermute | solution.py:359
  27.1 6.9 %collective-permute-start.11 = (bf16[2,3,3,16,128]{4,3,2,1,0:T(8,128)(2,1)S(1)}, bf16[2,3,3,16,128]{4,3,2,1,0:T(8,128)(2,1)S(1)}, u32[]{:S(2)}, u32[]{:S(2)}) collective-permute-start(bf16[2,3,3,16,128]{4,3,2,1,0:T(8,128)(2,1)S(1)} %get-tuple-element.61), channel_id=1, source_target_pairs={{0,6},{1,7},{2,4},{3,5},{4,2},{5,3},{6,0},{7,1},{8,14},{9,15},{10,... | collective-permute-start | bytes 221192 | tf_op jit(solution)/shard_map/ppermute | solution.py:359
  30.9 4.6 %collective-permute-start.12 = (bf16[2,3,3,16,128]{4,3,2,1,0:T(8,128)(2,1)S(1)}, bf16[2,3,3,16,128]{4,3,2,1,0:T(8,128)(2,1)S(1)}, u32[]{:S(2)}, u32[]{:S(2)}) collective-permute-start(bf16[2,3,3,16,128]{4,3,2,1,0:T(8,128)(2,1)S(1)} %get-tuple-element.62), channel_id=1, source_target_pairs={{0,2},{1,5},{2,0},{3,7},{4,6},{5,1},{6,4},{7,3},{8,10},{9,13},{10,... | collective-permute-start | bytes 221192 | tf_op jit(solution)/shard_map/ppermute | solution.py:359
  30.9 4.6 %collective-permute-start.13 = (bf16[2,3,3,16,128]{4,3,2,1,0:T(8,128)(2,1)S(1)}, bf16[2,3,3,16,128]{4,3,2,1,0:T(8,128)(2,1)S(1)}, u32[]{:S(2)}, u32[]{:S(2)}) collective-permute-start(bf16[2,3,3,16,128]{4,3,2,1,0:T(8,128)(2,1)S(1)} %get-tuple-element.63), channel_id=1, source_target_pairs={{0,4},{1,3},{2,6},{3,1},{4,0},{5,7},{6,2},{7,5},{8,12},{9,11},{10,... | collective-permute-start | bytes 221192 | tf_op jit(solution)/shard_map/ppermute | solution.py:359
  35.5 6.7 %collective-permute-start.14 = (bf16[2,3,3,16,128]{4,3,2,1,0:T(8,128)(2,1)S(1)}, bf16[2,3,3,16,128]{4,3,2,1,0:T(8,128)(2,1)S(1)}, u32[]{:S(2)}, u32[]{:S(2)}) collective-permute-start(bf16[2,3,3,16,128]{4,3,2,1,0:T(8,128)(2,1)S(1)} %add_convert_fusion.1), channel_id=1, source_target_pairs={{0,8},{1,9},{2,10},{3,11},{4,12},{5,13},{6,14},{7,15},{8,0},{9,1},... | collective-permute-start | bytes 221192 | tf_op jit(solution)/shard_map/ppermute | solution.py:359
  42.2 5.4 %collective-permute-start.17 = (bf16[2,3,3,16,128]{4,3,2,1,0:T(8,128)(2,1)S(1)}, bf16[2,3,3,16,128]{4,3,2,1,0:T(8,128)(2,1)S(1)}, u32[]{:S(2)}, u32[]{:S(2)}) collective-permute-start(bf16[2,3,3,16,128]{4,3,2,1,0:T(8,128)(2,1)S(1)} %add_convert_fusion.mine), channel_id=1, source_target_pairs={{0,6},{1,7},{2,4},{3,5},{4,2},{5,3},{6,0},{7,1},{8,14},{9,15},{10,... | collective-permute-start | bytes 221192 | tf_op jit(solution)/shard_map/ppermute | solution.py:359
  43.0 5.7 %collective-permute-start.16 = (bf16[2,3,3,16,128]{4,3,2,1,0:T(8,128)(2,1)S(1)}, bf16[2,3,3,16,128]{4,3,2,1,0:T(8,128)(2,1)S(1)}, u32[]{:S(2)}, u32[]{:S(2)}) collective-permute-start(bf16[2,3,3,16,128]{4,3,2,1,0:T(8,128)(2,1)S(1)} %add_convert_fusion.mine), channel_id=1, source_target_pairs={{0,2},{1,5},{2,0},{3,7},{4,6},{5,1},{6,4},{7,3},{8,10},{9,13},{10,... | collective-permute-start | bytes 221192 | tf_op jit(solution)/shard_map/ppermute | solution.py:359
  43.9 4.8 %collective-permute-start.15 = (bf16[2,3,3,16,128]{4,3,2,1,0:T(8,128)(2,1)S(1)}, bf16[2,3,3,16,128]{4,3,2,1,0:T(8,128)(2,1)S(1)}, u32[]{:S(2)}, u32[]{:S(2)}) collective-permute-start(bf16[2,3,3,16,128]{4,3,2,1,0:T(8,128)(2,1)S(1)} %add_convert_fusion.mine), channel_id=1, source_target_pairs={{0,4},{1,3},{2,6},{3,1},{4,0},{5,7},{6,2},{7,5},{8,12},{9,11},{10,... | collective-permute-start | bytes 221192 | tf_op jit(solution)/shard_map/ppermute | solution.py:359
  48.8 1.6 %collective-permute-start.18 = (bf16[2,3,3,64,128]{4,3,2,1,0:T(8,128)(2,1)S(1)}, bf16[2,3,3,64,128]{4,3,2,1,0:T(8,128)(2,1)S(1)}, u32[]{:S(2)}, u32[]{:S(2)}) collective-permute-start(bf16[2,3,3,64,128]{4,3,2,1,0:T(8,128)(2,1)S(1)} %shard_map.87.mine), channel_id=1, source_target_pairs={{0,1},{1,0},{2,3},{3,2},{4,5},{5,4},{6,7},{7,6},{8,9},{9,8},{10,11... | collective-permute-start | bytes 884744 | tf_op jit(solution)/shard_map/ppermute | solution.py:359

commit v17 on v16

--- a/solution.py
+++ b/solution.py
@@ -103,7 +103,7 @@
             skip[i] = silu(pre[i]).astype(BF16)
 
 
-def far_kernel(segments, strips, xa, ha, x_far, main, second, first, pre, hid, skip, xb, hb):
+def far_kernel(segments, strips, xa, ha, x_far, main, second, first, pre, skip, hb, xb):
     encoder, row, even = here(segments)
     own = x_far.shape[0]
     near = ha.shape[0]
@@ -130,11 +130,6 @@
         for i in range(own):
             keep = jnp.logical_or(far_in, jnp.logical_not(even) if i < 2 else even)
             skip[i] = masked(silu(pre[i]), keep).astype(BF16)
-        for i in range(own):
-            middle = slice(channels, 2 * channels)
-            at_even = hb[own - 1, :, middle] if i == 0 else ha[i - 1, :, middle]
-            at_odd = hb[2, :, middle] if i == own - 1 else ha[own - 1 + i, :, middle]
-            hid[i] = jnp.where(even, at_even, at_odd)
 
 
 def rows_kernel(g, g_core, g_other, out):
@@ -231,38 +226,49 @@
             edge_grad[i] = masked(value, far_in).astype(BF16)
 
 
-def second_kernel(
-    segments, g, edge_grad, back, back_core, near_pre, far_pre, hid, near, far, gw, kept, sent, ew
+def second_kernel(segments, g, back, near_pre, far_pre, ha, hb, near, far, gw, kept, sent, ew):
+    encoder, _, even = here(segments)
+    own = back.shape[0]
+
+    @pl.when(encoder)
+    def _():
+        for i in range(own):
+            value = g[i + 2].astype(F32) + back[i].astype(F32)
+            place(ew, i, value * slope(joined(even, near_pre, far_pre, i + 2)))
+        rows = []
+        for i in range(own + 2):
+            at_even = hb[own - 2 + i] if i < 2 else ha[i - 2]
+            at_odd = ha[2 + i] if i < own else hb[i - 2]
+            rows.append(jnp.where(even, at_even, at_odd))
+        columns, channels = back.shape[1:]
+        grad = ew[:, :, channels : 2 * channels].reshape(own * columns, channels)
+        for ty in range(3):
+            lhs = jnp.concatenate(rows[ty : ty + own], axis=0)
+            out = lax.dot_general(lhs, grad, (((0,), (0,)), ((), ())), preferred_element_type=F32)
+            for tx in range(3):
+                store(even, kept, sent)(ty, tx, out[tx * channels : (tx + 1) * channels])
+
+    @pl.when(jnp.logical_not(encoder))
+    def _():
+        skip = jnp.stack([joined(even, near, far, i + 2) for i in range(own)])
+        conv_weight(skip, gw, 0, store(even, kept, sent))
+
+
+def main_kernel(
+    segments, strips, x, g, edge_grad, back_core, near_pre, near_first, far_first, e_own, gw, second, kept, sent, hw, ew
 ):
     encoder, row, even = here(segments)
-    own = back.shape[0]
-
-    @pl.when(encoder)
-    def _():
+    own = x.shape[0]
+
+    @pl.when(encoder)
+    def _():
+        ew[2 : own + 2] = e_own[...]
         for i in range(2):
             place(ew, jnp.where(even, 0, own + 2) + i, edge_grad[i].astype(F32))
-        for i in range(own):
-            value = g[i + 2].astype(F32) + back[i].astype(F32)
-            place(ew, 2 + i, value * slope(joined(even, near_pre, far_pre, i + 2)))
-        for i in range(2):
             upstream = g[jnp.where(even, own + 2, 0) + i].astype(F32)
             returned = jnp.where(even, back_core[i].astype(F32), back_core[own - 2 + i].astype(F32))
             value = (upstream + returned) * slope(jnp.where(even, near_pre[2 + i], near_pre[i]))
             place(ew, jnp.where(even, own + 2, 0) + i, value)
-        conv_weight(hid[...], ew, 1, store(even, kept, sent))
-
-    @pl.when(jnp.logical_not(encoder))
-    def _():
-        skip = jnp.stack([joined(even, near, far, i + 2) for i in range(own)])
-        conv_weight(skip, gw, 0, store(even, kept, sent))
-
-
-def main_kernel(segments, strips, x, near_first, far_first, ew, gw, second, kept, sent, hw):
-    encoder, row, even = here(segments)
-    own = x.shape[0]
-
-    @pl.when(encoder)
-    def _():
         hidden_back = conv_back(ew, 0, own + 2, second)
         for i in range(own + 2):
             value = hidden_back[i] * slope(joined_first(even, near_first, far_first, i))
@@ -384,10 +390,10 @@
     near_there = swap(near_here, True, same)
     g_other = swap(edge, False, far)
     (g_rows,) = call(rows_kernel, [like(own + 4, BF16)], [], (g, g_core, g_other), 2 * 10**9)
-    far_first, far_pre, hid, far_here = call(
+    far_first, far_pre, far_here, hb = call(
         functools.partial(far_kernel, segments, strips),
-        [like(own, F32), like(own, F32), like(own, BF16), like(own, BF16)],
-        [wide(own + 2), wide(own + 2)],
+        [like(own, F32), like(own, F32), like(own, BF16), wide_out(own + 2)],
+        [wide(own + 2)],
         (xa, ha, x_far, main, second),
         work * 2 * own,
     )
@@ -415,18 +421,18 @@
     taps = (3, 3, channels, channels)
     halves = (3, 3, channels // 2, channels)
     terms = [jax.ShapeDtypeStruct(halves, F32), jax.ShapeDtypeStruct(halves, BF16)]
-    kept2, sent2, ew = call(
+    kept2, sent2, e_own = call(
         functools.partial(second_kernel, segments),
-        terms + [wide_out(own + 4)],
+        terms + [wide_out(own)],
         [],
-        (g_rows, edge_grad, back_own, back_core, near_pre, far_pre, hid, near_there, far_there, gw),
+        (g_rows, back_own, near_pre, far_pre, ha, hb, near_there, far_there, gw),
         work * own,
     )
     kept1, sent1, hw = call(
         functools.partial(main_kernel, segments, strips),
         terms + [wide_out(own + 2)],
-        [],
-        (x, near_first, far_first, ew, gw, second),
+        [wide(own + 4)],
+        (x, g_rows, edge_grad, back_core, near_pre, near_first, far_first, e_own, gw, second),
         work * (2 * own + 2),
     )
     input_grad, output = call(input_kernel, [like(own, BF16)] * 2, [], (hw, main, out), work * own)
@@ -440,7 +446,7 @@
 
     bits = strips.bit_length() - 1
     quarter = (2, 3, 3, channels // 8, channels)
-    (total2,) = call(sum_kernel, [jax.ShapeDtypeStruct(halves, F32)], [], (kept2, jump(sent2, 0)), 3 * 10**9)
+    (total2,) = call(sum_kernel, [jax.ShapeDtypeStruct(halves, F32)], [], (kept2, jump(sent2, 0)), 10**9)
     got1 = jump(sent1, 0)
     mine, *sends = call(
         pack_kernel,

time: 51.7 us -> 51.9 us (level)
  starting transfers between devices: 20.7 us -> 21.8 us
  waiting for transfers between devices: 23.1 us -> 22.2 us
    ppermute x19, starting transfers between devices: 20.7 us -> 21.8 us  [swap(): return lax.ppermute(array, ('segment', 'rows'), pairs)]
    ppermute x19, waiting for transfers between devices: 23.1 us -> 22.2 us  [swap(): return lax.ppermute(array, ('segment', 'rows'), pairs)]
  transfers between devices with their start and end apart: 19 -> 19, of which waited for: 13 -> 14; matrix products, arithmetic and copies ran while one was open for 0% -> 0% of each run, Pallas kernels for 10% -> 11%
where the time goes in v17:
time: 51.9 us; the launch traced here: 51.8 us
  waiting for transfers between devices  22.2 us (43%)
  starting transfers between devices  21.8 us (42%)
  Pallas kernels  6.9 us (13%)
  between operations  0.76 us (1%)
    ppermute x19, waiting for transfers between devices, swap(): return lax.ppermute(array, ('segment', 'rows'), pairs)  22.2 us
    ppermute x19, starting transfers between devices, swap(): return lax.ppermute(array, ('segment', 'rows'), pairs)  21.8 us
    pallas_call x14, Pallas kernels, call(): pl.pallas_call(kernel, out_shape=outs, in_specs=[pl.BlockSpec(memory_spac...  6.9 us
  transfers between devices with their start and end apart: 19, of which 14 were waited for; matrix products, arithmetic and copies ran while one was open for 0% of the time, Pallas kernels for 11%

profile of v17, /device:TPU:0, one launch (start us, length us, event | category | flops | bytes accessed | tf_op | source)
XLA Modules:
  0.0 51.8 jit_solution(4924999971604050196)
XLA Ops:
  0.6 0.5 %collective-permute-start.1 = (bf16[4,128,128]{2,1,0:T(8,128)(2,1)}, bf16[4,128,128]{2,1,0:T(8,128)(2,1)S(1)}, u32[]{:S(2)}, u32[]{:S(2)}) collective-permute-start(bf16[4,128,128]{2,1,0:T(8,128)(2,1)} %bitcast.16), channel_id=1, source_target_pairs={{0,1},{1,0},{2,3},{3,2},{4,5},{5,4},{6,7},{7,6},{8,9},{9,8},{10,11... | collective-permute-start | bytes 393224 | tf_op jit(solution)/shard_map/ppermute | solution.py:365
  1.3 1.1 %collective-permute-done.1.x_core = bf16[4,128,128]{2,1,0:T(8,128)(2,1)S(1)} collective-permute-done((bf16[4,128,128]{2,1,0:T(8,128)(2,1)}, bf16[4,128,128]{2,1,0:T(8,128)(2,1)S(1)}, u32[]{:S(2)}, u32[]{:S(2)}) %collective-permute-start.1) | collective-permute-done | bytes 131104 | tf_op jit(solution)/shard_map/ppermute | solution.py:365
  2.3 2.8 %collective-permute-start.3 = (bf16[4,128,128]{2,1,0:T(8,128)(2,1)S(1)}, bf16[4,128,128]{2,1,0:T(8,128)(2,1)S(1)}, u32[]{:S(2)}, u32[]{:S(2)}) collective-permute-start(bf16[4,128,128]{2,1,0:T(8,128)(2,1)S(1)} %collective-permute-done.1.x_core), channel_id=1, source_target_pairs={{0,2},{1,0},{2,4},{3,1},{4,6},{5,3},{6,8},{7,5},{8,10},{9,7},{10,1... | collective-permute-start | bytes 393224 | tf_op jit(solution)/shard_map/ppermute | solution.py:365
  5.2 1.3 %shard_map.76 = (bf16[8,128,384]{2,1,0:T(8,128)(2,1)S(1)}, f32[6,128,128]{2,1,0:T(8,128)S(1)}, bf16[6,128,384]{2,1,0:T(8,128)(2,1)S(1)}, f32[4,128,128]{2,1,0:T(8,128)S(1)}, bf16[4,128,128]{2,1,0:T(8,128)(2,1)S(1)}) custom-call(f32[8,128]{1,0:T(8,128)S(1)} %shard_map.75.token, bf16[4,128,128]{2,1,0:T(8,128)(2,1)S(1)} %bitcast.17, ...), custom_call_target="tpu_custom_call" | custom-call | flops 377487360 | bytes 3018752 | tf_op jit(solution)/shard_map/pallas_call | solution.py:328
  6.5 1.6 %collective-permute-start.2 = (bf16[2,128,128]{2,1,0:T(8,128)(2,1)S(1)}, bf16[2,128,128]{2,1,0:T(8,128)(2,1)S(1)}, u32[]{:S(2)}, u32[]{:S(2)}) collective-permute-start(bf16[2,128,128]{2,1,0:T(8,128)(2,1)S(1)} %slice_select_fusion), channel_id=1, source_target_pairs={{0,2},{1,0},{2,4},{3,1},{4,6},{5,3},{6,8},{7,5},{8,10},{9,7},{10,1... | collective-permute-start | bytes 196616 | tf_op jit(solution)/shard_map/ppermute | solution.py:365
  8.1 1.0 %collective-permute-start.5 = (bf16[4,128,128]{2,1,0:T(8,128)(2,1)S(1)}, bf16[4,128,128]{2,1,0:T(8,128)(2,1)S(1)}, u32[]{:S(2)}, u32[]{:S(2)}) collective-permute-start(bf16[4,128,128]{2,1,0:T(8,128)(2,1)S(1)} %get-tuple-element.39.near_here), channel_id=1, source_target_pairs={{0,16},{1,17},{2,18},{3,19},{4,20},{5,21},{6,22},{7,23},{8,24},{9,... | collective-permute-start | bytes 393224 | tf_op jit(solution)/shard_map/ppermute | solution.py:365
  9.1 0.6 %collective-permute-done.3.x_far = bf16[4,128,128]{2,1,0:T(8,128)(2,1)S(1)} collective-permute-done((bf16[4,128,128]{2,1,0:T(8,128)(2,1)S(1)}, bf16[4,128,128]{2,1,0:T(8,128)(2,1)S(1)}, u32[]{:S(2)}, u32[]{:S(2)}) %collective-permute-start.3) | collective-permute-done | bytes 131104 | tf_op jit(solution)/shard_map/ppermute | solution.py:365
  9.8 1.2 %shard_map.78 = (f32[4,128,128]{2,1,0:T(8,128)S(1)}, f32[4,128,128]{2,1,0:T(8,128)S(1)}, bf16[4,128,128]{2,1,0:T(8,128)(2,1)S(1)}, bf16[6,128,384]{2,1,0:T(8,128)(2,1)S(1)}) custom-call(bf16[8,128,384]{2,1,0:T(8,128)(2,1)S(1)} %get-tuple-element.40.xa, bf16[6,128,384]{2,1,0:T(8,128)(2,1)S(1)} %get-tuple-element.41.ha, ...), custom_call_target="tpu_custom_call" | custom-call | flops 301989888 | bytes 3342336 | tf_op jit(solution)/shard_map/pallas_call | solution.py:328
  11.0 1.0 %collective-permute-start.4 = (bf16[4,128,128]{2,1,0:T(8,128)(2,1)S(1)}, bf16[4,128,128]{2,1,0:T(8,128)(2,1)S(1)}, u32[]{:S(2)}, u32[]{:S(2)}) collective-permute-start(bf16[4,128,128]{2,1,0:T(8,128)(2,1)S(1)} %get-tuple-element.42.far_here), channel_id=1, source_target_pairs={{0,16},{1,17},{2,18},{3,19},{4,20},{5,21},{6,22},{7,23},{8,24},{9,... | collective-permute-start | bytes 393224 | tf_op jit(solution)/shard_map/ppermute | solution.py:365
  12.0 2.5 %collective-permute-done.5.near = bf16[4,128,128]{2,1,0:T(8,128)(2,1)S(1)} collective-permute-done((bf16[4,128,128]{2,1,0:T(8,128)(2,1)S(1)}, bf16[4,128,128]{2,1,0:T(8,128)(2,1)S(1)}, u32[]{:S(2)}, u32[]{:S(2)}) %collective-permute-start.5) | collective-permute-done | bytes 131104 | tf_op jit(solution)/shard_map/ppermute | solution.py:365
  14.5 1.6 %collective-permute-done.4.far = bf16[4,128,128]{2,1,0:T(8,128)(2,1)S(1)} collective-permute-done((bf16[4,128,128]{2,1,0:T(8,128)(2,1)S(1)}, bf16[4,128,128]{2,1,0:T(8,128)(2,1)S(1)}, u32[]{:S(2)}, u32[]{:S(2)}) %collective-permute-start.4) | collective-permute-done | bytes 131104 | tf_op jit(solution)/shard_map/ppermute | solution.py:365
  16.1 2.4 %collective-permute-start.7 = (bf16[4,128,128]{2,1,0:T(8,128)(2,1)S(1)}, bf16[4,128,128]{2,1,0:T(8,128)(2,1)S(1)}, u32[]{:S(2)}, u32[]{:S(2)}) collective-permute-start(bf16[4,128,128]{2,1,0:T(8,128)(2,1)S(1)} %get-tuple-element.47), channel_id=1, source_target_pairs={{0,16},{1,17},{2,18},{3,19},{4,20},{5,21},{6,22},{7,23},{8,24},{9,... | collective-permute-start | bytes 393224 | tf_op jit(solution)/shard_map/ppermute | solution.py:365
  18.5 2.9 %collective-permute-done.7.back = bf16[4,128,128]{2,1,0:T(8,128)(2,1)S(1)} collective-permute-done((bf16[4,128,128]{2,1,0:T(8,128)(2,1)S(1)}, bf16[4,128,128]{2,1,0:T(8,128)(2,1)S(1)}, u32[]{:S(2)}, u32[]{:S(2)}) %collective-permute-start.7) | collective-permute-done | bytes 131104 | tf_op jit(solution)/shard_map/ppermute | solution.py:365
  21.4 0.7 %shard_map.82 = (f32[3,3,64,128]{3,2,1,0:T(8,128)S(1)}, bf16[3,3,64,128]{3,2,1,0:T(8,128)(2,1)S(1)}, bf16[4,128,384]{2,1,0:T(8,128)(2,1)S(1)}) custom-call(bf16[8,128,128]{2,1,0:T(8,128)(2,1)S(1)} %shard_map.77.g, bf16[4,128,128]{2,1,0:T(8,128)(2,1)S(1)} %collective-permute-done.7.back, f32[4,128,128]{2,1,0:T(8,128)S(1)} %get-tuple-element.48.near_pre, ...), custom_call_target="tpu_custom_call" | custom-call | flops 150994944 | bytes 3784704 | tf_op jit(solution)/shard_map/pallas_call | solution.py:328
  22.2 0.5 collective-permute-start.8
  22.7 0.7 %collective-permute-done.6.back_other = bf16[2,128,128]{2,1,0:T(8,128)(2,1)S(1)} collective-permute-done((bf16[2,128,128]{2,1,0:T(8,128)(2,1)S(1)}, bf16[2,128,128]{2,1,0:T(8,128)(2,1)S(1)}, u32[]{:S(2)}, u32[]{:S(2)}) %collective-permute-start.6) | collective-permute-done | bytes 65568 | tf_op jit(solution)/shard_map/ppermute | solution.py:365
  23.7 1.2 %shard_map.83 = (f32[3,3,64,128]{3,2,1,0:T(8,128)S(1)}, bf16[3,3,64,128]{3,2,1,0:T(8,128)(2,1)S(1)}, bf16[6,128,384]{2,1,0:T(8,128)(2,1)S(1)}) custom-call(bf16[4,128,128]{2,1,0:T(8,128)(2,1)S(1)} %bitcast.18, bf16[8,128,128]{2,1,0:T(8,128)(2,1)S(1)} %shard_map.77.g, bf16[2,128,128]{2,1,0:T(8,128)(2,1)S(1)} %shard_map.81.edge_grad, ...), custom_call_target="tpu_custom_call" | custom-call | flops 377487360 | bytes 3817472 | tf_op jit(solution)/shard_map/pallas_call | solution.py:328
  25.0 0.4 collective-permute-start.9
  25.4 1.0 %collective-permute-done.9.got1 = bf16[3,3,64,128]{3,2,1,0:T(8,128)(2,1)S(1)} collective-permute-done((bf16[3,3,64,128]{3,2,1,0:T(8,128)(2,1)S(1)}, bf16[3,3,64,128]{3,2,1,0:T(8,128)(2,1)S(1)}, u32[]{:S(2)}, u32[]{:S(2)}) %collective-permute-start.9) | collective-permute-done | bytes 147488 | tf_op jit(solution)/shard_map/ppermute | solution.py:365
  26.5 4.5 %collective-permute-start.11 = (bf16[2,3,3,16,128]{4,3,2,1,0:T(8,128)(2,1)S(1)}, bf16[2,3,3,16,128]{4,3,2,1,0:T(8,128)(2,1)S(1)}, u32[]{:S(2)}, u32[]{:S(2)}) collective-permute-start(bf16[2,3,3,16,128]{4,3,2,1,0:T(8,128)(2,1)S(1)} %get-tuple-element.61), channel_id=1, source_target_pairs={{0,6},{1,7},{2,4},{3,5},{4,2},{5,3},{6,0},{7,1},{8,14},{9,15},{10,... | collective-permute-start | bytes 221192 | tf_op jit(solution)/shard_map/ppermute | solution.py:365
  31.0 0.6 %collective-permute-start.13 = (bf16[2,3,3,16,128]{4,3,2,1,0:T(8,128)(2,1)S(1)}, bf16[2,3,3,16,128]{4,3,2,1,0:T(8,128)(2,1)S(1)}, u32[]{:S(2)}, u32[]{:S(2)}) collective-permute-start(bf16[2,3,3,16,128]{4,3,2,1,0:T(8,128)(2,1)S(1)} %get-tuple-element.63), channel_id=1, source_target_pairs={{0,4},{1,3},{2,6},{3,1},{4,0},{5,7},{6,2},{7,5},{8,12},{9,11},{10,... | collective-permute-start | bytes 221192 | tf_op jit(solution)/shard_map/ppermute | solution.py:365
  31.6 2.4 %collective-permute-done.11 = bf16[2,3,3,16,128]{4,3,2,1,0:T(8,128)(2,1)S(1)} collective-permute-done((bf16[2,3,3,16,128]{4,3,2,1,0:T(8,128)(2,1)S(1)}, bf16[2,3,3,16,128]{4,3,2,1,0:T(8,128)(2,1)S(1)}, u32[]{:S(2)}, u32[]{:S(2)}) %collective-permute-start.11) | collective-permute-done | bytes 73760 | tf_op jit(solution)/shard_map/ppermute | solution.py:365
  34.0 1.5 %collective-permute-done.12 = bf16[2,3,3,16,128]{4,3,2,1,0:T(8,128)(2,1)S(1)} collective-permute-done((bf16[2,3,3,16,128]{4,3,2,1,0:T(8,128)(2,1)S(1)}, bf16[2,3,3,16,128]{4,3,2,1,0:T(8,128)(2,1)S(1)}, u32[]{:S(2)}, u32[]{:S(2)}) %collective-permute-start.12) | collective-permute-done | bytes 73760 | tf_op jit(solution)/shard_map/ppermute | solution.py:365
  35.5 2.5 %collective-permute-start.14 = (bf16[2,3,3,16,128]{4,3,2,1,0:T(8,128)(2,1)S(1)}, bf16[2,3,3,16,128]{4,3,2,1,0:T(8,128)(2,1)S(1)}, u32[]{:S(2)}, u32[]{:S(2)}) collective-permute-start(bf16[2,3,3,16,128]{4,3,2,1,0:T(8,128)(2,1)S(1)} %add_convert_fusion.1), channel_id=1, source_target_pairs={{0,8},{1,9},{2,10},{3,11},{4,12},{5,13},{6,14},{7,15},{8,0},{9,1},... | collective-permute-start | bytes 221192 | tf_op jit(solution)/shard_map/ppermute | solution.py:365
  38.0 4.1 %collective-permute-done.14 = bf16[2,3,3,16,128]{4,3,2,1,0:T(8,128)(2,1)S(1)} collective-permute-done((bf16[2,3,3,16,128]{4,3,2,1,0:T(8,128)(2,1)S(1)}, bf16[2,3,3,16,128]{4,3,2,1,0:T(8,128)(2,1)S(1)}, u32[]{:S(2)}, u32[]{:S(2)}) %collective-permute-start.14) | collective-permute-done | bytes 73760 | tf_op jit(solution)/shard_map/ppermute | solution.py:365
  42.1 1.0 %collective-permute-start.17 = (bf16[2,3,3,16,128]{4,3,2,1,0:T(8,128)(2,1)S(1)}, bf16[2,3,3,16,128]{4,3,2,1,0:T(8,128)(2,1)S(1)}, u32[]{:S(2)}, u32[]{:S(2)}) collective-permute-start(bf16[2,3,3,16,128]{4,3,2,1,0:T(8,128)(2,1)S(1)} %add_convert_fusion.mine), channel_id=1, source_target_pairs={{0,6},{1,7},{2,4},{3,5},{4,2},{5,3},{6,0},{7,1},{8,14},{9,15},{10,... | collective-permute-start | bytes 221192 | tf_op jit(solution)/shard_map/ppermute | solution.py:365
  43.1 1.0 %collective-permute-start.16 = (bf16[2,3,3,16,128]{4,3,2,1,0:T(8,128)(2,1)S(1)}, bf16[2,3,3,16,128]{4,3,2,1,0:T(8,128)(2,1)S(1)}, u32[]{:S(2)}, u32[]{:S(2)}) collective-permute-start(bf16[2,3,3,16,128]{4,3,2,1,0:T(8,128)(2,1)S(1)} %add_convert_fusion.mine), channel_id=1, source_target_pairs={{0,2},{1,5},{2,0},{3,7},{4,6},{5,1},{6,4},{7,3},{8,10},{9,13},{10,... | collective-permute-start | bytes 221192 | tf_op jit(solution)/shard_map/ppermute | solution.py:365
  44.1 1.6 %collective-permute-start.15 = (bf16[2,3,3,16,128]{4,3,2,1,0:T(8,128)(2,1)S(1)}, bf16[2,3,3,16,128]{4,3,2,1,0:T(8,128)(2,1)S(1)}, u32[]{:S(2)}, u32[]{:S(2)}) collective-permute-start(bf16[2,3,3,16,128]{4,3,2,1,0:T(8,128)(2,1)S(1)} %add_convert_fusion.mine), channel_id=1, source_target_pairs={{0,4},{1,3},{2,6},{3,1},{4,0},{5,7},{6,2},{7,5},{8,12},{9,11},{10,... | collective-permute-start | bytes 221192 | tf_op jit(solution)/shard_map/ppermute | solution.py:365
  45.7 1.9 %collective-permute-done.17.rest_2_ = bf16[2,3,3,16,128]{4,3,2,1,0:T(8,128)(2,1)S(1)} collective-permute-done((bf16[2,3,3,16,128]{4,3,2,1,0:T(8,128)(2,1)S(1)}, bf16[2,3,3,16,128]{4,3,2,1,0:T(8,128)(2,1)S(1)}, u32[]{:S(2)}, u32[]{:S(2)}) %collective-permute-start.17) | collective-permute-done | bytes 73760 | tf_op jit(solution)/shard_map/ppermute | solution.py:365
  47.6 1.4 %collective-permute-done.16.rest_1_ = bf16[2,3,3,16,128]{4,3,2,1,0:T(8,128)(2,1)S(1)} collective-permute-done((bf16[2,3,3,16,128]{4,3,2,1,0:T(8,128)(2,1)S(1)}, bf16[2,3,3,16,128]{4,3,2,1,0:T(8,128)(2,1)S(1)}, u32[]{:S(2)}, u32[]{:S(2)}) %collective-permute-start.16) | collective-permute-done | bytes 73760 | tf_op jit(solution)/shard_map/ppermute | solution.py:365
  49.2 1.1 %shard_map.84 = (bf16[4,128,128]{2,1,0:T(8,128)(2,1)}, bf16[4,128,128]{2,1,0:T(8,128)(2,1)}) custom-call(bf16[6,128,384]{2,1,0:T(8,128)(2,1)S(1)} %get-tuple-element.52.hw, bf16[3,3,128,128]{3,2,1,0:T(8,128)(2,1)S(1)} %bitcast.15, bf16[4,128,128]{2,1,0:T(8,128)(2,1)S(1)} %get-tuple-element.53.out), custom_call_target="tpu_custom_call" | custom-call | flops 150994944 | bytes 1277952 | tf_op jit(solution)/shard_map/pallas_call | solution.py:328
  50.7 1.1 %shard_map.88 = (f32[3,3,128,128]{3,2,1,0:T(8,128)}, f32[3,3,128,128]{3,2,1,0:T(8,128)}) custom-call(bf16[2,3,3,64,128]{4,3,2,1,0:T(8,128)(2,1)S(1)} %shard_map.87.mine, bf16[2,3,3,64,128]{4,3,2,1,0:T(8,128)(2,1)S(1)} %collective-permute-done.18.theirs), custom_call_target="tpu_custom_call" | custom-call | flops 73728 | bytes 1769472 | tf_op jit(solution)/shard_map/pallas_call | solution.py:328
  (31 shorter events, 1.4 us)
Async XLA Ops:
  0.6 1.7 %collective-permute-start.1 = (bf16[4,128,128]{2,1,0:T(8,128)(2,1)}, bf16[4,128,128]{2,1,0:T(8,128)(2,1)S(1)}, u32[]{:S(2)}, u32[]{:S(2)}) collective-permute-start(bf16[4,128,128]{2,1,0:T(8,128)(2,1)} %bitcast.16), channel_id=1, source_target_pairs={{0,1},{1,0},{2,3},{3,2},{4,5},{5,4},{6,7},{7,6},{8,9},{9,8},{10,11... | collective-permute-start | bytes 393224 | tf_op jit(solution)/shard_map/ppermute | solution.py:365
  1.1 4.1 %copy-start = (bf16[1,3,3,128,128]{4,3,2,1,0:T(8,128)(2,1)S(1)}, bf16[1,3,3,128,128]{4,3,2,1,0:T(8,128)(2,1)}, u32[]{:S(2)}) copy-start(bf16[1,3,3,128,128]{4,3,2,1,0:T(8,128)(2,1)} %param.7) | copy-start | bytes 884740
  1.2 4.1 %copy-start.1 = (bf16[1,3,3,128,128]{4,3,2,1,0:T(8,128)(2,1)S(1)}, bf16[1,3,3,128,128]{4,3,2,1,0:T(8,128)(2,1)}, u32[]{:S(2)}) copy-start(bf16[1,3,3,128,128]{4,3,2,1,0:T(8,128)(2,1)} %param.6) | copy-start | bytes 884740
  1.2 4.0 %collective-permute-start = (bf16[4,128,128]{2,1,0:T(8,128)(2,1)}, bf16[4,128,128]{2,1,0:T(8,128)(2,1)S(1)}, u32[]{:S(2)}, u32[]{:S(2)}) collective-permute-start(bf16[4,128,128]{2,1,0:T(8,128)(2,1)} %bitcast.19), channel_id=1, source_target_pairs={{0,1},{1,0},{2,3},{3,2},{4,5},{5,4},{6,7},{7,6},{8,9},{9,8},{10,11... | collective-permute-start | bytes 393224 | tf_op jit(solution)/shard_map/ppermute | solution.py:365
  1.3 4.0 %copy-start.2 = (bf16[1,4,128,128]{3,2,1,0:T(8,128)(2,1)S(1)}, bf16[1,4,128,128]{3,2,1,0:T(8,128)(2,1)}, u32[]{:S(2)}) copy-start(bf16[1,4,128,128]{3,2,1,0:T(8,128)(2,1)} %param.4) | copy-start | bytes 393220
  2.3 7.4 %collective-permute-start.3 = (bf16[4,128,128]{2,1,0:T(8,128)(2,1)S(1)}, bf16[4,128,128]{2,1,0:T(8,128)(2,1)S(1)}, u32[]{:S(2)}, u32[]{:S(2)}) collective-permute-start(bf16[4,128,128]{2,1,0:T(8,128)(2,1)S(1)} %collective-permute-done.1.x_core), channel_id=1, source_target_pairs={{0,2},{1,0},{2,4},{3,1},{4,6},{5,3},{6,8},{7,5},{8,10},{9,7},{10,1... | collective-permute-start | bytes 393224 | tf_op jit(solution)/shard_map/ppermute | solution.py:365
  6.5 5.5 %collective-permute-start.2 = (bf16[2,128,128]{2,1,0:T(8,128)(2,1)S(1)}, bf16[2,128,128]{2,1,0:T(8,128)(2,1)S(1)}, u32[]{:S(2)}, u32[]{:S(2)}) collective-permute-start(bf16[2,128,128]{2,1,0:T(8,128)(2,1)S(1)} %slice_select_fusion), channel_id=1, source_target_pairs={{0,2},{1,0},{2,4},{3,1},{4,6},{5,3},{6,8},{7,5},{8,10},{9,7},{10,1... | collective-permute-start | bytes 196616 | tf_op jit(solution)/shard_map/ppermute | solution.py:365
  8.1 6.4 %collective-permute-start.5 = (bf16[4,128,128]{2,1,0:T(8,128)(2,1)S(1)}, bf16[4,128,128]{2,1,0:T(8,128)(2,1)S(1)}, u32[]{:S(2)}, u32[]{:S(2)}) collective-permute-start(bf16[4,128,128]{2,1,0:T(8,128)(2,1)S(1)} %get-tuple-element.39.near_here), channel_id=1, source_target_pairs={{0,16},{1,17},{2,18},{3,19},{4,20},{5,21},{6,22},{7,23},{8,24},{9,... | collective-permute-start | bytes 393224 | tf_op jit(solution)/shard_map/ppermute | solution.py:365
  9.8 2.2 %copy-start.3 = (bf16[1,4,128,128]{3,2,1,0:T(8,128)(2,1)S(1)}, bf16[1,4,128,128]{3,2,1,0:T(8,128)(2,1)}, u32[]{:S(2)}) copy-start(bf16[1,4,128,128]{3,2,1,0:T(8,128)(2,1)} %param.5) | copy-start | bytes 393220
  11.0 5.0 %collective-permute-start.4 = (bf16[4,128,128]{2,1,0:T(8,128)(2,1)S(1)}, bf16[4,128,128]{2,1,0:T(8,128)(2,1)S(1)}, u32[]{:S(2)}, u32[]{:S(2)}) collective-permute-start(bf16[4,128,128]{2,1,0:T(8,128)(2,1)S(1)} %get-tuple-element.42.far_here), channel_id=1, source_target_pairs={{0,16},{1,17},{2,18},{3,19},{4,20},{5,21},{6,22},{7,23},{8,24},{9,... | collective-permute-start | bytes 393224 | tf_op jit(solution)/shard_map/ppermute | solution.py:365
  16.1 5.3 %collective-permute-start.7 = (bf16[4,128,128]{2,1,0:T(8,128)(2,1)S(1)}, bf16[4,128,128]{2,1,0:T(8,128)(2,1)S(1)}, u32[]{:S(2)}, u32[]{:S(2)}) collective-permute-start(bf16[4,128,128]{2,1,0:T(8,128)(2,1)S(1)} %get-tuple-element.47), channel_id=1, source_target_pairs={{0,16},{1,17},{2,18},{3,19},{4,20},{5,21},{6,22},{7,23},{8,24},{9,... | collective-permute-start | bytes 393224 | tf_op jit(solution)/shard_map/ppermute | solution.py:365
  18.5 4.9 %collective-permute-start.6 = (bf16[2,128,128]{2,1,0:T(8,128)(2,1)S(1)}, bf16[2,128,128]{2,1,0:T(8,128)(2,1)S(1)}, u32[]{:S(2)}, u32[]{:S(2)}) collective-permute-start(bf16[2,128,128]{2,1,0:T(8,128)(2,1)S(1)} %get-tuple-element.45), channel_id=1, source_target_pairs={{0,16},{1,18},{2,17},{3,20},{4,19},{5,22},{6,21},{7,24},{8,23},{9,... | collective-permute-start | bytes 196616 | tf_op jit(solution)/shard_map/ppermute | solution.py:365
  22.1 3.3 %collective-permute-start.10 = (bf16[3,3,64,128]{3,2,1,0:T(8,128)(2,1)S(1)}, bf16[3,3,64,128]{3,2,1,0:T(8,128)(2,1)S(1)}, u32[]{:S(2)}, u32[]{:S(2)}) collective-permute-start(bf16[3,3,64,128]{3,2,1,0:T(8,128)(2,1)S(1)} %get-tuple-element.59), channel_id=1, source_target_pairs={{0,1},{1,0},{2,3},{3,2},{4,5},{5,4},{6,7},{7,6},{8,9},{9,8},{10,11... | collective-permute-start | bytes 442376 | tf_op jit(solution)/shard_map/ppermute | solution.py:365
  22.2 1.5 %collective-permute-start.8 = (bf16[4,128,128]{2,1,0:T(8,128)(2,1)S(1)}, bf16[4,128,128]{2,1,0:T(8,128)(2,1)S(1)}, u32[]{:S(2)}, u32[]{:S(2)}) collective-permute-start(bf16[4,128,128]{2,1,0:T(8,128)(2,1)S(1)} %collective-permute-done.7.back), channel_id=1, source_target_pairs={{0,1},{1,0},{2,3},{3,2},{4,5},{5,4},{6,7},{7,6},{8,9},{9,8},{10,11... | collective-permute-start | bytes 393224 | tf_op jit(solution)/shard_map/ppermute | solution.py:365
  25.0 1.4 %collective-permute-start.9 = (bf16[3,3,64,128]{3,2,1,0:T(8,128)(2,1)S(1)}, bf16[3,3,64,128]{3,2,1,0:T(8,128)(2,1)S(1)}, u32[]{:S(2)}, u32[]{:S(2)}) collective-permute-start(bf16[3,3,64,128]{3,2,1,0:T(8,128)(2,1)S(1)} %get-tuple-element.57), channel_id=1, source_target_pairs={{0,1},{1,0},{2,3},{3,2},{4,5},{5,4},{6,7},{7,6},{8,9},{9,8},{10,11... | collective-permute-start | bytes 442376 | tf_op jit(solution)/shard_map/ppermute | solution.py:365
  26.5 7.5 %collective-permute-start.11 = (bf16[2,3,3,16,128]{4,3,2,1,0:T(8,128)(2,1)S(1)}, bf16[2,3,3,16,128]{4,3,2,1,0:T(8,128)(2,1)S(1)}, u32[]{:S(2)}, u32[]{:S(2)}) collective-permute-start(bf16[2,3,3,16,128]{4,3,2,1,0:T(8,128)(2,1)S(1)} %get-tuple-element.61), channel_id=1, source_target_pairs={{0,6},{1,7},{2,4},{3,5},{4,2},{5,3},{6,0},{7,1},{8,14},{9,15},{10,... | collective-permute-start | bytes 221192 | tf_op jit(solution)/shard_map/ppermute | solution.py:365
  31.0 4.5 %collective-permute-start.12 = (bf16[2,3,3,16,128]{4,3,2,1,0:T(8,128)(2,1)S(1)}, bf16[2,3,3,16,128]{4,3,2,1,0:T(8,128)(2,1)S(1)}, u32[]{:S(2)}, u32[]{:S(2)}) collective-permute-start(bf16[2,3,3,16,128]{4,3,2,1,0:T(8,128)(2,1)S(1)} %get-tuple-element.62), channel_id=1, source_target_pairs={{0,2},{1,5},{2,0},{3,7},{4,6},{5,1},{6,4},{7,3},{8,10},{9,13},{10,... | collective-permute-start | bytes 221192 | tf_op jit(solution)/shard_map/ppermute | solution.py:365
  31.0 4.5 %collective-permute-start.13 = (bf16[2,3,3,16,128]{4,3,2,1,0:T(8,128)(2,1)S(1)}, bf16[2,3,3,16,128]{4,3,2,1,0:T(8,128)(2,1)S(1)}, u32[]{:S(2)}, u32[]{:S(2)}) collective-permute-start(bf16[2,3,3,16,128]{4,3,2,1,0:T(8,128)(2,1)S(1)} %get-tuple-element.63), channel_id=1, source_target_pairs={{0,4},{1,3},{2,6},{3,1},{4,0},{5,7},{6,2},{7,5},{8,12},{9,11},{10,... | collective-permute-start | bytes 221192 | tf_op jit(solution)/shard_map/ppermute | solution.py:365
  35.5 6.6 %collective-permute-start.14 = (bf16[2,3,3,16,128]{4,3,2,1,0:T(8,128)(2,1)S(1)}, bf16[2,3,3,16,128]{4,3,2,1,0:T(8,128)(2,1)S(1)}, u32[]{:S(2)}, u32[]{:S(2)}) collective-permute-start(bf16[2,3,3,16,128]{4,3,2,1,0:T(8,128)(2,1)S(1)} %add_convert_fusion.1), channel_id=1, source_target_pairs={{0,8},{1,9},{2,10},{3,11},{4,12},{5,13},{6,14},{7,15},{8,0},{9,1},... | collective-permute-start | bytes 221192 | tf_op jit(solution)/shard_map/ppermute | solution.py:365
  42.1 5.4 %collective-permute-start.17 = (bf16[2,3,3,16,128]{4,3,2,1,0:T(8,128)(2,1)S(1)}, bf16[2,3,3,16,128]{4,3,2,1,0:T(8,128)(2,1)S(1)}, u32[]{:S(2)}, u32[]{:S(2)}) collective-permute-start(bf16[2,3,3,16,128]{4,3,2,1,0:T(8,128)(2,1)S(1)} %add_convert_fusion.mine), channel_id=1, source_target_pairs={{0,6},{1,7},{2,4},{3,5},{4,2},{5,3},{6,0},{7,1},{8,14},{9,15},{10,... | collective-permute-start | bytes 221192 | tf_op jit(solution)/shard_map/ppermute | solution.py:365
  43.1 5.9 %collective-permute-start.16 = (bf16[2,3,3,16,128]{4,3,2,1,0:T(8,128)(2,1)S(1)}, bf16[2,3,3,16,128]{4,3,2,1,0:T(8,128)(2,1)S(1)}, u32[]{:S(2)}, u32[]{:S(2)}) collective-permute-start(bf16[2,3,3,16,128]{4,3,2,1,0:T(8,128)(2,1)S(1)} %add_convert_fusion.mine), channel_id=1, source_target_pairs={{0,2},{1,5},{2,0},{3,7},{4,6},{5,1},{6,4},{7,3},{8,10},{9,13},{10,... | collective-permute-start | bytes 221192 | tf_op jit(solution)/shard_map/ppermute | solution.py:365
  44.1 4.9 %collective-permute-start.15 = (bf16[2,3,3,16,128]{4,3,2,1,0:T(8,128)(2,1)S(1)}, bf16[2,3,3,16,128]{4,3,2,1,0:T(8,128)(2,1)S(1)}, u32[]{:S(2)}, u32[]{:S(2)}) collective-permute-start(bf16[2,3,3,16,128]{4,3,2,1,0:T(8,128)(2,1)S(1)} %add_convert_fusion.mine), channel_id=1, source_target_pairs={{0,4},{1,3},{2,6},{3,1},{4,0},{5,7},{6,2},{7,5},{8,12},{9,11},{10,... | collective-permute-start | bytes 221192 | tf_op jit(solution)/shard_map/ppermute | solution.py:365
  49.0 1.6 %collective-permute-start.18 = (bf16[2,3,3,64,128]{4,3,2,1,0:T(8,128)(2,1)S(1)}, bf16[2,3,3,64,128]{4,3,2,1,0:T(8,128)(2,1)S(1)}, u32[]{:S(2)}, u32[]{:S(2)}) collective-permute-start(bf16[2,3,3,64,128]{4,3,2,1,0:T(8,128)(2,1)S(1)} %shard_map.87.mine), channel_id=1, source_target_pairs={{0,1},{1,0},{2,3},{3,2},{4,5},{5,4},{6,7},{7,6},{8,9},{9,8},{10,11... | collective-permute-start | bytes 884744 | tf_op jit(solution)/shard_map/ppermute | solution.py:365

commit v18 on v17

--- a/solution.py
+++ b/solution.py
@@ -214,7 +214,7 @@
     return put
 
 
-def edge_kernel(segments, strips, g, back_other, far_pre, edge_grad):
+def far_edge_kernel(segments, strips, g, back_other, far_pre, edge_grad):
     encoder, row, even = here(segments)
     far_in = jnp.where(even, row > 0, row < strips - 1)
 
@@ -224,6 +224,19 @@
             value = g[jnp.where(even, 0, g.shape[0] - 2) + i].astype(F32) + back_other[i].astype(F32)
             value = value * slope(jnp.where(even, far_pre[i], far_pre[2 + i]))
             edge_grad[i] = masked(value, far_in).astype(BF16)
+
+
+def core_edge_kernel(segments, g, back_core, near_pre, edge_grad):
+    encoder, _, even = here(segments)
+    own = back_core.shape[0]
+
+    @pl.when(encoder)
+    def _():
+        for i in range(2):
+            returned = jnp.where(even, back_core[i].astype(F32), back_core[own - 2 + i].astype(F32))
+            value = g[jnp.where(even, g.shape[0] - 2, 0) + i].astype(F32) + returned
+            value = value * slope(jnp.where(even, near_pre[2 + i], near_pre[i]))
+            edge_grad[i] = value.astype(BF16)
 
 
 def second_kernel(segments, g, back, near_pre, far_pre, ha, hb, near, far, gw, kept, sent, ew):
@@ -255,7 +268,7 @@
 
 
 def main_kernel(
-    segments, strips, x, g, edge_grad, back_core, near_pre, near_first, far_first, e_own, gw, second, kept, sent, hw, ew
+    segments, strips, x, far_edge, core_edge, near_first, far_first, e_own, gw, second, kept, sent, hw, ew
 ):
     encoder, row, even = here(segments)
     own = x.shape[0]
@@ -264,11 +277,8 @@
     def _():
         ew[2 : own + 2] = e_own[...]
         for i in range(2):
-            place(ew, jnp.where(even, 0, own + 2) + i, edge_grad[i].astype(F32))
-            upstream = g[jnp.where(even, own + 2, 0) + i].astype(F32)
-            returned = jnp.where(even, back_core[i].astype(F32), back_core[own - 2 + i].astype(F32))
-            value = (upstream + returned) * slope(jnp.where(even, near_pre[2 + i], near_pre[i]))
-            place(ew, jnp.where(even, own + 2, 0) + i, value)
+            place(ew, jnp.where(even, 0, own + 2) + i, far_edge[i].astype(F32))
+            place(ew, jnp.where(even, own + 2, 0) + i, core_edge[i].astype(F32))
         hidden_back = conv_back(ew, 0, own + 2, second)
         for i in range(own + 2):
             value = hidden_back[i] * slope(joined_first(even, near_first, far_first, i))
@@ -415,8 +425,11 @@
     back_own = swap(back, True, same)
     back_other = swap(edge_other, True, other)
     back_core = swap(back_own, False, core)
-    (edge_grad,) = call(
-        functools.partial(edge_kernel, segments, strips), [like(2, BF16)], [], (g_rows, back_other, far_pre), 2 * 10**9
+    (far_edge,) = call(
+        functools.partial(far_edge_kernel, segments, strips), [like(2, BF16)], [], (g_rows, back_other, far_pre), 10**9
+    )
+    (core_edge,) = call(
+        functools.partial(core_edge_kernel, segments), [like(2, BF16)], [], (g_rows, back_core, near_pre), 10**6
     )
     taps = (3, 3, channels, channels)
     halves = (3, 3, channels // 2, channels)
@@ -432,7 +445,7 @@
         functools.partial(main_kernel, segments, strips),
         terms + [wide_out(own + 2)],
         [wide(own + 4)],
-        (x, g_rows, edge_grad, back_core, near_pre, near_first, far_first, e_own, gw, second),
+        (x, far_edge, core_edge, near_first, far_first, e_own, gw, second),
         work * (2 * own + 2),
     )
     input_grad, output = call(input_kernel, [like(own, BF16)] * 2, [], (hw, main, out), work * own)
@@ -446,7 +459,7 @@
 
     bits = strips.bit_length() - 1
     quarter = (2, 3, 3, channels // 8, channels)
-    (total2,) = call(sum_kernel, [jax.ShapeDtypeStruct(halves, F32)], [], (kept2, jump(sent2, 0)), 10**9)
+    (total2,) = call(sum_kernel, [jax.ShapeDtypeStruct(halves, F32)], [], (kept2, jump(sent2, 0)), 6 * 10**9)
     got1 = jump(sent1, 0)
     mine, *sends = call(
         pack_kernel,

time: 51.9 us -> 50.6 us (0.975)
  starting transfers between devices: 21.8 us -> 20.6 us
    ppermute x19, starting transfers between devices: 21.8 us -> 20.6 us  [swap(): return lax.ppermute(array, ('segment', 'rows'), pairs)]
    pallas_call x14 -> x15, Pallas kernels: 6.9 us -> 6.94 us  [call(): pl.pallas_call(kernel, out_shape=outs, in_specs=[pl.BlockSpec(memory_spac...]
where the time goes in v18:
time: 50.6 us; the launch traced here: 50.4 us
  waiting for transfers between devices  22 us (43%)
  starting transfers between devices  20.6 us (41%)
  Pallas kernels  6.94 us (14%)
  between operations  0.79 us (2%)
    ppermute x19, waiting for transfers between devices, swap(): return lax.ppermute(array, ('segment', 'rows'), pairs)  22 us
    ppermute x19, starting transfers between devices, swap(): return lax.ppermute(array, ('segment', 'rows'), pairs)  20.6 us
    pallas_call x15, Pallas kernels, call(): pl.pallas_call(kernel, out_shape=outs, in_specs=[pl.BlockSpec(memory_spac...  6.94 us
  transfers between devices with their start and end apart: 19, of which 14 were waited for; matrix products, arithmetic and copies ran while one was open for 0% of the time, Pallas kernels for 11%

profile of v18, /device:TPU:0, one launch (start us, length us, event | category | flops | bytes accessed | tf_op | source)
XLA Modules:
  0.0 50.4 jit_solution(11255608623550460925)
XLA Ops:
  0.6 0.5 %collective-permute-start.1 = (bf16[4,128,128]{2,1,0:T(8,128)(2,1)}, bf16[4,128,128]{2,1,0:T(8,128)(2,1)S(1)}, u32[]{:S(2)}, u32[]{:S(2)}) collective-permute-start(bf16[4,128,128]{2,1,0:T(8,128)(2,1)} %bitcast.16), channel_id=1, source_target_pairs={{0,1},{1,0},{2,3},{3,2},{4,5},{5,4},{6,7},{7,6},{8,9},{9,8},{10,11... | collective-permute-start | bytes 393224 | tf_op jit(solution)/shard_map/ppermute | solution.py:375
  1.3 1.1 %collective-permute-done.1.x_core = bf16[4,128,128]{2,1,0:T(8,128)(2,1)S(1)} collective-permute-done((bf16[4,128,128]{2,1,0:T(8,128)(2,1)}, bf16[4,128,128]{2,1,0:T(8,128)(2,1)S(1)}, u32[]{:S(2)}, u32[]{:S(2)}) %collective-permute-start.1) | collective-permute-done | bytes 131104 | tf_op jit(solution)/shard_map/ppermute | solution.py:375
  2.3 2.8 %collective-permute-start.3 = (bf16[4,128,128]{2,1,0:T(8,128)(2,1)S(1)}, bf16[4,128,128]{2,1,0:T(8,128)(2,1)S(1)}, u32[]{:S(2)}, u32[]{:S(2)}) collective-permute-start(bf16[4,128,128]{2,1,0:T(8,128)(2,1)S(1)} %collective-permute-done.1.x_core), channel_id=1, source_target_pairs={{0,2},{1,0},{2,4},{3,1},{4,6},{5,3},{6,8},{7,5},{8,10},{9,7},{10,1... | collective-permute-start | bytes 393224 | tf_op jit(solution)/shard_map/ppermute | solution.py:375
  5.2 1.3 %shard_map.76 = (bf16[8,128,384]{2,1,0:T(8,128)(2,1)S(1)}, f32[6,128,128]{2,1,0:T(8,128)S(1)}, bf16[6,128,384]{2,1,0:T(8,128)(2,1)S(1)}, f32[4,128,128]{2,1,0:T(8,128)S(1)}, bf16[4,128,128]{2,1,0:T(8,128)(2,1)S(1)}) custom-call(f32[8,128]{1,0:T(8,128)S(1)} %shard_map.75.token, bf16[4,128,128]{2,1,0:T(8,128)(2,1)S(1)} %bitcast.17, ...), custom_call_target="tpu_custom_call" | custom-call | flops 377487360 | bytes 3018752 | tf_op jit(solution)/shard_map/pallas_call | solution.py:338
  6.5 1.6 %collective-permute-start.2 = (bf16[2,128,128]{2,1,0:T(8,128)(2,1)S(1)}, bf16[2,128,128]{2,1,0:T(8,128)(2,1)S(1)}, u32[]{:S(2)}, u32[]{:S(2)}) collective-permute-start(bf16[2,128,128]{2,1,0:T(8,128)(2,1)S(1)} %slice_select_fusion), channel_id=1, source_target_pairs={{0,2},{1,0},{2,4},{3,1},{4,6},{5,3},{6,8},{7,5},{8,10},{9,7},{10,1... | collective-permute-start | bytes 196616 | tf_op jit(solution)/shard_map/ppermute | solution.py:375
  8.1 1.0 %collective-permute-start.5 = (bf16[4,128,128]{2,1,0:T(8,128)(2,1)S(1)}, bf16[4,128,128]{2,1,0:T(8,128)(2,1)S(1)}, u32[]{:S(2)}, u32[]{:S(2)}) collective-permute-start(bf16[4,128,128]{2,1,0:T(8,128)(2,1)S(1)} %get-tuple-element.39.near_here), channel_id=1, source_target_pairs={{0,16},{1,17},{2,18},{3,19},{4,20},{5,21},{6,22},{7,23},{8,24},{9,... | collective-permute-start | bytes 393224 | tf_op jit(solution)/shard_map/ppermute | solution.py:375
  9.1 0.6 %collective-permute-done.3.x_far = bf16[4,128,128]{2,1,0:T(8,128)(2,1)S(1)} collective-permute-done((bf16[4,128,128]{2,1,0:T(8,128)(2,1)S(1)}, bf16[4,128,128]{2,1,0:T(8,128)(2,1)S(1)}, u32[]{:S(2)}, u32[]{:S(2)}) %collective-permute-start.3) | collective-permute-done | bytes 131104 | tf_op jit(solution)/shard_map/ppermute | solution.py:375
  9.8 1.2 %shard_map.78 = (f32[4,128,128]{2,1,0:T(8,128)S(1)}, f32[4,128,128]{2,1,0:T(8,128)S(1)}, bf16[4,128,128]{2,1,0:T(8,128)(2,1)S(1)}, bf16[6,128,384]{2,1,0:T(8,128)(2,1)S(1)}) custom-call(bf16[8,128,384]{2,1,0:T(8,128)(2,1)S(1)} %get-tuple-element.40.xa, bf16[6,128,384]{2,1,0:T(8,128)(2,1)S(1)} %get-tuple-element.41.ha, ...), custom_call_target="tpu_custom_call" | custom-call | flops 301989888 | bytes 3342336 | tf_op jit(solution)/shard_map/pallas_call | solution.py:338
  11.0 1.0 %collective-permute-start.4 = (bf16[4,128,128]{2,1,0:T(8,128)(2,1)S(1)}, bf16[4,128,128]{2,1,0:T(8,128)(2,1)S(1)}, u32[]{:S(2)}, u32[]{:S(2)}) collective-permute-start(bf16[4,128,128]{2,1,0:T(8,128)(2,1)S(1)} %get-tuple-element.42.far_here), channel_id=1, source_target_pairs={{0,16},{1,17},{2,18},{3,19},{4,20},{5,21},{6,22},{7,23},{8,24},{9,... | collective-permute-start | bytes 393224 | tf_op jit(solution)/shard_map/ppermute | solution.py:375
  12.0 2.5 %collective-permute-done.5.near = bf16[4,128,128]{2,1,0:T(8,128)(2,1)S(1)} collective-permute-done((bf16[4,128,128]{2,1,0:T(8,128)(2,1)S(1)}, bf16[4,128,128]{2,1,0:T(8,128)(2,1)S(1)}, u32[]{:S(2)}, u32[]{:S(2)}) %collective-permute-start.5) | collective-permute-done | bytes 131104 | tf_op jit(solution)/shard_map/ppermute | solution.py:375
  14.5 1.6 %collective-permute-done.4.far = bf16[4,128,128]{2,1,0:T(8,128)(2,1)S(1)} collective-permute-done((bf16[4,128,128]{2,1,0:T(8,128)(2,1)S(1)}, bf16[4,128,128]{2,1,0:T(8,128)(2,1)S(1)}, u32[]{:S(2)}, u32[]{:S(2)}) %collective-permute-start.4) | collective-permute-done | bytes 131104 | tf_op jit(solution)/shard_map/ppermute | solution.py:375
  16.1 2.4 %collective-permute-start.7 = (bf16[4,128,128]{2,1,0:T(8,128)(2,1)S(1)}, bf16[4,128,128]{2,1,0:T(8,128)(2,1)S(1)}, u32[]{:S(2)}, u32[]{:S(2)}) collective-permute-start(bf16[4,128,128]{2,1,0:T(8,128)(2,1)S(1)} %get-tuple-element.47), channel_id=1, source_target_pairs={{0,16},{1,17},{2,18},{3,19},{4,20},{5,21},{6,22},{7,23},{8,24},{9,... | collective-permute-start | bytes 393224 | tf_op jit(solution)/shard_map/ppermute | solution.py:375
  18.5 2.9 %collective-permute-done.7.back = bf16[4,128,128]{2,1,0:T(8,128)(2,1)S(1)} collective-permute-done((bf16[4,128,128]{2,1,0:T(8,128)(2,1)S(1)}, bf16[4,128,128]{2,1,0:T(8,128)(2,1)S(1)}, u32[]{:S(2)}, u32[]{:S(2)}) %collective-permute-start.7) | collective-permute-done | bytes 131104 | tf_op jit(solution)/shard_map/ppermute | solution.py:375
  21.4 0.7 %shard_map.83 = (f32[3,3,64,128]{3,2,1,0:T(8,128)S(1)}, bf16[3,3,64,128]{3,2,1,0:T(8,128)(2,1)S(1)}, bf16[4,128,384]{2,1,0:T(8,128)(2,1)S(1)}) custom-call(bf16[8,128,128]{2,1,0:T(8,128)(2,1)S(1)} %shard_map.77.g, bf16[4,128,128]{2,1,0:T(8,128)(2,1)S(1)} %collective-permute-done.7.back, f32[4,128,128]{2,1,0:T(8,128)S(1)} %get-tuple-element.48.near_pre, ...), custom_call_target="tpu_custom_call" | custom-call | flops 150994944 | bytes 3784704 | tf_op jit(solution)/shard_map/pallas_call | solution.py:338
  22.1 0.6 %collective-permute-start.10 = (bf16[3,3,64,128]{3,2,1,0:T(8,128)(2,1)S(1)}, bf16[3,3,64,128]{3,2,1,0:T(8,128)(2,1)S(1)}, u32[]{:S(2)}, u32[]{:S(2)}) collective-permute-start(bf16[3,3,64,128]{3,2,1,0:T(8,128)(2,1)S(1)} %get-tuple-element.59), channel_id=1, source_target_pairs={{0,1},{1,0},{2,3},{3,2},{4,5},{5,4},{6,7},{7,6},{8,9},{9,8},{10,11... | collective-permute-start | bytes 442376 | tf_op jit(solution)/shard_map/ppermute | solution.py:375
  22.7 0.7 %collective-permute-done.6.back_other = bf16[2,128,128]{2,1,0:T(8,128)(2,1)S(1)} collective-permute-done((bf16[2,128,128]{2,1,0:T(8,128)(2,1)S(1)}, bf16[2,128,128]{2,1,0:T(8,128)(2,1)S(1)}, u32[]{:S(2)}, u32[]{:S(2)}) %collective-permute-start.6) | collective-permute-done | bytes 65568 | tf_op jit(solution)/shard_map/ppermute | solution.py:375
  23.6 1.2 %shard_map.84 = (f32[3,3,64,128]{3,2,1,0:T(8,128)S(1)}, bf16[3,3,64,128]{3,2,1,0:T(8,128)(2,1)S(1)}, bf16[6,128,384]{2,1,0:T(8,128)(2,1)S(1)}) custom-call(bf16[4,128,128]{2,1,0:T(8,128)(2,1)S(1)} %bitcast.18, bf16[2,128,128]{2,1,0:T(8,128)(2,1)S(1)} %shard_map.81.far_edge, bf16[2,128,128]{2,1,0:T(8,128)(2,1)S(1)} %shard_map.82.core_edge, ...), custom_call_target="tpu_custom_call" | custom-call | flops 377487360 | bytes 3227648 | tf_op jit(solution)/shard_map/pallas_call | solution.py:338
  24.9 1.3 %collective-permute-done.9.got1 = bf16[3,3,64,128]{3,2,1,0:T(8,128)(2,1)S(1)} collective-permute-done((bf16[3,3,64,128]{3,2,1,0:T(8,128)(2,1)S(1)}, bf16[3,3,64,128]{3,2,1,0:T(8,128)(2,1)S(1)}, u32[]{:S(2)}, u32[]{:S(2)}) %collective-permute-start.9) | collective-permute-done | bytes 147488 | tf_op jit(solution)/shard_map/ppermute | solution.py:375
  26.3 3.8 %collective-permute-start.11 = (bf16[2,3,3,16,128]{4,3,2,1,0:T(8,128)(2,1)S(1)}, bf16[2,3,3,16,128]{4,3,2,1,0:T(8,128)(2,1)S(1)}, u32[]{:S(2)}, u32[]{:S(2)}) collective-permute-start(bf16[2,3,3,16,128]{4,3,2,1,0:T(8,128)(2,1)S(1)} %get-tuple-element.61), channel_id=1, source_target_pairs={{0,6},{1,7},{2,4},{3,5},{4,2},{5,3},{6,0},{7,1},{8,14},{9,15},{10,... | collective-permute-start | bytes 221192 | tf_op jit(solution)/shard_map/ppermute | solution.py:375
  30.1 0.6 %collective-permute-start.13 = (bf16[2,3,3,16,128]{4,3,2,1,0:T(8,128)(2,1)S(1)}, bf16[2,3,3,16,128]{4,3,2,1,0:T(8,128)(2,1)S(1)}, u32[]{:S(2)}, u32[]{:S(2)}) collective-permute-start(bf16[2,3,3,16,128]{4,3,2,1,0:T(8,128)(2,1)S(1)} %get-tuple-element.63), channel_id=1, source_target_pairs={{0,4},{1,3},{2,6},{3,1},{4,0},{5,7},{6,2},{7,5},{8,12},{9,11},{10,... | collective-permute-start | bytes 221192 | tf_op jit(solution)/shard_map/ppermute | solution.py:375
  30.7 2.4 %collective-permute-done.11 = bf16[2,3,3,16,128]{4,3,2,1,0:T(8,128)(2,1)S(1)} collective-permute-done((bf16[2,3,3,16,128]{4,3,2,1,0:T(8,128)(2,1)S(1)}, bf16[2,3,3,16,128]{4,3,2,1,0:T(8,128)(2,1)S(1)}, u32[]{:S(2)}, u32[]{:S(2)}) %collective-permute-start.11) | collective-permute-done | bytes 73760 | tf_op jit(solution)/shard_map/ppermute | solution.py:375
  33.1 1.4 %collective-permute-done.12 = bf16[2,3,3,16,128]{4,3,2,1,0:T(8,128)(2,1)S(1)} collective-permute-done((bf16[2,3,3,16,128]{4,3,2,1,0:T(8,128)(2,1)S(1)}, bf16[2,3,3,16,128]{4,3,2,1,0:T(8,128)(2,1)S(1)}, u32[]{:S(2)}, u32[]{:S(2)}) %collective-permute-start.12) | collective-permute-done | bytes 73760 | tf_op jit(solution)/shard_map/ppermute | solution.py:375
  34.5 2.4 %collective-permute-start.14 = (bf16[2,3,3,16,128]{4,3,2,1,0:T(8,128)(2,1)S(1)}, bf16[2,3,3,16,128]{4,3,2,1,0:T(8,128)(2,1)S(1)}, u32[]{:S(2)}, u32[]{:S(2)}) collective-permute-start(bf16[2,3,3,16,128]{4,3,2,1,0:T(8,128)(2,1)S(1)} %add_convert_fusion.1), channel_id=1, source_target_pairs={{0,8},{1,9},{2,10},{3,11},{4,12},{5,13},{6,14},{7,15},{8,0},{9,1},... | collective-permute-start | bytes 221192 | tf_op jit(solution)/shard_map/ppermute | solution.py:375
  37.0 4.4 %collective-permute-done.14 = bf16[2,3,3,16,128]{4,3,2,1,0:T(8,128)(2,1)S(1)} collective-permute-done((bf16[2,3,3,16,128]{4,3,2,1,0:T(8,128)(2,1)S(1)}, bf16[2,3,3,16,128]{4,3,2,1,0:T(8,128)(2,1)S(1)}, u32[]{:S(2)}, u32[]{:S(2)}) %collective-permute-start.14) | collective-permute-done | bytes 73760 | tf_op jit(solution)/shard_map/ppermute | solution.py:375
  41.4 0.9 %collective-permute-start.17 = (bf16[2,3,3,16,128]{4,3,2,1,0:T(8,128)(2,1)S(1)}, bf16[2,3,3,16,128]{4,3,2,1,0:T(8,128)(2,1)S(1)}, u32[]{:S(2)}, u32[]{:S(2)}) collective-permute-start(bf16[2,3,3,16,128]{4,3,2,1,0:T(8,128)(2,1)S(1)} %add_convert_fusion.mine), channel_id=1, source_target_pairs={{0,6},{1,7},{2,4},{3,5},{4,2},{5,3},{6,0},{7,1},{8,14},{9,15},{10,... | collective-permute-start | bytes 221192 | tf_op jit(solution)/shard_map/ppermute | solution.py:375
  42.3 0.8 %collective-permute-start.16 = (bf16[2,3,3,16,128]{4,3,2,1,0:T(8,128)(2,1)S(1)}, bf16[2,3,3,16,128]{4,3,2,1,0:T(8,128)(2,1)S(1)}, u32[]{:S(2)}, u32[]{:S(2)}) collective-permute-start(bf16[2,3,3,16,128]{4,3,2,1,0:T(8,128)(2,1)S(1)} %add_convert_fusion.mine), channel_id=1, source_target_pairs={{0,2},{1,5},{2,0},{3,7},{4,6},{5,1},{6,4},{7,3},{8,10},{9,13},{10,... | collective-permute-start | bytes 221192 | tf_op jit(solution)/shard_map/ppermute | solution.py:375
  43.1 1.8 %collective-permute-start.15 = (bf16[2,3,3,16,128]{4,3,2,1,0:T(8,128)(2,1)S(1)}, bf16[2,3,3,16,128]{4,3,2,1,0:T(8,128)(2,1)S(1)}, u32[]{:S(2)}, u32[]{:S(2)}) collective-permute-start(bf16[2,3,3,16,128]{4,3,2,1,0:T(8,128)(2,1)S(1)} %add_convert_fusion.mine), channel_id=1, source_target_pairs={{0,4},{1,3},{2,6},{3,1},{4,0},{5,7},{6,2},{7,5},{8,12},{9,11},{10,... | collective-permute-start | bytes 221192 | tf_op jit(solution)/shard_map/ppermute | solution.py:375
  45.0 1.9 %collective-permute-done.17.rest_2_ = bf16[2,3,3,16,128]{4,3,2,1,0:T(8,128)(2,1)S(1)} collective-permute-done((bf16[2,3,3,16,128]{4,3,2,1,0:T(8,128)(2,1)S(1)}, bf16[2,3,3,16,128]{4,3,2,1,0:T(8,128)(2,1)S(1)}, u32[]{:S(2)}, u32[]{:S(2)}) %collective-permute-start.17) | collective-permute-done | bytes 73760 | tf_op jit(solution)/shard_map/ppermute | solution.py:375
  46.8 0.6 %collective-permute-done.16.rest_1_ = bf16[2,3,3,16,128]{4,3,2,1,0:T(8,128)(2,1)S(1)} collective-permute-done((bf16[2,3,3,16,128]{4,3,2,1,0:T(8,128)(2,1)S(1)}, bf16[2,3,3,16,128]{4,3,2,1,0:T(8,128)(2,1)S(1)}, u32[]{:S(2)}, u32[]{:S(2)}) %collective-permute-start.16) | collective-permute-done | bytes 73760 | tf_op jit(solution)/shard_map/ppermute | solution.py:375
  47.8 1.1 %shard_map.85 = (bf16[4,128,128]{2,1,0:T(8,128)(2,1)}, bf16[4,128,128]{2,1,0:T(8,128)(2,1)}) custom-call(bf16[6,128,384]{2,1,0:T(8,128)(2,1)S(1)} %get-tuple-element.52.hw, bf16[3,3,128,128]{3,2,1,0:T(8,128)(2,1)S(1)} %bitcast.15, bf16[4,128,128]{2,1,0:T(8,128)(2,1)S(1)} %get-tuple-element.53.out), custom_call_target="tpu_custom_call" | custom-call | flops 150994944 | bytes 1277952 | tf_op jit(solution)/shard_map/pallas_call | solution.py:338
  48.9 0.4 collective-permute-done.18.theirs
  49.3 1.1 %shard_map.89 = (f32[3,3,128,128]{3,2,1,0:T(8,128)}, f32[3,3,128,128]{3,2,1,0:T(8,128)}) custom-call(bf16[2,3,3,64,128]{4,3,2,1,0:T(8,128)(2,1)S(1)} %shard_map.88.mine, bf16[2,3,3,64,128]{4,3,2,1,0:T(8,128)(2,1)S(1)} %collective-permute-done.18.theirs), custom_call_target="tpu_custom_call" | custom-call | flops 73728 | bytes 1769472 | tf_op jit(solution)/shard_map/pallas_call | solution.py:338
  (32 shorter events, 0.9 us)
Async XLA Ops:
  0.6 1.7 %collective-permute-start.1 = (bf16[4,128,128]{2,1,0:T(8,128)(2,1)}, bf16[4,128,128]{2,1,0:T(8,128)(2,1)S(1)}, u32[]{:S(2)}, u32[]{:S(2)}) collective-permute-start(bf16[4,128,128]{2,1,0:T(8,128)(2,1)} %bitcast.16), channel_id=1, source_target_pairs={{0,1},{1,0},{2,3},{3,2},{4,5},{5,4},{6,7},{7,6},{8,9},{9,8},{10,11... | collective-permute-start | bytes 393224 | tf_op jit(solution)/shard_map/ppermute | solution.py:375
  1.1 4.1 %copy-start = (bf16[1,3,3,128,128]{4,3,2,1,0:T(8,128)(2,1)S(1)}, bf16[1,3,3,128,128]{4,3,2,1,0:T(8,128)(2,1)}, u32[]{:S(2)}) copy-start(bf16[1,3,3,128,128]{4,3,2,1,0:T(8,128)(2,1)} %param.7) | copy-start | bytes 884740
  1.2 4.1 %copy-start.1 = (bf16[1,3,3,128,128]{4,3,2,1,0:T(8,128)(2,1)S(1)}, bf16[1,3,3,128,128]{4,3,2,1,0:T(8,128)(2,1)}, u32[]{:S(2)}) copy-start(bf16[1,3,3,128,128]{4,3,2,1,0:T(8,128)(2,1)} %param.6) | copy-start | bytes 884740
  1.2 4.0 %collective-permute-start = (bf16[4,128,128]{2,1,0:T(8,128)(2,1)}, bf16[4,128,128]{2,1,0:T(8,128)(2,1)S(1)}, u32[]{:S(2)}, u32[]{:S(2)}) collective-permute-start(bf16[4,128,128]{2,1,0:T(8,128)(2,1)} %bitcast.19), channel_id=1, source_target_pairs={{0,1},{1,0},{2,3},{3,2},{4,5},{5,4},{6,7},{7,6},{8,9},{9,8},{10,11... | collective-permute-start | bytes 393224 | tf_op jit(solution)/shard_map/ppermute | solution.py:375
  1.3 4.0 %copy-start.2 = (bf16[1,4,128,128]{3,2,1,0:T(8,128)(2,1)S(1)}, bf16[1,4,128,128]{3,2,1,0:T(8,128)(2,1)}, u32[]{:S(2)}) copy-start(bf16[1,4,128,128]{3,2,1,0:T(8,128)(2,1)} %param.4) | copy-start | bytes 393220
  2.3 7.4 %collective-permute-start.3 = (bf16[4,128,128]{2,1,0:T(8,128)(2,1)S(1)}, bf16[4,128,128]{2,1,0:T(8,128)(2,1)S(1)}, u32[]{:S(2)}, u32[]{:S(2)}) collective-permute-start(bf16[4,128,128]{2,1,0:T(8,128)(2,1)S(1)} %collective-permute-done.1.x_core), channel_id=1, source_target_pairs={{0,2},{1,0},{2,4},{3,1},{4,6},{5,3},{6,8},{7,5},{8,10},{9,7},{10,1... | collective-permute-start | bytes 393224 | tf_op jit(solution)/shard_map/ppermute | solution.py:375
  6.5 5.5 %collective-permute-start.2 = (bf16[2,128,128]{2,1,0:T(8,128)(2,1)S(1)}, bf16[2,128,128]{2,1,0:T(8,128)(2,1)S(1)}, u32[]{:S(2)}, u32[]{:S(2)}) collective-permute-start(bf16[2,128,128]{2,1,0:T(8,128)(2,1)S(1)} %slice_select_fusion), channel_id=1, source_target_pairs={{0,2},{1,0},{2,4},{3,1},{4,6},{5,3},{6,8},{7,5},{8,10},{9,7},{10,1... | collective-permute-start | bytes 196616 | tf_op jit(solution)/shard_map/ppermute | solution.py:375
  8.1 6.4 %collective-permute-start.5 = (bf16[4,128,128]{2,1,0:T(8,128)(2,1)S(1)}, bf16[4,128,128]{2,1,0:T(8,128)(2,1)S(1)}, u32[]{:S(2)}, u32[]{:S(2)}) collective-permute-start(bf16[4,128,128]{2,1,0:T(8,128)(2,1)S(1)} %get-tuple-element.39.near_here), channel_id=1, source_target_pairs={{0,16},{1,17},{2,18},{3,19},{4,20},{5,21},{6,22},{7,23},{8,24},{9,... | collective-permute-start | bytes 393224 | tf_op jit(solution)/shard_map/ppermute | solution.py:375
  9.8 2.2 %copy-start.3 = (bf16[1,4,128,128]{3,2,1,0:T(8,128)(2,1)S(1)}, bf16[1,4,128,128]{3,2,1,0:T(8,128)(2,1)}, u32[]{:S(2)}) copy-start(bf16[1,4,128,128]{3,2,1,0:T(8,128)(2,1)} %param.5) | copy-start | bytes 393220
  11.0 5.0 %collective-permute-start.4 = (bf16[4,128,128]{2,1,0:T(8,128)(2,1)S(1)}, bf16[4,128,128]{2,1,0:T(8,128)(2,1)S(1)}, u32[]{:S(2)}, u32[]{:S(2)}) collective-permute-start(bf16[4,128,128]{2,1,0:T(8,128)(2,1)S(1)} %get-tuple-element.42.far_here), channel_id=1, source_target_pairs={{0,16},{1,17},{2,18},{3,19},{4,20},{5,21},{6,22},{7,23},{8,24},{9,... | collective-permute-start | bytes 393224 | tf_op jit(solution)/shard_map/ppermute | solution.py:375
  16.1 5.3 %collective-permute-start.7 = (bf16[4,128,128]{2,1,0:T(8,128)(2,1)S(1)}, bf16[4,128,128]{2,1,0:T(8,128)(2,1)S(1)}, u32[]{:S(2)}, u32[]{:S(2)}) collective-permute-start(bf16[4,128,128]{2,1,0:T(8,128)(2,1)S(1)} %get-tuple-element.47), channel_id=1, source_target_pairs={{0,16},{1,17},{2,18},{3,19},{4,20},{5,21},{6,22},{7,23},{8,24},{9,... | collective-permute-start | bytes 393224 | tf_op jit(solution)/shard_map/ppermute | solution.py:375
  18.5 4.9 %collective-permute-start.6 = (bf16[2,128,128]{2,1,0:T(8,128)(2,1)S(1)}, bf16[2,128,128]{2,1,0:T(8,128)(2,1)S(1)}, u32[]{:S(2)}, u32[]{:S(2)}) collective-permute-start(bf16[2,128,128]{2,1,0:T(8,128)(2,1)S(1)} %get-tuple-element.45), channel_id=1, source_target_pairs={{0,16},{1,18},{2,17},{3,20},{4,19},{5,22},{6,21},{7,24},{8,23},{9,... | collective-permute-start | bytes 196616 | tf_op jit(solution)/shard_map/ppermute | solution.py:375
  21.4 2.1 %collective-permute-start.8 = (bf16[4,128,128]{2,1,0:T(8,128)(2,1)S(1)}, bf16[4,128,128]{2,1,0:T(8,128)(2,1)S(1)}, u32[]{:S(2)}, u32[]{:S(2)}) collective-permute-start(bf16[4,128,128]{2,1,0:T(8,128)(2,1)S(1)} %collective-permute-done.7.back), channel_id=1, source_target_pairs={{0,1},{1,0},{2,3},{3,2},{4,5},{5,4},{6,7},{7,6},{8,9},{9,8},{10,11... | collective-permute-start | bytes 393224 | tf_op jit(solution)/shard_map/ppermute | solution.py:375
  22.1 2.8 %collective-permute-start.10 = (bf16[3,3,64,128]{3,2,1,0:T(8,128)(2,1)S(1)}, bf16[3,3,64,128]{3,2,1,0:T(8,128)(2,1)S(1)}, u32[]{:S(2)}, u32[]{:S(2)}) collective-permute-start(bf16[3,3,64,128]{3,2,1,0:T(8,128)(2,1)S(1)} %get-tuple-element.59), channel_id=1, source_target_pairs={{0,1},{1,0},{2,3},{3,2},{4,5},{5,4},{6,7},{7,6},{8,9},{9,8},{10,11... | collective-permute-start | bytes 442376 | tf_op jit(solution)/shard_map/ppermute | solution.py:375
  24.8 1.4 %collective-permute-start.9 = (bf16[3,3,64,128]{3,2,1,0:T(8,128)(2,1)S(1)}, bf16[3,3,64,128]{3,2,1,0:T(8,128)(2,1)S(1)}, u32[]{:S(2)}, u32[]{:S(2)}) collective-permute-start(bf16[3,3,64,128]{3,2,1,0:T(8,128)(2,1)S(1)} %get-tuple-element.57), channel_id=1, source_target_pairs={{0,1},{1,0},{2,3},{3,2},{4,5},{5,4},{6,7},{7,6},{8,9},{9,8},{10,11... | collective-permute-start | bytes 442376 | tf_op jit(solution)/shard_map/ppermute | solution.py:375
  26.3 6.8 %collective-permute-start.11 = (bf16[2,3,3,16,128]{4,3,2,1,0:T(8,128)(2,1)S(1)}, bf16[2,3,3,16,128]{4,3,2,1,0:T(8,128)(2,1)S(1)}, u32[]{:S(2)}, u32[]{:S(2)}) collective-permute-start(bf16[2,3,3,16,128]{4,3,2,1,0:T(8,128)(2,1)S(1)} %get-tuple-element.61), channel_id=1, source_target_pairs={{0,6},{1,7},{2,4},{3,5},{4,2},{5,3},{6,0},{7,1},{8,14},{9,15},{10,... | collective-permute-start | bytes 221192 | tf_op jit(solution)/shard_map/ppermute | solution.py:375
  30.1 4.4 %collective-permute-start.12 = (bf16[2,3,3,16,128]{4,3,2,1,0:T(8,128)(2,1)S(1)}, bf16[2,3,3,16,128]{4,3,2,1,0:T(8,128)(2,1)S(1)}, u32[]{:S(2)}, u32[]{:S(2)}) collective-permute-start(bf16[2,3,3,16,128]{4,3,2,1,0:T(8,128)(2,1)S(1)} %get-tuple-element.62), channel_id=1, source_target_pairs={{0,2},{1,5},{2,0},{3,7},{4,6},{5,1},{6,4},{7,3},{8,10},{9,13},{10,... | collective-permute-start | bytes 221192 | tf_op jit(solution)/shard_map/ppermute | solution.py:375
  30.1 4.4 %collective-permute-start.13 = (bf16[2,3,3,16,128]{4,3,2,1,0:T(8,128)(2,1)S(1)}, bf16[2,3,3,16,128]{4,3,2,1,0:T(8,128)(2,1)S(1)}, u32[]{:S(2)}, u32[]{:S(2)}) collective-permute-start(bf16[2,3,3,16,128]{4,3,2,1,0:T(8,128)(2,1)S(1)} %get-tuple-element.63), channel_id=1, source_target_pairs={{0,4},{1,3},{2,6},{3,1},{4,0},{5,7},{6,2},{7,5},{8,12},{9,11},{10,... | collective-permute-start | bytes 221192 | tf_op jit(solution)/shard_map/ppermute | solution.py:375
  34.5 6.8 %collective-permute-start.14 = (bf16[2,3,3,16,128]{4,3,2,1,0:T(8,128)(2,1)S(1)}, bf16[2,3,3,16,128]{4,3,2,1,0:T(8,128)(2,1)S(1)}, u32[]{:S(2)}, u32[]{:S(2)}) collective-permute-start(bf16[2,3,3,16,128]{4,3,2,1,0:T(8,128)(2,1)S(1)} %add_convert_fusion.1), channel_id=1, source_target_pairs={{0,8},{1,9},{2,10},{3,11},{4,12},{5,13},{6,14},{7,15},{8,0},{9,1},... | collective-permute-start | bytes 221192 | tf_op jit(solution)/shard_map/ppermute | solution.py:375
  41.4 5.4 %collective-permute-start.17 = (bf16[2,3,3,16,128]{4,3,2,1,0:T(8,128)(2,1)S(1)}, bf16[2,3,3,16,128]{4,3,2,1,0:T(8,128)(2,1)S(1)}, u32[]{:S(2)}, u32[]{:S(2)}) collective-permute-start(bf16[2,3,3,16,128]{4,3,2,1,0:T(8,128)(2,1)S(1)} %add_convert_fusion.mine), channel_id=1, source_target_pairs={{0,6},{1,7},{2,4},{3,5},{4,2},{5,3},{6,0},{7,1},{8,14},{9,15},{10,... | collective-permute-start | bytes 221192 | tf_op jit(solution)/shard_map/ppermute | solution.py:375
  42.3 5.1 %collective-permute-start.16 = (bf16[2,3,3,16,128]{4,3,2,1,0:T(8,128)(2,1)S(1)}, bf16[2,3,3,16,128]{4,3,2,1,0:T(8,128)(2,1)S(1)}, u32[]{:S(2)}, u32[]{:S(2)}) collective-permute-start(bf16[2,3,3,16,128]{4,3,2,1,0:T(8,128)(2,1)S(1)} %add_convert_fusion.mine), channel_id=1, source_target_pairs={{0,2},{1,5},{2,0},{3,7},{4,6},{5,1},{6,4},{7,3},{8,10},{9,13},{10,... | collective-permute-start | bytes 221192 | tf_op jit(solution)/shard_map/ppermute | solution.py:375
  43.1 4.5 %collective-permute-start.15 = (bf16[2,3,3,16,128]{4,3,2,1,0:T(8,128)(2,1)S(1)}, bf16[2,3,3,16,128]{4,3,2,1,0:T(8,128)(2,1)S(1)}, u32[]{:S(2)}, u32[]{:S(2)}) collective-permute-start(bf16[2,3,3,16,128]{4,3,2,1,0:T(8,128)(2,1)S(1)} %add_convert_fusion.mine), channel_id=1, source_target_pairs={{0,4},{1,3},{2,6},{3,1},{4,0},{5,7},{6,2},{7,5},{8,12},{9,11},{10,... | collective-permute-start | bytes 221192 | tf_op jit(solution)/shard_map/ppermute | solution.py:375
  47.7 1.6 %collective-permute-start.18 = (bf16[2,3,3,64,128]{4,3,2,1,0:T(8,128)(2,1)S(1)}, bf16[2,3,3,64,128]{4,3,2,1,0:T(8,128)(2,1)S(1)}, u32[]{:S(2)}, u32[]{:S(2)}) collective-permute-start(bf16[2,3,3,64,128]{4,3,2,1,0:T(8,128)(2,1)S(1)} %shard_map.88.mine), channel_id=1, source_target_pairs={{0,1},{1,0},{2,3},{3,2},{4,5},{5,4},{6,7},{7,6},{8,9},{9,8},{10,11... | collective-permute-start | bytes 884744 | tf_op jit(solution)/shard_map/ppermute | solution.py:375

commit v19 on v18

--- a/solution.py
+++ b/solution.py
@@ -13,7 +13,7 @@
 TAPS = [(ty, tx) for ty in range(3) for tx in range(3)]
 
 
-TURNS = ((3, 3), (1, 2), (2, 1))
+TURNS = ((3, 3), (2, 1), (1, 2))
 
 
 def silu(values):

time: 50.6 us -> 51 us (level)
  transfers between devices with their start and end apart: 19 -> 19, of which waited for: 14 -> 15; matrix products, arithmetic and copies ran while one was open for 0% -> 0% of each run, Pallas kernels for 11% -> 11%
where the time goes in v19:
time: 51 us; the launch traced here: 50.9 us
  waiting for transfers between devices  22.3 us (44%)
  starting transfers between devices  20.7 us (41%)
  Pallas kernels  6.93 us (14%)
  between operations  0.79 us (2%)
    ppermute x19, waiting for transfers between devices, swap(): return lax.ppermute(array, ('segment', 'rows'), pairs)  22.3 us
    ppermute x19, starting transfers between devices, swap(): return lax.ppermute(array, ('segment', 'rows'), pairs)  20.7 us
    pallas_call x15, Pallas kernels, call(): pl.pallas_call(kernel, out_shape=outs, in_specs=[pl.BlockSpec(memory_spac...  6.93 us
  transfers between devices with their start and end apart: 19, of which 15 were waited for; matrix products, arithmetic and copies ran while one was open for 0% of the time, Pallas kernels for 11%

profile of v19, /device:TPU:0, one launch (start us, length us, event | category | flops | bytes accessed | tf_op | source)
XLA Modules:
  0.0 50.9 jit_solution(2651820581023503260)
XLA Ops:
  0.6 0.5 %collective-permute-start.1 = (bf16[4,128,128]{2,1,0:T(8,128)(2,1)}, bf16[4,128,128]{2,1,0:T(8,128)(2,1)S(1)}, u32[]{:S(2)}, u32[]{:S(2)}) collective-permute-start(bf16[4,128,128]{2,1,0:T(8,128)(2,1)} %bitcast.16), channel_id=1, source_target_pairs={{0,1},{1,0},{2,3},{3,2},{4,5},{5,4},{6,7},{7,6},{8,9},{9,8},{10,11... | collective-permute-start | bytes 393224 | tf_op jit(solution)/shard_map/ppermute | solution.py:375
  1.3 1.1 %collective-permute-done.1.x_core = bf16[4,128,128]{2,1,0:T(8,128)(2,1)S(1)} collective-permute-done((bf16[4,128,128]{2,1,0:T(8,128)(2,1)}, bf16[4,128,128]{2,1,0:T(8,128)(2,1)S(1)}, u32[]{:S(2)}, u32[]{:S(2)}) %collective-permute-start.1) | collective-permute-done | bytes 131104 | tf_op jit(solution)/shard_map/ppermute | solution.py:375
  2.3 2.8 %collective-permute-start.3 = (bf16[4,128,128]{2,1,0:T(8,128)(2,1)S(1)}, bf16[4,128,128]{2,1,0:T(8,128)(2,1)S(1)}, u32[]{:S(2)}, u32[]{:S(2)}) collective-permute-start(bf16[4,128,128]{2,1,0:T(8,128)(2,1)S(1)} %collective-permute-done.1.x_core), channel_id=1, source_target_pairs={{0,2},{1,0},{2,4},{3,1},{4,6},{5,3},{6,8},{7,5},{8,10},{9,7},{10,1... | collective-permute-start | bytes 393224 | tf_op jit(solution)/shard_map/ppermute | solution.py:375
  5.2 1.3 %shard_map.76 = (bf16[8,128,384]{2,1,0:T(8,128)(2,1)S(1)}, f32[6,128,128]{2,1,0:T(8,128)S(1)}, bf16[6,128,384]{2,1,0:T(8,128)(2,1)S(1)}, f32[4,128,128]{2,1,0:T(8,128)S(1)}, bf16[4,128,128]{2,1,0:T(8,128)(2,1)S(1)}) custom-call(f32[8,128]{1,0:T(8,128)S(1)} %shard_map.75.token, bf16[4,128,128]{2,1,0:T(8,128)(2,1)S(1)} %bitcast.17, ...), custom_call_target="tpu_custom_call" | custom-call | flops 377487360 | bytes 3018752 | tf_op jit(solution)/shard_map/pallas_call | solution.py:338
  6.5 1.6 %collective-permute-start.2 = (bf16[2,128,128]{2,1,0:T(8,128)(2,1)S(1)}, bf16[2,128,128]{2,1,0:T(8,128)(2,1)S(1)}, u32[]{:S(2)}, u32[]{:S(2)}) collective-permute-start(bf16[2,128,128]{2,1,0:T(8,128)(2,1)S(1)} %slice_select_fusion), channel_id=1, source_target_pairs={{0,2},{1,0},{2,4},{3,1},{4,6},{5,3},{6,8},{7,5},{8,10},{9,7},{10,1... | collective-permute-start | bytes 196616 | tf_op jit(solution)/shard_map/ppermute | solution.py:375
  8.1 1.0 %collective-permute-start.5 = (bf16[4,128,128]{2,1,0:T(8,128)(2,1)S(1)}, bf16[4,128,128]{2,1,0:T(8,128)(2,1)S(1)}, u32[]{:S(2)}, u32[]{:S(2)}) collective-permute-start(bf16[4,128,128]{2,1,0:T(8,128)(2,1)S(1)} %get-tuple-element.39.near_here), channel_id=1, source_target_pairs={{0,16},{1,17},{2,18},{3,19},{4,20},{5,21},{6,22},{7,23},{8,24},{9,... | collective-permute-start | bytes 393224 | tf_op jit(solution)/shard_map/ppermute | solution.py:375
  9.1 0.6 %collective-permute-done.3.x_far = bf16[4,128,128]{2,1,0:T(8,128)(2,1)S(1)} collective-permute-done((bf16[4,128,128]{2,1,0:T(8,128)(2,1)S(1)}, bf16[4,128,128]{2,1,0:T(8,128)(2,1)S(1)}, u32[]{:S(2)}, u32[]{:S(2)}) %collective-permute-start.3) | collective-permute-done | bytes 131104 | tf_op jit(solution)/shard_map/ppermute | solution.py:375
  9.8 1.2 %shard_map.78 = (f32[4,128,128]{2,1,0:T(8,128)S(1)}, f32[4,128,128]{2,1,0:T(8,128)S(1)}, bf16[4,128,128]{2,1,0:T(8,128)(2,1)S(1)}, bf16[6,128,384]{2,1,0:T(8,128)(2,1)S(1)}) custom-call(bf16[8,128,384]{2,1,0:T(8,128)(2,1)S(1)} %get-tuple-element.40.xa, bf16[6,128,384]{2,1,0:T(8,128)(2,1)S(1)} %get-tuple-element.41.ha, ...), custom_call_target="tpu_custom_call" | custom-call | flops 301989888 | bytes 3342336 | tf_op jit(solution)/shard_map/pallas_call | solution.py:338
  11.0 1.0 %collective-permute-start.4 = (bf16[4,128,128]{2,1,0:T(8,128)(2,1)S(1)}, bf16[4,128,128]{2,1,0:T(8,128)(2,1)S(1)}, u32[]{:S(2)}, u32[]{:S(2)}) collective-permute-start(bf16[4,128,128]{2,1,0:T(8,128)(2,1)S(1)} %get-tuple-element.42.far_here), channel_id=1, source_target_pairs={{0,16},{1,17},{2,18},{3,19},{4,20},{5,21},{6,22},{7,23},{8,24},{9,... | collective-permute-start | bytes 393224 | tf_op jit(solution)/shard_map/ppermute | solution.py:375
  12.0 2.5 %collective-permute-done.5.near = bf16[4,128,128]{2,1,0:T(8,128)(2,1)S(1)} collective-permute-done((bf16[4,128,128]{2,1,0:T(8,128)(2,1)S(1)}, bf16[4,128,128]{2,1,0:T(8,128)(2,1)S(1)}, u32[]{:S(2)}, u32[]{:S(2)}) %collective-permute-start.5) | collective-permute-done | bytes 131104 | tf_op jit(solution)/shard_map/ppermute | solution.py:375
  14.5 1.6 %collective-permute-done.4.far = bf16[4,128,128]{2,1,0:T(8,128)(2,1)S(1)} collective-permute-done((bf16[4,128,128]{2,1,0:T(8,128)(2,1)S(1)}, bf16[4,128,128]{2,1,0:T(8,128)(2,1)S(1)}, u32[]{:S(2)}, u32[]{:S(2)}) %collective-permute-start.4) | collective-permute-done | bytes 131104 | tf_op jit(solution)/shard_map/ppermute | solution.py:375
  16.1 2.4 %collective-permute-start.7 = (bf16[4,128,128]{2,1,0:T(8,128)(2,1)S(1)}, bf16[4,128,128]{2,1,0:T(8,128)(2,1)S(1)}, u32[]{:S(2)}, u32[]{:S(2)}) collective-permute-start(bf16[4,128,128]{2,1,0:T(8,128)(2,1)S(1)} %get-tuple-element.47), channel_id=1, source_target_pairs={{0,16},{1,17},{2,18},{3,19},{4,20},{5,21},{6,22},{7,23},{8,24},{9,... | collective-permute-start | bytes 393224 | tf_op jit(solution)/shard_map/ppermute | solution.py:375
  18.5 2.9 %collective-permute-done.7.back = bf16[4,128,128]{2,1,0:T(8,128)(2,1)S(1)} collective-permute-done((bf16[4,128,128]{2,1,0:T(8,128)(2,1)S(1)}, bf16[4,128,128]{2,1,0:T(8,128)(2,1)S(1)}, u32[]{:S(2)}, u32[]{:S(2)}) %collective-permute-start.7) | collective-permute-done | bytes 131104 | tf_op jit(solution)/shard_map/ppermute | solution.py:375
  21.4 0.7 %shard_map.83 = (f32[3,3,64,128]{3,2,1,0:T(8,128)S(1)}, bf16[3,3,64,128]{3,2,1,0:T(8,128)(2,1)S(1)}, bf16[4,128,384]{2,1,0:T(8,128)(2,1)S(1)}) custom-call(bf16[8,128,128]{2,1,0:T(8,128)(2,1)S(1)} %shard_map.77.g, bf16[4,128,128]{2,1,0:T(8,128)(2,1)S(1)} %collective-permute-done.7.back, f32[4,128,128]{2,1,0:T(8,128)S(1)} %get-tuple-element.48.near_pre, ...), custom_call_target="tpu_custom_call" | custom-call | flops 150994944 | bytes 3784704 | tf_op jit(solution)/shard_map/pallas_call | solution.py:338
  22.1 0.6 %collective-permute-start.10 = (bf16[3,3,64,128]{3,2,1,0:T(8,128)(2,1)S(1)}, bf16[3,3,64,128]{3,2,1,0:T(8,128)(2,1)S(1)}, u32[]{:S(2)}, u32[]{:S(2)}) collective-permute-start(bf16[3,3,64,128]{3,2,1,0:T(8,128)(2,1)S(1)} %get-tuple-element.59), channel_id=1, source_target_pairs={{0,1},{1,0},{2,3},{3,2},{4,5},{5,4},{6,7},{7,6},{8,9},{9,8},{10,11... | collective-permute-start | bytes 442376 | tf_op jit(solution)/shard_map/ppermute | solution.py:375
  22.7 0.7 %collective-permute-done.6.back_other = bf16[2,128,128]{2,1,0:T(8,128)(2,1)S(1)} collective-permute-done((bf16[2,128,128]{2,1,0:T(8,128)(2,1)S(1)}, bf16[2,128,128]{2,1,0:T(8,128)(2,1)S(1)}, u32[]{:S(2)}, u32[]{:S(2)}) %collective-permute-start.6) | collective-permute-done | bytes 65568 | tf_op jit(solution)/shard_map/ppermute | solution.py:375
  23.6 1.2 %shard_map.84 = (f32[3,3,64,128]{3,2,1,0:T(8,128)S(1)}, bf16[3,3,64,128]{3,2,1,0:T(8,128)(2,1)S(1)}, bf16[6,128,384]{2,1,0:T(8,128)(2,1)S(1)}) custom-call(bf16[4,128,128]{2,1,0:T(8,128)(2,1)S(1)} %bitcast.18, bf16[2,128,128]{2,1,0:T(8,128)(2,1)S(1)} %shard_map.81.far_edge, bf16[2,128,128]{2,1,0:T(8,128)(2,1)S(1)} %shard_map.82.core_edge, ...), custom_call_target="tpu_custom_call" | custom-call | flops 377487360 | bytes 3227648 | tf_op jit(solution)/shard_map/pallas_call | solution.py:338
  24.9 1.3 %collective-permute-done.9.got1 = bf16[3,3,64,128]{3,2,1,0:T(8,128)(2,1)S(1)} collective-permute-done((bf16[3,3,64,128]{3,2,1,0:T(8,128)(2,1)S(1)}, bf16[3,3,64,128]{3,2,1,0:T(8,128)(2,1)S(1)}, u32[]{:S(2)}, u32[]{:S(2)}) %collective-permute-start.9) | collective-permute-done | bytes 147488 | tf_op jit(solution)/shard_map/ppermute | solution.py:375
  26.3 3.8 %collective-permute-start.11 = (bf16[2,3,3,16,128]{4,3,2,1,0:T(8,128)(2,1)S(1)}, bf16[2,3,3,16,128]{4,3,2,1,0:T(8,128)(2,1)S(1)}, u32[]{:S(2)}, u32[]{:S(2)}) collective-permute-start(bf16[2,3,3,16,128]{4,3,2,1,0:T(8,128)(2,1)S(1)} %get-tuple-element.61), channel_id=1, source_target_pairs={{0,6},{1,7},{2,4},{3,5},{4,2},{5,3},{6,0},{7,1},{8,14},{9,15},{10,... | collective-permute-start | bytes 221192 | tf_op jit(solution)/shard_map/ppermute | solution.py:375
  30.1 0.4 collective-permute-start.12
  30.7 2.0 %collective-permute-done.11 = bf16[2,3,3,16,128]{4,3,2,1,0:T(8,128)(2,1)S(1)} collective-permute-done((bf16[2,3,3,16,128]{4,3,2,1,0:T(8,128)(2,1)S(1)}, bf16[2,3,3,16,128]{4,3,2,1,0:T(8,128)(2,1)S(1)}, u32[]{:S(2)}, u32[]{:S(2)}) %collective-permute-start.11) | collective-permute-done | bytes 73760 | tf_op jit(solution)/shard_map/ppermute | solution.py:375
  32.7 1.7 %collective-permute-done.12 = bf16[2,3,3,16,128]{4,3,2,1,0:T(8,128)(2,1)S(1)} collective-permute-done((bf16[2,3,3,16,128]{4,3,2,1,0:T(8,128)(2,1)S(1)}, bf16[2,3,3,16,128]{4,3,2,1,0:T(8,128)(2,1)S(1)}, u32[]{:S(2)}, u32[]{:S(2)}) %collective-permute-start.12) | collective-permute-done | bytes 73760 | tf_op jit(solution)/shard_map/ppermute | solution.py:375
  34.4 0.4 collective-permute-done.13
  34.9 2.5 %collective-permute-start.14 = (bf16[2,3,3,16,128]{4,3,2,1,0:T(8,128)(2,1)S(1)}, bf16[2,3,3,16,128]{4,3,2,1,0:T(8,128)(2,1)S(1)}, u32[]{:S(2)}, u32[]{:S(2)}) collective-permute-start(bf16[2,3,3,16,128]{4,3,2,1,0:T(8,128)(2,1)S(1)} %add_convert_fusion.1), channel_id=1, source_target_pairs={{0,8},{1,9},{2,10},{3,11},{4,12},{5,13},{6,14},{7,15},{8,0},{9,1},... | collective-permute-start | bytes 221192 | tf_op jit(solution)/shard_map/ppermute | solution.py:375
  37.5 2.8 %collective-permute-done.14 = bf16[2,3,3,16,128]{4,3,2,1,0:T(8,128)(2,1)S(1)} collective-permute-done((bf16[2,3,3,16,128]{4,3,2,1,0:T(8,128)(2,1)S(1)}, bf16[2,3,3,16,128]{4,3,2,1,0:T(8,128)(2,1)S(1)}, u32[]{:S(2)}, u32[]{:S(2)}) %collective-permute-start.14) | collective-permute-done | bytes 73760 | tf_op jit(solution)/shard_map/ppermute | solution.py:375
  40.3 1.7 %collective-permute-start.17 = (bf16[2,3,3,16,128]{4,3,2,1,0:T(8,128)(2,1)S(1)}, bf16[2,3,3,16,128]{4,3,2,1,0:T(8,128)(2,1)S(1)}, u32[]{:S(2)}, u32[]{:S(2)}) collective-permute-start(bf16[2,3,3,16,128]{4,3,2,1,0:T(8,128)(2,1)S(1)} %add_convert_fusion.mine), channel_id=1, source_target_pairs={{0,6},{1,7},{2,4},{3,5},{4,2},{5,3},{6,0},{7,1},{8,14},{9,15},{10,... | collective-permute-start | bytes 221192 | tf_op jit(solution)/shard_map/ppermute | solution.py:375
  41.9 1.8 %collective-permute-start.16 = (bf16[2,3,3,16,128]{4,3,2,1,0:T(8,128)(2,1)S(1)}, bf16[2,3,3,16,128]{4,3,2,1,0:T(8,128)(2,1)S(1)}, u32[]{:S(2)}, u32[]{:S(2)}) collective-permute-start(bf16[2,3,3,16,128]{4,3,2,1,0:T(8,128)(2,1)S(1)} %add_convert_fusion.mine), channel_id=1, source_target_pairs={{0,4},{1,3},{2,6},{3,1},{4,0},{5,7},{6,2},{7,5},{8,12},{9,11},{10,... | collective-permute-start | bytes 221192 | tf_op jit(solution)/shard_map/ppermute | solution.py:375
  43.8 2.0 %collective-permute-done.17.rest_2_ = bf16[2,3,3,16,128]{4,3,2,1,0:T(8,128)(2,1)S(1)} collective-permute-done((bf16[2,3,3,16,128]{4,3,2,1,0:T(8,128)(2,1)S(1)}, bf16[2,3,3,16,128]{4,3,2,1,0:T(8,128)(2,1)S(1)}, u32[]{:S(2)}, u32[]{:S(2)}) %collective-permute-start.17) | collective-permute-done | bytes 73760 | tf_op jit(solution)/shard_map/ppermute | solution.py:375
  45.8 1.1 %collective-permute-done.16.rest_1_ = bf16[2,3,3,16,128]{4,3,2,1,0:T(8,128)(2,1)S(1)} collective-permute-done((bf16[2,3,3,16,128]{4,3,2,1,0:T(8,128)(2,1)S(1)}, bf16[2,3,3,16,128]{4,3,2,1,0:T(8,128)(2,1)S(1)}, u32[]{:S(2)}, u32[]{:S(2)}) %collective-permute-start.16) | collective-permute-done | bytes 73760 | tf_op jit(solution)/shard_map/ppermute | solution.py:375
  46.9 1.2 %collective-permute-done.15.rest_0_ = bf16[2,3,3,16,128]{4,3,2,1,0:T(8,128)(2,1)S(1)} collective-permute-done((bf16[2,3,3,16,128]{4,3,2,1,0:T(8,128)(2,1)S(1)}, bf16[2,3,3,16,128]{4,3,2,1,0:T(8,128)(2,1)S(1)}, u32[]{:S(2)}, u32[]{:S(2)}) %collective-permute-start.15) | collective-permute-done | bytes 73760 | tf_op jit(solution)/shard_map/ppermute | solution.py:375
  48.2 1.1 %shard_map.85 = (bf16[4,128,128]{2,1,0:T(8,128)(2,1)}, bf16[4,128,128]{2,1,0:T(8,128)(2,1)}) custom-call(bf16[6,128,384]{2,1,0:T(8,128)(2,1)S(1)} %get-tuple-element.52.hw, bf16[3,3,128,128]{3,2,1,0:T(8,128)(2,1)S(1)} %bitcast.15, bf16[4,128,128]{2,1,0:T(8,128)(2,1)S(1)} %get-tuple-element.53.out), custom_call_target="tpu_custom_call" | custom-call | flops 150994944 | bytes 1277952 | tf_op jit(solution)/shard_map/pallas_call | solution.py:338
  49.8 1.1 %shard_map.89 = (f32[3,3,128,128]{3,2,1,0:T(8,128)}, f32[3,3,128,128]{3,2,1,0:T(8,128)}) custom-call(bf16[2,3,3,64,128]{4,3,2,1,0:T(8,128)(2,1)S(1)} %shard_map.88.mine, bf16[2,3,3,64,128]{4,3,2,1,0:T(8,128)(2,1)S(1)} %collective-permute-done.18.theirs), custom_call_target="tpu_custom_call" | custom-call | flops 73728 | bytes 1769472 | tf_op jit(solution)/shard_map/pallas_call | solution.py:338
  (32 shorter events, 1.5 us)
Async XLA Ops:
  0.6 1.7 %collective-permute-start.1 = (bf16[4,128,128]{2,1,0:T(8,128)(2,1)}, bf16[4,128,128]{2,1,0:T(8,128)(2,1)S(1)}, u32[]{:S(2)}, u32[]{:S(2)}) collective-permute-start(bf16[4,128,128]{2,1,0:T(8,128)(2,1)} %bitcast.16), channel_id=1, source_target_pairs={{0,1},{1,0},{2,3},{3,2},{4,5},{5,4},{6,7},{7,6},{8,9},{9,8},{10,11... | collective-permute-start | bytes 393224 | tf_op jit(solution)/shard_map/ppermute | solution.py:375
  1.1 4.1 %copy-start = (bf16[1,3,3,128,128]{4,3,2,1,0:T(8,128)(2,1)S(1)}, bf16[1,3,3,128,128]{4,3,2,1,0:T(8,128)(2,1)}, u32[]{:S(2)}) copy-start(bf16[1,3,3,128,128]{4,3,2,1,0:T(8,128)(2,1)} %param.7) | copy-start | bytes 884740
  1.2 4.1 %copy-start.1 = (bf16[1,3,3,128,128]{4,3,2,1,0:T(8,128)(2,1)S(1)}, bf16[1,3,3,128,128]{4,3,2,1,0:T(8,128)(2,1)}, u32[]{:S(2)}) copy-start(bf16[1,3,3,128,128]{4,3,2,1,0:T(8,128)(2,1)} %param.6) | copy-start | bytes 884740
  1.2 4.0 %collective-permute-start = (bf16[4,128,128]{2,1,0:T(8,128)(2,1)}, bf16[4,128,128]{2,1,0:T(8,128)(2,1)S(1)}, u32[]{:S(2)}, u32[]{:S(2)}) collective-permute-start(bf16[4,128,128]{2,1,0:T(8,128)(2,1)} %bitcast.19), channel_id=1, source_target_pairs={{0,1},{1,0},{2,3},{3,2},{4,5},{5,4},{6,7},{7,6},{8,9},{9,8},{10,11... | collective-permute-start | bytes 393224 | tf_op jit(solution)/shard_map/ppermute | solution.py:375
  1.3 4.0 %copy-start.2 = (bf16[1,4,128,128]{3,2,1,0:T(8,128)(2,1)S(1)}, bf16[1,4,128,128]{3,2,1,0:T(8,128)(2,1)}, u32[]{:S(2)}) copy-start(bf16[1,4,128,128]{3,2,1,0:T(8,128)(2,1)} %param.4) | copy-start | bytes 393220
  2.3 7.4 %collective-permute-start.3 = (bf16[4,128,128]{2,1,0:T(8,128)(2,1)S(1)}, bf16[4,128,128]{2,1,0:T(8,128)(2,1)S(1)}, u32[]{:S(2)}, u32[]{:S(2)}) collective-permute-start(bf16[4,128,128]{2,1,0:T(8,128)(2,1)S(1)} %collective-permute-done.1.x_core), channel_id=1, source_target_pairs={{0,2},{1,0},{2,4},{3,1},{4,6},{5,3},{6,8},{7,5},{8,10},{9,7},{10,1... | collective-permute-start | bytes 393224 | tf_op jit(solution)/shard_map/ppermute | solution.py:375
  6.5 5.5 %collective-permute-start.2 = (bf16[2,128,128]{2,1,0:T(8,128)(2,1)S(1)}, bf16[2,128,128]{2,1,0:T(8,128)(2,1)S(1)}, u32[]{:S(2)}, u32[]{:S(2)}) collective-permute-start(bf16[2,128,128]{2,1,0:T(8,128)(2,1)S(1)} %slice_select_fusion), channel_id=1, source_target_pairs={{0,2},{1,0},{2,4},{3,1},{4,6},{5,3},{6,8},{7,5},{8,10},{9,7},{10,1... | collective-permute-start | bytes 196616 | tf_op jit(solution)/shard_map/ppermute | solution.py:375
  8.1 6.4 %collective-permute-start.5 = (bf16[4,128,128]{2,1,0:T(8,128)(2,1)S(1)}, bf16[4,128,128]{2,1,0:T(8,128)(2,1)S(1)}, u32[]{:S(2)}, u32[]{:S(2)}) collective-permute-start(bf16[4,128,128]{2,1,0:T(8,128)(2,1)S(1)} %get-tuple-element.39.near_here), channel_id=1, source_target_pairs={{0,16},{1,17},{2,18},{3,19},{4,20},{5,21},{6,22},{7,23},{8,24},{9,... | collective-permute-start | bytes 393224 | tf_op jit(solution)/shard_map/ppermute | solution.py:375
  9.8 2.2 %copy-start.3 = (bf16[1,4,128,128]{3,2,1,0:T(8,128)(2,1)S(1)}, bf16[1,4,128,128]{3,2,1,0:T(8,128)(2,1)}, u32[]{:S(2)}) copy-start(bf16[1,4,128,128]{3,2,1,0:T(8,128)(2,1)} %param.5) | copy-start | bytes 393220
  11.0 5.0 %collective-permute-start.4 = (bf16[4,128,128]{2,1,0:T(8,128)(2,1)S(1)}, bf16[4,128,128]{2,1,0:T(8,128)(2,1)S(1)}, u32[]{:S(2)}, u32[]{:S(2)}) collective-permute-start(bf16[4,128,128]{2,1,0:T(8,128)(2,1)S(1)} %get-tuple-element.42.far_here), channel_id=1, source_target_pairs={{0,16},{1,17},{2,18},{3,19},{4,20},{5,21},{6,22},{7,23},{8,24},{9,... | collective-permute-start | bytes 393224 | tf_op jit(solution)/shard_map/ppermute | solution.py:375
  16.1 5.3 %collective-permute-start.7 = (bf16[4,128,128]{2,1,0:T(8,128)(2,1)S(1)}, bf16[4,128,128]{2,1,0:T(8,128)(2,1)S(1)}, u32[]{:S(2)}, u32[]{:S(2)}) collective-permute-start(bf16[4,128,128]{2,1,0:T(8,128)(2,1)S(1)} %get-tuple-element.47), channel_id=1, source_target_pairs={{0,16},{1,17},{2,18},{3,19},{4,20},{5,21},{6,22},{7,23},{8,24},{9,... | collective-permute-start | bytes 393224 | tf_op jit(solution)/shard_map/ppermute | solution.py:375
  18.5 4.9 %collective-permute-start.6 = (bf16[2,128,128]{2,1,0:T(8,128)(2,1)S(1)}, bf16[2,128,128]{2,1,0:T(8,128)(2,1)S(1)}, u32[]{:S(2)}, u32[]{:S(2)}) collective-permute-start(bf16[2,128,128]{2,1,0:T(8,128)(2,1)S(1)} %get-tuple-element.45), channel_id=1, source_target_pairs={{0,16},{1,18},{2,17},{3,20},{4,19},{5,22},{6,21},{7,24},{8,23},{9,... | collective-permute-start | bytes 196616 | tf_op jit(solution)/shard_map/ppermute | solution.py:375
  21.4 2.1 %collective-permute-start.8 = (bf16[4,128,128]{2,1,0:T(8,128)(2,1)S(1)}, bf16[4,128,128]{2,1,0:T(8,128)(2,1)S(1)}, u32[]{:S(2)}, u32[]{:S(2)}) collective-permute-start(bf16[4,128,128]{2,1,0:T(8,128)(2,1)S(1)} %collective-permute-done.7.back), channel_id=1, source_target_pairs={{0,1},{1,0},{2,3},{3,2},{4,5},{5,4},{6,7},{7,6},{8,9},{9,8},{10,11... | collective-permute-start | bytes 393224 | tf_op jit(solution)/shard_map/ppermute | solution.py:375
  22.1 2.8 %collective-permute-start.10 = (bf16[3,3,64,128]{3,2,1,0:T(8,128)(2,1)S(1)}, bf16[3,3,64,128]{3,2,1,0:T(8,128)(2,1)S(1)}, u32[]{:S(2)}, u32[]{:S(2)}) collective-permute-start(bf16[3,3,64,128]{3,2,1,0:T(8,128)(2,1)S(1)} %get-tuple-element.59), channel_id=1, source_target_pairs={{0,1},{1,0},{2,3},{3,2},{4,5},{5,4},{6,7},{7,6},{8,9},{9,8},{10,11... | collective-permute-start | bytes 442376 | tf_op jit(solution)/shard_map/ppermute | solution.py:375
  24.8 1.4 %collective-permute-start.9 = (bf16[3,3,64,128]{3,2,1,0:T(8,128)(2,1)S(1)}, bf16[3,3,64,128]{3,2,1,0:T(8,128)(2,1)S(1)}, u32[]{:S(2)}, u32[]{:S(2)}) collective-permute-start(bf16[3,3,64,128]{3,2,1,0:T(8,128)(2,1)S(1)} %get-tuple-element.57), channel_id=1, source_target_pairs={{0,1},{1,0},{2,3},{3,2},{4,5},{5,4},{6,7},{7,6},{8,9},{9,8},{10,11... | collective-permute-start | bytes 442376 | tf_op jit(solution)/shard_map/ppermute | solution.py:375
  26.3 6.4 %collective-permute-start.11 = (bf16[2,3,3,16,128]{4,3,2,1,0:T(8,128)(2,1)S(1)}, bf16[2,3,3,16,128]{4,3,2,1,0:T(8,128)(2,1)S(1)}, u32[]{:S(2)}, u32[]{:S(2)}) collective-permute-start(bf16[2,3,3,16,128]{4,3,2,1,0:T(8,128)(2,1)S(1)} %get-tuple-element.61), channel_id=1, source_target_pairs={{0,6},{1,7},{2,4},{3,5},{4,2},{5,3},{6,0},{7,1},{8,14},{9,15},{10,... | collective-permute-start | bytes 221192 | tf_op jit(solution)/shard_map/ppermute | solution.py:375
  30.1 4.4 %collective-permute-start.12 = (bf16[2,3,3,16,128]{4,3,2,1,0:T(8,128)(2,1)S(1)}, bf16[2,3,3,16,128]{4,3,2,1,0:T(8,128)(2,1)S(1)}, u32[]{:S(2)}, u32[]{:S(2)}) collective-permute-start(bf16[2,3,3,16,128]{4,3,2,1,0:T(8,128)(2,1)S(1)} %get-tuple-element.62), channel_id=1, source_target_pairs={{0,4},{1,3},{2,6},{3,1},{4,0},{5,7},{6,2},{7,5},{8,12},{9,11},{10,... | collective-permute-start | bytes 221192 | tf_op jit(solution)/shard_map/ppermute | solution.py:375
  30.5 4.4 %collective-permute-start.13 = (bf16[2,3,3,16,128]{4,3,2,1,0:T(8,128)(2,1)S(1)}, bf16[2,3,3,16,128]{4,3,2,1,0:T(8,128)(2,1)S(1)}, u32[]{:S(2)}, u32[]{:S(2)}) collective-permute-start(bf16[2,3,3,16,128]{4,3,2,1,0:T(8,128)(2,1)S(1)} %get-tuple-element.63), channel_id=1, source_target_pairs={{0,2},{1,5},{2,0},{3,7},{4,6},{5,1},{6,4},{7,3},{8,10},{9,13},{10,... | collective-permute-start | bytes 221192 | tf_op jit(solution)/shard_map/ppermute | solution.py:375
  34.9 5.3 %collective-permute-start.14 = (bf16[2,3,3,16,128]{4,3,2,1,0:T(8,128)(2,1)S(1)}, bf16[2,3,3,16,128]{4,3,2,1,0:T(8,128)(2,1)S(1)}, u32[]{:S(2)}, u32[]{:S(2)}) collective-permute-start(bf16[2,3,3,16,128]{4,3,2,1,0:T(8,128)(2,1)S(1)} %add_convert_fusion.1), channel_id=1, source_target_pairs={{0,8},{1,9},{2,10},{3,11},{4,12},{5,13},{6,14},{7,15},{8,0},{9,1},... | collective-permute-start | bytes 221192 | tf_op jit(solution)/shard_map/ppermute | solution.py:375
  40.3 5.5 %collective-permute-start.17 = (bf16[2,3,3,16,128]{4,3,2,1,0:T(8,128)(2,1)S(1)}, bf16[2,3,3,16,128]{4,3,2,1,0:T(8,128)(2,1)S(1)}, u32[]{:S(2)}, u32[]{:S(2)}) collective-permute-start(bf16[2,3,3,16,128]{4,3,2,1,0:T(8,128)(2,1)S(1)} %add_convert_fusion.mine), channel_id=1, source_target_pairs={{0,6},{1,7},{2,4},{3,5},{4,2},{5,3},{6,0},{7,1},{8,14},{9,15},{10,... | collective-permute-start | bytes 221192 | tf_op jit(solution)/shard_map/ppermute | solution.py:375
  41.9 4.9 %collective-permute-start.16 = (bf16[2,3,3,16,128]{4,3,2,1,0:T(8,128)(2,1)S(1)}, bf16[2,3,3,16,128]{4,3,2,1,0:T(8,128)(2,1)S(1)}, u32[]{:S(2)}, u32[]{:S(2)}) collective-permute-start(bf16[2,3,3,16,128]{4,3,2,1,0:T(8,128)(2,1)S(1)} %add_convert_fusion.mine), channel_id=1, source_target_pairs={{0,4},{1,3},{2,6},{3,1},{4,0},{5,7},{6,2},{7,5},{8,12},{9,11},{10,... | collective-permute-start | bytes 221192 | tf_op jit(solution)/shard_map/ppermute | solution.py:375
  43.8 4.4 %collective-permute-start.15 = (bf16[2,3,3,16,128]{4,3,2,1,0:T(8,128)(2,1)S(1)}, bf16[2,3,3,16,128]{4,3,2,1,0:T(8,128)(2,1)S(1)}, u32[]{:S(2)}, u32[]{:S(2)}) collective-permute-start(bf16[2,3,3,16,128]{4,3,2,1,0:T(8,128)(2,1)S(1)} %add_convert_fusion.mine), channel_id=1, source_target_pairs={{0,2},{1,5},{2,0},{3,7},{4,6},{5,1},{6,4},{7,3},{8,10},{9,13},{10,... | collective-permute-start | bytes 221192 | tf_op jit(solution)/shard_map/ppermute | solution.py:375
  48.2 1.6 %collective-permute-start.18 = (bf16[2,3,3,64,128]{4,3,2,1,0:T(8,128)(2,1)S(1)}, bf16[2,3,3,64,128]{4,3,2,1,0:T(8,128)(2,1)S(1)}, u32[]{:S(2)}, u32[]{:S(2)}) collective-permute-start(bf16[2,3,3,64,128]{4,3,2,1,0:T(8,128)(2,1)S(1)} %shard_map.88.mine), channel_id=1, source_target_pairs={{0,1},{1,0},{2,3},{3,2},{4,5},{5,4},{6,7},{7,6},{8,9},{9,8},{10,11... | collective-permute-start | bytes 884744 | tf_op jit(solution)/shard_map/ppermute | solution.py:375
